TPU v7x, 32 devices: a whole 2x2x4 slice. The times are simulated.
32 devices in a mesh: batch: 4 (over y, core), space: 8 (over z, x).
Axes of the slice: x: 2, y: 2, z: 4, core: 2. Of those that a mesh axis runs over, the one named last changes fastest.
Arguments:
- small_in: bfloat16 [1280, 32, 1024], P('batch', 'space'), may hold values from -45 to 45
- large_in: bfloat16 [320, 64, 2048], P('batch', 'space'), may hold values from -45 to 45
- small_teacher: bfloat16 [1280, 32, 4096], P('batch', 'space'), may hold values from -6 to 6
- large_teacher: bfloat16 [320, 64, 8192], P('batch', 'space'), may hold values from -6 to 6
- small_groups: int32 [1280], P('batch'), may hold values from 0 to 1
- large_groups: int32 [320], P('batch'), may hold values from 0 to 1
- small_cot: bfloat16 [1280, 16, 1024], P(('batch', 'space')), may hold values from -6 to 6
- large_cot: bfloat16 [320, 32, 2048], P(('batch', 'space')), may hold values from -6 to 6
- teacher_gains: float32 [2, 128], replicated, may hold values from 0.5 to 1.5
- teacher_first: bfloat16 [3, 3, 128, 256], replicated, may hold values from -0.1875 to 0.1875
- teacher_inner: float32 [2, 256], replicated, may hold values from 0.5 to 1.5
- teacher_second: bfloat16 [3, 3, 256, 256], replicated, may hold values from -0.125 to 0.125
- teacher_bypass: bfloat16 [128, 256], replicated, may hold values from -0.5 to 0.5
- entry_norm: float32 [2, 32], replicated, may hold values from 0.5 to 1.5
- first_conv: float32 [3, 3, 32, 64], replicated, may hold values from -0.375 to 0.375
- inner_norm: float32 [2, 64], replicated, may hold values from 0.5 to 1.5
- second_conv: float32 [3, 3, 64, 64], replicated, may hold values from -0.25 to 0.25
- shortcut: float32 [32, 64], replicated, may hold values from -1 to 1
- momentum_entry: float32 [2, 32], replicated, may hold values from -3072 to 3072
- momentum_first: float32 [3, 3, 32, 64], replicated, may hold values from -1536 to 1536
- momentum_inner: float32 [2, 64], replicated, may hold values from -1536 to 1536
- momentum_second: float32 [3, 3, 64, 64], replicated, may hold values from -1536 to 1536
- momentum_shortcut: float32 [32, 64], replicated, may hold values from -1536 to 1536
- average_entry: float32 [2, 32], replicated, may hold values from 0.5 to 1.5
- average_first: float32 [3, 3, 32, 64], replicated, may hold values from -0.375 to 0.375
- average_inner: float32 [2, 64], replicated, may hold values from 0.5 to 1.5
- average_second: float32 [3, 3, 64, 64], replicated, may hold values from -0.25 to 0.25
- average_shortcut: float32 [32, 64], replicated, may hold values from -1 to 1
Outputs:
- small_out: bfloat16 [1280, 16, 1024], P(('batch', 'space'))
- large_out: bfloat16 [320, 32, 2048], P(('batch', 'space'))
- small_grad: float32 [1280, 32, 1024], P('batch', 'space')
- large_grad: float32 [320, 64, 2048], P('batch', 'space')
- transfer_loss: float32 [], replicated
- entry_grads: float32 [2, 32], replicated
- entry_velocity: float32 [2, 32], replicated
- entry_average: float32 [2, 32], replicated
- entry_updated: float32 [2, 32], replicated
- first_grads: float32 [3, 3, 32, 64], replicated
- first_velocity: float32 [3, 3, 32, 64], replicated
- first_average: float32 [3, 3, 32, 64], replicated
- first_updated: float32 [3, 3, 32, 64], replicated
- first_copy: bfloat16 [3, 3, 32, 64], replicated
- inner_grads: float32 [2, 64], replicated
- inner_velocity: float32 [2, 64], replicated
- inner_average: float32 [2, 64], replicated
- inner_updated: float32 [2, 64], replicated
- second_grads: float32 [3, 3, 64, 64], replicated
- second_velocity: float32 [3, 3, 64, 64], replicated
- second_average: float32 [3, 3, 64, 64], replicated
- second_updated: float32 [3, 3, 64, 64], replicated
- second_copy: bfloat16 [3, 3, 64, 64], replicated
- shortcut_grads: float32 [32, 64], replicated
- shortcut_velocity: float32 [32, 64], replicated
- shortcut_average: float32 [32, 64], replicated
- shortcut_updated: float32 [32, 64], replicated
- shortcut_copy: bfloat16 [32, 64], replicated
All inputs are finite; a program needn't handle non-finite values.
Results may differ from a plain program's by a relative error of at most 0.0025.
The roundings to bfloat16 on the way count: a program that leaves them out, or rounds other values in their place, can miss the bound.
Values may be sent and summed in bfloat16 or wider, within the bound.
A program may use at most 384 MiB of HBM per device.

v0:
```python
import math

import jax
import jax.numpy as jnp
from jax import lax
from jax.sharding import PartitionSpec as P

CS_IN = 32
CS_OUT = 64
CT_IN = 128
SIDE = 32
GROUPS = 2


HIGHEST = lax.Precision.HIGHEST
EPSILON = 1e-05
TRANSFER_WEIGHT = 1000.0
MOMENTUM = 0.9
WEIGHT_DECAY = 0.0005
AVERAGING = 0.7
CONV_RATE = 0.06
NORM_RATE = 0.3


def as_sent(shard):

    def short(part):
        return part.astype(jnp.bfloat16) if part.dtype == jnp.float32 else part

    return jax.tree.map(short, shard)


def silu_slope(values):
    sigmoid = jax.nn.sigmoid(values)
    return sigmoid * (1.0 + values * (1.0 - sigmoid))


def group_table(labels):
    return (labels[:, None] == jnp.arange(GROUPS, dtype=jnp.int32)[None, :]).astype(jnp.float32)


def per_group(indicator, values):
    return lax.dot_general(indicator, values, (((0,), (0,)), ((), ())), precision=HIGHEST)


def group_sums(tables, fields):
    return per_group(tables[0], jnp.sum(fields[0], axis=(1, 2))) + per_group(
        tables[1], jnp.sum(fields[1], axis=(1, 2))
    )


def spread_group(indicator, values):
    return jnp.dot(indicator, values, precision=HIGHEST)[:, None, None, :]


def convolve(inputs, kernel, stride):
    return lax.conv_general_dilated(
        inputs,
        kernel,
        (stride, stride),
        ((1, 1), (1, 1)),
        dimension_numbers=("NHWC", "HWIO", "NHWC"),
        preferred_element_type=jnp.float32,
    )


def pointwise_strided(inputs, matrix):
    kernel = matrix.reshape(1, 1, matrix.shape[0], matrix.shape[1])
    return lax.conv_general_dilated(
        inputs,
        kernel,
        (2, 2),
        ((0, 0), (0, 0)),
        dimension_numbers=("NHWC", "HWIO", "NHWC"),
        preferred_element_type=jnp.float32,
    )


def convolve_back(gradient, kernel, stride):
    padding_high = 2 if stride == 2 else 1
    return lax.conv_general_dilated(
        gradient,
        kernel[::-1, ::-1],
        (1, 1),
        ((1, padding_high), (1, padding_high)),
        lhs_dilation=(stride, stride),
        dimension_numbers=("NHWC", "HWOI", "NHWC"),
        preferred_element_type=jnp.float32,
    )


def pointwise_back(gradient, matrix):
    kernel = matrix.reshape(1, 1, matrix.shape[0], matrix.shape[1])
    return lax.conv_general_dilated(
        gradient,
        kernel,
        (1, 1),
        ((0, 1), (0, 1)),
        lhs_dilation=(2, 2),
        dimension_numbers=("NHWC", "HWOI", "NHWC"),
        preferred_element_type=jnp.float32,
    )


def kernel_grads(inputs, gradient, stride, padding):
    return lax.conv_general_dilated(
        inputs,
        gradient,
        (1, 1),
        (padding, padding),
        rhs_dilation=(stride, stride),
        dimension_numbers=("CHWN", "IHWO", "HWNC"),
        preferred_element_type=jnp.float32,
    )


def attention_map(block_sum):
    energy = jnp.mean(block_sum * block_sum, axis=-1).reshape(block_sum.shape[0], -1)
    scaling = lax.rsqrt(jnp.sum(energy * energy, axis=-1, keepdims=True) + 1e-12)
    return (energy * scaling, scaling)


def renew(weights, gradient, moment, average, factor):
    descent = gradient + WEIGHT_DECAY * weights
    velocity = MOMENTUM * moment + descent
    updated = weights - factor * (descent + MOMENTUM * velocity)
    smoothed = AVERAGING * average + (1.0 - AVERAGING) * updated
    return (gradient, velocity, smoothed, updated)


def body(
    small_in,
    large_in,
    small_teacher,
    large_teacher,
    small_groups,
    large_groups,
    small_cot,
    large_cot,
    teacher_gains,
    teacher_first,
    teacher_inner,
    teacher_second,
    teacher_bypass,
    entry_norm,
    first_conv,
    inner_norm,
    second_conv,
    shortcut,
    momentum_entry,
    momentum_first,
    momentum_inner,
    momentum_second,
    momentum_shortcut,
    average_entry,
    average_first,
    average_inner,
    average_second,
    average_shortcut,
):
    spread = lax.axis_size("space")
    image_sides = [SIDE, 2 * SIDE]
    pixels_in = [small_in, large_in]
    labels = [small_groups, large_groups]
    teachers = [small_teacher, large_teacher]
    cotangents = [small_cot, large_cot]
    local_images = [small_in.shape[0], large_in.shape[0]]
    local_rows = [small_in.shape[1], large_in.shape[1]]
    per_device = [small_in.shape[0] // spread, large_in.shape[0] // spread]
    total_positions = lax.axis_size("batch") * (
        small_in.shape[0] * SIDE * SIDE // 4 + large_in.shape[0] * SIDE * SIDE
    )

    def teacher_map_of(teacher_piece, image_side):
        amount = teacher_piece.shape[1]
        raw_input = teacher_piece.reshape(amount, image_side, image_side, CT_IN).astype(jnp.float32)
        teacher_act = jax.nn.silu(teacher_gains[0] * raw_input + teacher_gains[1]).astype(
            jnp.bfloat16
        )
        teacher_mid = jax.nn.silu(
            teacher_inner[0] * convolve(teacher_act, teacher_first, 2) + teacher_inner[1]
        ).astype(jnp.bfloat16)
        teacher_out = convolve(teacher_mid, teacher_second, 1) + pointwise_strided(
            teacher_act, teacher_bypass
        )
        return attention_map(teacher_out)[0]

    def paired_pass(image_side, pieces):
        student_piece, teacher_piece = pieces
        amount = teacher_piece.shape[1]
        return (
            student_piece.reshape(amount, image_side, image_side * CS_IN),
            teacher_map_of(teacher_piece, image_side),
        )

    spatial = []
    squared = []
    tables = []
    for resolution in range(2):
        field = (
            pixels_in[resolution]
            .astype(jnp.float32)
            .reshape(
                local_images[resolution], local_rows[resolution], image_sides[resolution], CS_IN
            )
        )
        spatial.append(field)
        squared.append(field * field)
        tables.append(group_table(labels[resolution]))
    positions = jnp.sum(tables[0], axis=0) * (local_rows[0] * image_sides[0]) + jnp.sum(
        tables[1], axis=0
    ) * (local_rows[1] * image_sides[1])
    sums_entry, squares_entry, counts = lax.psum(
        (group_sums(tables, spatial), group_sums(tables, squared), positions), ("batch", "space")
    )
    mean_entry = sums_entry / counts[:, None]
    scale_entry = lax.rsqrt(squares_entry / counts[:, None] - mean_entry * mean_entry + EPSILON)
    normed_entry = []
    before_entry = []
    activated = []
    teacher_parts = []
    for resolution in range(2):
        normed = (
            spatial[resolution] - spread_group(tables[resolution], mean_entry)
        ) * spread_group(tables[resolution], scale_entry)
        before = entry_norm[0] * normed + entry_norm[1]
        normed_entry.append(normed)
        before_entry.append(before)
        activated.append(
            jax.nn.silu(before)
            .astype(jnp.bfloat16)
            .reshape(
                spread,
                per_device[resolution],
                local_rows[resolution],
                image_sides[resolution] * CS_IN,
            )
        )
        teacher_parts.append(
            teachers[resolution].reshape(
                spread,
                per_device[resolution],
                local_rows[resolution],
                image_sides[resolution] * CT_IN,
            )
        )
    small_arrived, small_map = paired_pass(
        SIDE,
        (
            lax.all_to_all(activated[0], "space", split_axis=0, concat_axis=2, tiled=True),
            lax.all_to_all(teacher_parts[0], "space", split_axis=0, concat_axis=2, tiled=True),
        ),
    )
    large_arrived, large_map = paired_pass(
        2 * SIDE,
        (
            lax.all_to_all(activated[1], "space", split_axis=0, concat_axis=2, tiled=True),
            lax.all_to_all(teacher_parts[1], "space", split_axis=0, concat_axis=2, tiled=True),
        ),
    )
    regrouped = [
        small_arrived.reshape(per_device[0], SIDE, SIDE, CS_IN),
        large_arrived.reshape(per_device[1], 2 * SIDE, 2 * SIDE, CS_IN),
    ]
    teacher_maps = [small_map, large_map]
    first_low = first_conv.astype(jnp.bfloat16)
    second_low = second_conv.astype(jnp.bfloat16)
    shortcut_low = shortcut.astype(jnp.bfloat16)
    tables_batch = []
    first_out = []
    first_squared = []
    for resolution in range(2):
        tables_batch.append(
            group_table(
                lax.dynamic_slice_in_dim(
                    labels[resolution],
                    lax.axis_index("space") * per_device[resolution],
                    per_device[resolution],
                )
            )
        )
        output = convolve(regrouped[resolution], first_low, 2)
        first_out.append(output)
        first_squared.append(output * output)
    sums_inner, squares_inner = lax.psum(
        (group_sums(tables_batch, first_out), group_sums(tables_batch, first_squared)),
        ("batch", "space"),
    )
    counts_inner = counts * 0.25
    mean_inner = sums_inner / counts_inner[:, None]
    scale_inner = lax.rsqrt(
        squares_inner / counts_inner[:, None] - mean_inner * mean_inner + EPSILON
    )
    normed_inner = []
    before_inner = []
    inner_acts = []
    block_outs = []
    block_lows = []
    local_loss = jnp.zeros((), jnp.float32)
    for resolution in range(2):
        count_here = per_device[resolution]
        out_side = image_sides[resolution] // 2
        normed = (
            first_out[resolution] - spread_group(tables_batch[resolution], mean_inner)
        ) * spread_group(tables_batch[resolution], scale_inner)
        before = inner_norm[0] * normed + inner_norm[1]
        inner_act = jax.nn.silu(before).astype(jnp.bfloat16)
        normed_inner.append(normed)
        before_inner.append(before)
        inner_acts.append(inner_act)
        block_sum = convolve(inner_act, second_low, 1) + pointwise_strided(
            regrouped[resolution], shortcut_low
        )
        block_outs.append(
            block_sum.astype(jnp.bfloat16).reshape(count_here, out_side, out_side * CS_OUT)
        )
        student_map, scaling = attention_map(block_sum)
        difference = student_map - teacher_maps[resolution]
        local_loss = local_loss + TRANSFER_WEIGHT / 2 * jnp.sum(difference * difference)
        pulled = TRANSFER_WEIGHT * difference
        energy_grad = (
            pulled - student_map * jnp.sum(pulled * student_map, axis=-1, keepdims=True)
        ) * scaling
        block_grad = (
            cotangents[resolution]
            .astype(jnp.float32)
            .reshape(count_here, out_side, out_side, CS_OUT)
            + energy_grad.reshape(count_here, out_side, out_side, 1) * (2.0 / CS_OUT) * block_sum
        )
        block_lows.append(block_grad.astype(jnp.bfloat16))
    replayed = (
        lax.all_to_all(activated[0], "space", split_axis=0, concat_axis=2, tiled=True),
        lax.all_to_all(activated[1], "space", split_axis=0, concat_axis=2, tiled=True),
    )
    sources = [
        replayed[0].reshape(per_device[0], SIDE, SIDE, CS_IN),
        replayed[1].reshape(per_device[1], 2 * SIDE, 2 * SIDE, CS_IN),
    ]
    shortcut_terms = []
    second_terms = []
    inner_flows = []
    crossed = []
    for resolution in range(2):
        shortcut_terms.append(
            kernel_grads(sources[resolution], block_lows[resolution], 2, (0, -1))[0, 0]
        )
        second_terms.append(kernel_grads(inner_acts[resolution], block_lows[resolution], 1, (1, 1)))
        inner_grad = convolve_back(block_lows[resolution], second_low, 1)
        flow = inner_grad * silu_slope(before_inner[resolution])
        inner_flows.append(flow)
        crossed.append(flow * normed_inner[resolution])
    shortcut_part = shortcut_terms[0] + shortcut_terms[1]
    second_part = second_terms[0] + second_terms[1]
    ones_inner = group_sums(tables_batch, inner_flows)
    cross_inner = group_sums(tables_batch, crossed)
    ones_inner, cross_inner = lax.psum((ones_inner, cross_inner), ("batch", "space"))
    inner_grads = jnp.stack([jnp.sum(cross_inner, axis=0), jnp.sum(ones_inner, axis=0)])
    first_terms = []
    entry_lows = []
    for resolution in range(2):
        count_here = per_device[resolution]
        image_side = image_sides[resolution]
        table_here = tables_batch[resolution]
        first_grad = (
            inner_norm[0]
            * spread_group(table_here, scale_inner)
            * (
                inner_flows[resolution]
                - spread_group(table_here, ones_inner / counts_inner[:, None])
                - normed_inner[resolution]
                * spread_group(table_here, cross_inner / counts_inner[:, None])
            )
        ).astype(jnp.bfloat16)
        first_terms.append(kernel_grads(sources[resolution], first_grad, 2, (1, 0)))
        entry_back = convolve_back(first_grad, first_low, 2) + pointwise_back(
            block_lows[resolution], shortcut_low
        )
        entry_lows.append(
            entry_back.astype(jnp.bfloat16).reshape(1, count_here, image_side, image_side * CS_IN)
        )
    first_part = first_terms[0] + first_terms[1]
    returned = (
        lax.all_to_all(as_sent(entry_lows[0]), "space", split_axis=2, concat_axis=0, tiled=True),
        lax.all_to_all(as_sent(entry_lows[1]), "space", split_axis=2, concat_axis=0, tiled=True),
    )
    entry_flows = []
    entry_crossed = []
    for resolution in range(2):
        entry_grad = (
            returned[resolution]
            .astype(jnp.float32)
            .reshape(
                local_images[resolution], local_rows[resolution], image_sides[resolution], CS_IN
            )
        )
        flow = entry_grad * silu_slope(before_entry[resolution])
        entry_flows.append(flow)
        entry_crossed.append(flow * normed_entry[resolution])
    ones_entry = group_sums(tables, entry_flows)
    cross_entry = group_sums(tables, entry_crossed)
    ones_entry, cross_entry, first_grads, second_grads, shortcut_grads, total_loss = lax.psum(
        (ones_entry, cross_entry, first_part, second_part, shortcut_part, local_loss),
        ("batch", "space"),
    )
    input_grads = []
    for resolution in range(2):
        table_here = tables[resolution]
        result = (
            entry_norm[0]
            * spread_group(table_here, scale_entry)
            * (
                entry_flows[resolution]
                - spread_group(table_here, ones_entry / counts[:, None])
                - normed_entry[resolution] * spread_group(table_here, cross_entry / counts[:, None])
            )
        )
        input_grads.append(
            result.reshape(
                local_images[resolution], local_rows[resolution], image_sides[resolution] * CS_IN
            )
        )
    entry_grads = jnp.stack([jnp.sum(cross_entry, axis=0), jnp.sum(ones_entry, axis=0)])
    rate_scale = 1.0 / math.sqrt(total_positions)
    entry_state = renew(
        entry_norm, entry_grads, momentum_entry, average_entry, NORM_RATE * rate_scale
    )
    first_state = renew(
        first_conv, first_grads, momentum_first, average_first, CONV_RATE * rate_scale
    )
    inner_state = renew(
        inner_norm, inner_grads, momentum_inner, average_inner, NORM_RATE * rate_scale
    )
    second_state = renew(
        second_conv, second_grads, momentum_second, average_second, CONV_RATE * rate_scale
    )
    bypass_state = renew(
        shortcut, shortcut_grads, momentum_shortcut, average_shortcut, CONV_RATE * rate_scale
    )
    return (
        block_outs[0],
        block_outs[1],
        input_grads[0],
        input_grads[1],
        total_loss / total_positions,
        entry_state[0],
        entry_state[1],
        entry_state[2],
        entry_state[3],
        first_state[0],
        first_state[1],
        first_state[2],
        first_state[3],
        first_state[3].astype(jnp.bfloat16),
        inner_state[0],
        inner_state[1],
        inner_state[2],
        inner_state[3],
        second_state[0],
        second_state[1],
        second_state[2],
        second_state[3],
        second_state[3].astype(jnp.bfloat16),
        bypass_state[0],
        bypass_state[1],
        bypass_state[2],
        bypass_state[3],
        bypass_state[3].astype(jnp.bfloat16),
    )


def solution(mesh):
    return jax.shard_map(
        body,
        mesh=mesh,
        in_specs=(
            P("batch", "space", None),
            P("batch", "space", None),
            P("batch", "space", None),
            P("batch", "space", None),
            P("batch"),
            P("batch"),
            P(("batch", "space"), None, None),
            P(("batch", "space"), None, None),
            P(),
            P(),
            P(),
            P(),
            P(),
            P(),
            P(),
            P(),
            P(),
            P(),
            P(),
            P(),
            P(),
            P(),
            P(),
            P(),
            P(),
            P(),
            P(),
            P(),
        ),
        out_specs=(
            P(("batch", "space"), None, None),
            P(("batch", "space"), None, None),
            P("batch", "space", None),
            P("batch", "space", None),
            P(),
            P(),
            P(),
            P(),
            P(),
            P(),
            P(),
            P(),
            P(),
            P(),
            P(),
            P(),
            P(),
            P(),
            P(),
            P(),
            P(),
            P(),
            P(),
            P(),
            P(),
            P(),
            P(),
            P(),
        ),
        check_vma=False,
    )
```

profile of v0, /device:TPU:0, one launch (start us, length us, event | category | flops | bytes accessed | tf_op | source)
XLA Modules:
  0.0 1349.6 jit_solution(14430396752608317772)
XLA Ops:
  27.8 42.1 %all-reduce.3 = (f32[2,32]{1,0:T(2,128)S(1)}, f32[2]{0:T(128)S(1)}, f32[2,32]{1,0:T(2,128)S(1)}) all-reduce(f32[2,32]{1,0:T(2,128)S(1)} %convolution_add_fusion.9, f32[2]{0:T(128)S(1)} %multiply_add_fusion.17, f32[2,32]{1,0:T(2,128)S(1)} %convolution_add_fusion.10), channel_id=1, replica_groups=mesh['batch'=4,'space'=8] {'batch','space'}, use_global_device_ids=true, to_apply=%region_12.13 | all-reduce | flops 130 | bytes 1040 | tf_op jit(solution)/shard_map/psum | solution.py:213
  113.6 34.4 %all-to-all-done.1 = bf16[8,10,8,2048]{3,2,1,0:T(8,128)(2,1)} async-done(((bf16[8,10,8,2048]{3,2,1,0:T(8,128)(2,1)}), bf16[8,10,8,2048]{3,2,1,0:T(8,128)(2,1)}, u32[]{:S(2)}, u32[]{:S(2)}) %all-to-all-start.1) | async-done | bytes 2621472 | tf_op jit(solution)/shard_map/all_to_all | solution.py:257
  148.0 63.5 %all_to_all.36 = bf16[8,40,4,1024]{3,1,2,0:T(8,128)(2,1)} all-to-all(bf16[8,40,4,1024]{3,1,2,0:T(8,128)(2,1)} %copy.434), channel_id=1, replica_groups=mesh['batch'=4,'space'=8] {'space'}, dimensions={0} | all-to-all | bytes 5242880 | tf_op jit(solution)/shard_map/all_to_all | solution.py:250
  227.2 13.9 %copy.444 = bf16[8,40,4,4096]{3,1,2,0:T(8,128)(2,1)} copy(bf16[8,40,4,4096]{3,2,1,0:T(4,128)(2,1)} %bitcast.213) | data formatting | bytes 20971520 | tf_op jit(solution)/shard_map/reshape | solution.py:240
  288.0 20.8 %fusion.108 = (f32[10,64]{1,0:T(8,128)S(1)}, f32[10,64]{1,0:T(8,128)S(1)}, f32[10,32,32,64]{3,0,2,1:T(8,128)}) fusion(bf16[3,3,32,64]{3,2,1,0:T(8,128)(2,1)S(1)} %convert_element_type.153, bf16[10,64,64,32]{3,2,1,0:T(8,128)(2,1)} %reshape_reshape.7), kind=kOutput, calls=%fused_computation.221 | convolution fusion | flops 371628800 | bytes 5284864 | tf_op jit(solution)/shard_map/conv_general_dilated | solution.py:57
  317.0 146.9 %all-reduce.2 = (f32[2,64]{1,0:T(2,128)S(1)}, f32[2,64]{1,0:T(2,128)S(1)}) all-reduce(f32[2,64]{1,0:T(2,128)S(1)} %convolution_add_fusion.5, f32[2,64]{1,0:T(2,128)S(1)} %convolution_add_fusion.6), channel_id=1, replica_groups=mesh['batch'=4,'space'=8] {'batch','space'}, use_global_device_ids=true, to_apply=%region_18.19 | all-reduce | flops 256 | bytes 2048 | tf_op jit(solution)/shard_map/psum | solution.py:285
  517.2 13.9 %convert_bitcast_fusion = f32[1,10,8,8,8192]{4,3,1,2,0:T(8,128)} fusion(bf16[8,10,8,8192]{3,2,1,0:T(8,128)(2,1)} %all-to-all-done.3), kind=kLoop, calls=%fused_computation.3 | loop fusion | flops 5242880 | bytes 31457280 | tf_op jit(solution)/shard_map/convert_element_type | solution.py:176
  531.1 15.9 %copy.449 = f32[1,10,8,8,8192]{4,3,2,1,0:T(8,128)} copy(f32[1,10,8,8,8192]{4,3,1,2,0:T(8,128)} %convert_bitcast_fusion) | data formatting | bytes 41943040 | tf_op jit(solution)/shard_map/convert_element_type | solution.py:176
  564.2 41.9 %multiply_convert_fusion.2 = bf16[10,32,32,256]{3,0,2,1:T(8,128)(2,1)S(1)} fusion(bf16[3,3,128,256]{3,2,1,0:T(8,128)(2,1)S(1)} %copy-done.109, bf16[10,64,64,128]{3,2,1,0:T(8,128)(2,1)S(1)} %multiply_convert_fusion, f32[256]{0:T(256)S(1)} %bitcast.234, f32[256]{0:T(256)S(1)} %bitcast.232), kind=kOutput, calls=%fused_computation.20 | convolution fusion | flops 5932974080 | bytes 16320512 | tf_op jit(solution)/shard_map/conv_general_dilated | solution.py:57
  606.1 24.9 %fusion.118 = f32[10,32,32,256]{3,0,2,1:T(8,128)} fusion(bf16[10,32,32,256]{3,0,2,1:T(8,128)(2,1)S(1)} %multiply_convert_fusion.2, bf16[3,3,256,256]{3,2,1,0:T(8,128)(2,1)S(1)} %copy-done), kind=kOutput, calls=%fused_computation.231 | convolution fusion | flops 11581521920 | bytes 16908288 | tf_op jit(solution)/shard_map/conv_general_dilated | solution.py:57
  643.1 60.8 %all-to-all-done.2 = bf16[8,40,4,4096]{3,1,2,0:T(8,128)(2,1)} async-done(((bf16[8,40,4,4096]{3,1,2,0:T(8,128)(2,1)}), bf16[8,40,4,4096]{3,1,2,0:T(8,128)(2,1)}, u32[]{:S(2)}, u32[]{:S(2)}) %all-to-all-start.2) | async-done | bytes 10485792 | tf_op jit(solution)/shard_map/all_to_all | solution.py:251
  703.9 14.0 %bitcast_convert_fusion = f32[8,1,40,4,4096]{4,2,3,0,1:T(8,128)} fusion(bf16[8,40,4,4096]{3,1,2,0:T(8,128)(2,1)} %all-to-all-done.2), kind=kLoop, calls=%fused_computation.21 | loop fusion | flops 5242880 | bytes 31457280 | tf_op jit(solution)/shard_map/convert_element_type | solution.py:176
  747.6 16.8 %fusion.28 = f32[40,16,16,256]{3,0,2,1:T(8,128)} fusion(bf16[3,3,256,256]{3,2,1,0:T(8,128)(2,1)S(1)} %copy-done, bf16[40,16,16,256]{3,0,2,1:T(8,128)(2,1)} %multiply_convert_fusion.13), kind=kOutput, calls=%fused_computation.69 | convolution fusion | flops 11093934080 | bytes 16908288 | tf_op jit(solution)/shard_map/conv_general_dilated | solution.py:57
  802.2 13.5 %fusion.21 = (bf16[10,32,32,64]{3,0,2,1:T(8,128)(2,1)S(1)}, bf16[10,32,32,64]{3,0,2,1:T(8,128)(2,1)}) fusion(f32[10,32,32,64]{3,2,1,0:T(8,128)} %reshape.531, f32[10,32,32,64]{3,0,2,1:T(8,128)} %get-tuple-element.239, f32[10,32,32]{0,2,1:T(8,128)S(1)} %copy.453), kind=kLoop, calls=%fused_computation.29 | loop fusion | flops 2621440 | bytes 7905280 | tf_op jit(solution)/shard_map/convert_element_type | solution.py:330
  815.8 18.7 %fusion.107 = (f32[10,64]{1,0:T(8,128)S(1)}, f32[10,64]{1,0:T(8,128)S(1)}, f32[10,32,32,64]{3,0,2,1:T(8,128)}) fusion(f32[10,64]{1,0:T(8,128)S(1)} %copy-done.81, f32[10,32,32,64]{3,0,2,1:T(8,128)} %get-tuple-element.234, f32[10,64]{1,0:T(8,128)S(1)} %copy-done.79, f32[64]{0:T(128)S(1)} %copy-done.92, f32[64]{0:T(128)S(1)} %copy-done.90, ...), kind=kOutput, calls=%fused_computation.220 | convolution fusion | flops 733674240 | bytes 6638080 | tf_op jit(solution)/shard_map/conv_general_dilated | solution.py:81
  835.5 38.8 %all-reduce.1 = (f32[2,64]{1,0:T(2,128)S(1)}, f32[2,64]{1,0:T(2,128)S(1)}) all-reduce(f32[2,64]{1,0:T(2,128)S(1)} %convolution_add_fusion.3, f32[2,64]{1,0:T(2,128)S(1)} %convolution_add_fusion.4), channel_id=1, replica_groups=mesh['batch'=4,'space'=8] {'batch','space'}, use_global_device_ids=true, to_apply=%region_34.35 | all-reduce | flops 256 | bytes 2048 | tf_op jit(solution)/shard_map/psum | solution.py:356
  875.2 16.2 %fusion.56 = f32[10,64,64,32]{3,0,2,1:T(8,128)} fusion(bf16[10,32,32,64]{3,0,2,1:T(8,128)(2,1)} %copy-done.4, bf16[32,64]{1,0:T(8,128)(2,1)S(1)} %copy-done.52), kind=kOutput, calls=%fused_computation.128 | convolution fusion | flops 41943040 | bytes 6557696 | tf_op jit(solution)/shard_map/conv_general_dilated | solution.py:94
  898.0 19.6 %add_convert_fusion = bf16[10,64,64,32]{3,0,2,1:T(8,128)(2,1)} fusion(f32[10,64,64,32]{3,0,2,1:T(8,128)} %fusion.56, bf16[10,32,32,64]{3,0,2,1:T(8,128)(2,1)S(1)} %multiply_convert_fusion.4, bf16[3,3,32,64]{3,2,1,0:T(8,128)(2,1)S(1)} %copy-done.68), kind=kOutput, calls=%fused_computation | convolution fusion | flops 372285440 | bytes 9211904 | tf_op jit(solution)/shard_map/conv_general_dilated | solution.py:81
  917.6 19.5 %copy.464 = bf16[10,64,64,32]{1,3,2,0:T(8,128)(2,1)} copy(bf16[10,64,64,32]{3,0,2,1:T(8,128)(2,1)} %add_convert_fusion) | data formatting | bytes 5242880 | tf_op jit(solution)/shard_map/convert_element_type | solution.py:379
  959.7 15.7 %fusion.119 = f32[40,32,32,32]{0,3,2,1:T(8,128)} fusion(bf16[40,16,16,64]{3,0,2,1:T(8,128)(2,1)S(1)} %multiply_convert_fusion.6, bf16[3,3,32,64]{3,2,1,0:T(8,128)(2,1)S(1)} %copy-done.68), kind=kOutput, calls=%fused_computation.232 | convolution fusion | flops 361922560 | bytes 6590464 | tf_op jit(solution)/shard_map/conv_general_dilated | solution.py:81
  1016.7 28.6 %all-to-all-done.5 = bf16[1,10,64,2048]{3,1,0,2:T(8,128)(2,1)} async-done(((bf16[1,10,64,2048]{3,1,0,2:T(8,128)(2,1)}), bf16[1,10,64,2048]{3,1,0,2:T(8,128)(2,1)}, u32[]{:S(2)}, u32[]{:S(2)}) %all-to-all-start.5) | async-done | bytes 2621472 | tf_op jit(solution)/shard_map/all_to_all | solution.py:384
  1049.7 15.7 %fusion.38 = f32[3,3,32,64]{3,2,1,0:T(8,128)} fusion(f32[3,3,32,64]{3,2,1,0:T(8,128)S(1)} %fusion.120, bf16[10,32,32,64]{3,0,2,1:T(8,128)(2,1)} %copy-done.28, bf16[10,64,64,32]{3,2,1,0:T(8,128)(2,1)} %reshape_reshape.7), kind=kOutput, calls=%fused_computation.76 | convolution fusion | flops 369682432 | bytes 4079616 | tf_op jit(solution)/shard_map/conv_general_dilated | solution.py:106
  1098.2 111.1 %all-reduce.7.cloned.1.call-done = (f32[3,3,32,64]{3,2,1,0:T(8,128)}, f32[3,3,64,64]{3,2,1,0:T(8,128)}) async-done(((f32[3,3,32,64]{3,2,1,0:T(8,128)}, f32[3,3,64,64]{3,2,1,0:T(8,128)}), (f32[3,3,32,64]{3,2,1,0:T(8,128)}, f32[3,3,64,64]{3,2,1,0:T(8,128)})) %all-reduce.7.cloned.1.call-update) | async-done | bytes 221200 | tf_op jit(solution)/shard_map/psum | solution.py:401
  1254.1 41.5 %all-reduce = (f32[2,32]{1,0:T(2,128)S(1)}, f32[2,32]{1,0:T(2,128)S(1)}, f32[]{:T(128)}, f32[32,64]{1,0:T(8,128)S(1)}) all-reduce(f32[2,32]{1,0:T(2,128)S(1)} %convolution_add_fusion.7, f32[2,32]{1,0:T(2,128)S(1)} %convolution_add_fusion.8, f32[]{:T(128)S(6)} %multiply.53, ...), channel_id=1, replica_groups=mesh['batch'=4,'space'=8] {'batch','space'}, use_global_device_ids=true, to_apply=%region_44.45 | all-reduce | flops 2177 | bytes 17416 | tf_op jit(solution)/shard_map/psum | solution.py:401
  (445 shorter events, 481.9 us)
Async XLA Ops:
  7.2 598.9 %copy-start = (bf16[3,3,256,256]{3,2,1,0:T(8,128)(2,1)S(1)}, bf16[3,3,256,256]{3,2,1,0:T(8,128)(2,1)}, u32[]{:S(2)}) copy-start(bf16[3,3,256,256]{3,2,1,0:T(8,128)(2,1)} %param.39) | copy-start | bytes 3538948
  69.9 193.7 %copy-start.110 = (f32[2]{0:T(128)}, f32[2]{0:T(128)S(1)}, u32[]{:S(2)}) copy-start(f32[2]{0:T(128)S(1)} %get-tuple-element.197) | copy-start | bytes 28
  84.3 63.7 %all-to-all-start.1 = ((bf16[8,10,8,2048]{3,2,1,0:T(8,128)(2,1)}), bf16[8,10,8,2048]{3,2,1,0:T(8,128)(2,1)}, u32[]{:S(2)}, u32[]{:S(2)}) async-start(bf16[8,10,8,2048]{3,2,1,0:T(8,128)(2,1)} %multiply_convert_fusion.8), calls=%async_computation.1 | async-start | bytes 5242880 | tf_op jit(solution)/shard_map/all_to_all | solution.py:257
  211.5 259.8 %all-to-all-start.3 = ((bf16[8,10,8,8192]{3,2,1,0:T(8,128)(2,1)}), bf16[8,10,8,8192]{3,2,1,0:T(8,128)(2,1)}, u32[]{:S(2)}, u32[]{:S(2)}) async-start(bf16[8,10,8,8192]{3,2,1,0:T(8,128)(2,1)} %bitcast.214), calls=%async_computation.3 | async-start | bytes 20971520 | tf_op jit(solution)/shard_map/all_to_all | solution.py:258
  221.9 242.2 %copy-start.112 = (s32[10]{0:T(128)}, s32[10]{0:T(128)S(1)}, u32[]{:S(2)}) copy-start(s32[10]{0:T(128)S(1)} %dynamic_slice.7) | copy-start | bytes 124
  222.0 274.4 %copy-start.114 = (s32[40]{0:T(128)}, s32[40]{0:T(128)S(1)}, u32[]{:S(2)}) copy-start(s32[40]{0:T(128)S(1)} %dynamic_slice.6) | copy-start | bytes 484
  222.0 279.4 %copy-start.55 = (bf16[3,3,64,64]{3,2,1,0:T(8,128)(2,1)}, bf16[3,3,64,64]{3,2,1,0:T(8,128)(2,1)S(1)}, u32[]{:S(2)}) copy-start(bf16[3,3,64,64]{3,2,1,0:T(8,128)(2,1)S(1)} %convert_element_type.156) | copy-start | bytes 221188
  222.0 285.7 %copy-start.51 = (bf16[32,64]{1,0:T(8,128)(2,1)}, bf16[32,64]{1,0:T(8,128)(2,1)S(1)}, u32[]{:S(2)}) copy-start(bf16[32,64]{1,0:T(8,128)(2,1)S(1)} %convert_element_type.157) | copy-start | bytes 12292
  263.6 232.8 %copy-start.116 = (f32[2]{0:T(128)}, f32[2]{0:T(128)S(1)}, u32[]{:S(2)}) copy-start(f32[2]{0:T(128)S(1)} %broadcast_multiply_fusion.6) | copy-start | bytes 28
  263.6 233.6 %copy-start.89 = (f32[64]{0:T(128)}, f32[64]{0:T(128)S(1)}, u32[]{:S(2)}) copy-start(f32[64]{0:T(128)S(1)} %get-tuple-element.226) | copy-start | bytes 772
  263.6 233.6 %copy-start.91 = (f32[64]{0:T(128)}, f32[64]{0:T(128)S(1)}, u32[]{:S(2)}) copy-start(f32[64]{0:T(128)S(1)} %get-tuple-element.227) | copy-start | bytes 772
  471.3 232.6 %all-to-all-start.2 = ((bf16[8,40,4,4096]{3,1,2,0:T(8,128)(2,1)}), bf16[8,40,4,4096]{3,1,2,0:T(8,128)(2,1)}, u32[]{:S(2)}, u32[]{:S(2)}) async-start(bf16[8,40,4,4096]{3,1,2,0:T(8,128)(2,1)} %copy.444), calls=%async_computation.2 | async-start | bytes 20971520 | tf_op jit(solution)/shard_map/all_to_all | solution.py:251
  946.6 98.6 %all-to-all-start.5 = ((bf16[1,10,64,2048]{3,1,0,2:T(8,128)(2,1)}), bf16[1,10,64,2048]{3,1,0,2:T(8,128)(2,1)}, u32[]{:S(2)}, u32[]{:S(2)}) async-start(bf16[1,10,64,2048]{3,1,0,2:T(8,128)(2,1)} %copy.465), calls=%async_computation.5 | async-start | bytes 8388608 | tf_op jit(solution)/shard_map/all_to_all | solution.py:384
  1045.2 182.5 %all-to-all-start.4 = ((bf16[1,40,32,1024]{3,1,0,2:T(8,128)(2,1)}), bf16[1,40,32,1024]{3,1,0,2:T(8,128)(2,1)}, u32[]{:S(2)}, u32[]{:S(2)}) async-start(bf16[1,40,32,1024]{3,1,0,2:T(8,128)(2,1)} %copy.455), calls=%async_computation.4 | async-start | bytes 5242880 | tf_op jit(solution)/shard_map/all_to_all | solution.py:383
  1049.7 159.6 %all-reduce.7.cloned.1.call-start = ((), (), s32[]{:S(2)}) async-start(), calls=%async_computation.6 | async-start | bytes 884736 | tf_op jit(solution)/shard_map/psum | solution.py:401
  1088.3 121.0 %copy-start.53 = (f32[3,3,32,64]{3,2,1,0:T(8,128)S(1)}, f32[3,3,32,64]{3,2,1,0:T(8,128)}, u32[]{:S(2)}) copy-start(f32[3,3,32,64]{3,2,1,0:T(8,128)} %param.47) | copy-start | bytes 221188
  1088.3 122.7 %copy-start.54 = (f32[3,3,32,64]{3,2,1,0:T(8,128)S(1)}, f32[3,3,32,64]{3,2,1,0:T(8,128)}, u32[]{:S(2)}) copy-start(f32[3,3,32,64]{3,2,1,0:T(8,128)} %param.52) | copy-start | bytes 221188
  1088.3 123.4 %copy-start.42 = (f32[3,3,64,64]{3,2,1,0:T(8,128)S(1)}, f32[3,3,64,64]{3,2,1,0:T(8,128)}, u32[]{:S(2)}) copy-start(f32[3,3,64,64]{3,2,1,0:T(8,128)} %param.44) | copy-start | bytes 442372
  1088.3 123.4 %copy-start.48 = (f32[3,3,64,64]{3,2,1,0:T(8,128)S(1)}, f32[3,3,64,64]{3,2,1,0:T(8,128)}, u32[]{:S(2)}) copy-start(f32[3,3,64,64]{3,2,1,0:T(8,128)} %param.49) | copy-start | bytes 442372
  1088.3 125.2 %copy-start.49 = (f32[3,3,64,64]{3,2,1,0:T(8,128)S(1)}, f32[3,3,64,64]{3,2,1,0:T(8,128)}, u32[]{:S(2)}) copy-start(f32[3,3,64,64]{3,2,1,0:T(8,128)} %param.54) | copy-start | bytes 442372
  1088.3 126.0 %copy-start.33 = (f32[8,10,2048]{2,0,1:T(8,128)S(1)}, f32[8,10,2048]{2,0,1:T(8,128)}, u32[]{:S(2)}) copy-start(f32[8,10,2048]{2,0,1:T(8,128)} %copy.469) | copy-start | bytes 1966084
  1088.3 126.0 %copy-start.34 = (f32[8,10,2048]{2,0,1:T(8,128)S(1)}, f32[8,10,2048]{2,0,1:T(8,128)}, u32[]{:S(2)}) copy-start(f32[8,10,2048]{2,0,1:T(8,128)} %copy.467) | copy-start | bytes 1966084
  1088.3 126.0 %copy-start.58 = (f32[2048]{0:T(1024)S(1)}, f32[2048]{0:T(1024)}, u32[]{:S(2)}) copy-start(f32[2048]{0:T(1024)} %copy-done.57) | copy-start | bytes 24580
  1088.3 125.9 %copy-start.61 = (f32[2048]{0:T(1024)S(1)}, f32[2048]{0:T(1024)}, u32[]{:S(2)}) copy-start(f32[2048]{0:T(1024)} %copy-done.60) | copy-start | bytes 24580
  (107 other events, 1389.7 us)
Sparse Core Ops, SparseCore 0:
  1065.6 143.5 all-reduce.6
where the time goes:
time: 1370 us; the launch traced here: 1350 us
  matrix products  336 us (25%)
  blocking collectives  333 us (24%)
  local copies, waits for them, and re-layouts  245 us (18%)
  waiting for transfers between devices  235 us (17%)
  other arithmetic  155 us (11%)
  starting transfers between devices  26.7 us (2%)
  between operations  19 us (1%)
    psum x1, blocking collectives, body(): lax.psum((group_sums(tables_batch, first_out), group_sums(tables_batch, f...  147 us
    conv_general_dilated x8, matrix products, convolve(): lax.conv_general_dilated(inputs, kernel, (stride, stride), ((1, 1), (1, 1...  136 us
    psum x1, waiting for transfers between devices, body(): lax.psum((ones_entry, cross_entry, first_part, second_part, shortcut_part...  111 us
    conv_general_dilated x4, matrix products, convolve_back(): lax.conv_general_dilated(gradient, kernel[::-1, ::-1], (1, 1), ((1, paddi...  64.5 us
    all_to_all x1, blocking collectives, body(): lax.all_to_all(activated[0], 'space', split_axis=0, concat_axis=2, tiled=...  63.5 us
    all_to_all x1, waiting for transfers between devices, body(): lax.all_to_all(teacher_parts[0], 'space', split_axis=0, concat_axis=2, ti...  60.8 us
    conv_general_dilated x6, matrix products, kernel_grads(): lax.conv_general_dilated(inputs, gradient, (1, 1), (padding, padding), rh...  59.4 us
    psum x1, blocking collectives, body(): lax.psum((group_sums(tables, spatial), group_sums(tables, squared), posit...  42.1 us
  transfers between devices with their start and end apart: 6, of which 4 were waited for; matrix products, arithmetic and copies ran while one was open for 31% of the time, Pallas kernels for 0%

commit v1 on v0

v1 whole, which is shorter than its diff:
```python
import functools
import math

import jax
import jax.numpy as jnp
import numpy as np
from jax import lax
from jax.experimental import pallas as pl
from jax.experimental.pallas import tpu as pltpu
from jax.sharding import PartitionSpec as P

CS_IN = 32
CS_OUT = 64
CT_IN = 128
CT_OUT = 256
SIDE = 32
SLABS = 4

EPSILON = 1e-05
TRANSFER_WEIGHT = 1000.0
MOMENTUM = 0.9
WEIGHT_DECAY = 0.0005
AVERAGING = 0.7
CONV_RATE = 0.06
NORM_RATE = 0.3

F32 = jnp.float32
BF16 = jnp.bfloat16
MESH = pl.DeviceIdType.MESH
VMEM_LIMIT = 56 << 20


def sigmoid(z):
    return 0.5 * jnp.tanh(0.5 * z) + 0.5


def matmul(a, b):
    return jnp.dot(a, b, preferred_element_type=F32)


def fold(rows, width):
    shift = width
    while shift < 128:
        rows = rows + pltpu.roll(rows, shift, 1)
        shift *= 2
    return rows


def group_norms(totals, counts, width):
    folded = fold(totals, width)
    means, scales = [], []
    for g in range(2):
        mean = folded[g : g + 1] / counts[g]
        variance = folded[2 + g : 3 + g] / counts[g] - mean * mean
        means.append(mean)
        scales.append(lax.rsqrt(variance + EPSILON))
    return means, scales


def per_image(w0, w1, pair):
    return w0 * pair[0] + w1 * pair[1]


def twice(table):
    return jnp.concatenate([table, table], axis=1)


def grouped_rows(w0, w1, values):
    rows = []
    for v in values:
        rows.append(jnp.sum(v * w0, axis=0, keepdims=True))
        rows.append(jnp.sum(v * w1, axis=0, keepdims=True))
    rows.append(jnp.zeros((8 - len(rows), 128), F32))
    return jnp.concatenate(rows, axis=0)


def entry_counts(tot_ref):
    return [tot_ref[4:5], tot_ref[5:6]]


def inner_counts(tot_ref):
    return [tot_ref[4:5] * 0.25, tot_ref[5:6] * 0.25]


def stats_kernel(x_refs, w_refs, out_ref):
    step = pl.program_id(0)
    total = jnp.zeros((8, 128), F32)
    for x_ref, (w0_ref, w1_ref) in zip(x_refs, w_refs):
        rows, images, lanes = x_ref.shape
        s = jnp.zeros((images, 128), F32)
        q = jnp.zeros((images, 128), F32)
        for r in range(rows):
            for c in range(0, lanes, 128):
                v = x_ref[r, :, c : c + 128].astype(F32)
                s = s + v
                q = q + v * v
        w0, w1 = w0_ref[...], w1_ref[...]
        positions = jnp.full((images, 128), float(rows * lanes // CS_IN), F32)
        total = total + grouped_rows(w0, w1, [s, q, positions])

    @pl.when(step == 0)
    def _():
        out_ref[...] = total

    @pl.when(step > 0)
    def _():
        out_ref[...] += total


def input_stats(slabs, weights):
    steps = 4

    def kernel(xs, xl, a0, a1, b0, b1, out_ref):
        stats_kernel((xs, xl), ((a0, a1), (b0, b1)), out_ref)

    specs = [
        pl.BlockSpec((x.shape[0] // steps,) + x.shape[1:], lambda i: (i, 0, 0)) for x in slabs
    ]
    tables = [w for pair in weights for w in pair]
    specs += [pl.BlockSpec(w.shape, lambda i: (0, 0)) for w in tables]
    return pl.pallas_call(
        kernel,
        grid=(steps,),
        in_specs=specs,
        out_specs=pl.BlockSpec((8, 128), lambda i: (0, 0)),
        out_shape=jax.ShapeDtypeStruct((8, 128), F32),
        compiler_params=pltpu.CompilerParams(vmem_limit_bytes=VMEM_LIMIT),
    )(*slabs, *tables)


def greet(axes):
    barrier = pltpu.get_barrier_semaphore()
    expected = 0
    for name, size in axes:
        me = lax.axis_index(name)
        for d in range(1, size):
            pl.semaphore_signal(
                barrier,
                inc=1,
                device_id={name: lax.rem(me + d, size)},
                device_id_type=MESH,
            )
            expected += 1
    pl.semaphore_wait(barrier, expected)


def total_kernel(axes, count, *refs):
    parts = refs[:count]
    out_ref, held, boxes_a, boxes_b, send_a, recv_a, send_b, recv_b = refs[count:]
    value = parts[0][...]
    for part in parts[1:]:
        value = value + part[...]
    held[0] = value
    greet(axes)
    for level, ((name, size), boxes, send, recv) in enumerate(
        zip(axes, (boxes_a, boxes_b), (send_a, send_b), (recv_a, recv_b))
    ):
        me = lax.axis_index(name)
        copies = []
        for d in range(1, size):
            copy = pltpu.make_async_remote_copy(
                src_ref=held.at[level],
                dst_ref=boxes.at[d],
                send_sem=send.at[d],
                recv_sem=recv.at[d],
                device_id={name: lax.rem(me + d, size)},
                device_id_type=MESH,
            )
            copy.start()
            copies.append(copy)
        for copy in copies:
            copy.wait_recv()
        value = jnp.zeros(value.shape, F32)
        for source in range(size):
            back = lax.rem(me - source + size, size)
            value = value + jnp.where(
                back == 0, held[level], boxes[jnp.maximum(back, 1)]
            )
        for copy in copies:
            copy.wait_send()
        if level == 0:
            held[1] = value
        else:
            out_ref[...] = value


def total_over_devices(parts, axes, collective_id):
    shape = parts[0].shape
    return pl.pallas_call(
        functools.partial(total_kernel, axes, len(parts)),
        out_shape=jax.ShapeDtypeStruct(shape, F32),
        in_specs=[pl.BlockSpec(memory_space=pltpu.VMEM)] * len(parts),
        out_specs=pl.BlockSpec(memory_space=pltpu.VMEM),
        scratch_shapes=[
            pltpu.VMEM((2,) + shape, F32),
            pltpu.VMEM((axes[0][1],) + shape, F32),
            pltpu.VMEM((axes[1][1],) + shape, F32),
            pltpu.SemaphoreType.DMA((axes[0][1],)),
            pltpu.SemaphoreType.DMA((axes[0][1],)),
            pltpu.SemaphoreType.DMA((axes[1][1],)),
            pltpu.SemaphoreType.DMA((axes[1][1],)),
        ],
        compiler_params=pltpu.CompilerParams(collective_id=collective_id, has_side_effects=True),
    )(*parts)


def spread_sum_kernel(axes, x_ref, out_ref, boxes_a, boxes_b, held, *sems):
    send_a, recv_a, send_b, recv_b, send_c, recv_c = sems
    (name_a, size_a), (name_b, size_b) = axes
    me_a, me_b = lax.axis_index(name_a), lax.axis_index(name_b)
    piece = x_ref.shape[0] // size_a
    greet(axes)

    def rows(index):
        return pl.ds(pl.multiple_of(index * piece, 8), piece)

    copies = []
    for d in range(1, size_a):
        peer = lax.rem(me_a + d, size_a)
        copy = pltpu.make_async_remote_copy(
            src_ref=x_ref.at[rows(peer)],
            dst_ref=boxes_a.at[d],
            send_sem=send_a.at[d],
            recv_sem=recv_a.at[d],
            device_id={name_a: peer},
            device_id_type=MESH,
        )
        copy.start()
        copies.append(copy)
    value = x_ref[rows(me_a)]
    for d in range(1, size_a):
        copies[d - 1].wait_recv()
        value = value + boxes_a[d]
    held[0] = value
    for copy in copies:
        copy.wait_send()
    copies = []
    for d in range(1, size_b):
        copy = pltpu.make_async_remote_copy(
            src_ref=held.at[0],
            dst_ref=boxes_b.at[d],
            send_sem=send_b.at[d],
            recv_sem=recv_b.at[d],
            device_id={name_b: lax.rem(me_b + d, size_b)},
            device_id_type=MESH,
        )
        copy.start()
        copies.append(copy)
    for copy in copies:
        copy.wait_recv()
    value = jnp.zeros(value.shape, F32)
    for source in range(size_b):
        back = lax.rem(me_b - source + size_b, size_b)
        value = value + jnp.where(back == 0, held[0], boxes_b[jnp.maximum(back, 1)])
    held[1] = value
    out_ref[rows(me_a)] = value
    for copy in copies:
        copy.wait_send()
    copies = []
    for d in range(1, size_a):
        copy = pltpu.make_async_remote_copy(
            src_ref=held.at[1],
            dst_ref=out_ref.at[rows(me_a)],
            send_sem=send_c.at[d],
            recv_sem=recv_c.at[d],
            device_id={name_a: lax.rem(me_a + d, size_a)},
            device_id_type=MESH,
        )
        copy.start()
        copies.append(copy)
    for copy in copies:
        copy.wait()


def spread_sum(x, axes, collective_id):
    (_, size_a), (_, size_b) = axes
    rows = x.shape[0]
    padded = -(-rows // (8 * size_a)) * 8 * size_a
    x = jnp.pad(x, ((0, padded - rows), (0, 0)))
    piece = padded // size_a
    sems = []
    for size in (size_a, size_b, size_a):
        sems += [pltpu.SemaphoreType.DMA((size,))] * 2
    total = pl.pallas_call(
        functools.partial(spread_sum_kernel, axes),
        out_shape=jax.ShapeDtypeStruct(x.shape, F32),
        in_specs=[pl.BlockSpec(memory_space=pltpu.VMEM)],
        out_specs=pl.BlockSpec(memory_space=pltpu.VMEM),
        scratch_shapes=[
            pltpu.VMEM((size_a, piece, 128), F32),
            pltpu.VMEM((size_b, piece, 128), F32),
            pltpu.VMEM((2, piece, 128), F32),
        ]
        + sems,
        compiler_params=pltpu.CompilerParams(collective_id=collective_id, has_side_effects=True),
    )(x)
    return total[:rows]


def teacher_kernel(
    p_rows, width, above, slab, below, first, second, bypass, inner, mask, out_ref, even, odd, mid
):
    images = slab.shape[1]
    lanes = slab.shape[2]
    m_rows = p_rows + 2
    zero = jnp.zeros((images, 128), BF16)
    for r in range(-3, 2 * p_rows + 2):
        if r < 0:
            source, at = above, r + 3
        elif r < 2 * p_rows:
            source, at = slab, r
        else:
            source, at = below, r - 2 * p_rows
        target, index = (even, r // 2 + 1) if r % 2 == 0 else (odd, (r + 1) // 2 + 1)
        target[index, :, 128 : 128 + lanes] = source[at]
    for i in range(m_rows):
        even[i, :, 0:128] = zero
    for i in range(m_rows + 1):
        odd[i, :, 0:128] = zero
    wide_zero = jnp.zeros((images, CT_OUT), BF16)
    for i in range(m_rows):
        mid[i, :, 0:CT_OUT] = wide_zero
        mid[i, :, (width + 1) * CT_OUT : (width + 2) * CT_OUT] = wide_zero
    scale, shift = inner[0:1], inner[1:2]
    top, bottom = mask[0:1], mask[1:2]

    def first_step(q, carry):
        at = pl.multiple_of(q * 256, 256)
        window = pl.ds(at, 384)
        left = jnp.concatenate(
            [odd[0:m_rows, :, window], even[0:m_rows, :, window], odd[1 : m_rows + 1, :, window]],
            axis=2,
        ).reshape(m_rows * images, 9 * CT_IN)
        z = scale * matmul(left, first[...]) + shift
        act = (z * sigmoid(z)).reshape(m_rows, images, CT_OUT)
        here = pl.ds(pl.multiple_of(at + CT_OUT, 256), CT_OUT)
        mid[0, :, here] = (act[0] * top).astype(BF16)
        mid[1 : p_rows + 1, :, here] = act[1 : p_rows + 1].astype(BF16)
        mid[p_rows + 1, :, here] = (act[p_rows + 1] * bottom).astype(BF16)
        return carry

    lax.fori_loop(0, width, first_step, 0)
    out_ref[...] = jnp.zeros(out_ref.shape, F32)
    lane = lax.broadcasted_iota(jnp.int32, (images, 128), 1)

    def second_step(q, carry):
        at = pl.multiple_of(q * 256, 256)
        window = pl.ds(at, 3 * CT_OUT)
        corner = pl.ds(pl.multiple_of(at + 128, 128), 128)
        left = jnp.concatenate(
            [mid[0:p_rows, :, window], mid[1 : p_rows + 1, :, window], mid[2 : p_rows + 2, :, window]],
            axis=2,
        ).reshape(p_rows * images, 9 * CT_OUT)
        corner_act = even[1 : p_rows + 1, :, corner].reshape(p_rows * images, CT_IN)
        y = matmul(left, second[...]) + matmul(corner_act, bypass[...])
        square = y * y
        energy = jnp.sum(square[:, 0:128] + square[:, 128:256], axis=1, keepdims=True)
        energy = (energy * (1.0 / CT_OUT)).reshape(p_rows, images, 1)
        for p in range(p_rows):
            chunk, start = divmod((p + 1) * width, 128)
            where = slice(chunk * 128, chunk * 128 + 128)
            out_ref[:, where] = jnp.where(lane == start + q, energy[p], out_ref[:, where])
        return carry

    lax.fori_loop(0, width, second_step, 0)


def teacher_energies(above, slab, below, first, second, bypass, inner, mask, tile):
    rows, images, lanes = slab.shape
    p_rows, width = rows // 2, lanes // (2 * CT_IN)
    out_lanes = -(-(p_rows + 3) * width // 128) * 128
    m_rows = p_rows + 2
    whole = lambda a: pl.BlockSpec(a.shape, lambda i: (0,) * a.ndim)
    by_image = lambda a: pl.BlockSpec((a.shape[0], tile, a.shape[2]), lambda i: (0, i, 0))
    positions = images * p_rows * width
    return pl.pallas_call(
        functools.partial(teacher_kernel, p_rows, width),
        grid=(images // tile,),
        in_specs=[by_image(above), by_image(slab), by_image(below)]
        + [whole(a) for a in (first, second, bypass, inner, mask)],
        out_specs=pl.BlockSpec((tile, out_lanes), lambda i: (i, 0)),
        out_shape=jax.ShapeDtypeStruct((images, out_lanes), F32),
        scratch_shapes=[
            pltpu.VMEM((m_rows, tile, 128 + lanes), BF16),
            pltpu.VMEM((m_rows + 1, tile, 128 + lanes), BF16),
            pltpu.VMEM((m_rows, tile, (width + 2) * CT_OUT), BF16),
        ],
        compiler_params=pltpu.CompilerParams(vmem_limit_bytes=VMEM_LIMIT),
        cost_estimate=pl.CostEstimate(
            flops=positions * 2 * CT_OUT * (9 * CT_IN + 9 * CT_OUT + CT_IN),
            bytes_accessed=images * (rows + 5) * lanes * 2,
            transcendentals=positions * CT_OUT,
        ),
    )(above, slab, below, first, second, bypass, inner, mask)


def entry_tables(tot_ref, norm_ref, w0, w1):
    means, scales = group_norms(tot_ref[...], entry_counts(tot_ref), CS_IN)
    scale = per_image(w0, w1, scales)
    shift = per_image(w0, w1, [-m * s for m, s in zip(means, scales)])
    gain, bias = norm_ref[0:1], norm_ref[1:2]
    present = w0 + w1
    return gain * scale, gain * shift + bias * present, scale, shift


def inner_tables(tot_ref, inner_ref, norm_ref, w0, w1):
    means, scales = group_norms(inner_ref[...], inner_counts(tot_ref), CS_OUT)
    scale = per_image(w0, w1, scales)
    shift = per_image(w0, w1, [-m * s for m, s in zip(means, scales)])
    gain, bias = norm_ref[0:1], norm_ref[1:2]
    present = w0 + w1
    return gain * scale, gain * shift + bias * present, scale, shift


def add_rows(ref, value):
    first = pl.program_id(0) == 0

    @pl.when(first)
    def _():
        ref[...] = value

    @pl.when(jnp.logical_not(first))
    def _():
        ref[...] += value


def forward_kernel(
    p_rows, raw, w0_ref, w1_ref, tot, norm, mask, weights, even, odd, out_ref, stats
):
    images, lanes = raw.shape[1:]
    w0, w1 = w0_ref[...], w1_ref[...]
    gain, bias, _, _ = entry_tables(tot, norm, w0, w1)
    gain2, bias2 = twice(gain), twice(bias)
    zero = jnp.zeros((images, 128), BF16)

    def activate(row, target, index):
        keep = twice(mask[pl.ds(row, 1)])
        target[index, :, 0:128] = zero
        for c in range(0, lanes, 256):
            z = raw[row, :, c : c + 256].astype(F32) * gain2 + bias2
            target[index, :, 128 + c : 384 + c] = (z * sigmoid(z) * keep).astype(BF16)

    def pair(i, carry):
        activate(2 * i, even, i)
        activate(2 * i + 1, odd, i)
        return carry

    f_rows = p_rows + 5
    lax.fori_loop(0, f_rows, pair, 0)
    activate(2 * f_rows, even, f_rows)

    def convolve(j, sums):
        window = pl.ds(pl.multiple_of(j * 256, 256), 384)
        left = jnp.concatenate(
            [even[0:f_rows, :, window], odd[0:f_rows, :, window], even[1 : f_rows + 1, :, window]],
            axis=2,
        ).reshape(f_rows * images, 9 * 128)
        y = matmul(left, weights[...]).reshape(f_rows, images, 256)
        out_ref[:, :, pl.ds(pl.multiple_of(j * 256, 256), 256)] = y
        own = y[2 : 2 + p_rows]
        s = jnp.sum(own, axis=0)
        q = jnp.sum(own * own, axis=0)
        return (sums[0] + s[:, 0:128] + s[:, 128:256], sums[1] + q[:, 0:128] + q[:, 128:256])

    blank = jnp.zeros((images, 128), F32)
    s, q = lax.fori_loop(0, lanes // 256, convolve, (blank, blank))
    add_rows(stats, grouped_rows(w0, w1, [s, q]))


def whole_spec(a):
    return pl.BlockSpec(a.shape, lambda i: (0,) * a.ndim)


def image_spec(a, tile):
    return pl.BlockSpec((a.shape[0], tile) + a.shape[2:], lambda i: (0, i) + (0,) * (a.ndim - 2))


def table_spec(a, tile):
    return pl.BlockSpec((tile, a.shape[1]), lambda i: (i, 0))


def shape_of(shape, dtype):
    return jax.ShapeDtypeStruct(shape, dtype)


def student_forward(raw, w0, w1, tot, norm, mask, weights, tile):
    rows, images, lanes = raw.shape
    p_rows = (rows - 11) // 2
    outs = [
        shape_of((p_rows + 6, images, 128 + lanes), BF16),
        shape_of((p_rows + 5, images, 128 + lanes), BF16),
        shape_of((p_rows + 5, images, lanes), F32),
    ]
    return pl.pallas_call(
        functools.partial(forward_kernel, p_rows),
        grid=(images // tile,),
        in_specs=[image_spec(raw, tile), table_spec(w0, tile), table_spec(w1, tile)]
        + [whole_spec(a) for a in (tot, norm, mask, weights)],
        out_specs=[image_spec(o, tile) for o in outs] + [pl.BlockSpec((8, 128), lambda i: (0, 0))],
        out_shape=outs + [shape_of((8, 128), F32)],
        compiler_params=pltpu.CompilerParams(vmem_limit_bytes=VMEM_LIMIT),
    )(raw, w0, w1, tot, norm, mask, weights)


def split_bf16(value):
    high = value.astype(BF16)
    return high, (value - high.astype(F32)).astype(BF16)


def block_kernel(
    p_rows,
    first_ref,
    odd,
    w0_ref,
    w1_ref,
    tot,
    inner,
    norm,
    mask,
    weights,
    spread,
    act,
    sum_ref,
    low_ref,
    energy,
):
    images, lanes = first_ref.shape[1:]
    w0, w1 = w0_ref[...], w1_ref[...]
    gain, bias, _, _ = inner_tables(tot, inner, norm, w0, w1)
    gain2, bias2 = twice(gain), twice(bias)
    zero = jnp.zeros((images, 128), BF16)
    f_rows, b_rows = p_rows + 5, p_rows + 3

    def activate(f, carry):
        keep = twice(mask[pl.ds(f, 1)])
        act[f, :, 0:128] = zero
        act[f, :, 128 + lanes : 256 + lanes] = zero
        for c in range(0, lanes, 256):
            z = first_ref[f, :, c : c + 256] * gain2 + bias2
            act[f, :, 128 + c : 384 + c] = (z * sigmoid(z) * keep).astype(BF16)
        return carry

    lax.fori_loop(0, f_rows, activate, 0)

    def convolve(j, carry):
        at = pl.multiple_of(j * 256, 256)
        window = pl.ds(at, 512)
        here = pl.ds(pl.multiple_of(at + 128, 128), 256)
        left = jnp.concatenate(
            [
                act[0:b_rows, :, window],
                act[1 : b_rows + 1, :, window],
                act[2 : b_rows + 2, :, window],
                odd[1 : b_rows + 1, :, here],
            ],
            axis=2,
        ).reshape(b_rows * images, 1792)
        y = matmul(left, weights[...]).reshape(b_rows, images, 256)
        sum_ref[:, :, pl.ds(at, 256)] = y
        low_ref[:, :, pl.ds(at, 256)] = y[1 : p_rows + 1].astype(BF16)
        return carry

    lax.fori_loop(0, lanes // 256, convolve, 0)
    per_chunk = spread.shape[0]
    energy[...] = jnp.zeros(energy.shape, F32)

    def measure(b, carry):
        v = sum_ref[b]
        high, low = split_bf16(v * v)
        table = spread[lax.rem(b, per_chunk)]
        contract = (((1,), (1,)), ((), ()))
        e = lax.dot_general(high, table, contract, preferred_element_type=F32)
        e = e + lax.dot_general(low, table, contract, preferred_element_type=F32)
        chunk = pl.ds(pl.multiple_of(lax.div(b, per_chunk) * 128, 128), 128)
        energy[:, chunk] += e * (1.0 / CS_OUT)
        return carry

    lax.fori_loop(0, b_rows, measure, 0)


def student_block(first_out, odd, w0, w1, tot, inner, norm, mask, weights, spread, tile):
    rows, images, lanes = first_out.shape
    p_rows = rows - 5
    width = lanes // CS_OUT
    energy_lanes = -(-(p_rows + 3) * width // 128) * 128
    outs = [
        shape_of((p_rows + 5, images, 256 + lanes), BF16),
        shape_of((p_rows + 3, images, lanes), F32),
        shape_of((p_rows, images, lanes), BF16),
    ]
    energy = shape_of((images, energy_lanes), F32)
    return pl.pallas_call(
        functools.partial(block_kernel, p_rows),
        grid=(images // tile,),
        in_specs=[image_spec(first_out, tile), image_spec(odd, tile)]
        + [table_spec(w0, tile), table_spec(w1, tile)]
        + [whole_spec(a) for a in (tot, inner, norm, mask, weights, spread)],
        out_specs=[image_spec(o, tile) for o in outs] + [table_spec(energy, tile)],
        out_shape=outs + [energy],
        compiler_params=pltpu.CompilerParams(vmem_limit_bytes=VMEM_LIMIT),
    )(first_out, odd, w0, w1, tot, inner, norm, mask, weights, spread)


def map_kernel(slabs, group, widths, p_counts, *refs):
    student, teacher, present = refs[0:2], refs[2:4], refs[4:6]
    outs, loss_ref = refs[6:8], refs[8]
    sums, boxes = refs[9:11], refs[11:13]
    from_above, from_below = refs[13:15], refs[15:17]
    send, recv, send_halo, recv_halo = refs[17:21]
    me = lax.axis_index("space")
    z, x = lax.div(me, group), lax.rem(me, group)
    greet_barrier = pltpu.get_barrier_semaphore()
    for d in range(1, slabs):
        pl.semaphore_signal(
            greet_barrier,
            inc=1,
            device_id={"space": lax.rem(z + d, slabs) * group + x},
            device_id_type=MESH,
        )
    pl.semaphore_wait(greet_barrier, slabs - 1)

    def halo_copies(res, direction):
        width, p_rows = widths[res], p_counts[res]
        lane = (p_rows * width if direction == 0 else width) // 128 * 128
        target = (from_above, from_below)[direction][res]
        return pltpu.make_async_remote_copy(
            src_ref=teacher[res].at[:, pl.ds(lane, 128)],
            dst_ref=target,
            send_sem=send_halo.at[2 * res + direction],
            recv_sem=recv_halo.at[2 * res + direction],
            device_id={"space": me + (group if direction == 0 else -group)},
            device_id_type=MESH,
        )

    for res in range(2):
        from_above[res][...] = jnp.zeros(from_above[res].shape, F32)
        from_below[res][...] = jnp.zeros(from_below[res].shape, F32)

    ready = refs[21]

    @pl.when(z > 0)
    def _():
        pl.semaphore_signal(
            ready.at[0], inc=1, device_id={"space": me - group}, device_id_type=MESH
        )

    @pl.when(z < slabs - 1)
    def _():
        pl.semaphore_signal(
            ready.at[1], inc=1, device_id={"space": me + group}, device_id_type=MESH
        )
        pl.semaphore_wait(ready.at[0], 1)
        halo_copies(0, 0).start()
        halo_copies(1, 0).start()

    @pl.when(z > 0)
    def _():
        pl.semaphore_wait(ready.at[1], 1)
        halo_copies(0, 1).start()
        halo_copies(1, 1).start()

    copies = []
    for res in range(2):
        width, p_rows = widths[res], p_counts[res]
        images, lanes = student[res].shape
        lane = lax.broadcasted_iota(jnp.int32, (images, lanes), 1)
        own = jnp.logical_and(lane >= width, lane < (p_rows + 1) * width)
        es = jnp.where(own, student[res][...], 0.0)
        et = jnp.where(own, teacher[res][...], 0.0)
        columns = [
            jnp.sum(v, axis=1, keepdims=True) for v in (es * es, et * et, es * et)
        ]
        small_lane = lax.broadcasted_iota(jnp.int32, (images, 128), 1)
        packed = jnp.zeros((images, 128), F32)
        for k, column in enumerate(columns):
            packed = jnp.where(small_lane == k, column, packed)
        padded = sums[res].shape[1]
        packed = jnp.concatenate([packed, jnp.zeros((padded - images, 128), F32)], axis=0)
        sums[res][...] = packed.T[0:8]
        for d in range(1, slabs):
            copy = pltpu.make_async_remote_copy(
                src_ref=sums[res],
                dst_ref=boxes[res].at[d],
                send_sem=send.at[res * slabs + d],
                recv_sem=recv.at[res * slabs + d],
                device_id={"space": lax.rem(z + d, slabs) * group + x},
                device_id_type=MESH,
            )
            copy.start()
            copies.append(copy)
    for copy in copies:
        copy.wait()

    @pl.when(z < slabs - 1)
    def _():
        halo_copies(0, 0).wait_send()
        halo_copies(1, 0).wait_send()
        halo_copies(0, 1).wait_recv()
        halo_copies(1, 1).wait_recv()

    @pl.when(z > 0)
    def _():
        halo_copies(0, 1).wait_send()
        halo_copies(1, 1).wait_send()
        halo_copies(0, 0).wait_recv()
        halo_copies(1, 0).wait_recv()

    loss = jnp.zeros((1, 128), F32)
    for res in range(2):
        width, p_rows = widths[res], p_counts[res]
        images, lanes = student[res].shape
        total = sums[res][...]
        for d in range(1, slabs):
            total = total + boxes[res][d]
        padded = total.shape[1]
        total = jnp.concatenate([total, jnp.zeros((120, padded), F32)], axis=0).T[0:images]
        ss, tt, st = total[:, 0:1], total[:, 1:2], total[:, 2:3]
        scale_s = lax.rsqrt(ss + 1e-12)
        scale_t = lax.rsqrt(tt + 1e-12)
        pulled = TRANSFER_WEIGHT * scale_s * (scale_s * ss - scale_t * st)
        lane = lax.broadcasted_iota(jnp.int32, (images, lanes), 1)
        shift = p_rows * width
        chunks = lanes // 128
        first_rows = from_below[res][...]
        last_rows = from_above[res][...]
        if shift % 128:
            first_rows = pltpu.roll(first_rows, shift % 128, 1)
            last_rows = pltpu.roll(last_rows, 128 - shift % 128, 1)
        blank = jnp.zeros((images, 128), F32)
        before = [last_rows] + [blank] * (chunks - 1)
        after = [blank] * (chunks - 1) + [first_rows]
        before = jnp.concatenate(before, axis=1) if chunks > 1 else before[0]
        after = jnp.concatenate(after, axis=1) if chunks > 1 else after[0]
        et = jnp.where(lane < width, before, teacher[res][...])
        et = jnp.where(lane >= (p_rows + 1) * width, after, et)
        u = student[res][...] * scale_s
        difference = u - et * scale_t
        own = jnp.logical_and(lane >= width, lane < (p_rows + 1) * width)
        squares = jnp.where(own, difference * difference, 0.0)
        kept = present[res][...]
        for c in range(chunks):
            loss = loss + jnp.sum(squares[:, c * 128 : c * 128 + 128] * kept, axis=0, keepdims=True)
        outs[res][...] = (TRANSFER_WEIGHT * difference - u * pulled) * (scale_s * (2.0 / CS_OUT))
    loss_ref[...] = jnp.concatenate(
        [loss * (TRANSFER_WEIGHT / 2), jnp.zeros((7, 128), F32)], axis=0
    )


def attention_maps(student, teacher, present, widths, p_counts, slabs, group, collective_id):
    padded = [-(-s.shape[0] // 128) * 128 for s in student]
    images = [s.shape[0] for s in student]
    vmem = pl.BlockSpec(memory_space=pltpu.VMEM)
    return pl.pallas_call(
        functools.partial(map_kernel, slabs, group, widths, p_counts),
        out_shape=[shape_of(s.shape, F32) for s in student] + [shape_of((8, 128), F32)],
        in_specs=[vmem] * 6,
        out_specs=[vmem] * 3,
        scratch_shapes=[pltpu.VMEM((8, n), F32) for n in padded]
        + [pltpu.VMEM((slabs, 8, n), F32) for n in padded]
        + [pltpu.VMEM((n, 128), F32) for n in images] * 2
        + [pltpu.SemaphoreType.DMA((2 * slabs,))] * 2
        + [pltpu.SemaphoreType.DMA((4,))] * 2
        + [pltpu.SemaphoreType.REGULAR((2,))],
        compiler_params=pltpu.CompilerParams(collective_id=collective_id, has_side_effects=True),
    )(*student, *teacher, *present)


def back_kernel(
    p_rows,
    sum_ref,
    cot,
    factor,
    spread,
    first_ref,
    act,
    odd,
    w0_ref,
    w1_ref,
    tot,
    inner,
    norm,
    mask,
    weights,
    flow_ref,
    grad,
    kernel_ref,
    stats,
):
    images, lanes = sum_ref.shape[1:]
    w0, w1 = w0_ref[...], w1_ref[...]
    gain, bias, scale, shift = inner_tables(tot, inner, norm, w0, w1)
    gain2, bias2, scale2, shift2 = twice(gain), twice(bias), twice(scale), twice(shift)
    zero = jnp.zeros((images, 128), BF16)
    b_rows, k_rows = p_rows + 3, p_rows + 1
    per_chunk = spread.shape[0]

    def block_grad(b, carry):
        keep = twice(mask[pl.ds(b, 1)])
        chunk = pl.ds(pl.multiple_of(lax.div(b, per_chunk) * 128, 128), 128)
        high, low = split_bf16(factor[:, chunk])
        table = spread[lax.rem(b, per_chunk)]
        wide = matmul(high, table) + matmul(low, table)
        grad[b, :, 0:128] = zero
        grad[b, :, 128 + lanes : 256 + lanes] = zero
        for c in range(0, lanes, 256):
            v = cot[b, :, c : c + 256].astype(F32) + wide[:, c : c + 256] * sum_ref[b, :, c : c + 256]
            grad[b, :, 128 + c : 384 + c] = (v * keep).astype(BF16)
        return carry

    lax.fori_loop(0, b_rows, block_grad, 0)

    @pl.when(pl.program_id(0) == 0)
    def _():
        kernel_ref[...] = jnp.zeros(kernel_ref.shape, F32)

    def step(j, sums):
        at = pl.multiple_of(j * 256, 256)
        window = pl.ds(at, 512)
        here = pl.ds(pl.multiple_of(at + 128, 128), 256)
        left = jnp.concatenate(
            [
                grad[0:k_rows, :, window],
                grad[1 : k_rows + 1, :, window],
                grad[2 : k_rows + 2, :, window],
            ],
            axis=2,
        ).reshape(k_rows * images, 1536)
        y = matmul(left, weights[...]).reshape(k_rows, images, 256)
        ones, cross = sums
        for k in range(k_rows):
            x = first_ref[k + 2, :, pl.ds(at, 256)]
            z = x * gain2 + bias2
            s = sigmoid(z)
            flow = y[k] * (s * (1.0 + z * (1.0 - s)))
            flow_ref[k, :, pl.ds(at, 256)] = flow
            if k < p_rows:
                crossed = flow * (x * scale2 + shift2)
                ones = ones + flow[:, 0:128] + flow[:, 128:256]
                cross = cross + crossed[:, 0:128] + crossed[:, 128:256]
        right = jnp.concatenate(
            [
                act[1 : p_rows + 1, :, window],
                act[2 : p_rows + 2, :, window],
                act[3 : p_rows + 3, :, window],
                odd[2 : p_rows + 2, :, here],
            ],
            axis=2,
        ).reshape(p_rows * images, 1792)
        own = grad[1 : p_rows + 1, :, here].reshape(p_rows * images, 256)
        kernel_ref[...] += lax.dot_general(
            own, right, (((0,), (0,)), ((), ())), preferred_element_type=F32
        )
        return ones, cross

    blank = jnp.zeros((images, 128), F32)
    ones, cross = lax.fori_loop(0, lanes // 256, step, (blank, blank))
    add_rows(stats, grouped_rows(w0, w1, [ones, cross]))


def student_back(
    block_sum, cot, factor, spread, first_out, act, odd, w0, w1, tot, inner, norm, mask, weights, tile
):
    rows, images, lanes = block_sum.shape
    p_rows = rows - 3
    outs = [
        shape_of((p_rows + 1, images, lanes), F32),
        shape_of((p_rows + 3, images, 256 + lanes), BF16),
    ]
    kernels = shape_of((256, 1792), F32)
    stats = shape_of((8, 128), F32)
    return pl.pallas_call(
        functools.partial(back_kernel, p_rows),
        grid=(images // tile,),
        in_specs=[image_spec(block_sum, tile), image_spec(cot, tile), table_spec(factor, tile)]
        + [whole_spec(spread), image_spec(first_out, tile), image_spec(act, tile)]
        + [image_spec(odd, tile), table_spec(w0, tile), table_spec(w1, tile)]
        + [whole_spec(a) for a in (tot, inner, norm, mask, weights)],
        out_specs=[image_spec(o, tile) for o in outs] + [whole_spec(kernels), whole_spec(stats)],
        out_shape=outs + [kernels, stats],
        compiler_params=pltpu.CompilerParams(vmem_limit_bytes=VMEM_LIMIT),
    )(block_sum, cot, factor, spread, first_out, act, odd, w0, w1, tot, inner, norm, mask, weights)


def entry_kernel(
    p_rows,
    flow_ref,
    first_ref,
    grad,
    even,
    odd,
    raw,
    w0_ref,
    w1_ref,
    tot,
    inner,
    pulled,
    norm_in,
    norm,
    mask,
    weights_even,
    weights_odd,
    out_ref,
    kernel_ref,
    stats,
    first_grad,
):
    images, lanes = first_ref.shape[1:]
    w0, w1 = w0_ref[...], w1_ref[...]
    gain, _, scale, shift = inner_tables(tot, inner, norm, w0, w1)
    counts = inner_counts(tot)
    folded = fold(pulled[...], CS_OUT)
    ones_mean = per_image(w0, w1, [folded[g : g + 1] / counts[g] for g in range(2)])
    cross_mean = per_image(w0, w1, [folded[2 + g : 3 + g] / counts[g] for g in range(2)])
    gain2, scale2, shift2 = twice(gain), twice(scale), twice(shift)
    ones2, cross2 = twice(ones_mean), twice(cross_mean)
    zero = jnp.zeros((images, 128), BF16)

    def first_rows(k, carry):
        keep = twice(mask[pl.ds(k, 1)])
        first_grad[k, :, lanes : lanes + 128] = zero
        for c in range(0, lanes, 256):
            normed = first_ref[k + 2, :, c : c + 256] * scale2 + shift2
            v = gain2 * (flow_ref[k, :, c : c + 256] - ones2 - normed * cross2)
            first_grad[k, :, c : c + 256] = (v * keep).astype(BF16)
        return carry

    lax.fori_loop(0, p_rows + 1, first_rows, 0)

    @pl.when(pl.program_id(0) == 0)
    def _():
        kernel_ref[...] = jnp.zeros(kernel_ref.shape, F32)

    gain, bias, scale, shift = entry_tables(tot, norm_in, w0, w1)
    gain2, bias2, scale2, shift2 = twice(gain), twice(bias), twice(scale), twice(shift)

    def step(j, sums):
        at = pl.multiple_of(j * 256, 256)
        window = pl.ds(at, 384)
        here = pl.ds(at, 256)
        middle = pl.ds(pl.multiple_of(at + 128, 128), 256)
        upper = first_grad[0:p_rows, :, window].reshape(p_rows * images, 384)
        lower = first_grad[1 : p_rows + 1, :, window].reshape(p_rows * images, 384)
        block = grad[1 : p_rows + 1, :, middle].reshape(p_rows * images, 256)
        rows_even = matmul(jnp.concatenate([upper, block], axis=1), weights_even[...])
        rows_odd = matmul(jnp.concatenate([upper, lower], axis=1), weights_odd[...])
        ones, cross = sums
        for parity, rows in enumerate((rows_even, rows_odd)):
            low = rows.astype(BF16).reshape(p_rows, images, 256)
            for p in range(p_rows):
                out_ref[2 * p + parity, :, here] = low[p]
                x = raw[2 * p + parity + 5, :, here].astype(F32)
                z = x * gain2 + bias2
                s = sigmoid(z)
                flow = low[p].astype(F32) * (s * (1.0 + z * (1.0 - s)))
                crossed = flow * (x * scale2 + shift2)
                ones = ones + flow[:, 0:128] + flow[:, 128:256]
                cross = cross + crossed[:, 0:128] + crossed[:, 128:256]
        right = jnp.concatenate(
            [
                even[2 : p_rows + 2, :, window],
                odd[2 : p_rows + 2, :, window],
                even[3 : p_rows + 3, :, window],
            ],
            axis=2,
        ).reshape(p_rows * images, 1152)
        own = first_grad[0:p_rows, :, here].reshape(p_rows * images, 256)
        kernel_ref[...] += lax.dot_general(
            own, right, (((0,), (0,)), ((), ())), preferred_element_type=F32
        )
        return ones, cross

    blank = jnp.zeros((images, 128), F32)
    ones, cross = lax.fori_loop(0, lanes // 256, step, (blank, blank))
    add_rows(stats, grouped_rows(w0, w1, [ones, cross]))


def student_entry(
    flow, first_out, grad, even, odd, raw, w0, w1, tot, inner, pulled, norm_in, norm, mask,
    weights_even, weights_odd, tile,
):
    rows, images, lanes = flow.shape
    p_rows = rows - 1
    out = shape_of((2 * p_rows, images, lanes), BF16)
    kernels = shape_of((256, 1152), F32)
    stats = shape_of((8, 128), F32)
    big = (flow, first_out, grad, even, odd, raw)
    shared = (tot, inner, pulled, norm_in, norm, mask, weights_even, weights_odd)
    return pl.pallas_call(
        functools.partial(entry_kernel, p_rows),
        grid=(images // tile,),
        in_specs=[image_spec(a, tile) for a in big]
        + [table_spec(w0, tile), table_spec(w1, tile)]
        + [whole_spec(a) for a in shared],
        out_specs=[image_spec(out, tile), whole_spec(kernels), whole_spec(stats)],
        out_shape=[out, kernels, stats],
        scratch_shapes=[pltpu.VMEM((p_rows + 1, tile, 128 + lanes), BF16)],
        compiler_params=pltpu.CompilerParams(vmem_limit_bytes=VMEM_LIMIT),
    )(*big, w0, w1, *shared)


def select(entries, shape):
    table = np.zeros(shape, np.float32)
    for index in entries:
        table[index] = 1.0
    return jnp.asarray(table, BF16)


def banded(selection, taps):
    k, n, b = selection.shape
    _, r, c = taps.shape
    out = jnp.einsum("knb,brc->krnc", selection, taps, preferred_element_type=F32)
    return out.astype(BF16).reshape(k * r, n * c)


def first_bands(kernel):
    pick = select([(2 * q + b + 3, q, b) for q in range(4) for b in range(3)], (12, 4, 3))
    return jnp.concatenate([banded(pick, kernel[a]) for a in range(3)], axis=0)


def second_bands(kernel, shortcut):
    pick = select([(q + b + 1, q, b) for q in range(4) for b in range(3)], (8, 4, 3))
    corner = select([(2 * q, q, 0) for q in range(4)], (8, 4, 1))
    return jnp.concatenate(
        [banded(pick, kernel[a]) for a in range(3)] + [banded(corner, shortcut[None])], axis=0
    )


def second_back_bands(kernel):
    pick = select([(s - b + 3, s, b) for s in range(4) for b in range(3)], (8, 4, 3))
    turned = jnp.swapaxes(kernel, 2, 3)
    return jnp.concatenate([banded(pick, turned[2 - d]) for d in range(3)], axis=0)


def first_back_bands(kernel, shortcut):
    entries = []
    for q in range(6):
        for b in range(3):
            s = 2 * q + b - 1
            if 0 <= s < 8:
                entries.append((q, s, b))
    pick = select(entries, (6, 8, 3))
    corner = select([(q, 2 * q, 0) for q in range(4)], (4, 8, 1))
    turned = jnp.swapaxes(kernel, 2, 3)
    rows_even = jnp.concatenate(
        [banded(pick, turned[1]), banded(corner, jnp.swapaxes(shortcut, 0, 1)[None])], axis=0
    )
    rows_odd = jnp.concatenate([banded(pick, turned[2]), banded(pick, turned[0])], axis=0)
    return rows_even, rows_odd


def spread_table(width):
    lanes = width * CS_OUT
    count = min(128 // width, 8)
    lane = lax.broadcasted_iota(jnp.int32, (count, 128, lanes), 1)
    column = lax.broadcasted_iota(jnp.int32, (count, 128, lanes), 2) // CS_OUT
    row = lax.broadcasted_iota(jnp.int32, (count, 128, lanes), 0)
    return (lane == row * width + column).astype(BF16)


def second_from_products(products):
    main = products[:, 0:1536].reshape(4, CS_OUT, 3, 8, CS_OUT)
    taps = []
    for b in range(3):
        taps.append(sum(main[q, :, :, q + b + 1] for q in range(4)))
    second = jnp.transpose(jnp.stack(taps), (2, 0, 3, 1))
    side = products[:, 1536:].reshape(4, CS_OUT, 8, CS_IN)
    shortcut = jnp.transpose(sum(side[q, :, 2 * q] for q in range(4)))
    return second, shortcut


def first_from_products(products):
    main = products.reshape(4, CS_OUT, 3, 12, CS_IN)
    taps = []
    for b in range(3):
        taps.append(sum(main[q, :, :, 2 * q + b + 3] for q in range(4)))
    return jnp.transpose(jnp.stack(taps), (2, 0, 3, 1))


def renew(weights, gradient, moment, average, factor):
    descent = gradient + WEIGHT_DECAY * weights
    velocity = MOMENTUM * moment + descent
    updated = weights - factor * (descent + MOMENTUM * velocity)
    smoothed = AVERAGING * average + (1.0 - AVERAGING) * updated
    return (gradient, velocity, smoothed, updated)


def body(
    space,
    batch,
    small_in,
    large_in,
    small_teacher,
    large_teacher,
    small_groups,
    large_groups,
    small_cot,
    large_cot,
    teacher_gains,
    teacher_first,
    teacher_inner,
    teacher_second,
    teacher_bypass,
    entry_norm,
    first_conv,
    inner_norm,
    second_conv,
    shortcut,
    momentum_entry,
    momentum_first,
    momentum_inner,
    momentum_second,
    momentum_shortcut,
    average_entry,
    average_first,
    average_inner,
    average_second,
    average_shortcut,
):
    slabs = SLABS
    group = space // slabs
    axes = (("space", space), ("batch", batch))
    me = lax.axis_index("space")
    z, x = me // group, me % group
    total_positions = batch * (small_in.shape[0] * SIDE * SIDE // 4 + large_in.shape[0] * SIDE * SIDE)
    pixels = [small_in, large_in]
    teachers = [small_teacher, large_teacher]
    labels = [small_groups, large_groups]
    cots = [small_cot, large_cot]
    sides = [SIDE, 2 * SIDE]
    per_device = [p.shape[0] // space for p in pixels]
    local_rows = [p.shape[1] for p in pixels]
    images = [slabs * n for n in per_device]
    padded = [-(-n // 16) * 16 for n in images]
    tiles = [32 if padded[0] % 32 == 0 else 16, padded[1]]
    p_counts = [s // (2 * slabs) for s in sides]
    widths = [s // 2 for s in sides]

    def to_sub(d):
        return [(k, k // group * group + (k % group + d) % group) for k in range(space)]

    def to_slab(d):
        return [(k, (k // group + d) % slabs * group + k % group) for k in range(space)]

    def down():
        return [(k, k + group) for k in range(space - group)]

    def up():
        return [(k, k - group) for k in range(group, space)]

    def pick_images(array, res, sub):
        n, rows, lanes = array.shape
        parts = array.reshape(slabs, group, per_device[res], rows, lanes)
        part = lax.dynamic_index_in_dim(parts, sub, 1, False)
        return jnp.transpose(part.reshape(images[res], rows, lanes), (1, 0, 2))

    def gather_rows(pieces):
        if group == 1:
            return pieces[0]
        ordered = [lax.select_n((x - s) % group, *pieces) for s in range(group)]
        return jnp.concatenate(ordered, axis=0)

    def exchange_rows(array, res):
        pieces = [pick_images(array, res, x)]
        for d in range(1, group):
            pieces.append(
                lax.ppermute(pick_images(array, res, (x + d) % group), "space", to_sub(d))
            )
        return gather_rows(pieces)

    def pad_images(array, res):
        extra = padded[res] - images[res]
        return jnp.pad(array, ((0, 0), (0, extra), (0, 0))) if extra else array

    def halos(slab, res, above, below):
        return (
            lax.ppermute(slab[slab.shape[0] - above :], "space", down()),
            lax.ppermute(slab[:below], "space", up()),
        )

    weights = []
    for res in range(2):
        mine = lax.dynamic_index_in_dim(
            labels[res].reshape(slabs, group, per_device[res]), x, 1, False
        ).reshape(images[res])
        mine = jnp.pad(mine, (0, padded[res] - images[res]), constant_values=-1)
        weights.append(
            [
                jnp.broadcast_to((mine == g).astype(F32)[:, None], (padded[res], 128))
                for g in range(2)
            ]
        )
    present = [w[0] + w[1] for w in weights]

    top = (z > 0).astype(F32)
    bottom = (z < slabs - 1).astype(F32)

    def row_mask(first, count, inside):
        row = lax.broadcasted_iota(jnp.int32, (-(-count // 8) * 8, 128), 0) + first
        return jnp.where(row < 0, top, jnp.where(row >= inside, bottom, 1.0))

    tile_norm = lambda n: jnp.pad(jnp.tile(n, (1, 128 // n.shape[1])), ((0, 6), (0, 0)))
    norm_in, norm_mid = tile_norm(entry_norm), tile_norm(inner_norm)
    first_low = first_conv.astype(BF16)
    second_low = second_conv.astype(BF16)
    shortcut_low = shortcut.astype(BF16)
    bands_first = first_bands(first_low)
    bands_second = second_bands(second_low, shortcut_low)
    bands_second_back = second_back_bands(second_low)
    bands_even, bands_odd = first_back_bands(first_low, shortcut_low)
    spreads = [spread_table(w) for w in widths]

    slabs_in = [exchange_rows(pixels[res], res) for res in range(2)]
    raw = []
    for res in range(2):
        above, below = halos(slabs_in[res], res, 5, 6)
        raw.append(pad_images(jnp.concatenate([above, slabs_in[res], below], axis=0), res))
    unpadded = [[w[: images[res]] for w in weights[res]] for res in range(2)]
    entry_sums = input_stats(slabs_in, unpadded)
    entry_total = total_over_devices([entry_sums], axes, 0)

    cot_rows = []
    for res in range(2):
        c = jnp.pad(jnp.transpose(cots[res], (1, 0, 2)), ((1, 2), (0, 0), (0, 0)))
        count = p_counts[res] + 3
        pieces = []
        for d in range(slabs):
            part = lax.dynamic_slice_in_dim(c, (z + d) % slabs * p_counts[res], count, 0)
            pieces.append(lax.ppermute(part, "space", to_slab(d)) if d else part)
        ordered = [lax.select_n((z - s) % slabs, *pieces) for s in range(slabs)]
        cot_rows.append(pad_images(jnp.concatenate(ordered, axis=1), res))

    evens, odds, firsts, first_sums = [], [], [], []
    for res in range(2):
        even, odd, first, sums = student_forward(
            raw[res],
            *weights[res],
            entry_total,
            norm_in,
            row_mask(-5, 2 * p_counts[res] + 11, 2 * p_counts[res]),
            bands_first,
            tiles[res],
        )
        evens.append(even)
        odds.append(odd)
        firsts.append(first)
        first_sums.append(sums)
    inner_total = total_over_devices(first_sums, axes, 1)
    acts, sums_out, lows, energies = [], [], [], []
    for res in range(2):
        act, block_sum, low, energy = student_block(
            firsts[res],
            odds[res],
            *weights[res],
            entry_total,
            inner_total,
            norm_mid,
            row_mask(-2, p_counts[res] + 5, p_counts[res]),
            bands_second,
            spreads[res],
            tiles[res],
        )
        acts.append(act)
        sums_out.append(block_sum)
        lows.append(low)
        energies.append(energy)
    block_outs = []
    for res in range(2):
        low = lows[res][:, : images[res]]
        rows, _, lanes = low.shape
        low = low.reshape(rows, slabs, per_device[res], lanes)
        pieces = []
        for d in range(slabs):
            part = lax.dynamic_index_in_dim(low, (z + d) % slabs, 1, False)
            pieces.append(lax.ppermute(part, "space", to_slab(d)) if d else part)
        ordered = [lax.select_n((z - s) % slabs, *pieces) for s in range(slabs)]
        block_outs.append(jnp.transpose(jnp.concatenate(ordered, axis=0), (1, 0, 2)))

    mask_mid = jnp.zeros((8, CT_OUT), F32).at[0].set(top).at[1].set(bottom)
    first_t = teacher_first.reshape(9 * CT_IN, CT_OUT)
    second_t = teacher_second.reshape(9 * CT_OUT, CT_OUT)
    teacher_maps = []
    for res in range(2):
        lanes = teachers[res].shape[2]
        gain = jnp.tile(teacher_gains[0], lanes // CT_IN)
        bias = jnp.tile(teacher_gains[1], lanes // CT_IN)
        active = jax.nn.silu(gain * teachers[res].astype(F32) + bias).astype(BF16)
        slab = exchange_rows(active, res)
        above, below = halos(slab, res, 3, 2)
        args = [pad_images(a, res) for a in (above, slab, below)]
        teacher_maps.append(
            teacher_energies(
                *args,
                first_t,
                second_t,
                teacher_bypass,
                jnp.pad(teacher_inner, ((0, 6), (0, 0))),
                mask_mid,
                tiles[0] if res == 0 else 16,
            )
        )
    factors = attention_maps(
        energies, teacher_maps, present, widths, p_counts, slabs, group, 2
    )
    loss_sums = factors[2]

    flows, grads, products, flow_sums = [], [], [], []
    for res in range(2):
        flow, grad, product, sums = student_back(
            sums_out[res],
            cot_rows[res],
            factors[res],
            spreads[res],
            firsts[res],
            acts[res],
            odds[res],
            *weights[res],
            entry_total,
            inner_total,
            norm_mid,
            row_mask(-1, p_counts[res] + 3, p_counts[res]),
            bands_second_back,
            tiles[res],
        )
        flows.append(flow)
        grads.append(grad)
        products.append(product)
        flow_sums.append(sums)
    flow_total = total_over_devices(flow_sums, axes, 3)
    entry_rows, first_products, entry_flow_sums = [], [], []
    for res in range(2):
        rows, product, sums = student_entry(
            flows[res],
            firsts[res],
            grads[res],
            evens[res],
            odds[res],
            raw[res],
            *weights[res],
            entry_total,
            inner_total,
            flow_total,
            norm_in,
            norm_mid,
            row_mask(0, p_counts[res] + 1, p_counts[res]),
            bands_even,
            bands_odd,
            tiles[res],
        )
        first_products.append(product)
        entry_flow_sums.append(sums)
        rows = rows[:, : images[res]]
        pieces = []
        for d in range(group):
            part = lax.dynamic_slice_in_dim(
                rows, (x + d) % group * local_rows[res], local_rows[res], 0
            )
            pieces.append(lax.ppermute(part, "space", to_sub(d)) if d else part)
        ordered = [lax.select_n((x - s) % group, *pieces) for s in range(group)]
        count, _, lanes = ordered[0].shape
        arrived = jnp.stack(ordered).reshape(group, count, slabs, per_device[res], lanes)
        entry_rows.append(
            jnp.transpose(arrived, (2, 0, 3, 1, 4)).reshape(-1, count, lanes)
        )

    second_part, shortcut_part = second_from_products(products[0] + products[1])
    first_part = first_from_products(first_products[0] + first_products[1])
    packed = jnp.concatenate(
        [
            first_part.reshape(-1, 128),
            second_part.reshape(-1, 128),
            shortcut_part.reshape(-1, 128),
            entry_flow_sums[0] + entry_flow_sums[1],
            loss_sums,
        ],
        axis=0,
    )
    packed = spread_sum(packed, axes, 4)
    sizes = [9 * CS_IN * CS_OUT // 128, 9 * CS_OUT * CS_OUT // 128, CS_IN * CS_OUT // 128, 8, 8]
    ends = np.cumsum(sizes)
    first_grads = packed[: ends[0]].reshape(3, 3, CS_IN, CS_OUT)
    second_grads = packed[ends[0] : ends[1]].reshape(3, 3, CS_OUT, CS_OUT)
    shortcut_grads = packed[ends[1] : ends[2]].reshape(CS_IN, CS_OUT)
    entry_pulled = packed[ends[2] : ends[3]].reshape(8, 128 // CS_IN, CS_IN).sum(axis=1)
    total_loss = jnp.sum(packed[ends[3]])

    entry_counts_ = entry_total[4:6, 0:1]
    entry_folded = entry_total.reshape(8, 128 // CS_IN, CS_IN).sum(axis=1)
    mean_entry = entry_folded[0:2] / entry_counts_
    scale_entry = lax.rsqrt(entry_folded[2:4] / entry_counts_ - mean_entry * mean_entry + EPSILON)
    ones_entry, cross_entry = entry_pulled[0:2], entry_pulled[2:4]
    inner_folded = flow_total.reshape(8, 128 // CS_OUT, CS_OUT).sum(axis=1)
    ones_inner, cross_inner = inner_folded[0:2], inner_folded[2:4]

    input_grads = []
    for res in range(2):
        n, rows, lanes = pixels[res].shape
        repeat = lanes // CS_IN
        one = (labels[res] == 1)[:, None]

        def by_image(pair):
            return jnp.tile(jnp.where(one, pair[1][None], pair[0][None]), (1, repeat))[:, None, :]

        scale = by_image(scale_entry)
        shift = by_image(-mean_entry * scale_entry)
        gain_row = jnp.tile(entry_norm[0], repeat)
        bias_row = jnp.tile(entry_norm[1], repeat)
        normed = pixels[res].astype(F32) * scale + shift
        before = gain_row * normed + bias_row
        s = jax.nn.sigmoid(before)
        flow = entry_rows[res].astype(F32) * (s * (1.0 + before * (1.0 - s)))
        input_grads.append(
            gain_row
            * scale
            * (
                flow
                - by_image(ones_entry / entry_counts_)
                - normed * by_image(cross_entry / entry_counts_)
            )
        )

    entry_grads = jnp.stack([jnp.sum(cross_entry, axis=0), jnp.sum(ones_entry, axis=0)])
    inner_grads = jnp.stack([jnp.sum(cross_inner, axis=0), jnp.sum(ones_inner, axis=0)])
    rate_scale = 1.0 / math.sqrt(total_positions)
    entry_state = renew(entry_norm, entry_grads, momentum_entry, average_entry, NORM_RATE * rate_scale)
    first_state = renew(first_conv, first_grads, momentum_first, average_first, CONV_RATE * rate_scale)
    inner_state = renew(inner_norm, inner_grads, momentum_inner, average_inner, NORM_RATE * rate_scale)
    second_state = renew(
        second_conv, second_grads, momentum_second, average_second, CONV_RATE * rate_scale
    )
    bypass_state = renew(
        shortcut, shortcut_grads, momentum_shortcut, average_shortcut, CONV_RATE * rate_scale
    )
    return (
        block_outs[0],
        block_outs[1],
        input_grads[0],
        input_grads[1],
        total_loss / total_positions,
        *entry_state,
        *first_state,
        first_state[3].astype(BF16),
        *inner_state,
        *second_state,
        second_state[3].astype(BF16),
        *bypass_state,
        bypass_state[3].astype(BF16),
    )


def solution(mesh):
    rows = P("batch", "space", None)
    blocks = P(("batch", "space"), None, None)
    return jax.shard_map(
        functools.partial(body, mesh.shape["space"], mesh.shape["batch"]),
        mesh=mesh,
        in_specs=(rows,) * 4 + (P("batch"),) * 2 + (blocks,) * 2 + (P(),) * 20,
        out_specs=(blocks,) * 2 + (rows,) * 2 + (P(),) * 24,
        check_vma=False,
    )
```

time: 1370 us -> 1030 us (0.75)
  Pallas kernels: 0 us -> 461 us
  blocking collectives: 333 us -> 0 us
  matrix products: 336 us -> 18 us
  waiting for transfers between devices: 235 us -> 56.7 us
  starting transfers between devices: 26.7 us -> 78.4 us
  local copies, waits for them, and re-layouts: 245 us -> 227 us
  other arithmetic: 155 us -> 172 us
  between operations: 19 us -> 4.28 us
    pallas_call x0 -> x16, Pallas kernels: none -> 461 us  [the longest x2 138 us: teacher_energies(): pl.pallas_call(functools.partial(teacher_kernel, p_rows, width), grid=(im...]
    conv_general_dilated x24 -> x0, matrix products: 328 us -> none  [the longest x8 136 us: convolve(): lax.conv_general_dilated(inputs, kernel, (stride, stride), ((1, 1), (1, 1...]
    psum x4 -> x0, blocking collectives: 269 us -> none  [the longest x1 147 us: body(): lax.psum((group_sums(tables_batch, first_out), group_sums(tables_batch, f...]
    all_to_all x5 -> x0, waiting for transfers between devices: 124 us -> none  [the longest x1 60.8 us: body(): lax.all_to_all(teacher_parts[0], 'space', split_axis=0, concat_axis=2, ti...]
    psum x1 -> x0, waiting for transfers between devices: 111 us -> none  [body(): lax.psum((ones_entry, cross_entry, first_part, second_part, shortcut_part...]
    ppermute x0 -> x26, starting transfers between devices: none -> 78.4 us  [the longest x4 37.3 us: halos(): lax.ppermute(slab[slab.shape[0] - above:], 'space', down())]
    convert_element_type x22 -> x13, other arithmetic: 106 us -> 40.5 us  [the longest x2 27.4 us: body(): active = jax.nn.silu(gain * teachers[res].astype(F32) + bias).astype(BF16)]
    all_to_all x1 -> x0, blocking collectives: 63.5 us -> none  [body(): lax.all_to_all(activated[0], 'space', split_axis=0, concat_axis=2, tiled=...]
  transfers between devices with their start and end apart: 6 -> 26, of which waited for: 4 -> 6; matrix products, arithmetic and copies ran while one was open for 31% -> 35% of each run, Pallas kernels for 0% -> 27%
where the time goes in v1:
time: 1030 us; the launch traced here: 1020 us
  Pallas kernels  461 us (45%)
  local copies, waits for them, and re-layouts  227 us (22%)
  other arithmetic  172 us (17%)
  starting transfers between devices  78.4 us (8%)
  waiting for transfers between devices  56.7 us (6%)
  matrix products  18 us (2%)
    pallas_call x2, Pallas kernels, teacher_energies(): pl.pallas_call(functools.partial(teacher_kernel, p_rows, width), grid=(im...  138 us
    pallas_call x3, Pallas kernels, total_over_devices(): pl.pallas_call(functools.partial(total_kernel, axes, len(parts)), out_sha...  132 us
    pallas_call x2, Pallas kernels, student_back(): pl.pallas_call(functools.partial(back_kernel, p_rows), grid=(images // ti...  45.6 us
    pallas_call x2, Pallas kernels, student_block(): pl.pallas_call(functools.partial(block_kernel, p_rows), grid=(images // t...  43.2 us
    ppermute x4, starting transfers between devices, halos(): lax.ppermute(slab[slab.shape[0] - above:], 'space', down())  37.3 us
    ppermute x12, waiting for transfers between devices, body(): pieces.append(lax.ppermute(part, 'space', to_slab(d)) if d else part)  37 us
    pallas_call x2, Pallas kernels, student_entry(): pl.pallas_call(functools.partial(entry_kernel, p_rows), grid=(images // t...  36 us
    unnamed x181, local copies, waits for them, and re-layouts  36 us
  transfers between devices with their start and end apart: 26, of which 6 were waited for; matrix products, arithmetic and copies ran while one was open for 35% of the time, Pallas kernels for 27%

profile of v1, /device:TPU:0, one launch (start us, length us, event | category | flops | bytes accessed | tf_op | source)
XLA Modules:
  0.0 1017.4 jit_solution(8238162355854979186)
XLA Ops:
  64.2 12.1 %multiply_convert_fusion = bf16[80,8,8192]{2,1,0:T(8,128)(2,1)} fusion(bf16[80,8,8192]{2,1,0:T(8,128)(2,1)} %param.41, f32[8192]{0:T(1024)} %get-tuple-element.252, f32[8192]{0:T(1024)} %get-tuple-element.253), kind=kLoop, calls=%fused_computation.4 | loop fusion | flops 41943040 | bytes 21037056 | tf_op jit(solution)/shard_map/convert_element_type | solution.py:1286
  94.6 15.2 %fusion.2 = bf16[320,4,4096]{2,1,0:T(4,128)(2,1)} fusion(bf16[320,4,4096]{2,1,0:T(4,128)(2,1)} %param.40, f32[4096]{0:T(1024)S(1)} %copy-done.37, f32[4096]{0:T(1024)S(1)} %copy-done.38), kind=kLoop, calls=%fused_computation.5 | loop fusion | flops 41943040 | bytes 21004288 | tf_op jit(solution)/shard_map/convert_element_type | solution.py:1286
  109.8 18.3 %constant_dynamic-slice_fusion.4 = (bf16[4,1,40,4,4096]{4,3,2,1,0:T(4,128)(2,1)}, bf16[4,1,40,4,4096]{4,3,2,1,0:T(4,128)(2,1)}) fusion(bf16[4,2,40,4,4096]{4,3,2,1,0:T(4,128)(2,1)} %bitcast.313, s32[]{:T(128)S(6)} %select_n.793, s32[]{:T(128)S(6)} %select_n.791), kind=kLoop, calls=%fused_computation.223 | loop fusion | bytes 20971528 | tf_op jit(solution)/shard_map/jit(dynamic_index_in_dim)/dynamic_slice | solution.py:1153
  247.8 20.6 %collective-permute-done.13 = bf16[7,40,1024]{2,1,0:T(8,128)(2,1)S(1)} collective-permute-done((bf16[7,40,1024]{2,1,0:T(8,128)(2,1)S(1)}, bf16[7,40,1024]{2,1,0:T(8,128)(2,1)S(1)}, u32[]{:S(2)}, u32[]{:S(2)}) %collective-permute-start.13) | collective-permute-done | bytes 573472 | tf_op jit(solution)/shard_map/ppermute | solution.py:1228
  279.6 15.4 %collective-permute-start.4 = (bf16[5,40,2048]{2,1,0:T(8,128)(2,1)}, bf16[5,40,2048]{2,1,0:T(8,128)(2,1)S(1)}, u32[]{:S(2)}, u32[]{:S(2)}) collective-permute-start(bf16[5,40,2048]{2,1,0:T(8,128)(2,1)} %slice.369), channel_id=1, source_target_pairs={{0,2},{1,3},{2,4},{3,5},{4,6},{5,7},{8,10},{9,11},{10,12},{11,13},... | collective-permute-start | bytes 2457608 | tf_op jit(solution)/shard_map/ppermute | solution.py:1176
  314.3 46.5 %shard_map.538.tot = f32[8,128]{1,0:T(8,128)} custom-call(f32[8,128]{1,0:T(8,128)} %shard_map.537.refs_0_), custom_call_target="tpu_custom_call" | custom-call | tf_op jit(solution)/shard_map/pallas_call | solution.py:189
  370.5 14.5 %shard_map.540 = (bf16[14,48,2176]{2,1,0:T(8,128)(2,1)}, bf16[13,48,2176]{2,1,0:T(8,128)(2,1)}, f32[13,48,2048]{2,1,0:T(8,128)}, f32[8,128]{1,0:T(8,128)}) custom-call(bf16[27,48,2048]{2,1,0:T(8,128)(2,1)} %fusion.10.raw, f32[48,128]{1,0:T(8,128)} %broadcast_in_dim.248.w0_ref, f32[48,128]{1,0:T(8,128)} %broadcast_in_dim.249.w1_ref, ...), custom_call_target="tpu_custom_call" | custom-call | tf_op jit(solution)/shard_map/pallas_call | solution.py:494
  390.3 15.7 %shard_map.539 = (bf16[10,160,1152]{2,1,0:T(8,128)(2,1)}, bf16[9,160,1152]{2,1,0:T(8,128)(2,1)}, f32[9,160,1024]{2,1,0:T(8,128)}, f32[8,128]{1,0:T(8,128)}) custom-call(bf16[19,160,1024]{2,1,0:T(8,128)(2,1)} %pad_maximum_fusion.1.raw, f32[160,128]{1,0:T(8,128)} %broadcast_in_dim.241.a0.w0_ref, f32[160,128]{1,0:T(8,128)} %broadcast_in_dim.242.a1.w1_ref, ...), custom_call_target="tpu_custom_call" | custom-call | tf_op jit(solution)/shard_map/pallas_call | solution.py:494
  406.1 74.2 %shard_map.541.inner = f32[8,128]{1,0:T(8,128)} custom-call(f32[8,128]{1,0:T(8,128)} %get-tuple-element.87.refs_0_, f32[8,128]{1,0:T(8,128)} %get-tuple-element.88.refs_1_), custom_call_target="tpu_custom_call" | custom-call | tf_op jit(solution)/shard_map/pallas_call | solution.py:189
  480.3 23.9 %shard_map.542 = (bf16[9,160,1280]{2,1,0:T(8,128)(2,1)}, f32[7,160,1024]{2,1,0:T(8,128)}, bf16[4,160,1024]{2,1,0:T(8,128)(2,1)}, f32[160,128]{1,0:T(8,128)}) custom-call(f32[9,160,1024]{2,1,0:T(8,128)} %get-tuple-element.85.first_ref, bf16[9,160,1152]{2,1,0:T(8,128)(2,1)} %get-tuple-element.86.odd, f32[160,128]{1,0:T(8,128)} %broadcast_in_dim.241.a0.w0_ref, ...), custom_call_target="tpu_custom_call" | custom-call | tf_op jit(solution)/shard_map/pallas_call | solution.py:592
  511.2 19.3 %shard_map.543 = (bf16[13,48,2304]{2,1,0:T(8,128)(2,1)}, f32[11,48,2048]{2,1,0:T(8,128)}, bf16[8,48,2048]{2,1,0:T(8,128)(2,1)}, f32[48,384]{1,0:T(8,128)}) custom-call(f32[13,48,2048]{2,1,0:T(8,128)} %get-tuple-element.90.first_ref, bf16[13,48,2176]{2,1,0:T(8,128)(2,1)} %get-tuple-element.91.odd, f32[48,128]{1,0:T(8,128)} %broadcast_in_dim.248.w0_ref, ...), custom_call_target="tpu_custom_call" | custom-call | tf_op jit(solution)/shard_map/pallas_call | solution.py:592
  549.2 10.5 %collective-permute-done.10 = bf16[8,10,2048]{2,0,1:T(8,128)(2,1)S(1)} collective-permute-done((bf16[8,10,2048]{2,0,1:T(8,128)(2,1)S(1)}, bf16[8,10,2048]{2,0,1:T(8,128)(2,1)S(1)}, u32[]{:S(2)}, u32[]{:S(2)}) %collective-permute-start.10) | collective-permute-done | bytes 327712 | tf_op jit(solution)/shard_map/ppermute | solution.py:1274
  561.1 13.6 %bitcast_select_fusion = (bf16[8,40,8192]{2,1,0:T(8,128)(2,1)}, bf16[8,40,8192]{2,1,0:T(8,128)(2,1)}) fusion(bf16[8,40,8192]{2,1,0:T(8,128)(2,1)} %collective-permute-done.18, pred[]{:T(512)S(6)} %select_n.789, bf16[40,8,8192]{2,1,0:T(8,128)(2,1)} %bitcast.327, pred[]{:T(512)S(6)} %select_n.796), kind=kLoop, calls=%fused_computation.25 | loop fusion | flops 5242880 | bytes 20971522 | tf_op jit(solution)/shard_map/select_n | solution.py:1159
  609.9 12.3 %fusion.3.slab = bf16[16,48,8192]{2,1,0:T(8,128)(2,1)} fusion(bf16[8,40,8192]{2,1,0:T(8,128)(2,1)} %get-tuple-element.144, bf16[8,40,8192]{2,1,0:T(8,128)(2,1)} %get-tuple-element.143), kind=kLoop, calls=%fused_computation.6 | loop fusion | flops 44040192 | bytes 23068672 | tf_op jit(solution)/shard_map/concatenate | solution.py:1160
  633.4 74.0 %shard_map.545.refs_3_ = f32[48,384]{1,0:T(8,128)} custom-call(bf16[3,48,8192]{2,1,0:T(8,128)(2,1)} %pad.59.above, bf16[16,48,8192]{2,1,0:T(8,128)(2,1)} %fusion.3.slab, bf16[2,48,8192]{2,1,0:T(8,128)(2,1)} %pad.61.below, bf16[1152,256]{1,0:T(8,128)(2,1)} %bitcast.374, bf16[2304,256]{1,0:T(8,128)(2,1)} %bitcast.372, bf16[128,256]{1,0:T(8,128)(2,1)} %bypass.3, ...), custom_call_target="tpu_custom_call" | custom-call | flops 22548578304 | bytes 16515072 | tf_op jit(solution)/shard_map/pallas_call | solution.py:376
  712.8 64.4 %shard_map.544.refs_2_ = f32[160,128]{1,0:T(8,128)} custom-call(bf16[3,160,4096]{2,1,0:T(8,128)(2,1)} %collective-permute-done.16.above, bf16[8,160,4096]{2,1,0:T(8,128)(2,1)} %pad_maximum_fusion.slab, bf16[2,160,4096]{2,1,0:T(8,128)(2,1)} %collective-permute-done.17.below, bf16[1152,256]{1,0:T(8,128)(2,1)} %bitcast.375, bf16[2304,256]{1,0:T(8,128)(2,1)} %bitcast.373, ...), custom_call_target="tpu_custom_call" | custom-call | flops 18790481920 | bytes 17039360 | tf_op jit(solution)/shard_map/pallas_call | solution.py:376
  778.6 11.1 %shard_map.546 = (f32[160,128]{1,0:T(8,128)}, f32[48,384]{1,0:T(8,128)}, f32[8,128]{1,0:T(8,128)}) custom-call(f32[160,128]{1,0:T(8,128)} %get-tuple-element.94.refs_0_, f32[48,384]{1,0:T(8,128)} %get-tuple-element.95.refs_1_, f32[160,128]{1,0:T(8,128)} %shard_map.544.refs_2_, f32[48,384]{1,0:T(8,128)} %shard_map.545.refs_3_, ...), custom_call_target="tpu_custom_call" | custom-call | tf_op jit(solution)/shard_map/pallas_call | solution.py:753
  789.7 20.9 %shard_map.548 = (f32[9,48,2048]{2,1,0:T(8,128)}, bf16[11,48,2304]{2,1,0:T(8,128)(2,1)}, f32[256,1792]{1,0:T(8,128)}, f32[8,128]{1,0:T(8,128)}) custom-call(f32[11,48,2048]{2,1,0:T(8,128)} %get-tuple-element.102.sum_ref, bf16[11,48,2048]{2,1,0:T(8,128)(2,1)} %fusion.25.cot, f32[48,384]{1,0:T(8,128)} %get-tuple-element.103.factor, ...), custom_call_target="tpu_custom_call" | custom-call | tf_op jit(solution)/shard_map/pallas_call | solution.py:871
  810.7 24.7 %shard_map.547 = (f32[5,160,1024]{2,1,0:T(8,128)}, bf16[7,160,1280]{2,1,0:T(8,128)(2,1)}, f32[256,1792]{1,0:T(8,128)}, f32[8,128]{1,0:T(8,128)}) custom-call(f32[7,160,1024]{2,1,0:T(8,128)} %get-tuple-element.93.sum_ref, bf16[7,160,1024]{2,1,0:T(8,128)(2,1)} %pad_maximum_fusion.4.cot, f32[160,128]{1,0:T(8,128)} %get-tuple-element.96.factor, ...), custom_call_target="tpu_custom_call" | custom-call | tf_op jit(solution)/shard_map/pallas_call | solution.py:871
  837.2 11.1 %shard_map.549.pulled = f32[8,128]{1,0:T(8,128)} custom-call(f32[8,128]{1,0:T(8,128)} %get-tuple-element.101.refs_0_, f32[8,128]{1,0:T(8,128)} %get-tuple-element.105.refs_1_), custom_call_target="tpu_custom_call" | custom-call | tf_op jit(solution)/shard_map/pallas_call | solution.py:189
  858.9 19.7 %shard_map.551 = (bf16[16,48,2048]{2,1,0:T(8,128)(2,1)}, f32[256,1152]{1,0:T(8,128)}, f32[8,128]{1,0:T(8,128)}) custom-call(f32[9,48,2048]{2,1,0:T(8,128)} %get-tuple-element.108.flow_ref, f32[13,48,2048]{2,1,0:T(8,128)} %get-tuple-element.90.first_ref, bf16[11,48,2304]{2,1,0:T(8,128)(2,1)} %get-tuple-element.109.grad, ...), custom_call_target="tpu_custom_call" | custom-call | tf_op jit(solution)/shard_map/pallas_call | solution.py:988
  879.3 16.3 %shard_map.550 = (bf16[8,160,1024]{2,1,0:T(8,128)(2,1)}, f32[256,1152]{1,0:T(8,128)}, f32[8,128]{1,0:T(8,128)}) custom-call(f32[5,160,1024]{2,1,0:T(8,128)} %get-tuple-element.98.flow_ref, f32[9,160,1024]{2,1,0:T(8,128)} %get-tuple-element.85.first_ref, bf16[7,160,1280]{2,1,0:T(8,128)(2,1)} %get-tuple-element.99.grad, ...), custom_call_target="tpu_custom_call" | custom-call | tf_op jit(solution)/shard_map/pallas_call | solution.py:988
  903.6 20.1 %shard_map.552 = f32[512,128]{1,0:T(8,128)} custom-call(f32[512,128]{1,0:T(8,128)} %pad.64.x_ref), custom_call_target="tpu_custom_call" | custom-call | tf_op jit(solution)/shard_map/pallas_call | solution.py:284
  982.2 14.0 %collective-permute-done.24 = bf16[4,160,1024]{2,1,0:T(8,128)(2,1)} collective-permute-done((bf16[4,160,1024]{2,1,0:T(8,128)(2,1)}, bf16[4,160,1024]{2,1,0:T(8,128)(2,1)}, u32[]{:S(2)}, u32[]{:S(2)}) %collective-permute-start.24) | collective-permute-done | bytes 1310752 | tf_op jit(solution)/shard_map/ppermute | solution.py:1357
  (491 shorter events, 424.5 us)
Async XLA Ops:
  5.6 263.1 %collective-permute-start.3 = (bf16[8,40,2048]{2,1,0:T(8,128)(2,1)}, bf16[8,40,2048]{2,1,0:T(8,128)(2,1)}, u32[]{:S(2)}, u32[]{:S(2)}) collective-permute-start(bf16[8,40,2048]{2,1,0:T(8,128)(2,1)} %bitcast.305), channel_id=1, source_target_pairs={{0,1},{1,0},{2,3},{3,2},{4,5},{5,4},{6,7},{7,6},{8,9},{9,8},{10,11... | collective-permute-start | bytes 3932168 | tf_op jit(solution)/shard_map/ppermute | solution.py:1166
  10.9 263.3 %collective-permute-start = (bf16[4,160,1024]{2,1,0:T(8,128)(2,1)}, bf16[4,160,1024]{2,1,0:T(8,128)(2,1)}, u32[]{:S(2)}, u32[]{:S(2)}) collective-permute-start(bf16[4,160,1024]{2,1,0:T(8,128)(2,1)} %bitcast.4), channel_id=1, source_target_pairs={{0,1},{1,0},{2,3},{3,2},{4,5},{5,4},{6,7},{7,6},{8,9},{9,8},{10,11... | collective-permute-start | bytes 3932168 | tf_op jit(solution)/shard_map/ppermute | solution.py:1166
  14.7 213.9 %collective-permute-start.21 = (bf16[11,10,2048]{2,0,1:T(8,128)(2,1)}, bf16[11,10,2048]{2,0,1:T(8,128)(2,1)}, u32[]{:S(2)}, u32[]{:S(2)}) collective-permute-start(bf16[11,10,2048]{2,0,1:T(8,128)(2,1)} %copy.391), channel_id=1, source_target_pairs={{0,2},{1,3},{2,4},{3,5},{4,6},{5,7},{6,0},{7,1},{8,10},{9,11},{10,... | collective-permute-start | bytes 1351688 | tf_op jit(solution)/shard_map/ppermute | solution.py:1228
  17.8 211.4 %collective-permute-start.22 = (bf16[11,10,2048]{2,0,1:T(8,128)(2,1)}, bf16[11,10,2048]{2,0,1:T(8,128)(2,1)}, u32[]{:S(2)}, u32[]{:S(2)}) collective-permute-start(bf16[11,10,2048]{2,0,1:T(8,128)(2,1)} %copy.393), channel_id=1, source_target_pairs={{0,4},{1,5},{2,6},{3,7},{4,0},{5,1},{6,2},{7,3},{8,12},{9,13},{10,... | collective-permute-start | bytes 1351688 | tf_op jit(solution)/shard_map/ppermute | solution.py:1228
  21.5 208.0 %collective-permute-start.23 = (bf16[11,10,2048]{2,0,1:T(8,128)(2,1)}, bf16[11,10,2048]{2,0,1:T(8,128)(2,1)}, u32[]{:S(2)}, u32[]{:S(2)}) collective-permute-start(bf16[11,10,2048]{2,0,1:T(8,128)(2,1)} %copy.394), channel_id=1, source_target_pairs={{0,6},{1,7},{2,0},{3,1},{4,2},{5,3},{6,4},{7,5},{8,14},{9,15},{10,... | collective-permute-start | bytes 1351688 | tf_op jit(solution)/shard_map/ppermute | solution.py:1228
  229.2 39.2 %collective-permute-start.13 = (bf16[7,40,1024]{2,1,0:T(8,128)(2,1)S(1)}, bf16[7,40,1024]{2,1,0:T(8,128)(2,1)S(1)}, u32[]{:S(2)}, u32[]{:S(2)}) collective-permute-start(bf16[7,40,1024]{2,1,0:T(8,128)(2,1)S(1)} %get-tuple-element.198), channel_id=1, source_target_pairs={{0,4},{1,5},{2,6},{3,7},{4,0},{5,1},{6,2},{7,3},{8,12},{9,13},{10,... | collective-permute-start | bytes 1720328 | tf_op jit(solution)/shard_map/ppermute | solution.py:1228
  229.5 38.9 %collective-permute-start.14 = (bf16[7,40,1024]{2,1,0:T(8,128)(2,1)S(1)}, bf16[7,40,1024]{2,1,0:T(8,128)(2,1)S(1)}, u32[]{:S(2)}, u32[]{:S(2)}) collective-permute-start(bf16[7,40,1024]{2,1,0:T(8,128)(2,1)S(1)} %get-tuple-element.199), channel_id=1, source_target_pairs={{0,6},{1,7},{2,0},{3,1},{4,2},{5,3},{6,4},{7,5},{8,14},{9,15},{10,... | collective-permute-start | bytes 1720328 | tf_op jit(solution)/shard_map/ppermute | solution.py:1228
  246.3 314.7 %collective-permute-start.18 = (bf16[8,40,8192]{2,1,0:T(8,128)(2,1)}, bf16[8,40,8192]{2,1,0:T(8,128)(2,1)}, u32[]{:S(2)}, u32[]{:S(2)}) collective-permute-start(bf16[8,40,8192]{2,1,0:T(8,128)(2,1)} %bitcast.302), channel_id=1, source_target_pairs={{0,1},{1,0},{2,3},{3,2},{4,5},{5,4},{6,7},{7,6},{8,9},{9,8},{10,11... | collective-permute-start | bytes 15728648 | tf_op jit(solution)/shard_map/ppermute | solution.py:1166
  272.9 90.3 %collective-permute-start.5 = (bf16[6,40,2048]{2,1,0:T(8,128)(2,1)}, bf16[6,40,2048]{2,1,0:T(8,128)(2,1)}, u32[]{:S(2)}, u32[]{:S(2)}) collective-permute-start(bf16[6,40,2048]{2,1,0:T(8,128)(2,1)} %slice.370), channel_id=1, source_target_pairs={{2,0},{3,1},{4,2},{5,3},{6,4},{7,5},{10,8},{11,9},{12,10},{13,11},... | collective-permute-start | bytes 2949128 | tf_op jit(solution)/shard_map/ppermute | solution.py:1177
  277.1 107.8 %collective-permute-start.2 = (bf16[6,160,1024]{2,1,0:T(8,128)(2,1)}, bf16[6,160,1024]{2,1,0:T(8,128)(2,1)}, u32[]{:S(2)}, u32[]{:S(2)}) collective-permute-start(bf16[6,160,1024]{2,1,0:T(8,128)(2,1)} %fusion.26), channel_id=1, source_target_pairs={{2,0},{3,1},{4,2},{5,3},{6,4},{7,5},{10,8},{11,9},{12,10},{13,11},... | collective-permute-start | bytes 5898248 | tf_op jit(solution)/shard_map/ppermute | solution.py:1177
  279.6 82.1 %collective-permute-start.4 = (bf16[5,40,2048]{2,1,0:T(8,128)(2,1)}, bf16[5,40,2048]{2,1,0:T(8,128)(2,1)S(1)}, u32[]{:S(2)}, u32[]{:S(2)}) collective-permute-start(bf16[5,40,2048]{2,1,0:T(8,128)(2,1)} %slice.369), channel_id=1, source_target_pairs={{0,2},{1,3},{2,4},{3,5},{4,6},{5,7},{8,10},{9,11},{10,12},{11,13},... | collective-permute-start | bytes 2457608 | tf_op jit(solution)/shard_map/ppermute | solution.py:1176
  296.3 88.7 %collective-permute-start.1 = (bf16[5,160,1024]{2,1,0:T(8,128)(2,1)}, bf16[5,160,1024]{2,1,0:T(8,128)(2,1)}, u32[]{:S(2)}, u32[]{:S(2)}) collective-permute-start(bf16[5,160,1024]{2,1,0:T(8,128)(2,1)} %fusion.27), channel_id=1, source_target_pairs={{0,2},{1,3},{2,4},{3,5},{4,6},{5,7},{8,10},{9,11},{10,12},{11,13},... | collective-permute-start | bytes 4915208 | tf_op jit(solution)/shard_map/ppermute | solution.py:1176
  361.6 230.1 %collective-permute-start.15 = (bf16[4,160,4096]{2,1,0:T(8,128)(2,1)}, bf16[4,160,4096]{2,1,0:T(8,128)(2,1)}, u32[]{:S(2)}, u32[]{:S(2)}) collective-permute-start(bf16[4,160,4096]{2,1,0:T(8,128)(2,1)} %bitcast.334), channel_id=1, source_target_pairs={{0,1},{1,0},{2,3},{3,2},{4,5},{5,4},{6,7},{7,6},{8,9},{9,8},{10,11... | collective-permute-start | bytes 15728648 | tf_op jit(solution)/shard_map/ppermute | solution.py:1166
  505.9 26.9 %collective-permute-start.6 = (bf16[4,40,1024]{2,0,1:T(4,128)(2,1)S(1)}, bf16[4,40,1024]{2,0,1:T(4,128)(2,1)S(1)}, u32[]{:S(2)}, u32[]{:S(2)}) collective-permute-start(bf16[4,40,1024]{2,0,1:T(4,128)(2,1)S(1)} %bitcast.355), channel_id=1, source_target_pairs={{0,2},{1,3},{2,4},{3,5},{4,6},{5,7},{6,0},{7,1},{8,10},{9,11},{10,... | collective-permute-start | bytes 983048 | tf_op jit(solution)/shard_map/ppermute | solution.py:1274
  506.2 28.7 %collective-permute-start.7 = (bf16[4,40,1024]{2,0,1:T(4,128)(2,1)S(1)}, bf16[4,40,1024]{2,0,1:T(4,128)(2,1)S(1)}, u32[]{:S(2)}, u32[]{:S(2)}) collective-permute-start(bf16[4,40,1024]{2,0,1:T(4,128)(2,1)S(1)} %bitcast.354), channel_id=1, source_target_pairs={{0,4},{1,5},{2,6},{3,7},{4,0},{5,1},{6,2},{7,3},{8,12},{9,13},{10,... | collective-permute-start | bytes 983048 | tf_op jit(solution)/shard_map/ppermute | solution.py:1274
  506.6 29.8 %collective-permute-start.8 = (bf16[4,40,1024]{2,0,1:T(4,128)(2,1)S(1)}, bf16[4,40,1024]{2,0,1:T(4,128)(2,1)S(1)}, u32[]{:S(2)}, u32[]{:S(2)}) collective-permute-start(bf16[4,40,1024]{2,0,1:T(4,128)(2,1)S(1)} %bitcast.353), channel_id=1, source_target_pairs={{0,6},{1,7},{2,0},{3,1},{4,2},{5,3},{6,4},{7,5},{8,14},{9,15},{10,... | collective-permute-start | bytes 983048 | tf_op jit(solution)/shard_map/ppermute | solution.py:1274
  532.8 26.9 %collective-permute-start.10 = (bf16[8,10,2048]{2,0,1:T(8,128)(2,1)S(1)}, bf16[8,10,2048]{2,0,1:T(8,128)(2,1)S(1)}, u32[]{:S(2)}, u32[]{:S(2)}) collective-permute-start(bf16[8,10,2048]{2,0,1:T(8,128)(2,1)S(1)} %get-tuple-element.201), channel_id=1, source_target_pairs={{0,4},{1,5},{2,6},{3,7},{4,0},{5,1},{6,2},{7,3},{8,12},{9,13},{10,... | collective-permute-start | bytes 983048 | tf_op jit(solution)/shard_map/ppermute | solution.py:1274
  534.9 24.8 %collective-permute-start.11 = (bf16[8,10,2048]{2,0,1:T(8,128)(2,1)S(1)}, bf16[8,10,2048]{2,0,1:T(8,128)(2,1)S(1)}, u32[]{:S(2)}, u32[]{:S(2)}) collective-permute-start(bf16[8,10,2048]{2,0,1:T(8,128)(2,1)S(1)} %get-tuple-element.200), channel_id=1, source_target_pairs={{0,6},{1,7},{2,0},{3,1},{4,2},{5,3},{6,4},{7,5},{8,14},{9,15},{10,... | collective-permute-start | bytes 983048 | tf_op jit(solution)/shard_map/ppermute | solution.py:1274
  577.8 52.4 %collective-permute-start.19 = (bf16[3,40,8192]{2,1,0:T(8,128)(2,1)}, bf16[3,40,8192]{2,1,0:T(8,128)(2,1)}, u32[]{:S(2)}, u32[]{:S(2)}) collective-permute-start(bf16[3,40,8192]{2,1,0:T(8,128)(2,1)} %slice.376), channel_id=1, source_target_pairs={{0,2},{1,3},{2,4},{3,5},{4,6},{5,7},{8,10},{9,11},{10,12},{11,13},... | collective-permute-start | bytes 5898248 | tf_op jit(solution)/shard_map/ppermute | solution.py:1176
  590.4 38.3 %collective-permute-start.20 = (bf16[2,40,8192]{2,1,0:T(8,128)(2,1)}, bf16[2,40,8192]{2,1,0:T(8,128)(2,1)S(1)}, u32[]{:S(2)}, u32[]{:S(2)}) collective-permute-start(bf16[2,40,8192]{2,1,0:T(8,128)(2,1)} %slice.377), channel_id=1, source_target_pairs={{2,0},{3,1},{4,2},{5,3},{6,4},{7,5},{10,8},{11,9},{12,10},{13,11},... | collective-permute-start | bytes 3932168 | tf_op jit(solution)/shard_map/ppermute | solution.py:1177
  603.3 109.5 %collective-permute-start.16 = (bf16[3,160,4096]{2,1,0:T(8,128)(2,1)S(1)}, bf16[3,160,4096]{2,1,0:T(8,128)(2,1)}, u32[]{:S(2)}, u32[]{:S(2)}) collective-permute-start(bf16[3,160,4096]{2,1,0:T(8,128)(2,1)S(1)} %slice.374), channel_id=1, source_target_pairs={{0,2},{1,3},{2,4},{3,5},{4,6},{5,7},{8,10},{9,11},{10,12},{11,13},... | collective-permute-start | bytes 11796488 | tf_op jit(solution)/shard_map/ppermute | solution.py:1176
  622.4 84.9 %collective-permute-start.17 = (bf16[2,160,4096]{2,1,0:T(8,128)(2,1)S(1)}, bf16[2,160,4096]{2,1,0:T(8,128)(2,1)}, u32[]{:S(2)}, u32[]{:S(2)}) collective-permute-start(bf16[2,160,4096]{2,1,0:T(8,128)(2,1)S(1)} %slice.375), channel_id=1, source_target_pairs={{2,0},{3,1},{4,2},{5,3},{6,4},{7,5},{10,8},{11,9},{12,10},{13,11},... | collective-permute-start | bytes 7864328 | tf_op jit(solution)/shard_map/ppermute | solution.py:1177
  937.2 41.3 %collective-permute-start.25 = (bf16[8,40,2048]{2,1,0:T(8,128)(2,1)}, bf16[8,40,2048]{2,1,0:T(8,128)(2,1)}, u32[]{:S(2)}, u32[]{:S(2)}) collective-permute-start(bf16[8,40,2048]{2,1,0:T(8,128)(2,1)} %constant_dynamic-slice_fusion), channel_id=1, source_target_pairs={{0,1},{1,0},{2,3},{3,2},{4,5},{5,4},{6,7},{7,6},{8,9},{9,8},{10,11... | collective-permute-start | bytes 3932168 | tf_op jit(solution)/shard_map/ppermute | solution.py:1357
  962.9 33.3 %collective-permute-start.24 = (bf16[4,160,1024]{2,1,0:T(8,128)(2,1)}, bf16[4,160,1024]{2,1,0:T(8,128)(2,1)}, u32[]{:S(2)}, u32[]{:S(2)}) collective-permute-start(bf16[4,160,1024]{2,1,0:T(8,128)(2,1)} %constant_dynamic-slice_fusion.1), channel_id=1, source_target_pairs={{0,1},{1,0},{2,3},{3,2},{4,5},{5,4},{6,7},{7,6},{8,9},{9,8},{10,11... | collective-permute-start | bytes 3932168 | tf_op jit(solution)/shard_map/ppermute | solution.py:1357
  (79 other events, 949.0 us)

commit v2 on v1

v2 whole, which is shorter than its diff:
```python
import functools
import math

import jax
import jax.numpy as jnp
import numpy as np
from jax import lax
from jax.experimental import pallas as pl
from jax.experimental.pallas import tpu as pltpu
from jax.sharding import PartitionSpec as P

CS_IN = 32
CS_OUT = 64
CT_IN = 128
CT_OUT = 256
SIDE = 32
SLABS = 4

EPSILON = 1e-05
TRANSFER_WEIGHT = 1000.0
MOMENTUM = 0.9
WEIGHT_DECAY = 0.0005
AVERAGING = 0.7
CONV_RATE = 0.06
NORM_RATE = 0.3

F32 = jnp.float32
BF16 = jnp.bfloat16
MESH = pl.DeviceIdType.MESH
VMEM_LIMIT = 56 << 20


def sigmoid(z):
    return 0.5 * jnp.tanh(0.5 * z) + 0.5


def matmul(a, b):
    return jnp.dot(a, b, preferred_element_type=F32)


def after(value, *others):
    return lax.optimization_barrier((value, others))[0]


def cost(microseconds):
    return pl.CostEstimate(
        flops=int(microseconds * 1e9), bytes_accessed=1 << 20, transcendentals=0
    )


def stacked(first, count, images, rows, parts):
    blocks = []
    for t in range(count):
        at = (first + t) * 256
        pieces = [ref[lo : lo + rows, :, at + off : at + off + size] for ref, lo, off, size in parts]
        block = jnp.concatenate(pieces, axis=2) if len(pieces) > 1 else pieces[0]
        blocks.append(block.reshape(rows * images, block.shape[2]))
    return jnp.concatenate(blocks, axis=0) if count > 1 else blocks[0]


def fold(rows, width):
    shift = width
    while shift < 128:
        rows = rows + pltpu.roll(rows, shift, 1)
        shift *= 2
    return rows


def group_norms(totals, counts, width):
    folded = fold(totals, width)
    means, scales = [], []
    for g in range(2):
        mean = folded[g : g + 1] / counts[g]
        variance = folded[2 + g : 3 + g] / counts[g] - mean * mean
        means.append(mean)
        scales.append(lax.rsqrt(variance + EPSILON))
    return means, scales


def per_image(w0, w1, pair):
    return w0 * pair[0] + w1 * pair[1]


def twice(table):
    return jnp.concatenate([table, table], axis=1)


def grouped_rows(w0, w1, values):
    rows = []
    for v in values:
        rows.append(jnp.sum(v * w0, axis=0, keepdims=True))
        rows.append(jnp.sum(v * w1, axis=0, keepdims=True))
    rows.append(jnp.zeros((8 - len(rows), 128), F32))
    return jnp.concatenate(rows, axis=0)


def entry_counts(tot_ref):
    return [tot_ref[4:5], tot_ref[5:6]]


def inner_counts(tot_ref):
    return [tot_ref[4:5] * 0.25, tot_ref[5:6] * 0.25]


def stats_kernel(x_refs, label_refs, out_ref):
    step = pl.program_id(0)
    total = jnp.zeros((8, 128), F32)
    for x_ref, label_ref in zip(x_refs, label_refs):
        rows, images, lanes = x_ref.shape
        s = jnp.zeros((images, 128), F32)
        q = jnp.zeros((images, 128), F32)
        for r in range(rows):
            for c in range(0, lanes, 128):
                v = x_ref[r, :, c : c + 128].astype(F32)
                s = s + v
                q = q + v * v
        w0, w1 = indicators(label_ref)
        positions = jnp.full((images, 128), float(rows * lanes // CS_IN), F32)
        total = total + grouped_rows(w0, w1, [s, q, positions])

    @pl.when(step == 0)
    def _():
        out_ref[...] = total

    @pl.when(step > 0)
    def _():
        out_ref[...] += total


def input_stats(pieces, tables):
    steps = min(4, min(x.shape[0] for x in pieces))
    count = len(pieces)

    def kernel(*refs):
        stats_kernel(refs[:count], refs[count:-1], refs[-1])

    specs = [
        pl.BlockSpec((x.shape[0] // steps,) + x.shape[1:], lambda i: (i, 0, 0)) for x in pieces
    ]
    specs += [pl.BlockSpec(w.shape, lambda i: (0, 0)) for w in tables]
    return pl.pallas_call(
        kernel,
        grid=(steps,),
        in_specs=specs,
        out_specs=pl.BlockSpec((8, 128), lambda i: (0, 0)),
        out_shape=jax.ShapeDtypeStruct((8, 128), F32),
        compiler_params=pltpu.CompilerParams(vmem_limit_bytes=VMEM_LIMIT),
        cost_estimate=cost(5),
    )(*pieces, *tables)


def greet(axes):
    barrier = pltpu.get_barrier_semaphore()
    expected = 0
    for name, size in axes:
        me = lax.axis_index(name)
        for d in range(1, size):
            pl.semaphore_signal(
                barrier,
                inc=1,
                device_id={name: lax.rem(me + d, size)},
                device_id_type=MESH,
            )
            expected += 1
    pl.semaphore_wait(barrier, expected)


def total_kernel(axes, count, *refs):
    parts = refs[:count]
    out_ref, held, boxes_a, boxes_b, send_a, recv_a, send_b, recv_b = refs[count:]
    value = parts[0][...]
    for part in parts[1:]:
        value = value + part[...]
    held[0] = value
    greet(axes)
    for level, ((name, size), boxes, send, recv) in enumerate(
        zip(axes, (boxes_a, boxes_b), (send_a, send_b), (recv_a, recv_b))
    ):
        me = lax.axis_index(name)
        copies = []
        for d in range(1, size):
            copy = pltpu.make_async_remote_copy(
                src_ref=held.at[level],
                dst_ref=boxes.at[d],
                send_sem=send.at[d],
                recv_sem=recv.at[d],
                device_id={name: lax.rem(me + d, size)},
                device_id_type=MESH,
            )
            copy.start()
            copies.append(copy)
        for copy in copies:
            copy.wait_recv()
        value = jnp.zeros(value.shape, F32)
        for source in range(size):
            back = lax.rem(me - source + size, size)
            value = value + jnp.where(
                back == 0, held[level], boxes[jnp.maximum(back, 1)]
            )
        for copy in copies:
            copy.wait_send()
        if level == 0:
            held[1] = value
        else:
            out_ref[...] = value


def total_over_devices(parts, axes, collective_id):
    shape = parts[0].shape
    return pl.pallas_call(
        functools.partial(total_kernel, axes, len(parts)),
        out_shape=jax.ShapeDtypeStruct(shape, F32),
        in_specs=[pl.BlockSpec(memory_space=pltpu.VMEM)] * len(parts),
        out_specs=pl.BlockSpec(memory_space=pltpu.VMEM),
        scratch_shapes=[
            pltpu.VMEM((2,) + shape, F32),
            pltpu.VMEM((axes[0][1],) + shape, F32),
            pltpu.VMEM((axes[1][1],) + shape, F32),
            pltpu.SemaphoreType.DMA((axes[0][1],)),
            pltpu.SemaphoreType.DMA((axes[0][1],)),
            pltpu.SemaphoreType.DMA((axes[1][1],)),
            pltpu.SemaphoreType.DMA((axes[1][1],)),
        ],
        compiler_params=pltpu.CompilerParams(collective_id=collective_id, has_side_effects=True),
        cost_estimate=cost(12),
    )(*parts)


def spread_sum_kernel(axes, layout, *refs):
    count = sum(len(parts) for parts in layout)
    inputs, out_ref, x_ref, boxes_a, boxes_b, held = refs[:count], *refs[count : count + 5]
    send_a, recv_a, send_b, recv_b, send_c, recv_c = refs[count + 5 :]
    at = 0
    for parts in layout:
        value = inputs[parts[0]][...]
        for k in parts[1:]:
            value = value + inputs[k][...]
        if value.shape[1] == 64:
            half = value.shape[0] // 2
            value = jnp.concatenate([value[:half], value[half:]], axis=1)
        x_ref[at : at + value.shape[0]] = value
        at += value.shape[0]
    if at < x_ref.shape[0]:
        x_ref[at:] = jnp.zeros((x_ref.shape[0] - at, 128), F32)
    (name_a, size_a), (name_b, size_b) = axes
    me_a, me_b = lax.axis_index(name_a), lax.axis_index(name_b)
    piece = x_ref.shape[0] // size_a
    greet(axes)

    def rows(index):
        return pl.ds(pl.multiple_of(index * piece, 8), piece)

    copies = []
    for d in range(1, size_a):
        peer = lax.rem(me_a + d, size_a)
        copy = pltpu.make_async_remote_copy(
            src_ref=x_ref.at[rows(peer)],
            dst_ref=boxes_a.at[d],
            send_sem=send_a.at[d],
            recv_sem=recv_a.at[d],
            device_id={name_a: peer},
            device_id_type=MESH,
        )
        copy.start()
        copies.append(copy)
    value = x_ref[rows(me_a)]
    for d in range(1, size_a):
        copies[d - 1].wait_recv()
        value = value + boxes_a[d]
    held[0] = value
    for copy in copies:
        copy.wait_send()
    copies = []
    for d in range(1, size_b):
        copy = pltpu.make_async_remote_copy(
            src_ref=held.at[0],
            dst_ref=boxes_b.at[d],
            send_sem=send_b.at[d],
            recv_sem=recv_b.at[d],
            device_id={name_b: lax.rem(me_b + d, size_b)},
            device_id_type=MESH,
        )
        copy.start()
        copies.append(copy)
    for copy in copies:
        copy.wait_recv()
    value = jnp.zeros(value.shape, F32)
    for source in range(size_b):
        back = lax.rem(me_b - source + size_b, size_b)
        value = value + jnp.where(back == 0, held[0], boxes_b[jnp.maximum(back, 1)])
    held[1] = value
    out_ref[rows(me_a)] = value
    for copy in copies:
        copy.wait_send()
    copies = []
    for d in range(1, size_a):
        copy = pltpu.make_async_remote_copy(
            src_ref=held.at[1],
            dst_ref=out_ref.at[rows(me_a)],
            send_sem=send_c.at[d],
            recv_sem=recv_c.at[d],
            device_id={name_a: lax.rem(me_a + d, size_a)},
            device_id_type=MESH,
        )
        copy.start()
        copies.append(copy)
    for copy in copies:
        copy.wait()


def spread_sum(groups, axes, collective_id):
    (_, size_a), (_, size_b) = axes
    arrays, layout, rows = [], [], []
    for members in groups:
        layout.append(tuple(range(len(arrays), len(arrays) + len(members))))
        arrays += members
        rows.append(members[0].shape[0] * members[0].shape[1] // 128)
    padded = -(-sum(rows) // (8 * size_a)) * 8 * size_a
    piece = padded // size_a
    sems = []
    for size in (size_a, size_b, size_a):
        sems += [pltpu.SemaphoreType.DMA((size,))] * 2
    total = pl.pallas_call(
        functools.partial(spread_sum_kernel, axes, tuple(layout)),
        out_shape=jax.ShapeDtypeStruct((padded, 128), F32),
        in_specs=[pl.BlockSpec(memory_space=pltpu.VMEM)] * len(arrays),
        out_specs=pl.BlockSpec(memory_space=pltpu.VMEM),
        scratch_shapes=[
            pltpu.VMEM((padded, 128), F32),
            pltpu.VMEM((size_a, piece, 128), F32),
            pltpu.VMEM((size_b, piece, 128), F32),
            pltpu.VMEM((2, piece, 128), F32),
        ]
        + sems,
        compiler_params=pltpu.CompilerParams(collective_id=collective_id, has_side_effects=True),
        cost_estimate=cost(20),
    )(*arrays)
    ends = np.cumsum(rows)
    return [total[e - n : e] for e, n in zip(ends, rows)]


def teacher_kernel(p_rows, width, group, columns, place, *refs):
    pieces, refs = refs[:group], refs[group:]
    above, below, first, second, bypass, inner, out_ref, even, odd, mid = refs
    local, lanes = pieces[0].shape[0], pieces[0].shape[-1]
    real, images = above.shape[1], even.shape[1]
    m_rows = p_rows + 2
    zero = jnp.zeros((images, 128), BF16)

    def put(row, source, at):
        if row % 2 == 0:
            even[row // 2 + 1, 0:real, 128 : 128 + lanes] = source[at]
        else:
            odd[(row + 1) // 2 + 1, 0:real, 128 : 128 + lanes] = source[at]

    for k in range(3):
        put(k - 3, above, k)
    for k in range(2):
        put(2 * p_rows + k, below, k)
    x = place[0]
    for s in range(group):
        distance = lax.rem(x - s + group, group)
        for d in range(group):

            @pl.when(distance == d)
            def _():
                for k in range(local):
                    at = (k, 0, 0) if len(pieces[d].shape) == 5 else k
                    put(s * local + k, pieces[d], at)

    for i in range(m_rows):
        even[i, :, 0:128] = zero
    for i in range(m_rows + 1):
        odd[i, :, 0:128] = zero
    wide_zero = jnp.zeros((images, CT_OUT), BF16)
    for i in range(m_rows):
        mid[i, :, 0:CT_OUT] = wide_zero
        mid[i, :, (width + 1) * CT_OUT : (width + 2) * CT_OUT] = wide_zero
    scale, shift = inner[0:1], inner[1:2]
    top, bottom = keep_row(place, -1, p_rows), keep_row(place, p_rows, p_rows)

    def first_step(g, carry):
        lefts = []
        for t in range(columns):
            window = pl.ds(pl.multiple_of((g * columns + t) * 256, 256), 384)
            parts = [odd[0:m_rows, :, window], even[0:m_rows, :, window]]
            parts.append(odd[1 : m_rows + 1, :, window])
            lefts.append(jnp.concatenate(parts, axis=2).reshape(m_rows * images, 9 * CT_IN))
        z = scale * matmul(jnp.concatenate(lefts, axis=0), first[...]) + shift
        act = (z * sigmoid(z)).reshape(columns, m_rows, images, CT_OUT)
        for t in range(columns):
            here = pl.ds(pl.multiple_of((g * columns + t + 1) * CT_OUT, 256), CT_OUT)
            mid[0, :, here] = (act[t, 0] * top).astype(BF16)
            mid[1 : p_rows + 1, :, here] = act[t, 1 : p_rows + 1].astype(BF16)
            mid[p_rows + 1, :, here] = (act[t, p_rows + 1] * bottom).astype(BF16)
        return carry

    lax.fori_loop(0, width // columns, first_step, 0)
    out_ref[...] = jnp.zeros(out_ref.shape, F32)
    lane = lax.broadcasted_iota(jnp.int32, (real, 128), 1)

    def second_step(g, carry):
        lefts, corners = [], []
        for t in range(columns):
            at = pl.multiple_of((g * columns + t) * 256, 256)
            window = pl.ds(at, 3 * CT_OUT)
            corner = pl.ds(pl.multiple_of(at + 128, 128), 128)
            parts = [mid[a : a + p_rows, :, window] for a in range(3)]
            lefts.append(jnp.concatenate(parts, axis=2).reshape(p_rows * images, 9 * CT_OUT))
            corners.append(even[1 : p_rows + 1, :, corner].reshape(p_rows * images, CT_IN))
        y = matmul(jnp.concatenate(lefts, axis=0), second[...])
        y = y + matmul(jnp.concatenate(corners, axis=0), bypass[...])
        square = y * y
        energy = jnp.sum(square[:, 0:128] + square[:, 128:256], axis=1, keepdims=True)
        energy = (energy * (1.0 / CT_OUT)).reshape(columns, p_rows, images, 1)
        for t in range(columns):
            for p in range(p_rows):
                chunk, start = divmod((p + 1) * width, 128)
                where = slice(chunk * 128, chunk * 128 + 128)
                here = lane == start + g * columns + t
                out_ref[:, where] = jnp.where(here, energy[t, p, 0:real], out_ref[:, where])
        return carry

    lax.fori_loop(0, width // columns, second_step, 0)


def teacher_energies(place, own, slab, received, above, below, shared, tile):
    group = len(received) + 1
    local, lanes = own.shape[0], own.shape[-1]
    images = above.shape[1]
    p_rows, width = group * local // 2, lanes // (2 * CT_IN)
    out_lanes = -(-(p_rows + 3) * width // 128) * 128
    m_rows = p_rows + 2
    space = -(-tile // 16) * 16
    if own.ndim == 5:
        own_spec = pl.BlockSpec(
            (local, 1, 1, tile, lanes), lambda i, place: (0, slab, place[0], i, 0)
        )
    else:
        own_spec = pl.BlockSpec((local, tile, lanes), lambda i, place: (0, i, 0))
    whole = lambda a: pl.BlockSpec(a.shape, lambda i, place: (0,) * a.ndim)
    by_image = lambda a: pl.BlockSpec((a.shape[0], tile, a.shape[2]), lambda i, place: (0, i, 0))
    grid_spec = pltpu.PrefetchScalarGridSpec(
        num_scalar_prefetch=1,
        grid=(images // tile,),
        in_specs=[own_spec]
        + [by_image(a) for a in received]
        + [by_image(above), by_image(below)]
        + [whole(a) for a in shared],
        out_specs=pl.BlockSpec((tile, out_lanes), lambda i, place: (i, 0)),
        scratch_shapes=[
            pltpu.VMEM((m_rows, space, 128 + lanes), BF16),
            pltpu.VMEM((m_rows + 1, space, 128 + lanes), BF16),
            pltpu.VMEM((m_rows, space, (width + 2) * CT_OUT), BF16),
        ],
    )
    return pl.pallas_call(
        functools.partial(teacher_kernel, p_rows, width, group, 4),
        grid_spec=grid_spec,
        out_shape=jax.ShapeDtypeStruct((images, out_lanes), F32),
        compiler_params=pltpu.CompilerParams(vmem_limit_bytes=VMEM_LIMIT),
        cost_estimate=cost(40 * images * p_rows * width / 10240),
    )(place, own, *received, above, below, *shared)


def entry_tables(tot_ref, norm_ref, w0, w1):
    means, scales = group_norms(tot_ref[...], entry_counts(tot_ref), CS_IN)
    scale = per_image(w0, w1, scales)
    shift = per_image(w0, w1, [-m * s for m, s in zip(means, scales)])
    gain, bias = norm_ref[0:1], norm_ref[1:2]
    present = w0 + w1
    return gain * scale, gain * shift + bias * present, scale, shift


def inner_tables(tot_ref, inner_ref, norm_ref, w0, w1):
    means, scales = group_norms(inner_ref[...], inner_counts(tot_ref), CS_OUT)
    scale = per_image(w0, w1, scales)
    shift = per_image(w0, w1, [-m * s for m, s in zip(means, scales)])
    gain, bias = norm_ref[0:1], norm_ref[1:2]
    present = w0 + w1
    return gain * scale, gain * shift + bias * present, scale, shift


def indicators(label_ref):
    label = label_ref[...]
    return (label == 0.0).astype(F32), (label == 1.0).astype(F32)


def keep_row(place, row, inside):
    z = place[1]
    outside = jnp.logical_or(
        jnp.logical_and(row < 0, z == 0), jnp.logical_and(row >= inside, z == SLABS - 1)
    )
    return jnp.where(outside, 0.0, 1.0)


def add_rows(ref, value):
    first = pl.program_id(0) == 0

    @pl.when(first)
    def _():
        ref[...] = value

    @pl.when(jnp.logical_not(first))
    def _():
        ref[...] += value


def forward_kernel(
    p_rows, group, blocks, place, *refs
):
    pieces, refs = refs[:group], refs[group:]
    above, below, label_ref, tot, norm, weights = refs[:6]
    raw, even, odd, out_ref, stats = refs[6:]
    images, lanes = raw.shape[1:]
    local = pieces[0].shape[0]
    w0, w1 = indicators(label_ref)
    gain, bias, _, _ = entry_tables(tot, norm, w0, w1)
    gain2, bias2 = twice(gain), twice(bias)
    zero = jnp.zeros((images, 128), BF16)
    raw[0:5] = above[...]
    raw[2 * p_rows + 5 : 2 * p_rows + 11] = below[...]
    x = place[0]
    for s in range(group):
        distance = lax.rem(x - s + group, group)
        for d in range(group):

            @pl.when(distance == d)
            def _():
                raw[5 + s * local : 5 + (s + 1) * local] = pieces[d][...]

    def activate(row, target, index):
        keep = keep_row(place, row - 5, 2 * p_rows)
        target[index, :, 0:128] = zero
        for c in range(0, lanes, 256):
            z = raw[row, :, c : c + 256].astype(F32) * gain2 + bias2
            target[index, :, 128 + c : 384 + c] = (z * sigmoid(z) * keep).astype(BF16)

    def pair(i, carry):
        activate(2 * i, even, i)
        activate(2 * i + 1, odd, i)
        return carry

    f_rows = p_rows + 5
    lax.fori_loop(0, f_rows, pair, 0)
    activate(2 * f_rows, even, f_rows)
    s = jnp.zeros((images, 128), F32)
    q = jnp.zeros((images, 128), F32)
    for j in range(0, lanes // 256, blocks):
        left = stacked(
            j, blocks, images, f_rows, [(even, 0, 0, 384), (odd, 0, 0, 384), (even, 1, 0, 384)]
        )
        y = matmul(left, weights[...]).reshape(blocks, f_rows, images, 256)
        for t in range(blocks):
            out_ref[:, :, (j + t) * 256 : (j + t + 1) * 256] = y[t]
            own = y[t, 2 : 2 + p_rows]
            u = jnp.sum(own, axis=0)
            v = jnp.sum(own * own, axis=0)
            s = s + u[:, 0:128] + u[:, 128:256]
            q = q + v[:, 0:128] + v[:, 128:256]
    add_rows(stats, grouped_rows(w0, w1, [s, q]))


def whole_spec(a):
    return pl.BlockSpec(a.shape, lambda i, *_: (0,) * len(a.shape))


def image_spec(a, tile):
    return pl.BlockSpec((a.shape[0], tile, a.shape[2]), lambda i, *_: (0, i, 0))


def table_spec(a, tile):
    return pl.BlockSpec((tile, a.shape[1]), lambda i, *_: (i, 0))


def shape_of(shape, dtype):
    return jax.ShapeDtypeStruct(shape, dtype)


def student_forward(place, pieces, above, below, label, tot, norm, weights, tile):
    group = len(pieces)
    local, images, lanes = pieces[0].shape
    p_rows = group * local // 2
    outs = [
        shape_of((2 * p_rows + 11, images, lanes), BF16),
        shape_of((p_rows + 6, images, 128 + lanes), BF16),
        shape_of((p_rows + 5, images, 128 + lanes), BF16),
        shape_of((p_rows + 5, images, lanes), F32),
    ]
    stats = shape_of((8, 128), F32)
    big = (*pieces, above, below)
    shared = (tot, norm, weights)
    grid_spec = pltpu.PrefetchScalarGridSpec(
        num_scalar_prefetch=1,
        grid=(images // tile,),
        in_specs=[image_spec(a, tile) for a in big]
        + [table_spec(label, tile)]
        + [whole_spec(a) for a in shared],
        out_specs=[image_spec(o, tile) for o in outs] + [whole_spec(stats)],
    )
    return pl.pallas_call(
        functools.partial(forward_kernel, p_rows, group, 4),
        grid_spec=grid_spec,
        out_shape=outs + [stats],
        compiler_params=pltpu.CompilerParams(vmem_limit_bytes=VMEM_LIMIT),
        cost_estimate=cost(15),
    )(place, *big, label, *shared)


def split_bf16(value):
    high = value.astype(BF16)
    return high, (value - high.astype(F32)).astype(BF16)


def block_kernel(
    p_rows,
    blocks,
    place,
    first_ref,
    odd,
    label_ref,
    tot,
    inner,
    norm,
    weights,
    spread,
    act,
    sum_ref,
    low_ref,
    energy,
):
    images, lanes = first_ref.shape[1:]
    w0, w1 = indicators(label_ref)
    gain, bias, _, _ = inner_tables(tot, inner, norm, w0, w1)
    gain2, bias2 = twice(gain), twice(bias)
    zero = jnp.zeros((images, 128), BF16)
    f_rows, b_rows = p_rows + 5, p_rows + 3

    def activate(f, carry):
        keep = keep_row(place, f - 2, p_rows)
        act[f, :, 0:128] = zero
        act[f, :, 128 + lanes : 256 + lanes] = zero
        for c in range(0, lanes, 256):
            z = first_ref[f, :, c : c + 256] * gain2 + bias2
            act[f, :, 128 + c : 384 + c] = (z * sigmoid(z) * keep).astype(BF16)
        return carry

    lax.fori_loop(0, f_rows, activate, 0)

    per_chunk = 128 // (lanes // CS_OUT)
    chunks = energy.shape[1] // 128
    measured = [jnp.zeros((images, 128), F32) for _ in range(chunks)]
    for j in range(0, lanes // 256, blocks):
        parts = [(act, a, 0, 512) for a in range(3)] + [(odd, 1, 128, 256)]
        left = stacked(j, blocks, images, b_rows, parts)
        flat = matmul(left, weights[...])
        y = flat.reshape(blocks, b_rows, images, 256)
        high, low = split_bf16(flat * flat)
        e = matmul(jnp.concatenate([high, low], axis=1), spread[...])
        e = e.reshape(blocks, b_rows, images, 128)
        for t in range(blocks):
            here = slice((j + t) * 256, (j + t + 1) * 256)
            sum_ref[:, :, here] = y[t]
            low_ref[:, :, here] = y[t, 1 : p_rows + 1].astype(BF16)
            for b in range(b_rows):
                shift = b % per_chunk * (128 // per_chunk) + 4 * (j + t)
                part = pltpu.roll(e[t, b], shift, 1) if shift else e[t, b]
                measured[b // per_chunk] = measured[b // per_chunk] + part
    for c in range(chunks):
        energy[:, c * 128 : c * 128 + 128] = measured[c]


def student_block(place, first_out, odd, label, tot, inner, norm, weights, spread, tile):
    rows, images, lanes = first_out.shape
    p_rows = rows - 5
    width = lanes // CS_OUT
    energy_lanes = -(-(p_rows + 3) * width // 128) * 128
    outs = [
        shape_of((p_rows + 5, images, 256 + lanes), BF16),
        shape_of((p_rows + 3, images, lanes), F32),
        shape_of((p_rows, images, lanes), BF16),
    ]
    energy = shape_of((images, energy_lanes), F32)
    return pl.pallas_call(
        functools.partial(block_kernel, p_rows, 4),
        grid_spec=pltpu.PrefetchScalarGridSpec(
            num_scalar_prefetch=1,
            grid=(images // tile,),
            in_specs=[image_spec(first_out, tile), image_spec(odd, tile), table_spec(label, tile)]
            + [whole_spec(a) for a in (tot, inner, norm, weights, spread)],
            out_specs=[image_spec(o, tile) for o in outs] + [table_spec(energy, tile)],
        ),
        out_shape=outs + [energy],
        compiler_params=pltpu.CompilerParams(vmem_limit_bytes=VMEM_LIMIT),
        cost_estimate=cost(18),
    )(place, first_out, odd, label, tot, inner, norm, weights, spread)


def map_kernel(slabs, group, widths, p_counts, pieces, *refs):
    student, present = refs[0:2], refs[2:4]
    given = refs[4 : 4 + sum(pieces)]
    refs = refs[4 + sum(pieces) :]
    outs, loss_ref = refs[0:2], refs[2]
    teacher, sums, boxes = refs[3:5], refs[5:7], refs[7:9]
    from_above, from_below = refs[9:11], refs[11:13]
    send, recv, send_halo, recv_halo, ready = refs[13:]
    for res in range(2):
        at = 0
        for part in given[res * pieces[0] : res * pieces[0] + pieces[res]]:
            teacher[res][at : at + part.shape[0]] = part[...]
            at += part.shape[0]
    me = lax.axis_index("space")
    z, x = lax.div(me, group), lax.rem(me, group)
    greet_barrier = pltpu.get_barrier_semaphore()
    for d in range(1, slabs):
        pl.semaphore_signal(
            greet_barrier,
            inc=1,
            device_id={"space": lax.rem(z + d, slabs) * group + x},
            device_id_type=MESH,
        )
    pl.semaphore_wait(greet_barrier, slabs - 1)

    def halo_copies(res, direction):
        width, p_rows = widths[res], p_counts[res]
        lane = (p_rows * width if direction == 0 else width) // 128 * 128
        target = (from_above, from_below)[direction][res]
        return pltpu.make_async_remote_copy(
            src_ref=teacher[res].at[:, pl.ds(lane, 128)],
            dst_ref=target,
            send_sem=send_halo.at[2 * res + direction],
            recv_sem=recv_halo.at[2 * res + direction],
            device_id={"space": me + (group if direction == 0 else -group)},
            device_id_type=MESH,
        )

    for res in range(2):
        from_above[res][...] = jnp.zeros(from_above[res].shape, F32)
        from_below[res][...] = jnp.zeros(from_below[res].shape, F32)

    @pl.when(z > 0)
    def _():
        pl.semaphore_signal(
            ready.at[0], inc=1, device_id={"space": me - group}, device_id_type=MESH
        )

    @pl.when(z < slabs - 1)
    def _():
        pl.semaphore_signal(
            ready.at[1], inc=1, device_id={"space": me + group}, device_id_type=MESH
        )
        pl.semaphore_wait(ready.at[0], 1)
        halo_copies(0, 0).start()
        halo_copies(1, 0).start()

    @pl.when(z > 0)
    def _():
        pl.semaphore_wait(ready.at[1], 1)
        halo_copies(0, 1).start()
        halo_copies(1, 1).start()

    copies = []
    for res in range(2):
        width, p_rows = widths[res], p_counts[res]
        images, lanes = student[res].shape
        lane = lax.broadcasted_iota(jnp.int32, (images, lanes), 1)
        own = jnp.logical_and(lane >= width, lane < (p_rows + 1) * width)
        es = jnp.where(own, student[res][...], 0.0)
        et = jnp.where(own, teacher[res][...], 0.0)
        columns = [
            jnp.sum(v, axis=1, keepdims=True) for v in (es * es, et * et, es * et)
        ]
        small_lane = lax.broadcasted_iota(jnp.int32, (images, 128), 1)
        packed = jnp.zeros((images, 128), F32)
        for k, column in enumerate(columns):
            packed = jnp.where(small_lane == k, column, packed)
        padded = sums[res].shape[1]
        packed = jnp.concatenate([packed, jnp.zeros((padded - images, 128), F32)], axis=0)
        sums[res][...] = packed.T[0:8]
        for d in range(1, slabs):
            copy = pltpu.make_async_remote_copy(
                src_ref=sums[res],
                dst_ref=boxes[res].at[d],
                send_sem=send.at[res * slabs + d],
                recv_sem=recv.at[res * slabs + d],
                device_id={"space": lax.rem(z + d, slabs) * group + x},
                device_id_type=MESH,
            )
            copy.start()
            copies.append(copy)
    for copy in copies:
        copy.wait()

    @pl.when(z < slabs - 1)
    def _():
        halo_copies(0, 0).wait_send()
        halo_copies(1, 0).wait_send()
        halo_copies(0, 1).wait_recv()
        halo_copies(1, 1).wait_recv()

    @pl.when(z > 0)
    def _():
        halo_copies(0, 1).wait_send()
        halo_copies(1, 1).wait_send()
        halo_copies(0, 0).wait_recv()
        halo_copies(1, 0).wait_recv()

    loss = jnp.zeros((1, 128), F32)
    for res in range(2):
        width, p_rows = widths[res], p_counts[res]
        images, lanes = student[res].shape
        total = sums[res][...]
        for d in range(1, slabs):
            total = total + boxes[res][d]
        padded = total.shape[1]
        total = jnp.concatenate([total, jnp.zeros((120, padded), F32)], axis=0).T[0:images]
        ss, tt, st = total[:, 0:1], total[:, 1:2], total[:, 2:3]
        scale_s = lax.rsqrt(ss + 1e-12)
        scale_t = lax.rsqrt(tt + 1e-12)
        pulled = TRANSFER_WEIGHT * scale_s * (scale_s * ss - scale_t * st)
        lane = lax.broadcasted_iota(jnp.int32, (images, lanes), 1)
        shift = p_rows * width
        chunks = lanes // 128
        first_rows = from_below[res][...]
        last_rows = from_above[res][...]
        if shift % 128:
            first_rows = pltpu.roll(first_rows, shift % 128, 1)
            last_rows = pltpu.roll(last_rows, 128 - shift % 128, 1)
        blank = jnp.zeros((images, 128), F32)
        before = [last_rows] + [blank] * (chunks - 1)
        after = [blank] * (chunks - 1) + [first_rows]
        before = jnp.concatenate(before, axis=1) if chunks > 1 else before[0]
        after = jnp.concatenate(after, axis=1) if chunks > 1 else after[0]
        et = jnp.where(lane < width, before, teacher[res][...])
        et = jnp.where(lane >= (p_rows + 1) * width, after, et)
        u = student[res][...] * scale_s
        difference = u - et * scale_t
        own = jnp.logical_and(lane >= width, lane < (p_rows + 1) * width)
        squares = jnp.where(own, difference * difference, 0.0)
        kept = (present[res][...] >= 0.0).astype(F32)
        for c in range(chunks):
            loss = loss + jnp.sum(squares[:, c * 128 : c * 128 + 128] * kept, axis=0, keepdims=True)
        factor = (TRANSFER_WEIGHT * difference - u * pulled) * (scale_s * (2.0 / CS_OUT))
        for c in range(chunks):
            here = slice(c * 128, c * 128 + 128)
            outs[res][:, here] = jnp.where(kept > 0.0, factor[:, here], 0.0)
    loss_ref[...] = jnp.concatenate(
        [loss * (TRANSFER_WEIGHT / 2), jnp.zeros((7, 128), F32)], axis=0
    )


def attention_maps(student, teacher, present, widths, p_counts, slabs, group, collective_id):
    padded = [-(-s.shape[0] // 128) * 128 for s in student]
    images = [s.shape[0] for s in student]
    vmem = pl.BlockSpec(memory_space=pltpu.VMEM)
    return pl.pallas_call(
        functools.partial(
            map_kernel, slabs, group, widths, p_counts, tuple(len(t) for t in teacher)
        ),
        out_shape=[shape_of(s.shape, F32) for s in student] + [shape_of((8, 128), F32)],
        in_specs=[vmem] * (4 + sum(len(t) for t in teacher)),
        out_specs=[vmem] * 3,
        scratch_shapes=[pltpu.VMEM(s.shape, F32) for s in student]
        + [pltpu.VMEM((8, n), F32) for n in padded]
        + [pltpu.VMEM((slabs, 8, n), F32) for n in padded]
        + [pltpu.VMEM((n, 128), F32) for n in images] * 2
        + [pltpu.SemaphoreType.DMA((2 * slabs,))] * 2
        + [pltpu.SemaphoreType.DMA((4,))] * 2
        + [pltpu.SemaphoreType.REGULAR((2,))],
        compiler_params=pltpu.CompilerParams(collective_id=collective_id, has_side_effects=True),
        cost_estimate=cost(11),
    )(*student, *present, *teacher[0], *teacher[1])


def back_kernel(
    p_rows,
    blocks,
    place,
    sum_ref,
    cot,
    factor,
    spread,
    first_ref,
    act,
    odd,
    label_ref,
    tot,
    inner,
    norm,
    weights,
    flow_ref,
    grad,
    stats,
    second_ref,
    shortcut_ref,
    kernel_ref,
):
    images, lanes = sum_ref.shape[1:]
    w0, w1 = indicators(label_ref)
    gain, bias, scale, shift = inner_tables(tot, inner, norm, w0, w1)
    gain2, bias2, scale2, shift2 = twice(gain), twice(bias), twice(scale), twice(shift)
    zero = jnp.zeros((images, 128), BF16)
    b_rows, k_rows = p_rows + 3, p_rows + 1
    width = lanes // CS_OUT
    per_chunk = 128 // width
    for b in range(b_rows):
        grad[b, :, 0:128] = zero
        grad[b, :, 128 + lanes : 256 + lanes] = zero
    halves = [split_bf16(factor[:, c * 128 : c * 128 + 128]) for c in range(factor.shape[1] // 128)]
    halves = [[h.astype(F32) for h in pair] for pair in halves]
    for j in range(0, lanes // 256, blocks):
        rows = []
        for t in range(blocks):
            for b in range(b_rows):
                shift = (128 - (b % per_chunk * width + 4 * (j + t))) % 128
                pair = halves[b // per_chunk]
                if shift:
                    pair = [pltpu.roll(h, shift, 1) for h in pair]
                rows.append(jnp.concatenate(pair, axis=1))
        wide = matmul(jnp.concatenate(rows, axis=0).astype(BF16), spread[...])
        wide = wide.reshape(blocks, b_rows, images, 256)
        for t in range(blocks):
            at = (j + t) * 256
            for b in range(b_rows):
                keep = keep_row(place, b - 1, p_rows)
                v = cot[b, :, at : at + 256].astype(F32) + wide[t, b] * sum_ref[b, :, at : at + 256]
                grad[b, :, 128 + at : 384 + at] = (v * keep).astype(BF16)

    @pl.when(pl.program_id(0) == 0)
    def _():
        kernel_ref[...] = jnp.zeros(kernel_ref.shape, F32)

    ones = jnp.zeros((images, 128), F32)
    cross = jnp.zeros((images, 128), F32)
    for j in range(0, lanes // 256, blocks):
        left = stacked(j, blocks, images, k_rows, [(grad, d, 0, 512) for d in range(3)])
        y = matmul(left, weights[...]).reshape(blocks, k_rows, images, 256)
        for t in range(blocks):
            here = slice((j + t) * 256, (j + t + 1) * 256)
            for k in range(k_rows):
                x = first_ref[k + 2, :, here]
                z = x * gain2 + bias2
                s = sigmoid(z)
                flow = y[t, k] * (s * (1.0 + z * (1.0 - s)))
                flow_ref[k, :, here] = flow
                if k < p_rows:
                    crossed = flow * (x * scale2 + shift2)
                    ones = ones + flow[:, 0:128] + flow[:, 128:256]
                    cross = cross + crossed[:, 0:128] + crossed[:, 128:256]
        right = stacked(
            j,
            blocks,
            images,
            p_rows,
            [(act, a, 0, 512) for a in range(1, 4)] + [(odd, 2, 128, 256)],
        )
        own = stacked(j, blocks, images, p_rows, [(grad, 1, 128, 256)])
        kernel_ref[...] += lax.dot_general(
            own, right, (((0,), (0,)), ((), ())), preferred_element_type=F32
        )
    add_rows(stats, grouped_rows(w0, w1, [ones, cross]))

    @pl.when(pl.program_id(0) == pl.num_programs(0) - 1)
    def _():
        turned = kernel_ref[...].T
        for a in range(3):
            for b in range(3):
                tap = jnp.zeros((CS_OUT, CS_OUT), F32)
                for q in range(4):
                    row = a * 512 + (q + b + 1) * CS_OUT
                    tap = tap + turned[row : row + CS_OUT, q * CS_OUT : (q + 1) * CS_OUT]
                row = (3 * a + b) * CS_OUT
                second_ref[row : row + CS_OUT] = tap
        tap = jnp.zeros((CS_IN, CS_OUT), F32)
        for q in range(4):
            row = 1536 + 2 * q * CS_IN
            tap = tap + turned[row : row + CS_IN, q * CS_OUT : (q + 1) * CS_OUT]
        shortcut_ref[...] = tap


def student_back(
    place, block_sum, cot, factor, spread, first_out, act, odd, label, tot, inner, norm, weights, tile
):
    rows, images, lanes = block_sum.shape
    p_rows = rows - 3
    outs = [
        shape_of((p_rows + 1, images, lanes), F32),
        shape_of((p_rows + 3, images, 256 + lanes), BF16),
    ]
    stats = shape_of((8, 128), F32)
    second = shape_of((9 * CS_OUT, CS_OUT), F32)
    shortcut = shape_of((CS_IN, CS_OUT), F32)
    return pl.pallas_call(
        functools.partial(back_kernel, p_rows, 4),
        grid_spec=pltpu.PrefetchScalarGridSpec(
            num_scalar_prefetch=1,
            grid=(images // tile,),
            in_specs=[image_spec(block_sum, tile), image_spec(cot, tile), table_spec(factor, tile)]
            + [whole_spec(spread), image_spec(first_out, tile), image_spec(act, tile)]
            + [image_spec(odd, tile), table_spec(label, tile)]
            + [whole_spec(a) for a in (tot, inner, norm, weights)],
            out_specs=[image_spec(o, tile) for o in outs]
            + [whole_spec(a) for a in (stats, second, shortcut)],
            scratch_shapes=[pltpu.VMEM((256, 1792), F32)],
        ),
        out_shape=outs + [stats, second, shortcut],
        compiler_params=pltpu.CompilerParams(vmem_limit_bytes=VMEM_LIMIT),
        cost_estimate=cost(18),
    )(place, block_sum, cot, factor, spread, first_out, act, odd, label, tot, inner, norm, weights)


def entry_kernel(
    p_rows,
    blocks,
    place,
    flow_ref,
    first_ref,
    grad,
    even,
    odd,
    raw,
    label_ref,
    tot,
    inner,
    pulled,
    norm_in,
    norm,
    weights_even,
    weights_odd,
    out_ref,
    taps_ref,
    stats,
    first_grad,
    kernel_ref,
):
    images, lanes = first_ref.shape[1:]
    w0, w1 = indicators(label_ref)
    gain, _, scale, shift = inner_tables(tot, inner, norm, w0, w1)
    counts = inner_counts(tot)
    folded = fold(pulled[...], CS_OUT)
    ones_mean = per_image(w0, w1, [folded[g : g + 1] / counts[g] for g in range(2)])
    cross_mean = per_image(w0, w1, [folded[2 + g : 3 + g] / counts[g] for g in range(2)])
    gain2, scale2, shift2 = twice(gain), twice(scale), twice(shift)
    ones2, cross2 = twice(ones_mean), twice(cross_mean)
    zero = jnp.zeros((images, 128), BF16)

    def first_rows(k, carry):
        keep = keep_row(place, k, p_rows)
        first_grad[k, :, lanes : lanes + 128] = zero
        for c in range(0, lanes, 256):
            normed = first_ref[k + 2, :, c : c + 256] * scale2 + shift2
            v = gain2 * (flow_ref[k, :, c : c + 256] - ones2 - normed * cross2)
            first_grad[k, :, c : c + 256] = (v * keep).astype(BF16)
        return carry

    lax.fori_loop(0, p_rows + 1, first_rows, 0)

    @pl.when(pl.program_id(0) == 0)
    def _():
        kernel_ref[...] = jnp.zeros(kernel_ref.shape, F32)

    gain, bias, scale, shift = entry_tables(tot, norm_in, w0, w1)
    gain2, bias2, scale2, shift2 = twice(gain), twice(bias), twice(scale), twice(shift)

    ones = jnp.zeros((images, 128), F32)
    cross = jnp.zeros((images, 128), F32)
    for j in range(0, lanes // 256, blocks):
        upper = (first_grad, 0, 0, 384)
        lower = (first_grad, 1, 0, 384)
        left = stacked(j, blocks, images, p_rows, [upper, (grad, 1, 128, 256)])
        rows_even = matmul(left, weights_even[...])
        rows_odd = matmul(stacked(j, blocks, images, p_rows, [upper, lower]), weights_odd[...])
        for parity, rows in enumerate((rows_even, rows_odd)):
            low = rows.astype(BF16).reshape(blocks, p_rows, images, 256)
            for t in range(blocks):
                here = slice((j + t) * 256, (j + t + 1) * 256)
                for p in range(p_rows):
                    out_ref[2 * p + parity, :, here] = low[t, p]
                    x = raw[2 * p + parity + 5, :, here].astype(F32)
                    z = x * gain2 + bias2
                    s = sigmoid(z)
                    flow = low[t, p].astype(F32) * (s * (1.0 + z * (1.0 - s)))
                    crossed = flow * (x * scale2 + shift2)
                    ones = ones + flow[:, 0:128] + flow[:, 128:256]
                    cross = cross + crossed[:, 0:128] + crossed[:, 128:256]
        right = stacked(
            j,
            blocks,
            images,
            p_rows,
            [(even, 2, 0, 384), (odd, 2, 0, 384), (even, 3, 0, 384)],
        )
        own = stacked(j, blocks, images, p_rows, [(first_grad, 0, 0, 256)])
        kernel_ref[...] += lax.dot_general(
            own, right, (((0,), (0,)), ((), ())), preferred_element_type=F32
        )
    add_rows(stats, grouped_rows(w0, w1, [ones, cross]))

    @pl.when(pl.program_id(0) == pl.num_programs(0) - 1)
    def _():
        turned = kernel_ref[...].T
        for a in range(3):
            for b in range(3):
                tap = jnp.zeros((CS_IN, CS_OUT), F32)
                for q in range(4):
                    row = a * 384 + (2 * q + b + 3) * CS_IN
                    tap = tap + turned[row : row + CS_IN, q * CS_OUT : (q + 1) * CS_OUT]
                row = (3 * a + b) * CS_IN
                taps_ref[row : row + CS_IN] = tap


def student_entry(
    place, flow, first_out, grad, even, odd, raw, label, tot, inner, pulled, norm_in, norm,
    weights_even, weights_odd, tile,
):
    rows, images, lanes = flow.shape
    p_rows = rows - 1
    out = shape_of((2 * p_rows, images, lanes), BF16)
    taps = shape_of((9 * CS_IN, CS_OUT), F32)
    stats = shape_of((8, 128), F32)
    big = (flow, first_out, grad, even, odd, raw)
    shared = (tot, inner, pulled, norm_in, norm, weights_even, weights_odd)
    return pl.pallas_call(
        functools.partial(entry_kernel, p_rows, 4),
        grid_spec=pltpu.PrefetchScalarGridSpec(
            num_scalar_prefetch=1,
            grid=(images // tile,),
            in_specs=[image_spec(a, tile) for a in big]
            + [table_spec(label, tile)]
            + [whole_spec(a) for a in shared],
            out_specs=[image_spec(out, tile), whole_spec(taps), whole_spec(stats)],
            scratch_shapes=[
                pltpu.VMEM((p_rows + 1, tile, 128 + lanes), BF16),
                pltpu.VMEM((256, 1152), F32),
            ],
        ),
        out_shape=[out, taps, stats],
        compiler_params=pltpu.CompilerParams(vmem_limit_bytes=VMEM_LIMIT),
        cost_estimate=cost(16),
    )(place, *big, label, *shared)


def bands_kernel(first, first_t, second, second_t, short, short_t, *outs):
    one, two, back, even, odd, gather, scatter, wide = outs

    def fill(out, entries):
        rows = out.shape[0]
        wide[0:rows] = jnp.zeros((rows, 256), F32)
        for row, lane, tap in entries:
            wide[row : row + tap.shape[0], lane : lane + tap.shape[1]] = tap
        out[...] = wide[0:rows].astype(BF16)

    def tap_of(ref, a, b):
        size = ref.shape[0] // 9
        return ref[(3 * a + b) * size : (3 * a + b + 1) * size]

    taps = [(a, b) for a in range(3) for b in range(3)]
    fill(
        one,
        [
            (a * 384 + (2 * q + b + 3) * CS_IN, q * CS_OUT, tap_of(first, a, b))
            for a, b in taps
            for q in range(4)
        ],
    )
    fill(
        two,
        [
            (a * 512 + (q + b + 1) * CS_OUT, q * CS_OUT, tap_of(second, a, b))
            for a, b in taps
            for q in range(4)
        ]
        + [(1536 + 2 * q * CS_IN, q * CS_OUT, short[...]) for q in range(4)],
    )
    fill(
        back,
        [
            ((2 - a) * 512 + (s - b + 3) * CS_OUT, s * CS_OUT, tap_of(second_t, a, b))
            for a, b in taps
            for s in range(4)
        ],
    )

    def backward(a, row):
        entries = []
        for q in range(6):
            for b in range(3):
                s = 2 * q + b - 1
                if 0 <= s < 8:
                    entries.append((row + q * CS_OUT, s * CS_IN, tap_of(first_t, a, b)))
        return entries

    corner = [(384 + q * CS_OUT, 2 * q * CS_IN, short_t[...]) for q in range(4)]
    fill(even, backward(1, 0) + corner)
    fill(odd, backward(2, 0) + backward(0, 384))
    channel = lax.rem(lax.broadcasted_iota(jnp.int32, gather.shape, 0), 256)
    lane = lax.broadcasted_iota(jnp.int32, gather.shape, 1)
    gather[...] = jnp.where(lax.div(channel, CS_OUT) == lane, 1.0 / CS_OUT, 0.0).astype(BF16)
    lane = lax.rem(lax.broadcasted_iota(jnp.int32, scatter.shape, 0), 128)
    channel = lax.broadcasted_iota(jnp.int32, scatter.shape, 1)
    scatter[...] = jnp.where(lax.div(channel, CS_OUT) == lane, 1.0, 0.0).astype(BF16)


def banded_kernels(first, second, shortcut):
    turn = lambda k: jnp.swapaxes(k, 2, 3).reshape(-1, k.shape[2])
    rounded = lambda k: k.astype(BF16).astype(F32)
    first, second, shortcut = rounded(first), rounded(second), rounded(shortcut)
    args = (
        first.reshape(-1, CS_OUT),
        turn(first),
        second.reshape(-1, CS_OUT),
        turn(second),
        shortcut,
        shortcut.T,
    )
    shapes = [(1152, 256), (1792, 256), (1536, 256), (640, 256), (768, 256), (512, 128), (256, 256)]
    return pl.pallas_call(
        bands_kernel,
        in_specs=[pl.BlockSpec(memory_space=pltpu.VMEM)] * 6,
        out_specs=[pl.BlockSpec(memory_space=pltpu.VMEM)] * len(shapes),
        out_shape=[shape_of(shape, BF16) for shape in shapes],
        scratch_shapes=[pltpu.VMEM((1792, 256), F32)],
        compiler_params=pltpu.CompilerParams(vmem_limit_bytes=VMEM_LIMIT),
        cost_estimate=cost(8),
    )(*args)


def renew(weights, gradient, moment, average, factor):
    descent = gradient + WEIGHT_DECAY * weights
    velocity = MOMENTUM * moment + descent
    updated = weights - factor * (descent + MOMENTUM * velocity)
    smoothed = AVERAGING * average + (1.0 - AVERAGING) * updated
    return (gradient, velocity, smoothed, updated)


def body(
    space,
    batch,
    small_in,
    large_in,
    small_teacher,
    large_teacher,
    small_groups,
    large_groups,
    small_cot,
    large_cot,
    teacher_gains,
    teacher_first,
    teacher_inner,
    teacher_second,
    teacher_bypass,
    entry_norm,
    first_conv,
    inner_norm,
    second_conv,
    shortcut,
    momentum_entry,
    momentum_first,
    momentum_inner,
    momentum_second,
    momentum_shortcut,
    average_entry,
    average_first,
    average_inner,
    average_second,
    average_shortcut,
):
    slabs = SLABS
    group = space // slabs
    axes = (("space", space), ("batch", batch))
    me = lax.axis_index("space")
    z, x = me // group, me % group
    place = jnp.stack([x, z]).astype(jnp.int32)
    total_positions = batch * (small_in.shape[0] * SIDE * SIDE // 4 + large_in.shape[0] * SIDE * SIDE)
    pixels = [small_in, large_in]
    teachers = [small_teacher, large_teacher]
    labels = [small_groups, large_groups]
    cots = [small_cot, large_cot]
    sides = [SIDE, 2 * SIDE]
    both = range(2)
    per_device = [p.shape[0] // space for p in pixels]
    local_rows = [p.shape[1] for p in pixels]
    images = [slabs * n for n in per_device]
    padded = [-(-n // 16) * 16 for n in images]
    tiles = [32 if padded[0] % 32 == 0 else 16, 16]
    p_counts = [s // (2 * slabs) for s in sides]
    widths = [s // 2 for s in sides]

    def to_sub(d):
        return [(k, k // group * group + (k % group + d) % group) for k in range(space)]

    def to_slab(d):
        return [(k, (k // group + d) % slabs * group + k % group) for k in range(space)]

    def send(array, pairs):
        return lax.ppermute(array, "space", pairs)

    down = [(k, k + group) for k in range(space - group)]
    up = [(k, k - group) for k in range(group, space)]

    def pick_images(array, res, sub):
        n, rows, lanes = array.shape
        parts = array.reshape(slabs, group, per_device[res], rows, lanes)
        part = lax.dynamic_index_in_dim(parts, sub, 1, False)
        return part.reshape(images[res], rows, lanes)

    def rows_first(array):
        return jnp.transpose(array, (1, 0, 2))

    def slab_rows(pieces, first, last):
        local = pieces[0].shape[0]
        out = []
        for s in range(first // local, (last - 1) // local + 1):
            lo, hi = max(first - s * local, 0), min(last - s * local, local)
            cut = [p[lo:hi] for p in pieces]
            out.append(lax.select_n((x - s) % group, *cut) if group > 1 else cut[0])
        return jnp.concatenate(out, axis=0) if len(out) > 1 else out[0]

    def edge_rows(pieces, above, below):
        rows = group * pieces[0].shape[0]
        return slab_rows(pieces, rows - above, rows), slab_rows(pieces, 0, below)

    def to_neighbours(rows):
        return send(rows[0], down), send(rows[1], up)

    def halos(pieces, above, below):
        return to_neighbours(edge_rows(pieces, above, below))

    def pad_to(array, size):
        extra = size - array.shape[1]
        return jnp.pad(array, ((0, 0), (0, extra), (0, 0))) if extra else array

    def pad_images(array, res):
        return pad_to(array, padded[res])

    def label_table(res, sub, size):
        mine = lax.dynamic_index_in_dim(
            labels[res].reshape(slabs, group, per_device[res]), sub, 1, False
        ).reshape(images[res])
        mine = jnp.pad(mine.astype(F32), (0, size - images[res]), constant_values=-1.0)
        return jnp.broadcast_to(mine[:, None], (size, 128))

    tables = [label_table(res, x, padded[res]) for res in both]
    norm_in = jnp.tile(entry_norm, (1, 128 // CS_IN))
    norm_mid = jnp.tile(inner_norm, (1, 128 // CS_OUT))
    by_slab = [[sub + group * k for k in range(slabs)] for sub in range(group)]

    def among_slabs(array, axis):
        if axis:
            array = jnp.moveaxis(array, axis, 0)
        return lax.all_to_all(array, "space", 0, 0, axis_index_groups=by_slab, tiled=True)

    subs = [(x + d) % group for d in range(group)]
    picked = [[rows_first(pick_images(pixels[res], res, sub)) for sub in subs] for res in both]
    arrived = [
        [picked[res][0]] + [send(picked[res][d], to_sub(d)) for d in range(1, group)]
        for res in both
    ]

    narrow = cots[0].shape[2]
    cot_stacks = []
    for res in both:
        c = jnp.pad(rows_first(cots[res]), ((1, 2), (0, 0), (0, 0)))
        count = p_counts[res]
        c = jnp.stack([c[k * count : (k + 1) * count + 3] for k in range(slabs)])
        if c.shape[3] > narrow:
            c = jnp.concatenate(
                [c[..., k : k + narrow] for k in range(0, c.shape[3], narrow)], axis=2
            )
        cot_stacks.append(c)
    flat = [c.reshape(slabs, -1, narrow) for c in cot_stacks]
    cot_flat = among_slabs(jnp.concatenate(flat, axis=1), 0)

    gains = jnp.tile(teacher_gains, (1, max(t.shape[2] for t in teachers) // CT_IN))

    def activated(array, size):
        lanes = array.shape[2]
        z_t = gains[0, :lanes] * array.astype(F32) + gains[1, :lanes]
        return pad_to(rows_first(jax.nn.silu(z_t).astype(BF16)), size)

    large_raw_in = after(large_teacher, [p[1:] for p in picked])
    own_large = pick_images(large_raw_in, 1, x)
    away_large = [pick_images(large_raw_in, 1, sub) for sub in subs[1:]]
    cut = min(16, images[1])
    sizes = [cut, -(-(images[1] - cut) // 16) * 16]
    ranges = [(0, cut), (cut, images[1])]

    def large_part(k, *others):
        lo, hi = ranges[k]
        return [
            send(after(away_large[d - 1][lo:hi], *others), to_sub(d)) for d in range(1, group)
        ]

    large_raw = [large_part(0)]

    stat_tables = [label_table(res, sub, images[res]) for res in both for sub in subs]
    entry_sums = input_stats(picked[0] + picked[1], stat_tables)
    entry_sums = after(entry_sums, [p[1:] for p in arrived], cot_flat, large_raw)
    entry_total = total_over_devices([entry_sums], axes, 0)

    raw_halos = [halos([after(p, entry_total) for p in arrived[res]], 5, 6) for res in both]
    large_raw.append(large_part(1, entry_total))
    large_own = [
        activated(after(own_large[lo:hi], large_raw_in), size)
        for (lo, hi), size in zip(ranges, sizes)
    ]
    large_pieces = [
        [own] + [activated(after(p, entry_total), size) for p in raw]
        for own, size, raw in zip(large_own, sizes, large_raw)
    ]

    def large_edges_of(k, *others):
        lo, hi = ranges[k]
        rows = [after(p[:, : hi - lo], *others) for p in large_pieces[k]]
        return [pad_to(h, sizes[k]) for h in halos(rows, 3, 2)]

    large_edges = [large_edges_of(0, raw_halos[1])]
    lanes = small_teacher.shape[2]
    z_t = after(small_teacher, large_raw_in).astype(F32) * gains[0, :lanes] + gains[1, :lanes]
    small_active = rows_first(jax.nn.silu(z_t).astype(BF16))
    small_active = small_active.reshape(local_rows[0], slabs, group, per_device[0], lanes)

    small_away = [
        [lax.dynamic_index_in_dim(small_active[:, k], sub, 1, False) for sub in subs[1:]]
        for k in range(slabs)
    ]
    cot_here = after(cot_flat, entry_total)
    cot_slabs = []
    at = 0
    for res, sent in zip(both, cot_stacks):
        size = sent.shape[1] * sent.shape[2]
        c = cot_here[:, at : at + size].reshape(sent.shape)
        at += size
        n = per_device[res]
        c = jnp.concatenate([c[:, :, k : k + n] for k in range(0, c.shape[2], n)], axis=3)
        c = jnp.moveaxis(c, 0, 1).reshape(c.shape[1], images[res], c.shape[3])
        cot_slabs.append(pad_images(c, res))

    bands = banded_kernels(*after((first_conv, second_conv, shortcut), large_raw_in))
    bands_first, bands_second, bands_second_back, bands_even, bands_odd, gather, scatter = bands
    raws, evens, odds, firsts, first_sums = [], [], [], [], []
    for res in both:
        raw, even, odd, first, sums = student_forward(
            place,
            [pad_images(p, res) for p in arrived[res]],
            *[pad_images(p, res) for p in raw_halos[res]],
            tables[res],
            entry_total,
            norm_in,
            bands_first,
            tiles[res],
        )
        raws.append(raw)
        evens.append(even)
        odds.append(odd)
        firsts.append(first)
        first_sums.append(sums)
    first_sums = after(first_sums, large_pieces, large_edges)
    inner_total = total_over_devices(first_sums, axes, 1)

    large_edges.append(large_edges_of(1, inner_total))
    order = list(range(slabs))[::-1]
    small_pieces = {}
    for k in order:
        waits = [inner_total]
        if k == order[-1]:
            waits.append(small_pieces[order[0]])
        small_pieces[k] = [
            send(after(p, *waits), to_sub(d + 1)) for d, p in enumerate(small_away[k])
        ]

    def small_rows(k, *others):
        own = lax.dynamic_index_in_dim(small_active[:, k], x, 1, False)
        return edge_rows([own] + after(small_pieces[k], *others), 3, 2)

    small_edge_rows = {order[0]: small_rows(order[0])}

    acts, sums_out, lows, energies = [], [], [], []
    for res in both:
        act, block_sum, low, energy = student_block(
            place,
            after(firsts[res], small_edge_rows[order[0]]) if res else firsts[res],
            odds[res],
            tables[res],
            entry_total,
            inner_total,
            norm_mid,
            bands_second,
            gather,
            tiles[res],
        )
        acts.append(act)
        sums_out.append(block_sum)
        lows.append(low)
        energies.append(energy)

    shared = (
        teacher_first.reshape(9 * CT_IN, CT_OUT),
        teacher_second.reshape(9 * CT_OUT, CT_OUT),
        teacher_bypass,
        teacher_inner,
    )
    def large_map(k, *others):
        pieces = large_pieces[k]
        own = after(pieces[0], *others)
        return teacher_energies(place, own, 0, pieces[1:], *large_edges[k], shared, tiles[1])

    def small_map(k, *others):
        edges = to_neighbours(small_edge_rows[k])
        pieces = after(small_pieces[k], *others)
        return teacher_energies(
            place, small_active, k, pieces, *edges, shared, per_device[0]
        )

    large_maps = [large_map(0, inner_total)]
    small_maps = {}
    small_edge_rows[order[1]] = small_rows(order[1], large_maps[0])
    large_maps.append(large_map(1, small_edge_rows[order[1]]))
    small_edge_rows[order[2]] = small_rows(order[2], large_maps[1])
    for k in order[:2]:
        small_maps[k] = small_map(k, small_edge_rows[order[2]])
    small_edge_rows[order[3]] = small_rows(order[3], small_maps[order[0]], small_maps[order[1]])
    for k in order[2:]:
        small_maps[k] = small_map(k, small_edge_rows[order[3]])
    small_maps = [small_maps[k] for k in range(slabs)]
    factors = attention_maps(
        energies, [small_maps, large_maps], tables, widths, p_counts, slabs, group, 2
    )
    loss_sums = factors[2]

    def to_owners(res, *others):
        low = after(lows[res][:, : images[res]], *others)
        rows, _, lanes = low.shape
        return among_slabs(low.reshape(rows, slabs, per_device[res], lanes), 1)

    out_parts = [to_owners(0, factors[2])]

    flows, grads, flow_sums, second_parts, shortcut_parts = [], [], [], [], []
    for res in both:
        flow, grad, sums, second_part, shortcut_part = student_back(
            place,
            sums_out[res],
            cot_slabs[res],
            factors[res],
            scatter,
            firsts[res],
            acts[res],
            odds[res],
            tables[res],
            entry_total,
            inner_total,
            norm_mid,
            bands_second_back,
            tiles[res],
        )
        flows.append(flow)
        grads.append(grad)
        flow_sums.append(sums)
        second_parts.append(second_part)
        shortcut_parts.append(shortcut_part)
    flow_total = total_over_devices(after(flow_sums, out_parts[0]), axes, 3)
    out_parts.append(to_owners(1, flow_total))

    entry_parts, first_parts, entry_flow_sums = [], [], []
    packed = None
    for res in both:
        rows, first_part, sums = student_entry(
            place,
            after(flows[res], entry_parts[0][0]) if res == 1 else flows[res],
            firsts[res],
            grads[res],
            evens[res],
            odds[res],
            raws[res],
            tables[res],
            entry_total,
            inner_total,
            flow_total,
            norm_in,
            norm_mid,
            bands_even,
            bands_odd,
            tiles[res],
        )
        first_parts.append(first_part)
        entry_flow_sums.append(sums)
        if res == 1:
            held = after(entry_flow_sums, entry_parts[0][1:], out_parts[1])
            packed = spread_sum(
                [first_parts, second_parts, shortcut_parts, held, [loss_sums]], axes, 4
            )
        rows = rows[:, : images[res]]
        parts = []
        for d in range(group):
            part = lax.dynamic_slice_in_dim(rows, subs[d] * local_rows[res], local_rows[res], 0)
            if d:
                part = send(after(part, packed) if res == 1 else part, to_sub(d))
            parts.append(part)
        entry_parts.append(parts)

    def unpack(pairs, shape):
        return jnp.concatenate([pairs[:, :64], pairs[:, 64:]], axis=0).reshape(shape)

    first_grads = unpack(packed[0], first_conv.shape)
    second_grads = unpack(packed[1], second_conv.shape)
    shortcut_grads = unpack(packed[2], shortcut.shape)
    entry_pulled = packed[3].reshape(8, 128 // CS_IN, CS_IN).sum(axis=1)
    total_loss = jnp.sum(packed[4])

    counts = entry_total[4:6, 0:1]
    entry_folded = entry_total.reshape(8, 128 // CS_IN, CS_IN).sum(axis=1)
    mean_entry = entry_folded[0:2] / counts
    scale_entry = lax.rsqrt(entry_folded[2:4] / counts - mean_entry * mean_entry + EPSILON)
    shift_entry = -mean_entry * scale_entry
    ones_entry, cross_entry = entry_pulled[0:2], entry_pulled[2:4]
    inner_folded = flow_total.reshape(8, 128 // CS_OUT, CS_OUT).sum(axis=1)
    ones_inner, cross_inner = inner_folded[0:2], inner_folded[2:4]

    gain_entry = entry_norm[0] * scale_entry
    bias_entry = entry_norm[0] * shift_entry + entry_norm[1]
    slope_entry = -gain_entry * (cross_entry / counts) * scale_entry
    level_entry = -gain_entry * ((ones_entry + cross_entry * shift_entry) / counts)
    block_outs = []
    for res in both:
        low = after(out_parts[res], packed)
        low = jnp.transpose(low, (2, 0, 1, 3))
        block_outs.append(low.reshape(low.shape[0], -1, low.shape[3]))
    entry_parts[0] = after(entry_parts[0], packed)
    input_grads = []
    for res in both:
        n, rows, lanes = pixels[res].shape
        ordered = [lax.select_n((x - s) % group, *entry_parts[res]) for s in range(group)]
        rows_in = jnp.stack(ordered).reshape(group, rows, slabs, per_device[res], lanes)
        rows_in = jnp.transpose(rows_in, (2, 0, 3, 1, 4)).reshape(n, rows, lanes)
        one = (labels[res] == 1)[:, None, None]

        def by_image(pair):
            wide = jnp.tile(pair, (1, lanes // CS_IN))
            return jnp.where(one, wide[1], wide[0])

        value = pixels[res].astype(F32)
        gain = by_image(gain_entry)
        before = value * gain + by_image(bias_entry)
        s = jax.nn.sigmoid(before)
        flow = rows_in.astype(F32) * (s * (1.0 + before * (1.0 - s)))
        input_grads.append(gain * flow + (value * by_image(slope_entry) + by_image(level_entry)))

    entry_grads = jnp.stack([jnp.sum(cross_entry, axis=0), jnp.sum(ones_entry, axis=0)])
    inner_grads = jnp.stack([jnp.sum(cross_inner, axis=0), jnp.sum(ones_inner, axis=0)])
    rate_scale = 1.0 / math.sqrt(total_positions)
    entry_state = renew(entry_norm, entry_grads, momentum_entry, average_entry, NORM_RATE * rate_scale)
    first_state = renew(first_conv, first_grads, momentum_first, average_first, CONV_RATE * rate_scale)
    inner_state = renew(inner_norm, inner_grads, momentum_inner, average_inner, NORM_RATE * rate_scale)
    second_state = renew(
        second_conv, second_grads, momentum_second, average_second, CONV_RATE * rate_scale
    )
    bypass_state = renew(
        shortcut, shortcut_grads, momentum_shortcut, average_shortcut, CONV_RATE * rate_scale
    )
    return (
        *block_outs,
        input_grads[0],
        input_grads[1],
        total_loss / total_positions,
        *entry_state,
        *first_state,
        first_state[3].astype(BF16),
        *inner_state,
        *second_state,
        second_state[3].astype(BF16),
        *bypass_state,
        bypass_state[3].astype(BF16),
    )


def solution(mesh):
    rows = P("batch", "space", None)
    blocks = P(("batch", "space"), None, None)
    return jax.shard_map(
        functools.partial(body, mesh.shape["space"], mesh.shape["batch"]),
        mesh=mesh,
        in_specs=(rows,) * 4 + (P("batch"),) * 2 + (blocks,) * 2 + (P(),) * 20,
        out_specs=(blocks,) * 2 + (rows,) * 2 + (P(),) * 24,
        check_vma=False,
    )
```

time: 1030 us -> 655 us (0.64)
  Pallas kernels: 461 us -> 296 us
  local copies, waits for them, and re-layouts: 227 us -> 137 us
  other arithmetic: 172 us -> 95 us
  waiting for transfers between devices: 56.7 us -> 36.1 us
  matrix products: 18 us -> 0 us
    pallas_call x3, Pallas kernels: 132 us -> 32.7 us  [total_over_devices(): pl.pallas_call(functools.partial(total_kernel, axes, len(parts)), out_sha...]
    pallas_call x11 -> x16, Pallas kernels: 313 us -> 247 us  [the longest x6 103 us: teacher_energies(): pl.pallas_call(functools.partial(teacher_kernel, p_rows, width, group, 4)...]
    reshape x33 -> x9, local copies, waits for them, and re-layouts: 47.7 us -> 9.9 us  [the longest x2 3.58 us: pick_images(): return part.reshape(images[res], rows, lanes)]
    ppermute x26, waiting for transfers between devices: 56.7 us -> 19.9 us  [send(): return lax.ppermute(array, 'space', pairs)]
    concatenate x11 -> x6, other arithmetic: 40 us -> 6.95 us  [the longest x2 4.33 us: slab_rows(): return jnp.concatenate(out, axis=0) if len(out) > 1 else out[0]]
    another operation x27 -> x22, local copies, waits for them, and re-layouts: 28.2 us -> 1.85 us  [the longest x2 0.65 us: body(): norm_in = jnp.tile(entry_norm, (1, 128 // CS_IN))]
    convert_element_type x10 -> x6, other arithmetic: 35.7 us -> 13.7 us  [the longest x1 12.9 us: body(): small_active = rows_first(jax.nn.silu(z_t).astype(BF16))]
    unnamed x181 -> x185, local copies, waits for them, and re-layouts: 36 us -> 14.6 us
  transfers between devices with their start and end apart: 26 -> 29, of which waited for: 6 -> 4; matrix products, arithmetic and copies ran while one was open for 35% -> 29% of each run, Pallas kernels for 27% -> 34%
where the time goes in v2:
time: 655 us; the launch traced here: 645 us
  Pallas kernels  296 us (45%)
  local copies, waits for them, and re-layouts  137 us (21%)
  other arithmetic  95 us (15%)
  starting transfers between devices  77.2 us (12%)
  waiting for transfers between devices  36.1 us (6%)
    pallas_call x6, Pallas kernels, teacher_energies(): pl.pallas_call(functools.partial(teacher_kernel, p_rows, width, group, 4)...  103 us
    ppermute x26, starting transfers between devices, send(): return lax.ppermute(array, 'space', pairs)  63.6 us
    pallas_call x3, Pallas kernels, total_over_devices(): pl.pallas_call(functools.partial(total_kernel, axes, len(parts)), out_sha...  32.7 us
    pallas_call x2, Pallas kernels, student_block(): pl.pallas_call(functools.partial(block_kernel, p_rows, 4), grid_spec=pltp...  31.8 us
    pallas_call x2, Pallas kernels, student_entry(): pl.pallas_call(functools.partial(entry_kernel, p_rows, 4), grid_spec=pltp...  30.2 us
    pallas_call x2, Pallas kernels, student_back(): pl.pallas_call(functools.partial(back_kernel, p_rows, 4), grid_spec=pltpu...  29.6 us
    pallas_call x2, Pallas kernels, student_forward(): pl.pallas_call(functools.partial(forward_kernel, p_rows, group, 4), grid_...  27.7 us
    select_n x17, other arithmetic, slab_rows(): out.append(lax.select_n((x - s) % group, *cut) if group > 1 else cut[0])  22.7 us
  transfers between devices with their start and end apart: 29, of which 4 were waited for; matrix products, arithmetic and copies ran while one was open for 29% of the time, Pallas kernels for 34%

profile of v2, /device:TPU:0, one launch (start us, length us, event | category | flops | bytes accessed | tf_op | source)
XLA Modules:
  0.0 645.4 jit_solution(9257997652926659)
XLA Ops:
  38.5 12.9 %multiply_convert_fusion = bf16[320,4,4096]{2,0,1:T(8,128)(2,1)} fusion(bf16[320,4,4096]{2,1,0:T(4,128)(2,1)} %param.30, f32[4096]{0:T(1024)S(1)} %bitcast.257, f32[4096]{0:T(1024)S(1)} %bitcast.256), kind=kLoop, calls=%fused_computation | loop fusion | flops 41943040 | bytes 21004288 | tf_op jit(solution)/shard_map/convert_element_type | solution.py:1420
  113.4 16.2 %all-to-all-done = bf16[4,500,1024]{2,1,0:T(8,128)(2,1)} async-done(((bf16[4,500,1024]{2,1,0:T(8,128)(2,1)}), bf16[4,500,1024]{2,1,0:T(8,128)(2,1)}, u32[]{:S(2)}, u32[]{:S(2)}) %all-to-all-start) | async-done | bytes 4096032 | tf_op jit(solution)/shard_map/all_to_all | solution.py:1351
  129.6 10.9 %shard_map.484.refs_5_.tot = f32[8,128]{1,0:T(8,128)} custom-call(f32[8,128]{1,0:T(8,128)} %shard_map.483.refs_0_), custom_call_target="tpu_custom_call" | custom-call | flops 12000000000 | bytes 1048576 | tf_op jit(solution)/shard_map/pallas_call | solution.py:210
  176.6 13.5 %fusion.27 = (bf16[8,16,8192]{2,1,0:T(8,128)(2,1)}, bf16[8,16,8192]{2,1,0:T(8,128)(2,1)}) fusion(bf16[16,8,8192]{2,0,1:T(8,128)(2,1)} %collective-permute-done.2, f32[8192]{0:T(1024)S(1)} %get-tuple-element.400, f32[8192]{0:T(1024)S(1)} %get-tuple-element.401, bf16[16,8,8192]{2,0,1:T(8,128)(2,1)S(1)} %copy-done.17), kind=kLoop, calls=%fused_computation.41 | loop fusion | flops 16777216 | bytes 8454144 | tf_op jit(solution)/shard_map/transpose | solution.py:1308
  218.6 13.0 %shard_map.487 = (bf16[27,48,2048]{2,1,0:T(8,128)(2,1)}, bf16[14,48,2176]{2,1,0:T(8,128)(2,1)}, bf16[13,48,2176]{2,1,0:T(8,128)(2,1)}, f32[13,48,2048]{2,1,0:T(8,128)}, f32[8,128]{1,0:T(8,128)}) custom-call(s32[2]{0:T(128)} %pad_add_fusion.place, bf16[8,48,2048]{2,1,0:T(8,128)(2,1)} %pad.48.refs_0_, bf16[8,48,2048]{2,1,0:T(8,128)(2,1)} %pad.49.refs_1_, ...), custom_call_target="tpu_custom_call" | custom-call | flops 15000000512 | bytes 1048576 | tf_op jit(solution)/shard_map/pallas_call | solution.py:601
  232.3 14.7 %shard_map.486 = (bf16[19,160,1024]{2,1,0:T(8,128)(2,1)}, bf16[10,160,1152]{2,1,0:T(8,128)(2,1)}, bf16[9,160,1152]{2,1,0:T(8,128)(2,1)}, f32[9,160,1024]{2,1,0:T(8,128)}, f32[8,128]{1,0:T(8,128)}) custom-call(s32[2]{0:T(128)} %pad_add_fusion.place, bf16[4,160,1024]{2,1,0:T(8,128)(2,1)} %bitcast.224, bf16[4,160,1024]{2,1,0:T(8,128)(2,1)} %collective-permute-done.refs_1_, ...), custom_call_target="tpu_custom_call" | custom-call | flops 15000000512 | bytes 1048576 | tf_op jit(solution)/shard_map/pallas_call | solution.py:601
  257.5 10.0 %shard_map.488.inner = f32[8,128]{1,0:T(8,128)} custom-call(f32[8,128]{1,0:T(8,128)} %get-tuple-element.141.refs_0_, f32[8,128]{1,0:T(8,128)} %get-tuple-element.142.refs_1_), custom_call_target="tpu_custom_call" | custom-call | flops 12000000000 | bytes 1048576 | tf_op jit(solution)/shard_map/pallas_call | solution.py:210
  280.8 15.1 %shard_map.489 = (bf16[9,160,1280]{2,1,0:T(8,128)(2,1)}, f32[7,160,1024]{2,1,0:T(8,128)}, bf16[4,160,1024]{2,1,0:T(8,128)(2,1)}, f32[160,128]{1,0:T(8,128)}) custom-call(s32[2]{0:T(128)} %pad_add_fusion.place, f32[9,160,1024]{2,1,0:T(8,128)} %get-tuple-element.128.first_ref, bf16[9,160,1152]{2,1,0:T(8,128)(2,1)} %get-tuple-element.129.odd, ...), custom_call_target="tpu_custom_call" | custom-call | flops 17999998976 | bytes 1048576 | tf_op jit(solution)/shard_map/pallas_call | solution.py:684
  295.8 17.5 %shard_map.491.refs_8_ = f32[16,384]{1,0:T(8,128)} custom-call(s32[2]{0:T(128)} %pad_add_fusion.place, bf16[8,16,8192]{2,1,0:T(8,128)(2,1)} %get-tuple-element.156.refs_0_, bf16[8,16,8192]{2,1,0:T(8,128)(2,1)} %get-tuple-element.140.refs_1_, bf16[3,16,8192]{2,1,0:T(8,128)(2,1)} %collective-permute-done.8.refs_2_, ...), custom_call_target="tpu_custom_call" | custom-call | flops 16000000000 | bytes 1048576 | tf_op jit(solution)/shard_map/pallas_call | solution.py:457
  326.2 30.6 %shard_map.492.refs_9_ = f32[32,384]{1,0:T(8,128)} custom-call(s32[2]{0:T(128)} %pad_add_fusion.place, bf16[8,32,8192]{2,1,0:T(8,128)(2,1)} %pad.53.refs_0_, bf16[8,32,8192]{2,1,0:T(8,128)(2,1)} %pad.54.refs_1_, bf16[3,32,8192]{2,1,0:T(8,128)(2,1)} %pad.55.refs_2_, bf16[2,32,8192]{2,1,0:T(8,128)(2,1)} %pad.56.refs_3_, bf16[1152,256]{1,0:T(8,128)(2,1)} %bitcast.269, ...), custom_call_target="tpu_custom_call" | custom-call | flops 32000000000 | bytes 1048576 | tf_op jit(solution)/shard_map/pallas_call | solution.py:457
  374.9 16.7 %shard_map.490 = (bf16[13,48,2304]{2,1,0:T(8,128)(2,1)}, f32[11,48,2048]{2,1,0:T(8,128)}, bf16[8,48,2048]{2,1,0:T(8,128)(2,1)}, f32[48,384]{1,0:T(8,128)}) custom-call(s32[2]{0:T(128)} %pad_add_fusion.place, f32[13,48,2048]{2,1,0:T(8,128)} %get-tuple-element.150.first_ref, bf16[13,48,2176]{2,1,0:T(8,128)(2,1)} %get-tuple-element.151.odd, ...), custom_call_target="tpu_custom_call" | custom-call | flops 17999998976 | bytes 1048576 | tf_op jit(solution)/shard_map/pallas_call | solution.py:684
  400.5 13.6 %shard_map.494.refs_6_ = f32[40,128]{1,0:T(8,128)} custom-call(s32[2]{0:T(128)} %pad_add_fusion.place, bf16[4,4,2,40,4096]{4,3,2,1,0:T(8,128)(2,1)} %bitcast.205, bf16[4,40,4096]{2,1,0:T(8,128)(2,1)} %copy-done.23, bf16[3,40,4096]{2,1,0:T(8,128)(2,1)} %collective-permute-done.18.refs_2_, bf16[2,40,4096]{2,1,0:T(8,128)(2,1)} %collective-permute-done.19.refs_3_, ...), custom_call_target="tpu_custom_call" | custom-call | flops 10000000000 | bytes 1048576 | tf_op jit(solution)/shard_map/pallas_call | solution.py:457
  414.1 13.9 %shard_map.493.refs_7_ = f32[40,128]{1,0:T(8,128)} custom-call(s32[2]{0:T(128)} %pad_add_fusion.place, bf16[4,4,2,40,4096]{4,3,2,1,0:T(8,128)(2,1)} %bitcast.206, bf16[4,40,4096]{2,1,0:T(8,128)(2,1)} %copy-done.22, bf16[3,40,4096]{2,1,0:T(8,128)(2,1)} %collective-permute-done.16.refs_2_, bf16[2,40,4096]{2,1,0:T(8,128)(2,1)} %collective-permute-done.17.refs_3_, ...), custom_call_target="tpu_custom_call" | custom-call | flops 10000000000 | bytes 1048576 | tf_op jit(solution)/shard_map/pallas_call | solution.py:457
  432.6 13.6 %shard_map.496.refs_5_ = f32[40,128]{1,0:T(8,128)} custom-call(s32[2]{0:T(128)} %pad_add_fusion.place, bf16[4,4,2,40,4096]{4,3,2,1,0:T(8,128)(2,1)} %bitcast.207, bf16[4,40,4096]{2,1,0:T(8,128)(2,1)} %copy-done.21, bf16[3,40,4096]{2,1,0:T(8,128)(2,1)} %collective-permute-done.22.refs_2_, bf16[2,40,4096]{2,1,0:T(8,128)(2,1)} %copy-done.85, ...), custom_call_target="tpu_custom_call" | custom-call | flops 10000000000 | bytes 1048576 | tf_op jit(solution)/shard_map/pallas_call | solution.py:457
  448.1 13.6 %shard_map.495.refs_4_ = f32[40,128]{1,0:T(8,128)} custom-call(s32[2]{0:T(128)} %pad_add_fusion.place, bf16[4,4,2,40,4096]{4,3,2,1,0:T(8,128)(2,1)} %bitcast.208, bf16[4,40,4096]{2,1,0:T(8,128)(2,1)} %copy-done.24, bf16[3,40,4096]{2,1,0:T(8,128)(2,1)} %collective-permute-done.20.refs_2_, bf16[2,40,4096]{2,1,0:T(8,128)(2,1)} %copy-done.86, ...), custom_call_target="tpu_custom_call" | custom-call | flops 10000000000 | bytes 1048576 | tf_op jit(solution)/shard_map/pallas_call | solution.py:457
  461.7 11.3 %shard_map.497 = (f32[160,128]{1,0:T(8,128)}, f32[48,384]{1,0:T(8,128)}, f32[8,128]{1,0:T(8,128)}) custom-call(f32[160,128]{1,0:T(8,128)} %get-tuple-element.146.refs_0_, f32[48,384]{1,0:T(8,128)} %get-tuple-element.152.refs_1_, f32[160,128]{1,0:T(8,128)} %broadcast_in_dim.160.refs_4_.label_ref.refs_2_, ...), custom_call_target="tpu_custom_call" | custom-call | flops 11000000512 | bytes 1048576 | tf_op jit(solution)/shard_map/pallas_call | solution.py:856
  477.7 14.3 %shard_map.499 = (f32[9,48,2048]{2,1,0:T(8,128)}, bf16[11,48,2304]{2,1,0:T(8,128)(2,1)}, f32[8,128]{1,0:T(8,128)}, f32[576,64]{1,0:T(8,128)}, f32[32,64]{1,0:T(8,128)}) custom-call(s32[2]{0:T(128)} %pad_add_fusion.place, f32[11,48,2048]{2,1,0:T(8,128)} %get-tuple-element.180.sum_ref, bf16[11,48,2048]{2,1,0:T(8,128)(2,1)} %pad.57.cot, ...), custom_call_target="tpu_custom_call" | custom-call | flops 17999998976 | bytes 1048576 | tf_op jit(solution)/shard_map/pallas_call | solution.py:993
  492.0 15.3 %shard_map.498 = (f32[5,160,1024]{2,1,0:T(8,128)}, bf16[7,160,1280]{2,1,0:T(8,128)(2,1)}, f32[8,128]{1,0:T(8,128)}, f32[576,64]{1,0:T(8,128)}, f32[32,64]{1,0:T(8,128)}) custom-call(s32[2]{0:T(128)} %pad_add_fusion.place, f32[7,160,1024]{2,1,0:T(8,128)} %get-tuple-element.169.sum_ref, bf16[7,160,1024]{2,1,0:T(8,128)(2,1)} %bitcast.245, ...), custom_call_target="tpu_custom_call" | custom-call | flops 17999998976 | bytes 1048576 | tf_op jit(solution)/shard_map/pallas_call | solution.py:993
  507.4 11.8 %shard_map.500.pulled = f32[8,128]{1,0:T(8,128)} custom-call(f32[8,128]{1,0:T(8,128)} %get-tuple-element.184.refs_0_, f32[8,128]{1,0:T(8,128)} %get-tuple-element.185.refs_1_), custom_call_target="tpu_custom_call" | custom-call | flops 12000000000 | bytes 1048576 | tf_op jit(solution)/shard_map/pallas_call | solution.py:210
  525.7 15.0 %shard_map.501 = (bf16[8,160,1024]{2,1,0:T(8,128)(2,1)}, f32[288,64]{1,0:T(8,128)}, f32[8,128]{1,0:T(8,128)}) custom-call(s32[2]{0:T(128)} %pad_add_fusion.place, f32[5,160,1024]{2,1,0:T(8,128)} %get-tuple-element.175.flow_ref, f32[9,160,1024]{2,1,0:T(8,128)} %get-tuple-element.128.first_ref, bf16[7,160,1280]{2,1,0:T(8,128)(2,1)} %get-tuple-element.176.grad, ...), custom_call_target="tpu_custom_call" | custom-call | flops 16000000000 | bytes 1048576 | tf_op jit(solution)/shard_map/pallas_call | solution.py:1123
  544.8 15.2 %shard_map.502 = (bf16[16,48,2048]{2,1,0:T(8,128)(2,1)}, f32[288,64]{1,0:T(8,128)}, f32[8,128]{1,0:T(8,128)}) custom-call(s32[2]{0:T(128)} %pad_add_fusion.place, f32[9,48,2048]{2,1,0:T(8,128)} %get-tuple-element.191.flow_ref, f32[13,48,2048]{2,1,0:T(8,128)} %get-tuple-element.150.first_ref, bf16[11,48,2304]{2,1,0:T(8,128)(2,1)} %get-tuple-element.192.grad, ...), custom_call_target="tpu_custom_call" | custom-call | flops 16000000000 | bytes 1048576 | tf_op jit(solution)/shard_map/pallas_call | solution.py:1123
  563.9 11.2 %collective-permute-done.24 = bf16[4,160,1024]{2,1,0:T(8,128)(2,1)} collective-permute-done((bf16[4,160,1024]{2,1,0:T(8,128)(2,1)}, bf16[4,160,1024]{2,1,0:T(8,128)(2,1)}, u32[]{:S(2)}, u32[]{:S(2)}) %collective-permute-start.24) | collective-permute-done | bytes 1310752 | tf_op jit(solution)/shard_map/ppermute | solution.py:1296
  575.1 21.2 %shard_map.503 = f32[512,128]{1,0:T(8,128)} custom-call(f32[288,64]{1,0:T(8,128)} %get-tuple-element.188.refs_0_, f32[288,64]{1,0:T(8,128)} %get-tuple-element.195.refs_1_, f32[576,64]{1,0:T(8,128)} %get-tuple-element.196.refs_2_, f32[576,64]{1,0:T(8,128)} %get-tuple-element.197.refs_3_, f32[32,64]{1,0:T(8,128)} %get-tuple-element.198.refs_4_, ...), custom_call_target="tpu_custom_call" | custom-call | flops 20000000000 | bytes 1048576 | tf_op jit(solution)/shard_map/pallas_call | solution.py:323
  614.8 10.4 %fusion.10 = f32[320,4,1024]{2,1,0:T(4,128)} fusion(bf16[320,4,1024]{2,1,0:T(4,128)(2,1)S(1)} %copy-done.13, f32[4,2,40,4,1024]{4,3,2,1,0:T(4,128)S(1)} %copy.220, f32[320,1024]{1,0:T(8,128)S(1)} %get-tuple-element.399, f32[320,1024]{1,0:T(8,128)S(1)} %get-tuple-element.398, f32[320,1024]{1,0:T(8,128)S(1)} %get-tuple-element.397, ...), kind=kLoop, calls=%fused_computation.17 | loop fusion | flops 19660800 | bytes 18350080 | tf_op jit(solution)/shard_map/add | solution.py:1646
  (420 shorter events, 289.7 us)
Async XLA Ops:
  4.4 106.4 %collective-permute-start.1 = (bf16[8,40,2048]{2,1,0:T(8,128)(2,1)}, bf16[8,40,2048]{2,1,0:T(8,128)(2,1)}, u32[]{:S(2)}, u32[]{:S(2)}) collective-permute-start(bf16[8,40,2048]{2,1,0:T(8,128)(2,1)} %bitcast.201.refs_3_), channel_id=1, source_target_pairs={{0,1},{1,0},{2,3},{3,2},{4,5},{5,4},{6,7},{7,6},{8,9},{9,8},{10,11... | collective-permute-start | bytes 3932168 | tf_op jit(solution)/shard_map/ppermute | solution.py:1296
  9.7 103.7 %collective-permute-start = (bf16[4,160,1024]{2,1,0:T(8,128)(2,1)}, bf16[4,160,1024]{2,1,0:T(8,128)(2,1)}, u32[]{:S(2)}, u32[]{:S(2)}) collective-permute-start(bf16[4,160,1024]{2,1,0:T(8,128)(2,1)} %bitcast.6.refs_1_), channel_id=1, source_target_pairs={{0,1},{1,0},{2,3},{3,2},{4,5},{5,4},{6,7},{7,6},{8,9},{9,8},{10,11... | collective-permute-start | bytes 3932168 | tf_op jit(solution)/shard_map/ppermute | solution.py:1296
  23.4 90.0 %collective-permute-start.2 = (bf16[16,8,8192]{2,0,1:T(8,128)(2,1)}, bf16[16,8,8192]{2,0,1:T(8,128)(2,1)}, u32[]{:S(2)}, u32[]{:S(2)}) collective-permute-start(bf16[16,8,8192]{2,0,1:T(8,128)(2,1)} %copy.227), channel_id=1, source_target_pairs={{0,1},{1,0},{2,3},{3,2},{4,5},{5,4},{6,7},{7,6},{8,9},{9,8},{10,11... | collective-permute-start | bytes 6291464 | tf_op jit(solution)/shard_map/ppermute | solution.py:1296
  33.1 96.5 %all-to-all-start = ((bf16[4,500,1024]{2,1,0:T(8,128)(2,1)}), bf16[4,500,1024]{2,1,0:T(8,128)(2,1)}, u32[]{:S(2)}, u32[]{:S(2)}) async-start(bf16[4,500,1024]{2,1,0:T(8,128)(2,1)} %pad_maximum_fusion), calls=%async_computation | async-start | bytes 8257536 | tf_op jit(solution)/shard_map/all_to_all | solution.py:1351
  156.4 50.1 %collective-permute-start.6 = (bf16[6,40,2048]{2,1,0:T(8,128)(2,1)}, bf16[6,40,2048]{2,1,0:T(8,128)(2,1)}, u32[]{:S(2)}, u32[]{:S(2)}) collective-permute-start(bf16[6,40,2048]{2,1,0:T(8,128)(2,1)} %slice_select_fusion.2), channel_id=1, source_target_pairs={{2,0},{3,1},{4,2},{5,3},{6,4},{7,5},{10,8},{11,9},{12,10},{13,11},... | collective-permute-start | bytes 2949128 | tf_op jit(solution)/shard_map/ppermute | solution.py:1296
  157.7 46.5 %collective-permute-start.5 = (bf16[5,40,2048]{2,1,0:T(8,128)(2,1)}, bf16[5,40,2048]{2,1,0:T(8,128)(2,1)}, u32[]{:S(2)}, u32[]{:S(2)}) collective-permute-start(bf16[5,40,2048]{2,1,0:T(8,128)(2,1)} %slice_select_fusion.3), channel_id=1, source_target_pairs={{0,2},{1,3},{2,4},{3,5},{4,6},{5,7},{8,10},{9,11},{10,12},{11,13},... | collective-permute-start | bytes 2457608 | tf_op jit(solution)/shard_map/ppermute | solution.py:1296
  163.2 83.9 %collective-permute-start.7 = (bf16[24,8,8192]{2,0,1:T(8,128)(2,1)}, bf16[24,8,8192]{2,0,1:T(8,128)(2,1)}, u32[]{:S(2)}, u32[]{:S(2)}) collective-permute-start(bf16[24,8,8192]{2,0,1:T(8,128)(2,1)} %copy.230), channel_id=1, source_target_pairs={{0,1},{1,0},{2,3},{3,2},{4,5},{5,4},{6,7},{7,6},{8,9},{9,8},{10,11... | collective-permute-start | bytes 9437192 | tf_op jit(solution)/shard_map/ppermute | solution.py:1296
  166.7 64.9 %collective-permute-start.4 = (bf16[6,160,1024]{2,1,0:T(8,128)(2,1)}, bf16[6,160,1024]{2,1,0:T(8,128)(2,1)}, u32[]{:S(2)}, u32[]{:S(2)}) collective-permute-start(bf16[6,160,1024]{2,1,0:T(8,128)(2,1)} %pad_maximum_fusion.3), channel_id=1, source_target_pairs={{2,0},{3,1},{4,2},{5,3},{6,4},{7,5},{10,8},{11,9},{12,10},{13,11},... | collective-permute-start | bytes 5898248 | tf_op jit(solution)/shard_map/ppermute | solution.py:1296
  169.4 62.2 %collective-permute-start.3 = (bf16[5,160,1024]{2,1,0:T(8,128)(2,1)}, bf16[5,160,1024]{2,1,0:T(8,128)(2,1)}, u32[]{:S(2)}, u32[]{:S(2)}) collective-permute-start(bf16[5,160,1024]{2,1,0:T(8,128)(2,1)} %pad_maximum_fusion.4), channel_id=1, source_target_pairs={{0,2},{1,3},{2,4},{3,5},{4,6},{5,7},{8,10},{9,11},{10,12},{11,13},... | collective-permute-start | bytes 4915208 | tf_op jit(solution)/shard_map/ppermute | solution.py:1296
  208.8 48.7 %collective-permute-start.9 = (bf16[2,16,8192]{2,1,0:T(8,128)(2,1)S(1)}, bf16[2,16,8192]{2,1,0:T(8,128)(2,1)}, u32[]{:S(2)}, u32[]{:S(2)}) collective-permute-start(bf16[2,16,8192]{2,1,0:T(8,128)(2,1)S(1)} %slice_select_fusion.8), channel_id=1, source_target_pairs={{2,0},{3,1},{4,2},{5,3},{6,4},{7,5},{10,8},{11,9},{12,10},{13,11},... | collective-permute-start | bytes 1572872 | tf_op jit(solution)/shard_map/ppermute | solution.py:1296
  210.1 47.4 %collective-permute-start.8 = (bf16[3,16,8192]{2,1,0:T(8,128)(2,1)S(1)}, bf16[3,16,8192]{2,1,0:T(8,128)(2,1)}, u32[]{:S(2)}, u32[]{:S(2)}) collective-permute-start(bf16[3,16,8192]{2,1,0:T(8,128)(2,1)S(1)} %slice_select_fusion.5), channel_id=1, source_target_pairs={{0,2},{1,3},{2,4},{3,5},{4,6},{5,7},{8,10},{9,11},{10,12},{11,13},... | collective-permute-start | bytes 2359304 | tf_op jit(solution)/shard_map/ppermute | solution.py:1296
  271.2 42.1 %collective-permute-start.15 = (bf16[2,24,8192]{2,1,0:T(8,128)(2,1)S(1)}, bf16[2,24,8192]{2,1,0:T(8,128)(2,1)}, u32[]{:S(2)}, u32[]{:S(2)}) collective-permute-start(bf16[2,24,8192]{2,1,0:T(8,128)(2,1)S(1)} %slice_select_fusion.4), channel_id=1, source_target_pairs={{2,0},{3,1},{4,2},{5,3},{6,4},{7,5},{10,8},{11,9},{12,10},{13,11},... | collective-permute-start | bytes 2359304 | tf_op jit(solution)/shard_map/ppermute | solution.py:1296
  272.5 43.1 %collective-permute-start.14 = (bf16[3,24,8192]{2,1,0:T(8,128)(2,1)}, bf16[3,24,8192]{2,1,0:T(8,128)(2,1)S(1)}, u32[]{:S(2)}, u32[]{:S(2)}) collective-permute-start(bf16[3,24,8192]{2,1,0:T(8,128)(2,1)} %slice_select_fusion), channel_id=1, source_target_pairs={{0,2},{1,3},{2,4},{3,5},{4,6},{5,7},{8,10},{9,11},{10,12},{11,13},... | collective-permute-start | bytes 3538952 | tf_op jit(solution)/shard_map/ppermute | solution.py:1296
  277.2 39.8 %collective-permute-start.13 = (bf16[4,40,4096]{2,1,0:T(8,128)(2,1)S(1)}, bf16[4,40,4096]{2,1,0:T(8,128)(2,1)S(1)}, u32[]{:S(2)}, u32[]{:S(2)}) collective-permute-start(bf16[4,40,4096]{2,1,0:T(8,128)(2,1)S(1)} %copy-done.27), channel_id=1, source_target_pairs={{0,1},{1,0},{2,3},{3,2},{4,5},{5,4},{6,7},{7,6},{8,9},{9,8},{10,11... | collective-permute-start | bytes 3932168 | tf_op jit(solution)/shard_map/ppermute | solution.py:1296
  278.7 87.0 %collective-permute-start.12 = (bf16[4,40,4096]{2,1,0:T(8,128)(2,1)}, bf16[4,40,4096]{2,1,0:T(8,128)(2,1)S(1)}, u32[]{:S(2)}, u32[]{:S(2)}) collective-permute-start(bf16[4,40,4096]{2,1,0:T(8,128)(2,1)} %dynamic-slice_bitcast_fusion.1), channel_id=1, source_target_pairs={{0,1},{1,0},{2,3},{3,2},{4,5},{5,4},{6,7},{7,6},{8,9},{9,8},{10,11... | collective-permute-start | bytes 3932168 | tf_op jit(solution)/shard_map/ppermute | solution.py:1296
  279.3 84.4 %collective-permute-start.10 = (bf16[4,40,4096]{2,1,0:T(8,128)(2,1)}, bf16[4,40,4096]{2,1,0:T(8,128)(2,1)S(1)}, u32[]{:S(2)}, u32[]{:S(2)}) collective-permute-start(bf16[4,40,4096]{2,1,0:T(8,128)(2,1)} %dynamic-slice_bitcast_fusion.3), channel_id=1, source_target_pairs={{0,1},{1,0},{2,3},{3,2},{4,5},{5,4},{6,7},{7,6},{8,9},{9,8},{10,11... | collective-permute-start | bytes 3932168 | tf_op jit(solution)/shard_map/ppermute | solution.py:1296
  319.1 74.3 %collective-permute-start.19 = (bf16[2,40,4096]{2,1,0:T(8,128)(2,1)}, bf16[2,40,4096]{2,1,0:T(8,128)(2,1)}, u32[]{:S(2)}, u32[]{:S(2)}) collective-permute-start(bf16[2,40,4096]{2,1,0:T(8,128)(2,1)} %fusion.35), channel_id=1, source_target_pairs={{2,0},{3,1},{4,2},{5,3},{6,4},{7,5},{10,8},{11,9},{12,10},{13,11},... | collective-permute-start | bytes 1966088 | tf_op jit(solution)/shard_map/ppermute | solution.py:1296
  320.7 78.3 %collective-permute-start.18 = (bf16[3,40,4096]{2,1,0:T(8,128)(2,1)}, bf16[3,40,4096]{2,1,0:T(8,128)(2,1)}, u32[]{:S(2)}, u32[]{:S(2)}) collective-permute-start(bf16[3,40,4096]{2,1,0:T(8,128)(2,1)} %fusion.28), channel_id=1, source_target_pairs={{0,2},{1,3},{2,4},{3,5},{4,6},{5,7},{8,10},{9,11},{10,12},{11,13},... | collective-permute-start | bytes 2949128 | tf_op jit(solution)/shard_map/ppermute | solution.py:1296
  366.8 47.3 %collective-permute-start.17 = (bf16[2,40,4096]{2,1,0:T(8,128)(2,1)}, bf16[2,40,4096]{2,1,0:T(8,128)(2,1)}, u32[]{:S(2)}, u32[]{:S(2)}) collective-permute-start(bf16[2,40,4096]{2,1,0:T(8,128)(2,1)} %slice_select_fusion.6), channel_id=1, source_target_pairs={{2,0},{3,1},{4,2},{5,3},{6,4},{7,5},{10,8},{11,9},{12,10},{13,11},... | collective-permute-start | bytes 1966088 | tf_op jit(solution)/shard_map/ppermute | solution.py:1296
  368.1 46.0 %collective-permute-start.16 = (bf16[3,40,4096]{2,1,0:T(8,128)(2,1)}, bf16[3,40,4096]{2,1,0:T(8,128)(2,1)}, u32[]{:S(2)}, u32[]{:S(2)}) collective-permute-start(bf16[3,40,4096]{2,1,0:T(8,128)(2,1)} %slice_select_fusion.1), channel_id=1, source_target_pairs={{0,2},{1,3},{2,4},{3,5},{4,6},{5,7},{8,10},{9,11},{10,12},{11,13},... | collective-permute-start | bytes 2949128 | tf_op jit(solution)/shard_map/ppermute | solution.py:1296
  373.6 58.2 %collective-permute-start.23 = (bf16[2,40,4096]{2,1,0:T(8,128)(2,1)}, bf16[2,40,4096]{2,1,0:T(8,128)(2,1)S(1)}, u32[]{:S(2)}, u32[]{:S(2)}) collective-permute-start(bf16[2,40,4096]{2,1,0:T(8,128)(2,1)} %fusion.34), channel_id=1, source_target_pairs={{2,0},{3,1},{4,2},{5,3},{6,4},{7,5},{10,8},{11,9},{12,10},{13,11},... | collective-permute-start | bytes 1966088 | tf_op jit(solution)/shard_map/ppermute | solution.py:1296
  393.5 38.3 %collective-permute-start.22 = (bf16[3,40,4096]{2,1,0:T(8,128)(2,1)}, bf16[3,40,4096]{2,1,0:T(8,128)(2,1)}, u32[]{:S(2)}, u32[]{:S(2)}) collective-permute-start(bf16[3,40,4096]{2,1,0:T(8,128)(2,1)} %fusion.29), channel_id=1, source_target_pairs={{0,2},{1,3},{2,4},{3,5},{4,6},{5,7},{8,10},{9,11},{10,12},{11,13},... | collective-permute-start | bytes 2949128 | tf_op jit(solution)/shard_map/ppermute | solution.py:1296
  474.2 33.2 %all-to-all-start.1 = ((bf16[4,4,40,1024]{3,2,1,0:T(8,128)(2,1)}), bf16[4,4,40,1024]{3,2,1,0:T(8,128)(2,1)S(1)}, u32[]{:S(2)}, u32[]{:S(2)}) async-start(bf16[4,4,40,1024]{3,2,1,0:T(8,128)(2,1)} %bitcast.234), calls=%async_computation.1 | async-start | bytes 2621440 | tf_op jit(solution)/shard_map/all_to_all | solution.py:1351
  520.9 54.2 %all-to-all-start.2 = ((bf16[4,8,10,2048]{3,1,2,0:T(8,128)(2,1)}), bf16[4,8,10,2048]{3,1,2,0:T(8,128)(2,1)}, u32[]{:S(2)}, u32[]{:S(2)}) async-start(bf16[4,8,10,2048]{3,1,2,0:T(8,128)(2,1)} %bitcast.233), calls=%async_computation.2 | async-start | bytes 2621440 | tf_op jit(solution)/shard_map/all_to_all | solution.py:1351
  (94 other events, 810.1 us)

commit v3 on v2

--- a/solution.py
+++ b/solution.py
@@ -100,6 +100,14 @@
 
 def inner_counts(tot_ref):
     return [tot_ref[4:5] * 0.25, tot_ref[5:6] * 0.25]
+
+
+def renew(weights, gradient, moment, average, factor):
+    descent = gradient + WEIGHT_DECAY * weights
+    velocity = MOMENTUM * moment + descent
+    updated = weights - factor * (descent + MOMENTUM * velocity)
+    smoothed = AVERAGING * average + (1.0 - AVERAGING) * updated
+    return (gradient, velocity, smoothed, updated)
 
 
 def stats_kernel(x_refs, label_refs, out_ref):
@@ -167,7 +175,7 @@
 
 def total_kernel(axes, count, *refs):
     parts = refs[:count]
-    out_ref, held, boxes_a, boxes_b, send_a, recv_a, send_b, recv_b = refs[count:]
+    out_ref, held, boxes_a, boxes_b, send_a, recv_a, send_b, recv_b = refs[-8:]
     value = parts[0][...]
     for part in parts[1:]:
         value = value + part[...]
@@ -205,12 +213,14 @@
             out_ref[...] = value
 
 
-def total_over_devices(parts, axes, collective_id):
+def total_over_devices(parts, axes, collective_id, waits):
+    waits = jax.tree.leaves(waits)
     shape = parts[0].shape
     return pl.pallas_call(
         functools.partial(total_kernel, axes, len(parts)),
         out_shape=jax.ShapeDtypeStruct(shape, F32),
-        in_specs=[pl.BlockSpec(memory_space=pltpu.VMEM)] * len(parts),
+        in_specs=[pl.BlockSpec(memory_space=pltpu.VMEM)] * len(parts)
+        + [pl.BlockSpec(memory_space=pl.ANY)] * len(waits),
         out_specs=pl.BlockSpec(memory_space=pltpu.VMEM),
         scratch_shapes=[
             pltpu.VMEM((2,) + shape, F32),
@@ -223,13 +233,18 @@
         ],
         compiler_params=pltpu.CompilerParams(collective_id=collective_id, has_side_effects=True),
         cost_estimate=cost(12),
-    )(*parts)
-
-
-def spread_sum_kernel(axes, layout, *refs):
+    )(*parts, *waits)
+
+
+def finish_kernel(axes, layout, rates, waits, *refs):
     count = sum(len(parts) for parts in layout)
-    inputs, out_ref, x_ref, boxes_a, boxes_b, held = refs[:count], *refs[count : count + 5]
-    send_a, recv_a, send_b, recv_b, send_c, recv_c = refs[count + 5 :]
+    inputs, states, entry = refs[:count], refs[count : count + 9], refs[count + 9 : count + 12]
+    tot, norm = refs[count + 12 : count + 14]
+    refs = refs[waits:]
+    outs = refs[count + 14 : count + 35]
+    out_ref, x_ref, boxes_a, boxes_b, held = refs[count + 35 : count + 40]
+    send_a, recv_a, send_b, recv_b, send_c, recv_c = refs[count + 40 :]
+    conv_rate, norm_rate, per_position = rates
     at = 0
     for parts in layout:
         value = inputs[parts[0]][...]
@@ -307,8 +322,39 @@
     for copy in copies:
         copy.wait()
 
-
-def spread_sum(groups, axes, collective_id):
+    at = 0
+    for k in range(3):
+        weights, moment, average = [ref[...] for ref in states[3 * k : 3 * k + 3]]
+        half = weights.shape[0] // 2
+        pairs = out_ref[at : at + half]
+        at += half
+        gradient = jnp.concatenate([pairs[:, 0:64], pairs[:, 64:128]], axis=0)
+        state = renew(weights, gradient, moment, average, conv_rate)
+        for ref, value in zip(outs[5 * k : 5 * k + 4], state):
+            ref[...] = value
+        outs[5 * k + 4][...] = state[3].astype(BF16)
+    pulled = fold(out_ref[at : at + 8], CS_IN)
+    ones, cross = [pulled[0:1], pulled[1:2]], [pulled[2:3], pulled[3:4]]
+    gradient = jnp.concatenate([cross[0] + cross[1], ones[0] + ones[1]], axis=0)[:, 0:CS_IN]
+    state = renew(entry[0][...], gradient, entry[1][...], entry[2][...], norm_rate)
+    for ref, value in zip(outs[15:19], state):
+        ref[...] = value
+    counts = entry_counts(tot)
+    means, scales = group_norms(tot[...], counts, CS_IN)
+    gains, biases, slopes, levels = [], [], [], []
+    for g in range(2):
+        shift = -means[g] * scales[g]
+        gain = norm[0:1] * scales[g]
+        gains.append(gain)
+        biases.append(norm[0:1] * shift + norm[1:2])
+        slopes.append(-gain * (cross[g] / counts[g]) * scales[g])
+        levels.append(-gain * ((ones[g] + cross[g] * shift) / counts[g]))
+    outs[19][...] = jnp.concatenate(gains + biases + slopes + levels, axis=0)
+    losses = out_ref[at + 8 : at + 9]
+    outs[20][...] = jnp.sum(losses, axis=1, keepdims=True) * per_position
+
+
+def finish(groups, states, entry, tot, norm, rates, axes, collective_id, waits):
     (_, size_a), (_, size_b) = axes
     arrays, layout, rows = [], [], []
     for members in groups:
@@ -320,12 +366,20 @@
     sems = []
     for size in (size_a, size_b, size_a):
         sems += [pltpu.SemaphoreType.DMA((size,))] * 2
-    total = pl.pallas_call(
-        functools.partial(spread_sum_kernel, axes, tuple(layout)),
-        out_shape=jax.ShapeDtypeStruct((padded, 128), F32),
-        in_specs=[pl.BlockSpec(memory_space=pltpu.VMEM)] * len(arrays),
-        out_specs=pl.BlockSpec(memory_space=pltpu.VMEM),
+    given = arrays + [a for state in states for a in state] + entry + [tot, norm]
+    outs = []
+    for state in states:
+        outs += [shape_of(state[0].shape, F32)] * 4 + [shape_of(state[0].shape, BF16)]
+    outs += [shape_of(entry[0].shape, F32)] * 4 + [shape_of((8, 128), F32), shape_of((1, 1), F32)]
+    waits = jax.tree.leaves(waits)
+    vmem = pl.BlockSpec(memory_space=pltpu.VMEM)
+    got = pl.pallas_call(
+        functools.partial(finish_kernel, axes, tuple(layout), rates, len(waits)),
+        out_shape=outs,
+        in_specs=[vmem] * len(given) + [pl.BlockSpec(memory_space=pl.ANY)] * len(waits),
+        out_specs=[vmem] * len(outs),
         scratch_shapes=[
+            pltpu.VMEM((padded, 128), F32),
             pltpu.VMEM((padded, 128), F32),
             pltpu.VMEM((size_a, piece, 128), F32),
             pltpu.VMEM((size_b, piece, 128), F32),
@@ -334,16 +388,15 @@
         + sems,
         compiler_params=pltpu.CompilerParams(collective_id=collective_id, has_side_effects=True),
         cost_estimate=cost(20),
-    )(*arrays)
-    ends = np.cumsum(rows)
-    return [total[e - n : e] for e, n in zip(ends, rows)]
+    )(*given, *waits)
+    return got[0:5], got[5:10], got[10:15], got[15:19], got[19], got[20]
 
 
 def teacher_kernel(p_rows, width, group, columns, place, *refs):
     pieces, refs = refs[:group], refs[group:]
-    above, below, first, second, bypass, inner, out_ref, even, odd, mid = refs
+    edge_a, edge_b, first, second, bypass, inner, out_ref, even, odd, mid = refs
     local, lanes = pieces[0].shape[0], pieces[0].shape[-1]
-    real, images = above.shape[1], even.shape[1]
+    real, images = edge_a.shape[1], even.shape[1]
     m_rows = p_rows + 2
     zero = jnp.zeros((images, 128), BF16)
 
@@ -353,10 +406,25 @@
         else:
             odd[(row + 1) // 2 + 1, 0:real, 128 : 128 + lanes] = source[at]
 
-    for k in range(3):
-        put(k - 3, above, k)
-    for k in range(2):
-        put(2 * p_rows + k, below, k)
+    def put_edges(above, below):
+        for k in range(3):
+            put(k - 3, above, k)
+        for k in range(2):
+            put(2 * p_rows + k, below, k)
+
+    rows_of_neighbours(place, edge_a, edge_b, put_edges)
+    nothing = jnp.zeros((1, real, lanes), BF16)
+
+    @pl.when(place[1] == 0)
+    def _():
+        for k in range(3):
+            put(k - 3, nothing, 0)
+
+    @pl.when(place[1] == SLABS - 1)
+    def _():
+        for k in range(2):
+            put(2 * p_rows + k, nothing, 0)
+
     x = place[0]
     for s in range(group):
         distance = lax.rem(x - s + group, group)
@@ -424,17 +492,17 @@
     lax.fori_loop(0, width // columns, second_step, 0)
 
 
-def teacher_energies(place, own, slab, received, above, below, shared, tile):
+def teacher_energies(place, own, slab, received, edge_a, edge_b, shared, tile):
     group = len(received) + 1
     local, lanes = own.shape[0], own.shape[-1]
-    images = above.shape[1]
+    images = edge_a.shape[1]
     p_rows, width = group * local // 2, lanes // (2 * CT_IN)
     out_lanes = -(-(p_rows + 3) * width // 128) * 128
     m_rows = p_rows + 2
     space = -(-tile // 16) * 16
     if own.ndim == 5:
         own_spec = pl.BlockSpec(
-            (local, 1, 1, tile, lanes), lambda i, place: (0, slab, place[0], i, 0)
+            (local, 1, 1, tile, lanes), lambda i, place: (0, slab + i, place[0], 0, 0)
         )
     else:
         own_spec = pl.BlockSpec((local, tile, lanes), lambda i, place: (0, i, 0))
@@ -445,7 +513,7 @@
         grid=(images // tile,),
         in_specs=[own_spec]
         + [by_image(a) for a in received]
-        + [by_image(above), by_image(below)]
+        + [by_image(edge_a), by_image(edge_b)]
         + [whole(a) for a in shared],
         out_specs=pl.BlockSpec((tile, out_lanes), lambda i, place: (i, 0)),
         scratch_shapes=[
@@ -460,7 +528,7 @@
         out_shape=jax.ShapeDtypeStruct((images, out_lanes), F32),
         compiler_params=pltpu.CompilerParams(vmem_limit_bytes=VMEM_LIMIT),
         cost_estimate=cost(40 * images * p_rows * width / 10240),
-    )(place, own, *received, above, below, *shared)
+    )(place, own, *received, edge_a, edge_b, *shared)
 
 
 def entry_tables(tot_ref, norm_ref, w0, w1):
@@ -494,6 +562,18 @@
     return jnp.where(outside, 0.0, 1.0)
 
 
+def rows_of_neighbours(place, first, second, use):
+    even = lax.rem(place[1], 2) == 0
+
+    @pl.when(even)
+    def _():
+        use(second, first)
+
+    @pl.when(jnp.logical_not(even))
+    def _():
+        use(first, second)
+
+
 def add_rows(ref, value):
     first = pl.program_id(0) == 0
 
@@ -510,16 +590,20 @@
     p_rows, group, blocks, place, *refs
 ):
     pieces, refs = refs[:group], refs[group:]
-    above, below, label_ref, tot, norm, weights = refs[:6]
-    raw, even, odd, out_ref, stats = refs[6:]
+    first, second, label_ref, tot, norm, weights = refs[:6]
+    raw_ref, even_ref, odd_ref, out_ref, stats, raw, even, odd = refs[6:]
     images, lanes = raw.shape[1:]
     local = pieces[0].shape[0]
     w0, w1 = indicators(label_ref)
     gain, bias, _, _ = entry_tables(tot, norm, w0, w1)
     gain2, bias2 = twice(gain), twice(bias)
     zero = jnp.zeros((images, 128), BF16)
-    raw[0:5] = above[...]
-    raw[2 * p_rows + 5 : 2 * p_rows + 11] = below[...]
+
+    def put_edges(above, below):
+        raw[0:5] = above[1:6]
+        raw[2 * p_rows + 5 : 2 * p_rows + 11] = below[...]
+
+    rows_of_neighbours(place, first, second, put_edges)
     x = place[0]
     for s in range(group):
         distance = lax.rem(x - s + group, group)
@@ -544,6 +628,9 @@
     f_rows = p_rows + 5
     lax.fori_loop(0, f_rows, pair, 0)
     activate(2 * f_rows, even, f_rows)
+    raw_ref[...] = raw[5 : 2 * p_rows + 5]
+    even_ref[...] = even[2 : p_rows + 3]
+    odd_ref[...] = odd[1 : p_rows + 4]
     s = jnp.zeros((images, 128), F32)
     q = jnp.zeros((images, 128), F32)
     for j in range(0, lanes // 256, blocks):
@@ -577,18 +664,18 @@
     return jax.ShapeDtypeStruct(shape, dtype)
 
 
-def student_forward(place, pieces, above, below, label, tot, norm, weights, tile):
+def student_forward(place, pieces, first, second, label, tot, norm, weights, tile):
     group = len(pieces)
     local, images, lanes = pieces[0].shape
     p_rows = group * local // 2
     outs = [
-        shape_of((2 * p_rows + 11, images, lanes), BF16),
-        shape_of((p_rows + 6, images, 128 + lanes), BF16),
-        shape_of((p_rows + 5, images, 128 + lanes), BF16),
+        shape_of((2 * p_rows, images, lanes), BF16),
+        shape_of((p_rows + 1, images, 128 + lanes), BF16),
+        shape_of((p_rows + 3, images, 128 + lanes), BF16),
         shape_of((p_rows + 5, images, lanes), F32),
     ]
     stats = shape_of((8, 128), F32)
-    big = (*pieces, above, below)
+    big = (*pieces, first, second)
     shared = (tot, norm, weights)
     grid_spec = pltpu.PrefetchScalarGridSpec(
         num_scalar_prefetch=1,
@@ -597,6 +684,11 @@
         + [table_spec(label, tile)]
         + [whole_spec(a) for a in shared],
         out_specs=[image_spec(o, tile) for o in outs] + [whole_spec(stats)],
+        scratch_shapes=[
+            pltpu.VMEM((2 * p_rows + 11, tile, lanes), BF16),
+            pltpu.VMEM((p_rows + 6, tile, 128 + lanes), BF16),
+            pltpu.VMEM((p_rows + 5, tile, 128 + lanes), BF16),
+        ],
     )
     return pl.pallas_call(
         functools.partial(forward_kernel, p_rows, group, 4),
@@ -624,10 +716,12 @@
     norm,
     weights,
     spread,
-    act,
+    act_ref,
+    own_ref,
     sum_ref,
     low_ref,
     energy,
+    act,
 ):
     images, lanes = first_ref.shape[1:]
     w0, w1 = indicators(label_ref)
@@ -646,12 +740,14 @@
         return carry
 
     lax.fori_loop(0, f_rows, activate, 0)
+    act_ref[...] = act[1 : p_rows + 3]
+    own_ref[...] = first_ref[2 : p_rows + 3]
 
     per_chunk = 128 // (lanes // CS_OUT)
     chunks = energy.shape[1] // 128
     measured = [jnp.zeros((images, 128), F32) for _ in range(chunks)]
     for j in range(0, lanes // 256, blocks):
-        parts = [(act, a, 0, 512) for a in range(3)] + [(odd, 1, 128, 256)]
+        parts = [(act, a, 0, 512) for a in range(3)] + [(odd, 0, 128, 256)]
         left = stacked(j, blocks, images, b_rows, parts)
         flat = matmul(left, weights[...])
         y = flat.reshape(blocks, b_rows, images, 256)
@@ -676,7 +772,8 @@
     width = lanes // CS_OUT
     energy_lanes = -(-(p_rows + 3) * width // 128) * 128
     outs = [
-        shape_of((p_rows + 5, images, 256 + lanes), BF16),
+        shape_of((p_rows + 2, images, 256 + lanes), BF16),
+        shape_of((p_rows + 1, images, lanes), F32),
         shape_of((p_rows + 3, images, lanes), F32),
         shape_of((p_rows, images, lanes), BF16),
     ]
@@ -689,6 +786,7 @@
             in_specs=[image_spec(first_out, tile), image_spec(odd, tile), table_spec(label, tile)]
             + [whole_spec(a) for a in (tot, inner, norm, weights, spread)],
             out_specs=[image_spec(o, tile) for o in outs] + [table_spec(energy, tile)],
+            scratch_shapes=[pltpu.VMEM((p_rows + 5, tile, 256 + lanes), BF16)],
         ),
         out_shape=outs + [energy],
         compiler_params=pltpu.CompilerParams(vmem_limit_bytes=VMEM_LIMIT),
@@ -889,11 +987,12 @@
     norm,
     weights,
     flow_ref,
-    grad,
+    grad_ref,
     stats,
     second_ref,
     shortcut_ref,
     kernel_ref,
+    grad,
 ):
     images, lanes = sum_ref.shape[1:]
     w0, w1 = indicators(label_ref)
@@ -926,6 +1025,8 @@
                 v = cot[b, :, at : at + 256].astype(F32) + wide[t, b] * sum_ref[b, :, at : at + 256]
                 grad[b, :, 128 + at : 384 + at] = (v * keep).astype(BF16)
 
+    grad_ref[...] = grad[1 : p_rows + 1, :, 128 : 128 + lanes]
+
     @pl.when(pl.program_id(0) == 0)
     def _():
         kernel_ref[...] = jnp.zeros(kernel_ref.shape, F32)
@@ -938,7 +1039,7 @@
         for t in range(blocks):
             here = slice((j + t) * 256, (j + t + 1) * 256)
             for k in range(k_rows):
-                x = first_ref[k + 2, :, here]
+                x = first_ref[k, :, here]
                 z = x * gain2 + bias2
                 s = sigmoid(z)
                 flow = y[t, k] * (s * (1.0 + z * (1.0 - s)))
@@ -952,7 +1053,7 @@
             blocks,
             images,
             p_rows,
-            [(act, a, 0, 512) for a in range(1, 4)] + [(odd, 2, 128, 256)],
+            [(act, a, 0, 512) for a in range(3)] + [(odd, 1, 128, 256)],
         )
         own = stacked(j, blocks, images, p_rows, [(grad, 1, 128, 256)])
         kernel_ref[...] += lax.dot_general(
@@ -985,7 +1086,7 @@
     p_rows = rows - 3
     outs = [
         shape_of((p_rows + 1, images, lanes), F32),
-        shape_of((p_rows + 3, images, 256 + lanes), BF16),
+        shape_of((p_rows, images, lanes), BF16),
     ]
     stats = shape_of((8, 128), F32)
     second = shape_of((9 * CS_OUT, CS_OUT), F32)
@@ -1001,7 +1102,10 @@
             + [whole_spec(a) for a in (tot, inner, norm, weights)],
             out_specs=[image_spec(o, tile) for o in outs]
             + [whole_spec(a) for a in (stats, second, shortcut)],
-            scratch_shapes=[pltpu.VMEM((256, 1792), F32)],
+            scratch_shapes=[
+                pltpu.VMEM((256, 1792), F32),
+                pltpu.VMEM((p_rows + 3, tile, 256 + lanes), BF16),
+            ],
         ),
         out_shape=outs + [stats, second, shortcut],
         compiler_params=pltpu.CompilerParams(vmem_limit_bytes=VMEM_LIMIT),
@@ -1027,12 +1131,9 @@
     norm,
     weights_even,
     weights_odd,
-    out_ref,
-    taps_ref,
-    stats,
-    first_grad,
-    kernel_ref,
+    *refs,
 ):
+    outs, (taps_ref, stats, first_grad, kernel_ref, rows_ref) = refs[:-5], refs[-5:]
     images, lanes = first_ref.shape[1:]
     w0, w1 = indicators(label_ref)
     gain, _, scale, shift = inner_tables(tot, inner, norm, w0, w1)
@@ -1048,7 +1149,7 @@
         keep = keep_row(place, k, p_rows)
         first_grad[k, :, lanes : lanes + 128] = zero
         for c in range(0, lanes, 256):
-            normed = first_ref[k + 2, :, c : c + 256] * scale2 + shift2
+            normed = first_ref[k, :, c : c + 256] * scale2 + shift2
             v = gain2 * (flow_ref[k, :, c : c + 256] - ones2 - normed * cross2)
             first_grad[k, :, c : c + 256] = (v * keep).astype(BF16)
         return carry
@@ -1067,7 +1168,7 @@
     for j in range(0, lanes // 256, blocks):
         upper = (first_grad, 0, 0, 384)
         lower = (first_grad, 1, 0, 384)
-        left = stacked(j, blocks, images, p_rows, [upper, (grad, 1, 128, 256)])
+        left = stacked(j, blocks, images, p_rows, [upper, (grad, 0, 0, 256)])
         rows_even = matmul(left, weights_even[...])
         rows_odd = matmul(stacked(j, blocks, images, p_rows, [upper, lower]), weights_odd[...])
         for parity, rows in enumerate((rows_even, rows_odd)):
@@ -1075,8 +1176,8 @@
             for t in range(blocks):
                 here = slice((j + t) * 256, (j + t + 1) * 256)
                 for p in range(p_rows):
-                    out_ref[2 * p + parity, :, here] = low[t, p]
-                    x = raw[2 * p + parity + 5, :, here].astype(F32)
+                    rows_ref[2 * p + parity, :, here] = low[t, p]
+                    x = raw[2 * p + parity, :, here].astype(F32)
                     z = x * gain2 + bias2
                     s = sigmoid(z)
                     flow = low[t, p].astype(F32) * (s * (1.0 + z * (1.0 - s)))
@@ -1088,12 +1189,21 @@
             blocks,
             images,
             p_rows,
-            [(even, 2, 0, 384), (odd, 2, 0, 384), (even, 3, 0, 384)],
+            [(even, 0, 0, 384), (odd, 1, 0, 384), (even, 1, 0, 384)],
         )
         own = stacked(j, blocks, images, p_rows, [(first_grad, 0, 0, 256)])
         kernel_ref[...] += lax.dot_general(
             own, right, (((0,), (0,)), ((), ())), preferred_element_type=F32
         )
+    group, local = len(outs), outs[0].shape[0]
+    for s in range(group):
+        distance = lax.rem(s - place[0] + group, group)
+        for d in range(group):
+
+            @pl.when(distance == d)
+            def _():
+                outs[d][...] = rows_ref[s * local : (s + 1) * local]
+
     add_rows(stats, grouped_rows(w0, w1, [ones, cross]))
 
     @pl.when(pl.program_id(0) == pl.num_programs(0) - 1)
@@ -1111,11 +1221,11 @@
 
 def student_entry(
     place, flow, first_out, grad, even, odd, raw, label, tot, inner, pulled, norm_in, norm,
-    weights_even, weights_odd, tile,
+    weights_even, weights_odd, tile, group,
 ):
     rows, images, lanes = flow.shape
     p_rows = rows - 1
-    out = shape_of((2 * p_rows, images, lanes), BF16)
+    outs = [shape_of((2 * p_rows // group, images, lanes), BF16)] * group
     taps = shape_of((9 * CS_IN, CS_OUT), F32)
     stats = shape_of((8, 128), F32)
     big = (flow, first_out, grad, even, odd, raw)
@@ -1128,13 +1238,14 @@
             in_specs=[image_spec(a, tile) for a in big]
             + [table_spec(label, tile)]
             + [whole_spec(a) for a in shared],
-            out_specs=[image_spec(out, tile), whole_spec(taps), whole_spec(stats)],
+            out_specs=[image_spec(o, tile) for o in outs] + [whole_spec(taps), whole_spec(stats)],
             scratch_shapes=[
                 pltpu.VMEM((p_rows + 1, tile, 128 + lanes), BF16),
                 pltpu.VMEM((256, 1152), F32),
+                pltpu.VMEM((2 * p_rows, tile, lanes), BF16),
             ],
         ),
-        out_shape=[out, taps, stats],
+        out_shape=outs + [taps, stats],
         compiler_params=pltpu.CompilerParams(vmem_limit_bytes=VMEM_LIMIT),
         cost_estimate=cost(16),
     )(place, *big, label, *shared)
@@ -1223,14 +1334,6 @@
         compiler_params=pltpu.CompilerParams(vmem_limit_bytes=VMEM_LIMIT),
         cost_estimate=cost(8),
     )(*args)
-
-
-def renew(weights, gradient, moment, average, factor):
-    descent = gradient + WEIGHT_DECAY * weights
-    velocity = MOMENTUM * moment + descent
-    updated = weights - factor * (descent + MOMENTUM * velocity)
-    smoothed = AVERAGING * average + (1.0 - AVERAGING) * updated
-    return (gradient, velocity, smoothed, updated)
 
 
 def body(
@@ -1295,9 +1398,6 @@
     def send(array, pairs):
         return lax.ppermute(array, "space", pairs)
 
-    down = [(k, k + group) for k in range(space - group)]
-    up = [(k, k - group) for k in range(group, space)]
-
     def pick_images(array, res, sub):
         n, rows, lanes = array.shape
         parts = array.reshape(slabs, group, per_device[res], rows, lanes)
@@ -1316,15 +1416,26 @@
             out.append(lax.select_n((x - s) % group, *cut) if group > 1 else cut[0])
         return jnp.concatenate(out, axis=0) if len(out) > 1 else out[0]
 
-    def edge_rows(pieces, above, below):
+    def partner(b, k, first):
+        slab = k // group
+        other = slab ^ 1 if first else ((slab + 1) ^ 1) - 1
+        if 0 <= other < slabs:
+            return b * space + other * group + k % group
+        return (b ^ 1) * space + k
+
+    pair_lists = [
+        [(b * space + k, partner(b, k, first)) for b in range(batch) for k in range(space)]
+        for first in (True, False)
+    ]
+
+    def edge_rows(pieces, count):
         rows = group * pieces[0].shape[0]
-        return slab_rows(pieces, rows - above, rows), slab_rows(pieces, 0, below)
+        last, first = slab_rows(pieces, rows - count, rows), slab_rows(pieces, 0, count)
+        even = z % 2 == 0
+        return lax.select(even, last, first), lax.select(even, first, last)
 
     def to_neighbours(rows):
-        return send(rows[0], down), send(rows[1], up)
-
-    def halos(pieces, above, below):
-        return to_neighbours(edge_rows(pieces, above, below))
+        return [lax.ppermute(r, ("batch", "space"), pairs) for r, pairs in zip(rows, pair_lists)]
 
     def pad_to(array, size):
         extra = size - array.shape[1]
@@ -1369,7 +1480,9 @@
             )
         cot_stacks.append(c)
     flat = [c.reshape(slabs, -1, narrow) for c in cot_stacks]
-    cot_flat = among_slabs(jnp.concatenate(flat, axis=1), 0)
+    cot_flat = jnp.concatenate(flat, axis=1)
+    cots_ready = cot_flat
+    cot_flat = among_slabs(cot_flat, 0)
 
     gains = jnp.tile(teacher_gains, (1, max(t.shape[2] for t in teachers) // CT_IN))
 
@@ -1378,7 +1491,7 @@
         z_t = gains[0, :lanes] * array.astype(F32) + gains[1, :lanes]
         return pad_to(rows_first(jax.nn.silu(z_t).astype(BF16)), size)
 
-    large_raw_in = after(large_teacher, [p[1:] for p in picked])
+    large_raw_in = after(large_teacher, [p[1:] for p in picked], cots_ready)
     own_large = pick_images(large_raw_in, 1, x)
     away_large = [pick_images(large_raw_in, 1, sub) for sub in subs[1:]]
     cut = min(16, images[1])
@@ -1395,54 +1508,64 @@
 
     stat_tables = [label_table(res, sub, images[res]) for res in both for sub in subs]
     entry_sums = input_stats(picked[0] + picked[1], stat_tables)
-    entry_sums = after(entry_sums, [p[1:] for p in arrived], cot_flat, large_raw)
-    entry_total = total_over_devices([entry_sums], axes, 0)
-
-    raw_halos = [halos([after(p, entry_total) for p in arrived[res]], 5, 6) for res in both]
+    large_own = [activated(own_large[lo:hi], size) for (lo, hi), size in zip(ranges, sizes)]
+    raw_edges = [edge_rows(arrived[res], 6) for res in both]
+    corners = lambda parts: [p[:1, :, :128] for p in parts]
+    waits = ([p[1:] for p in arrived], cot_flat, corners(large_raw[0]), large_own, raw_edges)
+    entry_total = total_over_devices([entry_sums], axes, 0, waits)
+
+    raw_halos = [to_neighbours(after(raw_edges[res], entry_total)) for res in both]
     large_raw.append(large_part(1, entry_total))
-    large_own = [
-        activated(after(own_large[lo:hi], large_raw_in), size)
-        for (lo, hi), size in zip(ranges, sizes)
-    ]
     large_pieces = [
-        [own] + [activated(after(p, entry_total), size) for p in raw]
-        for own, size, raw in zip(large_own, sizes, large_raw)
+        [own] + [activated(after(p, *others), size) for p in raw]
+        for own, size, raw, others in zip(
+            large_own, sizes, large_raw, ([entry_total], [])
+        )
     ]
 
     def large_edges_of(k, *others):
         lo, hi = ranges[k]
         rows = [after(p[:, : hi - lo], *others) for p in large_pieces[k]]
-        return [pad_to(h, sizes[k]) for h in halos(rows, 3, 2)]
-
-    large_edges = [large_edges_of(0, raw_halos[1])]
+        return to_neighbours(edge_rows(rows, 3))
+
     lanes = small_teacher.shape[2]
     z_t = after(small_teacher, large_raw_in).astype(F32) * gains[0, :lanes] + gains[1, :lanes]
     small_active = rows_first(jax.nn.silu(z_t).astype(BF16))
     small_active = small_active.reshape(local_rows[0], slabs, group, per_device[0], lanes)
 
-    small_away = [
-        [lax.dynamic_index_in_dim(small_active[:, k], sub, 1, False) for sub in subs[1:]]
-        for k in range(slabs)
-    ]
-    cot_here = after(cot_flat, entry_total)
-    cot_slabs = []
-    at = 0
-    for res, sent in zip(both, cot_stacks):
-        size = sent.shape[1] * sent.shape[2]
-        c = cot_here[:, at : at + size].reshape(sent.shape)
-        at += size
-        n = per_device[res]
-        c = jnp.concatenate([c[:, :, k : k + n] for k in range(0, c.shape[2], n)], axis=3)
-        c = jnp.moveaxis(c, 0, 1).reshape(c.shape[1], images[res], c.shape[3])
-        cot_slabs.append(pad_images(c, res))
-
+    parts_of = [list(range(slabs // 2)), *([k] for k in range(slabs // 2, slabs))]
+
+    def small_part(ks, sub):
+        part = lax.dynamic_slice(
+            small_active,
+            (0, ks[0], sub, 0, 0),
+            (local_rows[0], len(ks), 1, per_device[0], lanes),
+        )
+        return part.reshape(local_rows[0], len(ks) * per_device[0], lanes)
+
+    small_away = [[small_part(ks, sub) for sub in subs[1:]] for ks in parts_of]
     bands = banded_kernels(*after((first_conv, second_conv, shortcut), large_raw_in))
     bands_first, bands_second, bands_second_back, bands_even, bands_odd, gather, scatter = bands
-    raws, evens, odds, firsts, first_sums = [], [], [], [], []
-    for res in both:
+    raws, evens, odds, firsts, first_sums = ([None, None] for _ in range(5))
+    for res in (1, 0):
+        pieces = [pad_images(p, res) for p in arrived[res]]
+        if res == 0:
+            large_edges = [large_edges_of(0, sums)]
+            cot_here = after(cot_flat, sums)
+            cot_slabs = []
+            at = 0
+            for at_res, sent in zip(both, cot_stacks):
+                size = sent.shape[1] * sent.shape[2]
+                c = cot_here[:, at : at + size].reshape(sent.shape)
+                at += size
+                n = per_device[at_res]
+                c = jnp.concatenate([c[:, :, k : k + n] for k in range(0, c.shape[2], n)], axis=3)
+                c = jnp.moveaxis(c, 0, 1).reshape(c.shape[1], images[at_res], c.shape[3])
+                cot_slabs.append(pad_images(c, at_res))
+            pieces = after(pieces, cot_slabs)
         raw, even, odd, first, sums = student_forward(
             place,
-            [pad_images(p, res) for p in arrived[res]],
+            pieces,
             *[pad_images(p, res) for p in raw_halos[res]],
             tables[res],
             entry_total,
@@ -1450,36 +1573,28 @@
             bands_first,
             tiles[res],
         )
-        raws.append(raw)
-        evens.append(even)
-        odds.append(odd)
-        firsts.append(first)
-        first_sums.append(sums)
-    first_sums = after(first_sums, large_pieces, large_edges)
-    inner_total = total_over_devices(first_sums, axes, 1)
+        raws[res] = raw
+        evens[res] = even
+        odds[res] = odd
+        firsts[res] = first
+        first_sums[res] = sums
+    inner_total = total_over_devices(first_sums, axes, 1, (corners(large_raw[1]), large_edges))
 
     large_edges.append(large_edges_of(1, inner_total))
-    order = list(range(slabs))[::-1]
-    small_pieces = {}
-    for k in order:
-        waits = [inner_total]
-        if k == order[-1]:
-            waits.append(small_pieces[order[0]])
-        small_pieces[k] = [
-            send(after(p, *waits), to_sub(d + 1)) for d, p in enumerate(small_away[k])
-        ]
-
-    def small_rows(k, *others):
-        own = lax.dynamic_index_in_dim(small_active[:, k], x, 1, False)
-        return edge_rows([own] + after(small_pieces[k], *others), 3, 2)
-
-    small_edge_rows = {order[0]: small_rows(order[0])}
-
-    acts, sums_out, lows, energies = [], [], [], []
+    small_pieces = [
+        [send(after(p, inner_total), to_sub(d + 1)) for d, p in enumerate(away)]
+        for away in small_away[::-1]
+    ][::-1]
+
+    def small_rows(n, *others):
+        own = small_part(parts_of[n], x)
+        return edge_rows([own] + after(small_pieces[n], *others), 3)
+
+    acts, own_firsts, sums_out, lows, energies = [], [], [], [], []
     for res in both:
-        act, block_sum, low, energy = student_block(
+        act, own_first, block_sum, low, energy = student_block(
             place,
-            after(firsts[res], small_edge_rows[order[0]]) if res else firsts[res],
+            firsts[res],
             odds[res],
             tables[res],
             entry_total,
@@ -1490,6 +1605,7 @@
             tiles[res],
         )
         acts.append(act)
+        own_firsts.append(own_first)
         sums_out.append(block_sum)
         lows.append(low)
         energies.append(energy)
@@ -1503,26 +1619,29 @@
     def large_map(k, *others):
         pieces = large_pieces[k]
         own = after(pieces[0], *others)
-        return teacher_energies(place, own, 0, pieces[1:], *large_edges[k], shared, tiles[1])
-
-    def small_map(k, *others):
-        edges = to_neighbours(small_edge_rows[k])
-        pieces = after(small_pieces[k], *others)
-        return teacher_energies(
-            place, small_active, k, pieces, *edges, shared, per_device[0]
-        )
+        edges = [pad_to(h, sizes[k]) for h in large_edges[k]]
+        return teacher_energies(place, own, 0, pieces[1:], *edges, shared, tiles[1])
+
+    def small_map(n, edges, *others):
+        arrays = after((*small_pieces[n], *edges), *others)
+        return [
+            teacher_energies(
+                place, small_active, parts_of[n][0], arrays[:-2], *arrays[-2:], shared, per_device[0]
+            )
+        ]
 
     large_maps = [large_map(0, inner_total)]
-    small_maps = {}
-    small_edge_rows[order[1]] = small_rows(order[1], large_maps[0])
-    large_maps.append(large_map(1, small_edge_rows[order[1]]))
-    small_edge_rows[order[2]] = small_rows(order[2], large_maps[1])
-    for k in order[:2]:
-        small_maps[k] = small_map(k, small_edge_rows[order[2]])
-    small_edge_rows[order[3]] = small_rows(order[3], small_maps[order[0]], small_maps[order[1]])
-    for k in order[2:]:
-        small_maps[k] = small_map(k, small_edge_rows[order[3]])
-    small_maps = [small_maps[k] for k in range(slabs)]
+    rows = small_rows(0, large_maps[0], energies)
+    edges = [to_neighbours(rows)]
+    large_maps.append(large_map(1, rows))
+    rows = small_rows(1, large_maps[1])
+    edges.append(to_neighbours(rows))
+    small_maps = small_map(0, edges[0], rows)
+    for n in range(2, len(parts_of)):
+        rows = small_rows(n, small_maps)
+        edges.append(to_neighbours(rows))
+        small_maps = small_maps + small_map(n - 1, edges[n - 1], rows)
+    small_maps = small_maps + small_map(len(parts_of) - 1, edges[-1])
     factors = attention_maps(
         energies, [small_maps, large_maps], tables, widths, p_counts, slabs, group, 2
     )
@@ -1543,7 +1662,7 @@
             cot_slabs[res],
             factors[res],
             scatter,
-            firsts[res],
+            own_firsts[res],
             acts[res],
             odds[res],
             tables[res],
@@ -1558,16 +1677,16 @@
         flow_sums.append(sums)
         second_parts.append(second_part)
         shortcut_parts.append(shortcut_part)
-    flow_total = total_over_devices(after(flow_sums, out_parts[0]), axes, 3)
-    out_parts.append(to_owners(1, flow_total))
+    flow_total = total_over_devices(flow_sums, axes, 3, out_parts)
 
     entry_parts, first_parts, entry_flow_sums = [], [], []
-    packed = None
+    held = None
     for res in both:
-        rows, first_part, sums = student_entry(
+        flow = flows[res] if held is None else after(flows[res], held)
+        *rows, first_part, sums = student_entry(
             place,
-            after(flows[res], entry_parts[0][0]) if res == 1 else flows[res],
-            firsts[res],
+            flow,
+            own_firsts[res],
             grads[res],
             evens[res],
             odds[res],
@@ -1581,95 +1700,80 @@
             bands_even,
             bands_odd,
             tiles[res],
-        )
+            group,
+        )
+        if res == 0:
+            held = rows[0]
         first_parts.append(first_part)
         entry_flow_sums.append(sums)
-        if res == 1:
-            held = after(entry_flow_sums, entry_parts[0][1:], out_parts[1])
-            packed = spread_sum(
-                [first_parts, second_parts, shortcut_parts, held, [loss_sums]], axes, 4
-            )
-        rows = rows[:, : images[res]]
-        parts = []
-        for d in range(group):
-            part = lax.dynamic_slice_in_dim(rows, subs[d] * local_rows[res], local_rows[res], 0)
-            if d:
-                part = send(after(part, packed) if res == 1 else part, to_sub(d))
-            parts.append(part)
-        entry_parts.append(parts)
-
-    def unpack(pairs, shape):
-        return jnp.concatenate([pairs[:, :64], pairs[:, 64:]], axis=0).reshape(shape)
-
-    first_grads = unpack(packed[0], first_conv.shape)
-    second_grads = unpack(packed[1], second_conv.shape)
-    shortcut_grads = unpack(packed[2], shortcut.shape)
-    entry_pulled = packed[3].reshape(8, 128 // CS_IN, CS_IN).sum(axis=1)
-    total_loss = jnp.sum(packed[4])
-
-    counts = entry_total[4:6, 0:1]
-    entry_folded = entry_total.reshape(8, 128 // CS_IN, CS_IN).sum(axis=1)
-    mean_entry = entry_folded[0:2] / counts
-    scale_entry = lax.rsqrt(entry_folded[2:4] / counts - mean_entry * mean_entry + EPSILON)
-    shift_entry = -mean_entry * scale_entry
-    ones_entry, cross_entry = entry_pulled[0:2], entry_pulled[2:4]
+        rows = [r[:, : images[res]] for r in rows]
+        if res == 0:
+            rows[1:] = [send(r, to_sub(d + 1)) for d, r in enumerate(rows[1:])]
+        entry_parts.append(rows)
+    def native_rows(res):
+        ordered = [lax.select_n((x - s) % group, *entry_parts[res]) for s in range(group)]
+        n, rows, lanes = pixels[res].shape
+        rows_in = jnp.stack(ordered).reshape(group, rows, slabs, per_device[res], lanes)
+        return jnp.transpose(rows_in, (2, 0, 3, 1, 4)).reshape(n, rows, lanes)
+
+    arrived_rows = [native_rows(0)]
+    rate_scale = 1.0 / math.sqrt(total_positions)
+    flat = lambda k: k.reshape(-1, k.shape[-1])
+    kernel_states = [
+        [flat(k) for k in (first_conv, momentum_first, average_first)],
+        [flat(k) for k in (second_conv, momentum_second, average_second)],
+        [shortcut, momentum_shortcut, average_shortcut],
+    ]
+    first_state, second_state, bypass_state, entry_state, image_tables, total_loss = finish(
+        [first_parts, second_parts, shortcut_parts, entry_flow_sums, [loss_sums]],
+        kernel_states,
+        [entry_norm, momentum_entry, average_entry],
+        entry_total,
+        norm_in,
+        (CONV_RATE * rate_scale, NORM_RATE * rate_scale, 1.0 / total_positions),
+        axes,
+        4,
+        (entry_parts[0][1:], entry_parts[1]),
+    )
+    rows = entry_parts[1]
+    rows[1:] = [send(after(r, image_tables), to_sub(d + 1)) for d, r in enumerate(rows[1:])]
+    arrived_rows.append(native_rows(1))
+    out_parts.append(to_owners(1, image_tables))
+    first_state = [k.reshape(first_conv.shape) for k in first_state]
+    second_state = [k.reshape(second_conv.shape) for k in second_state]
     inner_folded = flow_total.reshape(8, 128 // CS_OUT, CS_OUT).sum(axis=1)
     ones_inner, cross_inner = inner_folded[0:2], inner_folded[2:4]
-
-    gain_entry = entry_norm[0] * scale_entry
-    bias_entry = entry_norm[0] * shift_entry + entry_norm[1]
-    slope_entry = -gain_entry * (cross_entry / counts) * scale_entry
-    level_entry = -gain_entry * ((ones_entry + cross_entry * shift_entry) / counts)
     block_outs = []
     for res in both:
-        low = after(out_parts[res], packed)
-        low = jnp.transpose(low, (2, 0, 1, 3))
+        low = jnp.transpose(out_parts[res], (2, 0, 1, 3))
         block_outs.append(low.reshape(low.shape[0], -1, low.shape[3]))
-    entry_parts[0] = after(entry_parts[0], packed)
+
     input_grads = []
     for res in both:
-        n, rows, lanes = pixels[res].shape
-        ordered = [lax.select_n((x - s) % group, *entry_parts[res]) for s in range(group)]
-        rows_in = jnp.stack(ordered).reshape(group, rows, slabs, per_device[res], lanes)
-        rows_in = jnp.transpose(rows_in, (2, 0, 3, 1, 4)).reshape(n, rows, lanes)
+        lanes = pixels[res].shape[2]
         one = (labels[res] == 1)[:, None, None]
-
-        def by_image(pair):
-            wide = jnp.tile(pair, (1, lanes // CS_IN))
-            return jnp.where(one, wide[1], wide[0])
-
+        wide = jnp.tile(image_tables, (1, lanes // 128))
+        gain, bias, slope, level = [
+            jnp.where(one, wide[2 * k + 1], wide[2 * k]) for k in range(4)
+        ]
         value = pixels[res].astype(F32)
-        gain = by_image(gain_entry)
-        before = value * gain + by_image(bias_entry)
+        before = value * gain + bias
         s = jax.nn.sigmoid(before)
-        flow = rows_in.astype(F32) * (s * (1.0 + before * (1.0 - s)))
-        input_grads.append(gain * flow + (value * by_image(slope_entry) + by_image(level_entry)))
-
-    entry_grads = jnp.stack([jnp.sum(cross_entry, axis=0), jnp.sum(ones_entry, axis=0)])
+        flow = arrived_rows[res].astype(F32) * (s * (1.0 + before * (1.0 - s)))
+        input_grads.append(gain * flow + (value * slope + level))
+
     inner_grads = jnp.stack([jnp.sum(cross_inner, axis=0), jnp.sum(ones_inner, axis=0)])
-    rate_scale = 1.0 / math.sqrt(total_positions)
-    entry_state = renew(entry_norm, entry_grads, momentum_entry, average_entry, NORM_RATE * rate_scale)
-    first_state = renew(first_conv, first_grads, momentum_first, average_first, CONV_RATE * rate_scale)
     inner_state = renew(inner_norm, inner_grads, momentum_inner, average_inner, NORM_RATE * rate_scale)
-    second_state = renew(
-        second_conv, second_grads, momentum_second, average_second, CONV_RATE * rate_scale
-    )
-    bypass_state = renew(
-        shortcut, shortcut_grads, momentum_shortcut, average_shortcut, CONV_RATE * rate_scale
-    )
     return (
         *block_outs,
         input_grads[0],
         input_grads[1],
-        total_loss / total_positions,
+        total_loss.reshape(()),
         *entry_state,
         *first_state,
-        first_state[3].astype(BF16),
         *inner_state,
         *second_state,
-        second_state[3].astype(BF16),
         *bypass_state,
-        bypass_state[3].astype(BF16),
     )
 
 

time: 655 us -> 610 us (0.931)
  starting transfers between devices: 77.2 us -> 38.3 us
  other arithmetic: 95 us -> 72.4 us
  waiting for transfers between devices: 36.1 us -> 52.7 us
    ppermute x26 -> x9, starting transfers between devices: 63.6 us -> 11.7 us  [send(): return lax.ppermute(array, 'space', pairs)]
    ppermute x0 -> x14, waiting for transfers between devices: none -> 30.1 us  [to_neighbours(): lax.ppermute(r, ('batch', 'space'), pairs)]
    select_n x17 -> x2, other arithmetic: 22.7 us -> 2.95 us  [slab_rows(): out.append(lax.select_n((x - s) % group, *cut) if group > 1 else cut[0])]
    select_n x4 -> x11, other arithmetic: 4.43 us -> 19.1 us  [the longest x7 15.1 us: edge_rows(): return (lax.select(even, last, first), lax.select(even, first, last))]
    unnamed x185 -> x151, local copies, waits for them, and re-layouts: 14.6 us -> 28.2 us
    ppermute x0 -> x14, starting transfers between devices: none -> 12.2 us  [to_neighbours(): lax.ppermute(r, ('batch', 'space'), pairs)]
    all_to_all x3, waiting for transfers between devices: 16.2 us -> 8.59 us  [among_slabs(): lax.all_to_all(array, 'space', 0, 0, axis_index_groups=by_slab, tiled=True)]
    squeeze x4 -> x0, local copies, waits for them, and re-layouts: 6.93 us -> none  [body(): lax.dynamic_index_in_dim(small_active[:, k], sub, 1, False)]
  transfers between devices with their start and end apart: 29 -> 26, of which waited for: 4 -> 8; matrix products, arithmetic and copies ran while one was open for 29% -> 30% of each run, Pallas kernels for 34% -> 33%
where the time goes in v3:
time: 610 us; the launch traced here: 601 us
  Pallas kernels  291 us (48%)
  local copies, waits for them, and re-layouts  143 us (23%)
  other arithmetic  72.4 us (12%)
  waiting for transfers between devices  52.7 us (9%)
  starting transfers between devices  38.3 us (6%)
    pallas_call x5, Pallas kernels, teacher_energies(): pl.pallas_call(functools.partial(teacher_kernel, p_rows, width, group, 4)...  99.7 us
    pallas_call x3, Pallas kernels, total_over_devices(): pl.pallas_call(functools.partial(total_kernel, axes, len(parts)), out_sha...  34.1 us
    pallas_call x2, Pallas kernels, student_block(): pl.pallas_call(functools.partial(block_kernel, p_rows, 4), grid_spec=pltp...  33 us
    ppermute x14, waiting for transfers between devices, to_neighbours(): lax.ppermute(r, ('batch', 'space'), pairs)  30.1 us
    unnamed x151, local copies, waits for them, and re-layouts  28.2 us
    pallas_call x2, Pallas kernels, student_forward(): pl.pallas_call(functools.partial(forward_kernel, p_rows, group, 4), grid_...  27.9 us
    pallas_call x2, Pallas kernels, student_entry(): pl.pallas_call(functools.partial(entry_kernel, p_rows, 4), grid_spec=pltp...  27.7 us
    pallas_call x2, Pallas kernels, student_back(): pl.pallas_call(functools.partial(back_kernel, p_rows, 4), grid_spec=pltpu...  27.6 us
  transfers between devices with their start and end apart: 26, of which 8 were waited for; matrix products, arithmetic and copies ran while one was open for 30% of the time, Pallas kernels for 33%

profile of v3, /device:TPU:0, one launch (start us, length us, event | category | flops | bytes accessed | tf_op | source)
XLA Modules:
  0.0 601.3 jit_solution(14971635562012452548)
XLA Ops:
  24.5 9.4 %constant_dynamic-slice_fusion.5 = (bf16[4,1,10,8,8192]{4,3,2,1,0:T(8,128)(2,1)}, bf16[4,1,10,8,8192]{4,3,2,1,0:T(8,128)(2,1)}) fusion(bf16[4,2,10,8,8192]{4,3,2,1,0:T(8,128)(2,1)} %bitcast.254, s32[]{:T(128)S(6)} %select_n.393, s32[]{:T(128)S(6)} %select_n.381), kind=kLoop, calls=%fused_computation.117 | loop fusion | bytes 20971528 | tf_op jit(solution)/shard_map/jit(dynamic_index_in_dim)/dynamic_slice | solution.py:1404
  74.2 13.0 %multiply_convert_fusion = bf16[320,4,4096]{2,0,1:T(8,128)(2,1)} fusion(bf16[320,4,4096]{2,1,0:T(4,128)(2,1)} %param.30, f32[4096]{0:T(1024)S(1)} %bitcast.293, f32[4096]{0:T(1024)S(1)} %bitcast.292), kind=kLoop, calls=%fused_computation | loop fusion | flops 41943040 | bytes 21004288 | tf_op jit(solution)/shard_map/convert_element_type | solution.py:1533
  126.8 11.7 %shard_map.484.refs_5_.tot.refs_21_ = f32[8,128]{1,0:T(8,128)} custom-call(f32[8,128]{1,0:T(8,128)} %shard_map.483.refs_0_, bf16[4,160,1024]{2,1,0:T(8,128)(2,1)} %collective-permute-done.refs_1_, bf16[8,40,2048]{2,1,0:T(8,128)(2,1)} %collective-permute-done.1.refs_2_, bf16[4,500,1024]{2,1,0:T(8,128)(2,1)} %all-to-all-done.refs_3_, ...), custom_call_target="tpu_custom_call" | custom-call | flops 12000000000 | bytes 1048576 | tf_op jit(solution)/shard_map/pallas_call | solution.py:219
  146.7 16.7 %collective-permute-done.3 = bf16[6,40,2048]{2,1,0:T(8,128)(2,1)S(1)} collective-permute-done((bf16[6,40,2048]{2,1,0:T(8,128)(2,1)}, bf16[6,40,2048]{2,1,0:T(8,128)(2,1)S(1)}, u32[]{:S(2)}, u32[]{:S(2)}) %collective-permute-start.3) | collective-permute-done | bytes 983072 | tf_op jit(solution)/shard_map/ppermute | solution.py:1438
  166.3 13.3 %shard_map.486 = (bf16[16,48,2048]{2,1,0:T(8,128)(2,1)}, bf16[9,48,2176]{2,1,0:T(8,128)(2,1)}, bf16[11,48,2176]{2,1,0:T(8,128)(2,1)}, f32[13,48,2048]{2,1,0:T(8,128)}, f32[8,128]{1,0:T(8,128)}) custom-call(s32[2]{0:T(128)} %pad_add_fusion.place, bf16[8,48,2048]{2,1,0:T(8,128)(2,1)} %pad.46.refs_0_, bf16[8,48,2048]{2,1,0:T(8,128)(2,1)} %pad.47.refs_1_, ...), custom_call_target="tpu_custom_call" | custom-call | flops 15000000512 | bytes 1048576 | tf_op jit(solution)/shard_map/pallas_call | solution.py:693
  206.3 14.6 %shard_map.487 = (bf16[8,160,1024]{2,1,0:T(8,128)(2,1)}, bf16[5,160,1152]{2,1,0:T(8,128)(2,1)}, bf16[7,160,1152]{2,1,0:T(8,128)(2,1)}, f32[9,160,1024]{2,1,0:T(8,128)}, f32[8,128]{1,0:T(8,128)}) custom-call(s32[2]{0:T(128)} %pad_add_fusion.place, bf16[4,160,1024]{2,1,0:T(8,128)(2,1)} %bitcast.250, bf16[4,160,1024]{2,1,0:T(8,128)(2,1)} %collective-permute-done.refs_1_, ...), custom_call_target="tpu_custom_call" | custom-call | flops 15000000512 | bytes 1048576 | tf_op jit(solution)/shard_map/pallas_call | solution.py:693
  222.3 11.5 %shard_map.488.inner = f32[8,128]{1,0:T(8,128)} custom-call(f32[8,128]{1,0:T(8,128)} %get-tuple-element.151.refs_0_, f32[8,128]{1,0:T(8,128)} %get-tuple-element.143.refs_1_, bf16[1,8,128]{2,1,0:T(8,128)(2,1)} %copy.205.refs_2_, bf16[3,16,8192]{2,1,0:T(8,128)(2,1)} %collective-permute-done.8.refs_3_.refs_2_, ...), custom_call_target="tpu_custom_call" | custom-call | flops 12000000000 | bytes 1048576 | tf_op jit(solution)/shard_map/pallas_call | solution.py:219
  244.8 17.3 %shard_map.490 = (bf16[10,48,2304]{2,1,0:T(8,128)(2,1)}, f32[9,48,2048]{2,1,0:T(8,128)}, f32[11,48,2048]{2,1,0:T(8,128)}, bf16[8,48,2048]{2,1,0:T(8,128)(2,1)}, f32[48,384]{1,0:T(8,128)}) custom-call(s32[2]{0:T(128)} %pad_add_fusion.place, f32[13,48,2048]{2,1,0:T(8,128)} %get-tuple-element.160.first_ref, bf16[11,48,2176]{2,1,0:T(8,128)(2,1)} %get-tuple-element.161.odd, ...), custom_call_target="tpu_custom_call" | custom-call | flops 17999998976 | bytes 1048576 | tf_op jit(solution)/shard_map/pallas_call | solution.py:781
  262.1 15.6 %shard_map.489 = (bf16[6,160,1280]{2,1,0:T(8,128)(2,1)}, f32[5,160,1024]{2,1,0:T(8,128)}, f32[7,160,1024]{2,1,0:T(8,128)}, bf16[4,160,1024]{2,1,0:T(8,128)(2,1)}, f32[160,128]{1,0:T(8,128)}) custom-call(s32[2]{0:T(128)} %pad_add_fusion.place, f32[9,160,1024]{2,1,0:T(8,128)} %get-tuple-element.149.first_ref, bf16[7,160,1152]{2,1,0:T(8,128)(2,1)} %get-tuple-element.150.odd, ...), custom_call_target="tpu_custom_call" | custom-call | flops 17999998976 | bytes 1048576 | tf_op jit(solution)/shard_map/pallas_call | solution.py:781
  277.8 17.6 %shard_map.491.refs_7_ = f32[16,384]{1,0:T(8,128)} custom-call(s32[2]{0:T(128)} %pad_add_fusion.place, bf16[8,16,8192]{2,1,0:T(8,128)(2,1)} %fusion.26.refs_5_.refs_0_, bf16[8,16,8192]{2,1,0:T(8,128)(2,1)} %copy-done.12, bf16[3,16,8192]{2,1,0:T(8,128)(2,1)} %collective-permute-done.8.refs_3_.refs_2_, ...), custom_call_target="tpu_custom_call" | custom-call | flops 16000000000 | bytes 1048576 | tf_op jit(solution)/shard_map/pallas_call | solution.py:525
  307.0 30.9 %shard_map.492.refs_8_ = f32[32,384]{1,0:T(8,128)} custom-call(s32[2]{0:T(128)} %pad_add_fusion.place, bf16[8,32,8192]{2,1,0:T(8,128)(2,1)} %pad.48.refs_6_.refs_0_, bf16[8,32,8192]{2,1,0:T(8,128)(2,1)} %pad.53.refs_1_, bf16[3,32,8192]{2,1,0:T(8,128)(2,1)} %pad.54.refs_2_, bf16[3,32,8192]{2,1,0:T(8,128)(2,1)} %pad.55.refs_3_, bf16[1152,256]{1,0:T(8,128)(2,1)} %bitcast.302, ...), custom_call_target="tpu_custom_call" | custom-call | flops 32000000000 | bytes 1048576 | tf_op jit(solution)/shard_map/pallas_call | solution.py:525
  340.7 10.3 %collective-permute-done.11.refs_2_ = bf16[3,80,4096]{2,1,0:T(8,128)(2,1)} collective-permute-done((bf16[3,80,4096]{2,1,0:T(8,128)(2,1)}, bf16[3,80,4096]{2,1,0:T(8,128)(2,1)}, u32[]{:S(2)}, u32[]{:S(2)}) %collective-permute-start.11) | collective-permute-done | bytes 1966112 | tf_op jit(solution)/shard_map/ppermute | solution.py:1438
  351.0 23.6 %shard_map.493.refs_4_ = f32[80,128]{1,0:T(8,128)} custom-call(s32[2]{0:T(128)} %pad_add_fusion.place, bf16[4,4,2,40,4096]{4,3,2,1,0:T(8,128)(2,1)} %bitcast.238, bf16[4,80,4096]{2,1,0:T(8,128)(2,1)} %copy-done.13, bf16[3,80,4096]{2,1,0:T(8,128)(2,1)} %collective-permute-done.11.refs_2_, bf16[3,80,4096]{2,1,0:T(8,128)(2,1)} %collective-permute-done.12.refs_3_, ...), custom_call_target="tpu_custom_call" | custom-call | flops 20000000000 | bytes 1048576 | tf_op jit(solution)/shard_map/pallas_call | solution.py:525
  381.5 13.9 %shard_map.494.refs_5_ = f32[40,128]{1,0:T(8,128)} custom-call(s32[2]{0:T(128)} %pad_add_fusion.place, bf16[4,4,2,40,4096]{4,3,2,1,0:T(8,128)(2,1)} %bitcast.240, bf16[4,40,4096]{2,1,0:T(8,128)(2,1)} %copy-done.21, bf16[3,40,4096]{2,1,0:T(8,128)(2,1)} %copy-done.60, bf16[3,40,4096]{2,1,0:T(8,128)(2,1)} %collective-permute-done.17.refs_3_, ...), custom_call_target="tpu_custom_call" | custom-call | flops 10000000000 | bytes 1048576 | tf_op jit(solution)/shard_map/pallas_call | solution.py:525
  397.4 13.8 %shard_map.495.refs_6_ = f32[40,128]{1,0:T(8,128)} custom-call(s32[2]{0:T(128)} %pad_add_fusion.place, bf16[4,4,2,40,4096]{4,3,2,1,0:T(8,128)(2,1)} %bitcast.241, bf16[4,40,4096]{2,1,0:T(8,128)(2,1)} %copy-done.20, bf16[3,40,4096]{2,1,0:T(8,128)(2,1)} %copy-done.61, bf16[3,40,4096]{2,1,0:T(8,128)(2,1)} %copy-done.62, bf16[1152,256]{1,0:T(8,128)(2,1)} %bitcast.305, ...), custom_call_target="tpu_custom_call" | custom-call | flops 10000000000 | bytes 1048576 | tf_op jit(solution)/shard_map/pallas_call | solution.py:525
  411.2 11.1 %shard_map.496 = (f32[160,128]{1,0:T(8,128)}, f32[48,384]{1,0:T(8,128)}, f32[8,128]{1,0:T(8,128)}) custom-call(f32[160,128]{1,0:T(8,128)} %get-tuple-element.159.refs_0_, f32[48,384]{1,0:T(8,128)} %get-tuple-element.162.refs_1_, f32[160,128]{1,0:T(8,128)} %broadcast_in_dim.161.refs_4_.label_ref.refs_2_, ...), custom_call_target="tpu_custom_call" | custom-call | flops 11000000512 | bytes 1048576 | tf_op jit(solution)/shard_map/pallas_call | solution.py:954
  427.0 13.5 %shard_map.498 = (f32[9,48,2048]{2,1,0:T(8,128)}, bf16[8,48,2048]{2,1,0:T(8,128)(2,1)}, f32[8,128]{1,0:T(8,128)}, f32[576,64]{1,0:T(8,128)}, f32[32,64]{1,0:T(8,128)}) custom-call(s32[2]{0:T(128)} %pad_add_fusion.place, f32[11,48,2048]{2,1,0:T(8,128)} %get-tuple-element.197.sum_ref, bf16[11,48,2048]{2,1,0:T(8,128)(2,1)} %pad.52.cot, ...), custom_call_target="tpu_custom_call" | custom-call | flops 17999998976 | bytes 1048576 | tf_op jit(solution)/shard_map/pallas_call | solution.py:1094
  440.5 14.1 %shard_map.497 = (f32[5,160,1024]{2,1,0:T(8,128)}, bf16[4,160,1024]{2,1,0:T(8,128)(2,1)}, f32[8,128]{1,0:T(8,128)}, f32[576,64]{1,0:T(8,128)}, f32[32,64]{1,0:T(8,128)}) custom-call(s32[2]{0:T(128)} %pad_add_fusion.place, f32[7,160,1024]{2,1,0:T(8,128)} %get-tuple-element.186.sum_ref, bf16[7,160,1024]{2,1,0:T(8,128)(2,1)} %bitcast.273, ...), custom_call_target="tpu_custom_call" | custom-call | flops 17999998976 | bytes 1048576 | tf_op jit(solution)/shard_map/pallas_call | solution.py:1094
  458.0 11.0 %shard_map.499.pulled = f32[8,128]{1,0:T(8,128)} custom-call(f32[8,128]{1,0:T(8,128)} %get-tuple-element.196.refs_0_, f32[8,128]{1,0:T(8,128)} %get-tuple-element.201.refs_1_, bf16[4,4,40,1024]{3,2,1,0:T(8,128)(2,1)} %copy-done.17), custom_call_target="tpu_custom_call" | custom-call | flops 12000000000 | bytes 1048576 | tf_op jit(solution)/shard_map/pallas_call | solution.py:219
  469.8 13.2 %shard_map.500 = (bf16[4,160,1024]{2,1,0:T(8,128)(2,1)}, bf16[4,160,1024]{2,1,0:T(8,128)(2,1)}, f32[288,64]{1,0:T(8,128)}, f32[8,128]{1,0:T(8,128)}) custom-call(s32[2]{0:T(128)} %pad_add_fusion.place, f32[5,160,1024]{2,1,0:T(8,128)} %get-tuple-element.192.flow_ref, f32[5,160,1024]{2,1,0:T(8,128)} %get-tuple-element.189.first_ref, ...), custom_call_target="tpu_custom_call" | custom-call | flops 16000000000 | bytes 1048576 | tf_op jit(solution)/shard_map/pallas_call | solution.py:1233
  484.2 14.5 %shard_map.501 = (bf16[8,48,2048]{2,1,0:T(8,128)(2,1)}, bf16[8,48,2048]{2,1,0:T(8,128)(2,1)}, f32[288,64]{1,0:T(8,128)}, f32[8,128]{1,0:T(8,128)}) custom-call(s32[2]{0:T(128)} %pad_add_fusion.place, f32[9,48,2048]{2,1,0:T(8,128)} %get-tuple-element.207.flow_ref, f32[9,48,2048]{2,1,0:T(8,128)} %get-tuple-element.199.first_ref, ...), custom_call_target="tpu_custom_call" | custom-call | flops 16000000000 | bytes 1048576 | tf_op jit(solution)/shard_map/pallas_call | solution.py:1233
  505.1 8.9 %collective-permute-done.21.refs_23_ = bf16[4,160,1024]{2,1,0:T(8,128)(2,1)S(1)} collective-permute-done((bf16[4,160,1024]{2,1,0:T(8,128)(2,1)}, bf16[4,160,1024]{2,1,0:T(8,128)(2,1)S(1)}, u32[]{:S(2)}, u32[]{:S(2)}) %collective-permute-start.21) | collective-permute-done | bytes 1310752 | tf_op jit(solution)/shard_map/ppermute | solution.py:1399
  515.1 20.8 %shard_map.502 = (f32[288,64]{1,0:T(8,128)}, f32[288,64]{1,0:T(8,128)}, f32[288,64]{1,0:T(8,128)}, f32[288,64]{1,0:T(8,128)}, bf16[288,64]{1,0:T(8,128)(2,1)}, /...) custom-call(f32[288,64]{1,0:T(8,128)} %get-tuple-element.204.refs_0_, ...), custom_call_target="tpu_custom_call" | custom-call | flops 20000000000 | bytes 1048576 | tf_op jit(solution)/shard_map/pallas_call | solution.py:376
  556.1 10.1 %fusion.10 = f32[320,4,1024]{2,1,0:T(4,128)} fusion(bf16[320,4,1024]{2,1,0:T(4,128)(2,1)S(1)} %copy-done.4, f32[4,2,40,4,1024]{4,3,2,1,0:T(4,128)S(1)} %copy-done, f32[320,1024]{1,0:T(8,128)S(1)} %get-tuple-element.463, f32[320,1024]{1,0:T(8,128)S(1)} %get-tuple-element.462, f32[320,1024]{1,0:T(8,128)S(1)} %get-tuple-element.461, ...), kind=kLoop, calls=%fused_computation.17 | loop fusion | flops 19660800 | bytes 18350080 | tf_op jit(solution)/shard_map/add | solution.py:1763
  (333 shorter events, 246.9 us)
Async XLA Ops:
  4.8 112.4 %collective-permute-start = (bf16[4,160,1024]{2,1,0:T(8,128)(2,1)}, bf16[4,160,1024]{2,1,0:T(8,128)(2,1)}, u32[]{:S(2)}, u32[]{:S(2)}) collective-permute-start(bf16[4,160,1024]{2,1,0:T(8,128)(2,1)} %bitcast.6.refs_1_), channel_id=1, source_target_pairs={{0,1},{1,0},{2,3},{3,2},{4,5},{5,4},{6,7},{7,6},{8,9},{9,8},{10,11... | collective-permute-start | bytes 3932168 | tf_op jit(solution)/shard_map/ppermute | solution.py:1399
  9.9 104.5 %collective-permute-start.1 = (bf16[8,40,2048]{2,1,0:T(8,128)(2,1)}, bf16[8,40,2048]{2,1,0:T(8,128)(2,1)}, u32[]{:S(2)}, u32[]{:S(2)}) collective-permute-start(bf16[8,40,2048]{2,1,0:T(8,128)(2,1)} %bitcast.231.refs_3_), channel_id=1, source_target_pairs={{0,1},{1,0},{2,3},{3,2},{4,5},{5,4},{6,7},{7,6},{8,9},{9,8},{10,11... | collective-permute-start | bytes 3932168 | tf_op jit(solution)/shard_map/ppermute | solution.py:1399
  19.4 107.4 %all-to-all-start = ((bf16[4,500,1024]{2,1,0:T(8,128)(2,1)}), bf16[4,500,1024]{2,1,0:T(8,128)(2,1)}, u32[]{:S(2)}, u32[]{:S(2)}) async-start(bf16[4,500,1024]{2,1,0:T(8,128)(2,1)} %pad_maximum_fusion), calls=%async_computation | async-start | bytes 8257536 | tf_op jit(solution)/shard_map/all_to_all | solution.py:1462
  38.2 87.3 %collective-permute-start.2 = (bf16[16,8,8192]{2,0,1:T(8,128)(2,1)}, bf16[16,8,8192]{2,0,1:T(8,128)(2,1)}, u32[]{:S(2)}, u32[]{:S(2)}) collective-permute-start(bf16[16,8,8192]{2,0,1:T(8,128)(2,1)} %copy.219), channel_id=1, source_target_pairs={{0,1},{1,0},{2,3},{3,2},{4,5},{5,4},{6,7},{7,6},{8,9},{9,8},{10,11... | collective-permute-start | bytes 6291464 | tf_op jit(solution)/shard_map/ppermute | solution.py:1399
  138.5 24.9 %collective-permute-start.3 = (bf16[6,40,2048]{2,1,0:T(8,128)(2,1)}, bf16[6,40,2048]{2,1,0:T(8,128)(2,1)S(1)}, u32[]{:S(2)}, u32[]{:S(2)}) collective-permute-start(bf16[6,40,2048]{2,1,0:T(8,128)(2,1)} %get-tuple-element.137.refs_9_), channel_id=1, source_target_pairs={{0,2},{1,3},{2,0},{3,1},{4,6},{5,7},{6,4},{7,5},{8,10},{9,11},{10,... | collective-permute-start | bytes 2949128 | tf_op jit(solution)/shard_map/ppermute | solution.py:1438
  139.8 24.7 %collective-permute-start.4 = (bf16[6,40,2048]{2,1,0:T(8,128)(2,1)}, bf16[6,40,2048]{2,1,0:T(8,128)(2,1)S(1)}, u32[]{:S(2)}, u32[]{:S(2)}) collective-permute-start(bf16[6,40,2048]{2,1,0:T(8,128)(2,1)} %get-tuple-element.138.refs_10_), channel_id=1, source_target_pairs={{0,8},{1,9},{2,4},{3,5},{4,2},{5,3},{6,14},{7,15},{8,0},{9,1},{10,... | collective-permute-start | bytes 2949128 | tf_op jit(solution)/shard_map/ppermute | solution.py:1438
  139.8 81.1 %collective-permute-start.7 = (bf16[24,8,8192]{2,0,1:T(8,128)(2,1)}, bf16[24,8,8192]{2,0,1:T(8,128)(2,1)}, u32[]{:S(2)}, u32[]{:S(2)}) collective-permute-start(bf16[24,8,8192]{2,0,1:T(8,128)(2,1)} %copy.222), channel_id=1, source_target_pairs={{0,1},{1,0},{2,3},{3,2},{4,5},{5,4},{6,7},{7,6},{8,9},{9,8},{10,11... | collective-permute-start | bytes 9437192 | tf_op jit(solution)/shard_map/ppermute | solution.py:1399
  140.8 64.8 %collective-permute-start.5 = (bf16[6,160,1024]{2,1,0:T(8,128)(2,1)}, bf16[6,160,1024]{2,1,0:T(8,128)(2,1)}, u32[]{:S(2)}, u32[]{:S(2)}) collective-permute-start(bf16[6,160,1024]{2,1,0:T(8,128)(2,1)} %get-tuple-element.147.refs_7_), channel_id=1, source_target_pairs={{0,2},{1,3},{2,0},{3,1},{4,6},{5,7},{6,4},{7,5},{8,10},{9,11},{10,... | collective-permute-start | bytes 5898248 | tf_op jit(solution)/shard_map/ppermute | solution.py:1438
  143.9 61.7 %collective-permute-start.6 = (bf16[6,160,1024]{2,1,0:T(8,128)(2,1)}, bf16[6,160,1024]{2,1,0:T(8,128)(2,1)}, u32[]{:S(2)}, u32[]{:S(2)}) collective-permute-start(bf16[6,160,1024]{2,1,0:T(8,128)(2,1)} %get-tuple-element.148.refs_8_), channel_id=1, source_target_pairs={{0,8},{1,9},{2,4},{3,5},{4,2},{5,3},{6,14},{7,15},{8,0},{9,1},{10,... | collective-permute-start | bytes 5898248 | tf_op jit(solution)/shard_map/ppermute | solution.py:1438
  186.1 36.2 %collective-permute-start.8 = (bf16[3,16,8192]{2,1,0:T(8,128)(2,1)}, bf16[3,16,8192]{2,1,0:T(8,128)(2,1)}, u32[]{:S(2)}, u32[]{:S(2)}) collective-permute-start(bf16[3,16,8192]{2,1,0:T(8,128)(2,1)} %get-tuple-element.411), channel_id=1, source_target_pairs={{0,2},{1,3},{2,0},{3,1},{4,6},{5,7},{6,4},{7,5},{8,10},{9,11},{10,... | collective-permute-start | bytes 2359304 | tf_op jit(solution)/shard_map/ppermute | solution.py:1438
  187.4 34.9 %collective-permute-start.9 = (bf16[3,16,8192]{2,1,0:T(8,128)(2,1)}, bf16[3,16,8192]{2,1,0:T(8,128)(2,1)}, u32[]{:S(2)}, u32[]{:S(2)}) collective-permute-start(bf16[3,16,8192]{2,1,0:T(8,128)(2,1)} %get-tuple-element.410), channel_id=1, source_target_pairs={{0,8},{1,9},{2,4},{3,5},{4,2},{5,3},{6,14},{7,15},{8,0},{9,1},{10,... | collective-permute-start | bytes 2359304 | tf_op jit(solution)/shard_map/ppermute | solution.py:1438
  241.1 54.3 %collective-permute-start.14 = (bf16[3,24,8192]{2,1,0:T(8,128)(2,1)}, bf16[3,24,8192]{2,1,0:T(8,128)(2,1)S(1)}, u32[]{:S(2)}, u32[]{:S(2)}) collective-permute-start(bf16[3,24,8192]{2,1,0:T(8,128)(2,1)} %get-tuple-element.409), channel_id=1, source_target_pairs={{0,2},{1,3},{2,0},{3,1},{4,6},{5,7},{6,4},{7,5},{8,10},{9,11},{10,... | collective-permute-start | bytes 3538952 | tf_op jit(solution)/shard_map/ppermute | solution.py:1438
  241.7 54.9 %collective-permute-start.15 = (bf16[3,24,8192]{2,1,0:T(8,128)(2,1)}, bf16[3,24,8192]{2,1,0:T(8,128)(2,1)S(1)}, u32[]{:S(2)}, u32[]{:S(2)}) collective-permute-start(bf16[3,24,8192]{2,1,0:T(8,128)(2,1)} %get-tuple-element.408), channel_id=1, source_target_pairs={{0,8},{1,9},{2,4},{3,5},{4,2},{5,3},{6,14},{7,15},{8,0},{9,1},{10,... | collective-permute-start | bytes 3538952 | tf_op jit(solution)/shard_map/ppermute | solution.py:1438
  241.8 59.9 %collective-permute-start.10 = (bf16[4,80,4096]{2,1,0:T(8,128)(2,1)}, bf16[4,80,4096]{2,1,0:T(8,128)(2,1)S(1)}, u32[]{:S(2)}, u32[]{:S(2)}) collective-permute-start(bf16[4,80,4096]{2,1,0:T(8,128)(2,1)} %bitcast.52), channel_id=1, source_target_pairs={{0,1},{1,0},{2,3},{3,2},{4,5},{5,4},{6,7},{7,6},{8,9},{9,8},{10,11... | collective-permute-start | bytes 7864328 | tf_op jit(solution)/shard_map/ppermute | solution.py:1399
  242.8 95.1 %collective-permute-start.13 = (bf16[4,40,4096]{2,1,0:T(8,128)(2,1)}, bf16[4,40,4096]{2,1,0:T(8,128)(2,1)S(1)}, u32[]{:S(2)}, u32[]{:S(2)}) collective-permute-start(bf16[4,40,4096]{2,1,0:T(8,128)(2,1)} %get-tuple-element.167), channel_id=1, source_target_pairs={{0,1},{1,0},{2,3},{3,2},{4,5},{5,4},{6,7},{7,6},{8,9},{9,8},{10,11... | collective-permute-start | bytes 3932168 | tf_op jit(solution)/shard_map/ppermute | solution.py:1399
  243.8 130.8 %collective-permute-start.18 = (bf16[4,40,4096]{2,1,0:T(8,128)(2,1)}, bf16[4,40,4096]{2,1,0:T(8,128)(2,1)S(1)}, u32[]{:S(2)}, u32[]{:S(2)}) collective-permute-start(bf16[4,40,4096]{2,1,0:T(8,128)(2,1)} %get-tuple-element.175), channel_id=1, source_target_pairs={{0,1},{1,0},{2,3},{3,2},{4,5},{5,4},{6,7},{7,6},{8,9},{9,8},{10,11... | collective-permute-start | bytes 3932168 | tf_op jit(solution)/shard_map/ppermute | solution.py:1399
  303.8 47.2 %collective-permute-start.11 = (bf16[3,80,4096]{2,1,0:T(8,128)(2,1)}, bf16[3,80,4096]{2,1,0:T(8,128)(2,1)}, u32[]{:S(2)}, u32[]{:S(2)}) collective-permute-start(bf16[3,80,4096]{2,1,0:T(8,128)(2,1)} %get-tuple-element.407), channel_id=1, source_target_pairs={{0,2},{1,3},{2,0},{3,1},{4,6},{5,7},{6,4},{7,5},{8,10},{9,11},{10,... | collective-permute-start | bytes 5898248 | tf_op jit(solution)/shard_map/ppermute | solution.py:1438
  307.0 44.1 %collective-permute-start.12 = (bf16[3,80,4096]{2,1,0:T(8,128)(2,1)S(1)}, bf16[3,80,4096]{2,1,0:T(8,128)(2,1)}, u32[]{:S(2)}, u32[]{:S(2)}) collective-permute-start(bf16[3,80,4096]{2,1,0:T(8,128)(2,1)S(1)} %get-tuple-element.406), channel_id=1, source_target_pairs={{0,8},{1,9},{2,4},{3,5},{4,2},{5,3},{6,14},{7,15},{8,0},{9,1},{10,... | collective-permute-start | bytes 5898248 | tf_op jit(solution)/shard_map/ppermute | solution.py:1438
  340.1 40.5 %collective-permute-start.16 = (bf16[3,40,4096]{2,1,0:T(8,128)(2,1)S(1)}, bf16[3,40,4096]{2,1,0:T(8,128)(2,1)S(1)}, u32[]{:S(2)}, u32[]{:S(2)}) collective-permute-start(bf16[3,40,4096]{2,1,0:T(8,128)(2,1)S(1)} %get-tuple-element.399), channel_id=1, source_target_pairs={{0,2},{1,3},{2,0},{3,1},{4,6},{5,7},{6,4},{7,5},{8,10},{9,11},{10,... | collective-permute-start | bytes 2949128 | tf_op jit(solution)/shard_map/ppermute | solution.py:1438
  340.4 40.1 %collective-permute-start.17 = (bf16[3,40,4096]{2,1,0:T(8,128)(2,1)S(1)}, bf16[3,40,4096]{2,1,0:T(8,128)(2,1)}, u32[]{:S(2)}, u32[]{:S(2)}) collective-permute-start(bf16[3,40,4096]{2,1,0:T(8,128)(2,1)S(1)} %get-tuple-element.398), channel_id=1, source_target_pairs={{0,8},{1,9},{2,4},{3,5},{4,2},{5,3},{6,14},{7,15},{8,0},{9,1},{10,... | collective-permute-start | bytes 2949128 | tf_op jit(solution)/shard_map/ppermute | solution.py:1438
  423.5 33.5 %all-to-all-start.1 = ((bf16[4,4,40,1024]{3,2,1,0:T(8,128)(2,1)}), bf16[4,4,40,1024]{3,2,1,0:T(8,128)(2,1)S(1)}, u32[]{:S(2)}, u32[]{:S(2)}) async-start(bf16[4,4,40,1024]{3,2,1,0:T(8,128)(2,1)} %bitcast.230), calls=%async_computation.1 | async-start | bytes 2621440 | tf_op jit(solution)/shard_map/all_to_all | solution.py:1462
  483.0 31.1 %collective-permute-start.21 = (bf16[4,160,1024]{2,1,0:T(8,128)(2,1)}, bf16[4,160,1024]{2,1,0:T(8,128)(2,1)S(1)}, u32[]{:S(2)}, u32[]{:S(2)}) collective-permute-start(bf16[4,160,1024]{2,1,0:T(8,128)(2,1)} %get-tuple-element.218), channel_id=1, source_target_pairs={{0,1},{1,0},{2,3},{3,2},{4,5},{5,4},{6,7},{7,6},{8,9},{9,8},{10,11... | collective-permute-start | bytes 3932168 | tf_op jit(solution)/shard_map/ppermute | solution.py:1399
  537.0 31.0 %collective-permute-start.22 = (bf16[8,40,2048]{2,1,0:T(8,128)(2,1)}, bf16[8,40,2048]{2,1,0:T(8,128)(2,1)}, u32[]{:S(2)}, u32[]{:S(2)}) collective-permute-start(bf16[8,40,2048]{2,1,0:T(8,128)(2,1)} %slice.351.refs_25_), channel_id=1, source_target_pairs={{0,1},{1,0},{2,3},{3,2},{4,5},{5,4},{6,7},{7,6},{8,9},{9,8},{10,11... | collective-permute-start | bytes 3932168 | tf_op jit(solution)/shard_map/ppermute | solution.py:1399
  547.9 36.4 %all-to-all-start.2 = ((bf16[4,8,10,2048]{3,1,2,0:T(8,128)(2,1)}), bf16[4,8,10,2048]{3,1,2,0:T(8,128)(2,1)}, u32[]{:S(2)}, u32[]{:S(2)}) async-start(bf16[4,8,10,2048]{3,1,2,0:T(8,128)(2,1)} %bitcast.262), calls=%async_computation.2 | async-start | bytes 2621440 | tf_op jit(solution)/shard_map/all_to_all | solution.py:1462
  (65 other events, 504.5 us)

commit v4 on v3

--- a/solution.py
+++ b/solution.py
@@ -236,23 +236,20 @@
     )(*parts, *waits)
 
 
-def finish_kernel(axes, layout, rates, waits, *refs):
+def gradient_sum_kernel(axes, layout, waits, *refs):
     count = sum(len(parts) for parts in layout)
-    inputs, states, entry = refs[:count], refs[count : count + 9], refs[count + 9 : count + 12]
-    tot, norm = refs[count + 12 : count + 14]
-    refs = refs[waits:]
-    outs = refs[count + 14 : count + 35]
-    out_ref, x_ref, boxes_a, boxes_b, held = refs[count + 35 : count + 40]
-    send_a, recv_a, send_b, recv_b, send_c, recv_c = refs[count + 40 :]
-    conv_rate, norm_rate, per_position = rates
+    inputs, refs = refs[:count], refs[count + waits :]
+    out_ref, x_ref, boxes_a, boxes_b, held = refs[:5]
+    send_a, recv_a, send_b, recv_b, send_c, recv_c = refs[5:]
     at = 0
     for parts in layout:
         value = inputs[parts[0]][...]
         for k in parts[1:]:
             value = value + inputs[k][...]
-        if value.shape[1] == 64:
-            half = value.shape[0] // 2
-            value = jnp.concatenate([value[:half], value[half:]], axis=1)
+        parts = 128 // value.shape[1]
+        if parts > 1:
+            n = value.shape[0] // parts
+            value = jnp.concatenate([value[k * n : k * n + n] for k in range(parts)], axis=1)
         x_ref[at : at + value.shape[0]] = value
         at += value.shape[0]
     if at < x_ref.shape[0]:
@@ -322,13 +319,24 @@
     for copy in copies:
         copy.wait()
 
+
+def update_kernel(rates, *refs):
+    out_ref, tot, norm = refs[:3]
+    states, entry, outs = refs[3:12], refs[12:15], refs[15:]
+    conv_rate, norm_rate, per_position = rates
     at = 0
     for k in range(3):
         weights, moment, average = [ref[...] for ref in states[3 * k : 3 * k + 3]]
-        half = weights.shape[0] // 2
-        pairs = out_ref[at : at + half]
-        at += half
-        gradient = jnp.concatenate([pairs[:, 0:64], pairs[:, 64:128]], axis=0)
+        width = (CS_IN, CS_OUT, CS_IN)[k]
+        n = weights.shape[0] * weights.shape[1] // 128
+        packed = out_ref[at : at + n]
+        at += n
+        parts = [packed[:, lane : lane + width] for lane in range(0, 128, width)]
+        turned = jnp.concatenate(parts, axis=0)
+        taps = turned.shape[0] // CS_OUT
+        gradient = jnp.concatenate(
+            [turned[t * CS_OUT : (t + 1) * CS_OUT].T for t in range(taps)], axis=0
+        )
         state = renew(weights, gradient, moment, average, conv_rate)
         for ref, value in zip(outs[5 * k : 5 * k + 4], state):
             ref[...] = value
@@ -354,7 +362,7 @@
     outs[20][...] = jnp.sum(losses, axis=1, keepdims=True) * per_position
 
 
-def finish(groups, states, entry, tot, norm, rates, axes, collective_id, waits):
+def gradient_sum(groups, axes, collective_id, waits):
     (_, size_a), (_, size_b) = axes
     arrays, layout, rows = [], [], []
     for members in groups:
@@ -366,20 +374,14 @@
     sems = []
     for size in (size_a, size_b, size_a):
         sems += [pltpu.SemaphoreType.DMA((size,))] * 2
-    given = arrays + [a for state in states for a in state] + entry + [tot, norm]
-    outs = []
-    for state in states:
-        outs += [shape_of(state[0].shape, F32)] * 4 + [shape_of(state[0].shape, BF16)]
-    outs += [shape_of(entry[0].shape, F32)] * 4 + [shape_of((8, 128), F32), shape_of((1, 1), F32)]
     waits = jax.tree.leaves(waits)
     vmem = pl.BlockSpec(memory_space=pltpu.VMEM)
-    got = pl.pallas_call(
-        functools.partial(finish_kernel, axes, tuple(layout), rates, len(waits)),
-        out_shape=outs,
-        in_specs=[vmem] * len(given) + [pl.BlockSpec(memory_space=pl.ANY)] * len(waits),
-        out_specs=[vmem] * len(outs),
+    return pl.pallas_call(
+        functools.partial(gradient_sum_kernel, axes, tuple(layout), len(waits)),
+        out_shape=jax.ShapeDtypeStruct((padded, 128), F32),
+        in_specs=[vmem] * len(arrays) + [pl.BlockSpec(memory_space=pl.ANY)] * len(waits),
+        out_specs=vmem,
         scratch_shapes=[
-            pltpu.VMEM((padded, 128), F32),
             pltpu.VMEM((padded, 128), F32),
             pltpu.VMEM((size_a, piece, 128), F32),
             pltpu.VMEM((size_b, piece, 128), F32),
@@ -388,7 +390,24 @@
         + sems,
         compiler_params=pltpu.CompilerParams(collective_id=collective_id, has_side_effects=True),
         cost_estimate=cost(20),
-    )(*given, *waits)
+    )(*arrays, *waits)
+
+
+def update(total, states, entry, tot, norm, rates):
+    given = [total, tot, norm] + [a for state in states for a in state] + entry
+    outs = []
+    for state in states:
+        outs += [shape_of(state[0].shape, F32)] * 4 + [shape_of(state[0].shape, BF16)]
+    outs += [shape_of(entry[0].shape, F32)] * 4 + [shape_of((8, 128), F32), shape_of((1, 1), F32)]
+    vmem = pl.BlockSpec(memory_space=pltpu.VMEM)
+    got = pl.pallas_call(
+        functools.partial(update_kernel, rates),
+        out_shape=outs,
+        in_specs=[vmem] * len(given),
+        out_specs=[vmem] * len(outs),
+        compiler_params=pltpu.CompilerParams(vmem_limit_bytes=VMEM_LIMIT),
+        cost_estimate=cost(4),
+    )(*given)
     return got[0:5], got[5:10], got[10:15], got[15:19], got[19], got[20]
 
 
@@ -807,6 +826,9 @@
         for part in given[res * pieces[0] : res * pieces[0] + pieces[res]]:
             teacher[res][at : at + part.shape[0]] = part[...]
             at += part.shape[0]
+        rest = teacher[res].shape[0] - at
+        if rest:
+            teacher[res][at:] = jnp.zeros((rest, teacher[res].shape[1]), F32)
     me = lax.axis_index("space")
     z, x = lax.div(me, group), lax.rem(me, group)
     greet_barrier = pltpu.get_barrier_semaphore()
@@ -1063,19 +1085,18 @@
 
     @pl.when(pl.program_id(0) == pl.num_programs(0) - 1)
     def _():
-        turned = kernel_ref[...].T
         for a in range(3):
             for b in range(3):
                 tap = jnp.zeros((CS_OUT, CS_OUT), F32)
                 for q in range(4):
-                    row = a * 512 + (q + b + 1) * CS_OUT
-                    tap = tap + turned[row : row + CS_OUT, q * CS_OUT : (q + 1) * CS_OUT]
+                    lane = a * 512 + (q + b + 1) * CS_OUT
+                    tap = tap + kernel_ref[q * CS_OUT : (q + 1) * CS_OUT, lane : lane + CS_OUT]
                 row = (3 * a + b) * CS_OUT
                 second_ref[row : row + CS_OUT] = tap
-        tap = jnp.zeros((CS_IN, CS_OUT), F32)
+        tap = jnp.zeros((CS_OUT, CS_IN), F32)
         for q in range(4):
-            row = 1536 + 2 * q * CS_IN
-            tap = tap + turned[row : row + CS_IN, q * CS_OUT : (q + 1) * CS_OUT]
+            lane = 1536 + 2 * q * CS_IN
+            tap = tap + kernel_ref[q * CS_OUT : (q + 1) * CS_OUT, lane : lane + CS_IN]
         shortcut_ref[...] = tap
 
 
@@ -1090,7 +1111,7 @@
     ]
     stats = shape_of((8, 128), F32)
     second = shape_of((9 * CS_OUT, CS_OUT), F32)
-    shortcut = shape_of((CS_IN, CS_OUT), F32)
+    shortcut = shape_of((CS_OUT, CS_IN), F32)
     return pl.pallas_call(
         functools.partial(back_kernel, p_rows, 4),
         grid_spec=pltpu.PrefetchScalarGridSpec(
@@ -1208,15 +1229,14 @@
 
     @pl.when(pl.program_id(0) == pl.num_programs(0) - 1)
     def _():
-        turned = kernel_ref[...].T
         for a in range(3):
             for b in range(3):
-                tap = jnp.zeros((CS_IN, CS_OUT), F32)
+                tap = jnp.zeros((CS_OUT, CS_IN), F32)
                 for q in range(4):
-                    row = a * 384 + (2 * q + b + 3) * CS_IN
-                    tap = tap + turned[row : row + CS_IN, q * CS_OUT : (q + 1) * CS_OUT]
-                row = (3 * a + b) * CS_IN
-                taps_ref[row : row + CS_IN] = tap
+                    lane = a * 384 + (2 * q + b + 3) * CS_IN
+                    tap = tap + kernel_ref[q * CS_OUT : (q + 1) * CS_OUT, lane : lane + CS_IN]
+                row = (3 * a + b) * CS_OUT
+                taps_ref[row : row + CS_OUT] = tap
 
 
 def student_entry(
@@ -1226,7 +1246,7 @@
     rows, images, lanes = flow.shape
     p_rows = rows - 1
     outs = [shape_of((2 * p_rows // group, images, lanes), BF16)] * group
-    taps = shape_of((9 * CS_IN, CS_OUT), F32)
+    taps = shape_of((9 * CS_OUT, CS_IN), F32)
     stats = shape_of((8, 128), F32)
     big = (flow, first_out, grad, even, odd, raw)
     shared = (tot, inner, pulled, norm_in, norm, weights_even, weights_odd)
@@ -1462,16 +1482,12 @@
         return lax.all_to_all(array, "space", 0, 0, axis_index_groups=by_slab, tiled=True)
 
     subs = [(x + d) % group for d in range(group)]
-    picked = [[rows_first(pick_images(pixels[res], res, sub)) for sub in subs] for res in both]
-    arrived = [
-        [picked[res][0]] + [send(picked[res][d], to_sub(d)) for d in range(1, group)]
-        for res in both
-    ]
-
+    picked_small = [rows_first(pick_images(small_in, 0, sub)) for sub in subs]
+    cots_here = after(cots, picked_small[1:])
     narrow = cots[0].shape[2]
     cot_stacks = []
     for res in both:
-        c = jnp.pad(rows_first(cots[res]), ((1, 2), (0, 0), (0, 0)))
+        c = jnp.pad(rows_first(cots_here[res]), ((1, 2), (0, 0), (0, 0)))
         count = p_counts[res]
         c = jnp.stack([c[k * count : (k + 1) * count + 3] for k in range(slabs)])
         if c.shape[3] > narrow:
@@ -1483,6 +1499,14 @@
     cot_flat = jnp.concatenate(flat, axis=1)
     cots_ready = cot_flat
     cot_flat = among_slabs(cot_flat, 0)
+    large_source = after(large_in, cots_ready)
+    picked_large = [rows_first(pick_images(large_source, 1, sub)) for sub in subs]
+    picked = [picked_small, picked_large]
+    arrived = [
+        [picked[res][0]] + [send(picked[res][d], to_sub(d)) for d in range(1, group)]
+        for res in both
+    ]
+
 
     gains = jnp.tile(teacher_gains, (1, max(t.shape[2] for t in teachers) // CT_IN))
 
@@ -1495,7 +1519,7 @@
     own_large = pick_images(large_raw_in, 1, x)
     away_large = [pick_images(large_raw_in, 1, sub) for sub in subs[1:]]
     cut = min(16, images[1])
-    sizes = [cut, -(-(images[1] - cut) // 16) * 16]
+    sizes = [cut, images[1] - cut]
     ranges = [(0, cut), (cut, images[1])]
 
     def large_part(k, *others):
@@ -1508,7 +1532,8 @@
 
     stat_tables = [label_table(res, sub, images[res]) for res in both for sub in subs]
     entry_sums = input_stats(picked[0] + picked[1], stat_tables)
-    large_own = [activated(own_large[lo:hi], size) for (lo, hi), size in zip(ranges, sizes)]
+    (lo, hi), size = ranges[0], sizes[0]
+    large_own = [activated(own_large[lo:hi], size)]
     raw_edges = [edge_rows(arrived[res], 6) for res in both]
     corners = lambda parts: [p[:1, :, :128] for p in parts]
     waits = ([p[1:] for p in arrived], cot_flat, corners(large_raw[0]), large_own, raw_edges)
@@ -1517,10 +1542,7 @@
     raw_halos = [to_neighbours(after(raw_edges[res], entry_total)) for res in both]
     large_raw.append(large_part(1, entry_total))
     large_pieces = [
-        [own] + [activated(after(p, *others), size) for p in raw]
-        for own, size, raw, others in zip(
-            large_own, sizes, large_raw, ([entry_total], [])
-        )
+        [large_own[0]] + [activated(after(p, entry_total), sizes[0]) for p in large_raw[0]]
     ]
 
     def large_edges_of(k, *others):
@@ -1544,7 +1566,7 @@
         return part.reshape(local_rows[0], len(ks) * per_device[0], lanes)
 
     small_away = [[small_part(ks, sub) for sub in subs[1:]] for ks in parts_of]
-    bands = banded_kernels(*after((first_conv, second_conv, shortcut), large_raw_in))
+    bands = banded_kernels(*after((first_conv, second_conv, shortcut), entry_total))
     bands_first, bands_second, bands_second_back, bands_even, bands_odd, gather, scatter = bands
     raws, evens, odds, firsts, first_sums = ([None, None] for _ in range(5))
     for res in (1, 0):
@@ -1580,6 +1602,10 @@
         first_sums[res] = sums
     inner_total = total_over_devices(first_sums, axes, 1, (corners(large_raw[1]), large_edges))
 
+    (lo, hi), size = ranges[1], sizes[1]
+    large_pieces.append(
+        [activated(after(p, inner_total), size) for p in (own_large[lo:hi], *large_raw[1])]
+    )
     large_edges.append(large_edges_of(1, inner_total))
     small_pieces = [
         [send(after(p, inner_total), to_sub(d + 1)) for d, p in enumerate(away)]
@@ -1620,7 +1646,7 @@
         pieces = large_pieces[k]
         own = after(pieces[0], *others)
         edges = [pad_to(h, sizes[k]) for h in large_edges[k]]
-        return teacher_energies(place, own, 0, pieces[1:], *edges, shared, tiles[1])
+        return teacher_energies(place, own, 0, pieces[1:], *edges, shared, sizes[k])
 
     def small_map(n, edges, *others):
         arrays = after((*small_pieces[n], *edges), *others)
@@ -1716,7 +1742,6 @@
         rows_in = jnp.stack(ordered).reshape(group, rows, slabs, per_device[res], lanes)
         return jnp.transpose(rows_in, (2, 0, 3, 1, 4)).reshape(n, rows, lanes)
 
-    arrived_rows = [native_rows(0)]
     rate_scale = 1.0 / math.sqrt(total_positions)
     flat = lambda k: k.reshape(-1, k.shape[-1])
     kernel_states = [
@@ -1724,21 +1749,23 @@
         [flat(k) for k in (second_conv, momentum_second, average_second)],
         [shortcut, momentum_shortcut, average_shortcut],
     ]
-    first_state, second_state, bypass_state, entry_state, image_tables, total_loss = finish(
+    packed = gradient_sum(
         [first_parts, second_parts, shortcut_parts, entry_flow_sums, [loss_sums]],
+        axes,
+        4,
+        (entry_parts[0][1:], entry_parts[1]),
+    )
+    first_state, second_state, bypass_state, entry_state, image_tables, total_loss = update(
+        packed,
         kernel_states,
         [entry_norm, momentum_entry, average_entry],
         entry_total,
         norm_in,
         (CONV_RATE * rate_scale, NORM_RATE * rate_scale, 1.0 / total_positions),
-        axes,
-        4,
-        (entry_parts[0][1:], entry_parts[1]),
     )
     rows = entry_parts[1]
-    rows[1:] = [send(after(r, image_tables), to_sub(d + 1)) for d, r in enumerate(rows[1:])]
-    arrived_rows.append(native_rows(1))
-    out_parts.append(to_owners(1, image_tables))
+    rows[1:] = [send(after(r, packed), to_sub(d + 1)) for d, r in enumerate(rows[1:])]
+    out_parts.append(to_owners(1, packed))
     first_state = [k.reshape(first_conv.shape) for k in first_state]
     second_state = [k.reshape(second_conv.shape) for k in second_state]
     inner_folded = flow_total.reshape(8, 128 // CS_OUT, CS_OUT).sum(axis=1)
@@ -1747,14 +1774,19 @@
     for res in both:
         low = jnp.transpose(out_parts[res], (2, 0, 1, 3))
         block_outs.append(low.reshape(low.shape[0], -1, low.shape[3]))
-
+    def wide_rows(lanes):
+        wide = jnp.tile(image_tables, (1, lanes // 128))
+        return [wide[k] for k in range(8)]
+
+    wide = [wide_rows(p.shape[2]) for p in pixels]
+    arrived_rows = [native_rows(0)]
+    entry_parts[1] = after(entry_parts[1], block_outs, wide[1])
+    arrived_rows.append(native_rows(1))
     input_grads = []
     for res in both:
-        lanes = pixels[res].shape[2]
         one = (labels[res] == 1)[:, None, None]
-        wide = jnp.tile(image_tables, (1, lanes // 128))
         gain, bias, slope, level = [
-            jnp.where(one, wide[2 * k + 1], wide[2 * k]) for k in range(4)
+            jnp.where(one, wide[res][2 * k + 1], wide[res][2 * k]) for k in range(4)
         ]
         value = pixels[res].astype(F32)
         before = value * gain + bias

time: 610 us -> 590 us (0.967)
  local copies, waits for them, and re-layouts: 143 us -> 121 us
    unnamed x151 -> x120, local copies, waits for them, and re-layouts: 28.2 us -> 20 us
    pad x9 -> x5, local copies, waits for them, and re-layouts: 17 us -> 10.6 us  [pad_to(): return jnp.pad(array, ((0, 0), (0, extra), (0, 0))) if extra else array]
    optimization_barrier x2 -> x3, local copies, waits for them, and re-layouts: 7.07 us -> 12.4 us  [after(): return lax.optimization_barrier((value, others))[0]]
    pallas_call x1 -> x2, Pallas kernels: 20.8 us -> 24.1 us  [the longest x1 20.8 us: gradient_sum(): pl.pallas_call(functools.partial(gradient_sum_kernel, axes, tuple(layout)...]
    transpose x4 -> x3, other arithmetic: 13 us -> 12.3 us  [rows_first(): return jnp.transpose(array, (1, 0, 2))]
  transfers between devices with their start and end apart: 26 -> 26, of which waited for: 8 -> 9; matrix products, arithmetic and copies ran while one was open for 30% -> 27% of each run, Pallas kernels for 33% -> 34%
where the time goes in v4:
time: 590 us; the launch traced here: 582 us
  Pallas kernels  291 us (49%)
  local copies, waits for them, and re-layouts  121 us (21%)
  other arithmetic  72.9 us (12%)
  waiting for transfers between devices  58.1 us (10%)
  starting transfers between devices  37 us (6%)
    pallas_call x5, Pallas kernels, teacher_energies(): pl.pallas_call(functools.partial(teacher_kernel, p_rows, width, group, 4)...  97.3 us
    pallas_call x3, Pallas kernels, total_over_devices(): pl.pallas_call(functools.partial(total_kernel, axes, len(parts)), out_sha...  33.1 us
    pallas_call x2, Pallas kernels, student_block(): pl.pallas_call(functools.partial(block_kernel, p_rows, 4), grid_spec=pltp...  33 us
    ppermute x14, waiting for transfers between devices, to_neighbours(): lax.ppermute(r, ('batch', 'space'), pairs)  28.7 us
    pallas_call x2, Pallas kernels, student_forward(): pl.pallas_call(functools.partial(forward_kernel, p_rows, group, 4), grid_...  27.9 us
    pallas_call x2, Pallas kernels, student_entry(): pl.pallas_call(functools.partial(entry_kernel, p_rows, 4), grid_spec=pltp...  27.8 us
    pallas_call x2, Pallas kernels, student_back(): pl.pallas_call(functools.partial(back_kernel, p_rows, 4), grid_spec=pltpu...  27.4 us
    pallas_call x1, Pallas kernels, gradient_sum(): pl.pallas_call(functools.partial(gradient_sum_kernel, axes, tuple(layout)...  20.8 us
  transfers between devices with their start and end apart: 26, of which 9 were waited for; matrix products, arithmetic and copies ran while one was open for 27% of the time, Pallas kernels for 34%

profile of v4, /device:TPU:0, one launch (start us, length us, event | category | flops | bytes accessed | tf_op | source)
XLA Modules:
  0.0 582.5 jit_solution(18232204735889501246)
XLA Ops:
  26.9 9.4 %constant_dynamic-slice_fusion.5 = (bf16[4,1,10,8,8192]{4,3,2,1,0:T(8,128)(2,1)}, bf16[4,1,10,8,8192]{4,3,2,1,0:T(8,128)(2,1)}) fusion(bf16[4,2,10,8,8192]{4,3,2,1,0:T(8,128)(2,1)} %bitcast.256, s32[]{:T(128)S(6)} %select_n.393, s32[]{:T(128)S(6)} %select_n.381), kind=kLoop, calls=%fused_computation.117 | loop fusion | bytes 20971528 | tf_op jit(solution)/shard_map/jit(dynamic_index_in_dim)/dynamic_slice | solution.py:1424
  68.3 13.0 %multiply_convert_fusion = bf16[320,4,4096]{2,0,1:T(8,128)(2,1)} fusion(bf16[320,4,4096]{2,1,0:T(4,128)(2,1)} %param.30, f32[4096]{0:T(1024)S(1)} %bitcast.285, f32[4096]{0:T(1024)S(1)} %bitcast.284), kind=kLoop, calls=%fused_computation | loop fusion | flops 41943040 | bytes 21004288 | tf_op jit(solution)/shard_map/convert_element_type | solution.py:1555
  115.0 11.1 %shard_map.484.refs_5_.tot.refs_1_ = f32[8,128]{1,0:T(8,128)} custom-call(f32[8,128]{1,0:T(8,128)} %shard_map.483.refs_0_, bf16[4,160,1024]{2,1,0:T(8,128)(2,1)} %collective-permute-done.refs_1_, bf16[8,40,2048]{2,1,0:T(8,128)(2,1)} %copy-done.11, bf16[4,500,1024]{2,1,0:T(8,128)(2,1)} %all-to-all-done.refs_3_, bf16[1,8,128]{2,1,0:T(8,128)(2,1)} %copy.195.refs_4_, ...), custom_call_target="tpu_custom_call" | custom-call | flops 12000000000 | bytes 1048576 | tf_op jit(solution)/shard_map/pallas_call | solution.py:219
  157.2 13.3 %shard_map.486 = (bf16[16,48,2048]{2,1,0:T(8,128)(2,1)}, bf16[9,48,2176]{2,1,0:T(8,128)(2,1)}, bf16[11,48,2176]{2,1,0:T(8,128)(2,1)}, f32[13,48,2048]{2,1,0:T(8,128)}, f32[8,128]{1,0:T(8,128)}) custom-call(s32[2]{0:T(128)} %pad_add_fusion.place, bf16[8,48,2048]{2,1,0:T(8,128)(2,1)} %pad.32.refs_0_, bf16[8,48,2048]{2,1,0:T(8,128)(2,1)} %pad.33.refs_1_, ...), custom_call_target="tpu_custom_call" | custom-call | flops 15000000512 | bytes 1048576 | tf_op jit(solution)/shard_map/pallas_call | solution.py:712
  194.6 14.6 %shard_map.487 = (bf16[8,160,1024]{2,1,0:T(8,128)(2,1)}, bf16[5,160,1152]{2,1,0:T(8,128)(2,1)}, bf16[7,160,1152]{2,1,0:T(8,128)(2,1)}, f32[9,160,1024]{2,1,0:T(8,128)}, f32[8,128]{1,0:T(8,128)}) custom-call(s32[2]{0:T(128)} %pad_add_fusion.place, bf16[4,160,1024]{2,1,0:T(8,128)(2,1)} %bitcast.252, bf16[4,160,1024]{2,1,0:T(8,128)(2,1)} %collective-permute-done.refs_1_, ...), custom_call_target="tpu_custom_call" | custom-call | flops 15000000512 | bytes 1048576 | tf_op jit(solution)/shard_map/pallas_call | solution.py:712
  210.6 11.0 %shard_map.488.inner = f32[8,128]{1,0:T(8,128)} custom-call(f32[8,128]{1,0:T(8,128)} %get-tuple-element.161.refs_0_, f32[8,128]{1,0:T(8,128)} %get-tuple-element.153.refs_1_, bf16[1,8,128]{2,1,0:T(8,128)(2,1)} %copy.204.refs_2_, bf16[3,16,8192]{2,1,0:T(8,128)(2,1)} %collective-permute-done.8.refs_3_.refs_2_, ...), custom_call_target="tpu_custom_call" | custom-call | flops 12000000000 | bytes 1048576 | tf_op jit(solution)/shard_map/pallas_call | solution.py:219
  233.5 17.8 %shard_map.490 = (bf16[10,48,2304]{2,1,0:T(8,128)(2,1)}, f32[9,48,2048]{2,1,0:T(8,128)}, f32[11,48,2048]{2,1,0:T(8,128)}, bf16[8,48,2048]{2,1,0:T(8,128)(2,1)}, f32[48,384]{1,0:T(8,128)}) custom-call(s32[2]{0:T(128)} %pad_add_fusion.place, f32[13,48,2048]{2,1,0:T(8,128)} %get-tuple-element.170.first_ref, bf16[11,48,2176]{2,1,0:T(8,128)(2,1)} %get-tuple-element.171.odd, ...), custom_call_target="tpu_custom_call" | custom-call | flops 17999998976 | bytes 1048576 | tf_op jit(solution)/shard_map/pallas_call | solution.py:800
  251.2 15.2 %shard_map.489 = (bf16[6,160,1280]{2,1,0:T(8,128)(2,1)}, f32[5,160,1024]{2,1,0:T(8,128)}, f32[7,160,1024]{2,1,0:T(8,128)}, bf16[4,160,1024]{2,1,0:T(8,128)(2,1)}, f32[160,128]{1,0:T(8,128)}) custom-call(s32[2]{0:T(128)} %pad_add_fusion.place, f32[9,160,1024]{2,1,0:T(8,128)} %get-tuple-element.159.first_ref, bf16[7,160,1152]{2,1,0:T(8,128)(2,1)} %get-tuple-element.160.odd, ...), custom_call_target="tpu_custom_call" | custom-call | flops 17999998976 | bytes 1048576 | tf_op jit(solution)/shard_map/pallas_call | solution.py:800
  266.5 18.1 %shard_map.491.refs_7_ = f32[16,384]{1,0:T(8,128)} custom-call(s32[2]{0:T(128)} %pad_add_fusion.place, bf16[8,16,8192]{2,1,0:T(8,128)(2,1)} %fusion.26.refs_5_.refs_0_, bf16[8,16,8192]{2,1,0:T(8,128)(2,1)} %copy-done.15, bf16[3,16,8192]{2,1,0:T(8,128)(2,1)} %collective-permute-done.8.refs_3_.refs_2_, ...), custom_call_target="tpu_custom_call" | custom-call | flops 16000000000 | bytes 1048576 | tf_op jit(solution)/shard_map/pallas_call | solution.py:544
  296.4 28.0 %shard_map.492.refs_8_ = f32[24,384]{1,0:T(8,128)} custom-call(s32[2]{0:T(128)} %pad_add_fusion.place, bf16[8,24,8192]{2,1,0:T(8,128)(2,1)} %copy-done.9, bf16[8,24,8192]{2,1,0:T(8,128)(2,1)} %copy-done.8, bf16[3,24,8192]{2,1,0:T(8,128)(2,1)} %collective-permute-done.14.refs_2_, bf16[3,24,8192]{2,1,0:T(8,128)(2,1)} %collective-permute-done.15.refs_3_, ...), custom_call_target="tpu_custom_call" | custom-call | flops 24000000000 | bytes 1048576 | tf_op jit(solution)/shard_map/pallas_call | solution.py:544
  327.4 12.9 %collective-permute-done.11.refs_2_ = bf16[3,80,4096]{2,1,0:T(8,128)(2,1)S(1)} collective-permute-done((bf16[3,80,4096]{2,1,0:T(8,128)(2,1)}, bf16[3,80,4096]{2,1,0:T(8,128)(2,1)S(1)}, u32[]{:S(2)}, u32[]{:S(2)}) %collective-permute-start.11) | collective-permute-done | bytes 1966112 | tf_op jit(solution)/shard_map/ppermute | solution.py:1458
  342.9 23.6 %shard_map.493.refs_4_ = f32[80,128]{1,0:T(8,128)} custom-call(s32[2]{0:T(128)} %pad_add_fusion.place, bf16[4,4,2,40,4096]{4,3,2,1,0:T(8,128)(2,1)} %bitcast.236, bf16[4,80,4096]{2,1,0:T(8,128)(2,1)} %copy-done.16, bf16[3,80,4096]{2,1,0:T(8,128)(2,1)} %copy-done.50, bf16[3,80,4096]{2,1,0:T(8,128)(2,1)} %copy-done.51, bf16[1152,256]{1,0:T(8,128)(2,1)} %bitcast.295, ...), custom_call_target="tpu_custom_call" | custom-call | flops 20000000000 | bytes 1048576 | tf_op jit(solution)/shard_map/pallas_call | solution.py:544
  371.5 13.8 %shard_map.494.refs_5_ = f32[40,128]{1,0:T(8,128)} custom-call(s32[2]{0:T(128)} %pad_add_fusion.place, bf16[4,4,2,40,4096]{4,3,2,1,0:T(8,128)(2,1)} %bitcast.238, bf16[4,40,4096]{2,1,0:T(8,128)(2,1)} %collective-permute-done.13.refs_1_, bf16[3,40,4096]{2,1,0:T(8,128)(2,1)} %collective-permute-done.16.refs_2_, ...), custom_call_target="tpu_custom_call" | custom-call | flops 10000000000 | bytes 1048576 | tf_op jit(solution)/shard_map/pallas_call | solution.py:544
  389.0 13.8 %shard_map.495.refs_6_ = f32[40,128]{1,0:T(8,128)} custom-call(s32[2]{0:T(128)} %pad_add_fusion.place, bf16[4,4,2,40,4096]{4,3,2,1,0:T(8,128)(2,1)} %bitcast.239, bf16[4,40,4096]{2,1,0:T(8,128)(2,1)} %copy-done.23, bf16[3,40,4096]{2,1,0:T(8,128)(2,1)} %copy-done.52, bf16[3,40,4096]{2,1,0:T(8,128)(2,1)} %copy-done.53, bf16[1152,256]{1,0:T(8,128)(2,1)} %bitcast.297, ...), custom_call_target="tpu_custom_call" | custom-call | flops 10000000000 | bytes 1048576 | tf_op jit(solution)/shard_map/pallas_call | solution.py:544
  402.7 11.1 %shard_map.496 = (f32[160,128]{1,0:T(8,128)}, f32[48,384]{1,0:T(8,128)}, f32[8,128]{1,0:T(8,128)}) custom-call(f32[160,128]{1,0:T(8,128)} %get-tuple-element.169.refs_0_, f32[48,384]{1,0:T(8,128)} %get-tuple-element.172.refs_1_, f32[160,128]{1,0:T(8,128)} %broadcast_in_dim.161.refs_4_.label_ref.refs_2_, ...), custom_call_target="tpu_custom_call" | custom-call | flops 11000000512 | bytes 1048576 | tf_op jit(solution)/shard_map/pallas_call | solution.py:976
  418.8 13.4 %shard_map.498 = (f32[9,48,2048]{2,1,0:T(8,128)}, bf16[8,48,2048]{2,1,0:T(8,128)(2,1)}, f32[8,128]{1,0:T(8,128)}, f32[576,64]{1,0:T(8,128)}, f32[64,32]{1,0:T(8,128)}) custom-call(s32[2]{0:T(128)} %pad_add_fusion.place, f32[11,48,2048]{2,1,0:T(8,128)} %get-tuple-element.209.sum_ref, bf16[11,48,2048]{2,1,0:T(8,128)(2,1)} %pad.37.cot, ...), custom_call_target="tpu_custom_call" | custom-call | flops 17999998976 | bytes 1048576 | tf_op jit(solution)/shard_map/pallas_call | solution.py:1115
  432.3 14.0 %shard_map.497 = (f32[5,160,1024]{2,1,0:T(8,128)}, bf16[4,160,1024]{2,1,0:T(8,128)(2,1)}, f32[8,128]{1,0:T(8,128)}, f32[576,64]{1,0:T(8,128)}, f32[64,32]{1,0:T(8,128)}) custom-call(s32[2]{0:T(128)} %pad_add_fusion.place, f32[7,160,1024]{2,1,0:T(8,128)} %get-tuple-element.198.sum_ref, bf16[7,160,1024]{2,1,0:T(8,128)(2,1)} %bitcast.275, ...), custom_call_target="tpu_custom_call" | custom-call | flops 17999998976 | bytes 1048576 | tf_op jit(solution)/shard_map/pallas_call | solution.py:1115
  448.0 11.0 %shard_map.499.pulled = f32[8,128]{1,0:T(8,128)} custom-call(f32[8,128]{1,0:T(8,128)} %get-tuple-element.208.refs_0_, f32[8,128]{1,0:T(8,128)} %get-tuple-element.213.refs_1_, bf16[4,4,40,1024]{3,2,1,0:T(8,128)(2,1)} %copy-done.19), custom_call_target="tpu_custom_call" | custom-call | flops 12000000000 | bytes 1048576 | tf_op jit(solution)/shard_map/pallas_call | solution.py:219
  459.8 13.3 %shard_map.500 = (bf16[4,160,1024]{2,1,0:T(8,128)(2,1)}, bf16[4,160,1024]{2,1,0:T(8,128)(2,1)}, f32[576,32]{1,0:T(8,128)}, f32[8,128]{1,0:T(8,128)}) custom-call(s32[2]{0:T(128)} %pad_add_fusion.place, f32[5,160,1024]{2,1,0:T(8,128)} %get-tuple-element.204.flow_ref, f32[5,160,1024]{2,1,0:T(8,128)} %get-tuple-element.201.first_ref, ...), custom_call_target="tpu_custom_call" | custom-call | flops 16000000000 | bytes 1048576 | tf_op jit(solution)/shard_map/pallas_call | solution.py:1253
  473.9 14.5 %shard_map.501 = (bf16[8,48,2048]{2,1,0:T(8,128)(2,1)}, bf16[8,48,2048]{2,1,0:T(8,128)(2,1)}, f32[576,32]{1,0:T(8,128)}, f32[8,128]{1,0:T(8,128)}) custom-call(s32[2]{0:T(128)} %pad_add_fusion.place, f32[9,48,2048]{2,1,0:T(8,128)} %get-tuple-element.219.flow_ref, f32[9,48,2048]{2,1,0:T(8,128)} %get-tuple-element.211.first_ref, ...), custom_call_target="tpu_custom_call" | custom-call | flops 16000000000 | bytes 1048576 | tf_op jit(solution)/shard_map/pallas_call | solution.py:1253
  494.8 9.4 %collective-permute-done.21.refs_9_ = bf16[4,160,1024]{2,1,0:T(8,128)(2,1)S(1)} collective-permute-done((bf16[4,160,1024]{2,1,0:T(8,128)(2,1)}, bf16[4,160,1024]{2,1,0:T(8,128)(2,1)S(1)}, u32[]{:S(2)}, u32[]{:S(2)}) %collective-permute-start.21) | collective-permute-done | bytes 1310752 | tf_op jit(solution)/shard_map/ppermute | solution.py:1419
  505.3 20.8 %shard_map.502.refs_0_ = f32[512,128]{1,0:T(8,128)} custom-call(f32[576,32]{1,0:T(8,128)} %get-tuple-element.216.refs_0_, f32[576,32]{1,0:T(8,128)} %get-tuple-element.223.refs_1_, f32[576,64]{1,0:T(8,128)} %get-tuple-element.224.refs_2_, f32[576,64]{1,0:T(8,128)} %get-tuple-element.225.refs_3_, f32[64,32]{1,0:T(8,128)} %get-tuple-element.226.refs_4_, ...), custom_call_target="tpu_custom_call" | custom-call | flops 20000000000 | bytes 1048576 | tf_op jit(solution)/shard_map/pallas_call | solution.py:379
  546.5 10.1 %fusion.10 = f32[320,4,1024]{2,1,0:T(4,128)} fusion(bf16[320,4,1024]{2,1,0:T(4,128)(2,1)S(1)} %copy-done.5, f32[4,2,40,4,1024]{4,3,2,1,0:T(4,128)S(1)} %copy.212, f32[320,1024]{1,0:T(8,128)S(1)} %get-tuple-element.479, f32[320,1024]{1,0:T(8,128)S(1)} %get-tuple-element.478, f32[320,1024]{1,0:T(8,128)S(1)} %get-tuple-element.477, ...), kind=kLoop, calls=%fused_computation.17 | loop fusion | flops 19660800 | bytes 18350080 | tf_op jit(solution)/shard_map/add | solution.py:1795
  558.1 12.2 %all-to-all-done.2 = bf16[4,8,10,2048]{3,1,2,0:T(8,128)(2,1)S(1)} async-done(((bf16[4,8,10,2048]{3,1,2,0:T(8,128)(2,1)}), bf16[4,8,10,2048]{3,1,2,0:T(8,128)(2,1)S(1)}, u32[]{:S(2)}, u32[]{:S(2)}) %all-to-all-start.2) | async-done | bytes 1310752 | tf_op jit(solution)/shard_map/all_to_all | solution.py:1482
  (300 shorter events, 234.9 us)
Async XLA Ops:
  5.8 99.0 %collective-permute-start = (bf16[4,160,1024]{2,1,0:T(8,128)(2,1)}, bf16[4,160,1024]{2,1,0:T(8,128)(2,1)}, u32[]{:S(2)}, u32[]{:S(2)}) collective-permute-start(bf16[4,160,1024]{2,1,0:T(8,128)(2,1)} %bitcast.6.refs_1_), channel_id=1, source_target_pairs={{0,1},{1,0},{2,3},{3,2},{4,5},{5,4},{6,7},{7,6},{8,9},{9,8},{10,11... | collective-permute-start | bytes 3932168 | tf_op jit(solution)/shard_map/ppermute | solution.py:1419
  17.6 97.4 %all-to-all-start = ((bf16[4,500,1024]{2,1,0:T(8,128)(2,1)}), bf16[4,500,1024]{2,1,0:T(8,128)(2,1)}, u32[]{:S(2)}, u32[]{:S(2)}) async-start(bf16[4,500,1024]{2,1,0:T(8,128)(2,1)} %pad_maximum_fusion), calls=%async_computation | async-start | bytes 8257536 | tf_op jit(solution)/shard_map/all_to_all | solution.py:1482
  26.3 77.2 %collective-permute-start.1 = (bf16[8,40,2048]{2,1,0:T(8,128)(2,1)}, bf16[8,40,2048]{2,1,0:T(8,128)(2,1)S(1)}, u32[]{:S(2)}, u32[]{:S(2)}) collective-permute-start(bf16[8,40,2048]{2,1,0:T(8,128)(2,1)} %bitcast.231.refs_3_), channel_id=1, source_target_pairs={{0,1},{1,0},{2,3},{3,2},{4,5},{5,4},{6,7},{7,6},{8,9},{9,8},{10,11... | collective-permute-start | bytes 3932168 | tf_op jit(solution)/shard_map/ppermute | solution.py:1419
  40.5 72.0 %collective-permute-start.2 = (bf16[16,8,8192]{2,0,1:T(8,128)(2,1)}, bf16[16,8,8192]{2,0,1:T(8,128)(2,1)}, u32[]{:S(2)}, u32[]{:S(2)}) collective-permute-start(bf16[16,8,8192]{2,0,1:T(8,128)(2,1)} %copy.219), channel_id=1, source_target_pairs={{0,1},{1,0},{2,3},{3,2},{4,5},{5,4},{6,7},{7,6},{8,9},{9,8},{10,11... | collective-permute-start | bytes 6291464 | tf_op jit(solution)/shard_map/ppermute | solution.py:1419
  126.9 24.9 %collective-permute-start.3 = (bf16[6,40,2048]{2,1,0:T(8,128)(2,1)}, bf16[6,40,2048]{2,1,0:T(8,128)(2,1)}, u32[]{:S(2)}, u32[]{:S(2)}) collective-permute-start(bf16[6,40,2048]{2,1,0:T(8,128)(2,1)} %get-tuple-element.147.refs_8_), channel_id=1, source_target_pairs={{0,2},{1,3},{2,0},{3,1},{4,6},{5,7},{6,4},{7,5},{8,10},{9,11},{10,... | collective-permute-start | bytes 2949128 | tf_op jit(solution)/shard_map/ppermute | solution.py:1458
  127.7 26.4 %collective-permute-start.4 = (bf16[6,40,2048]{2,1,0:T(8,128)(2,1)S(1)}, bf16[6,40,2048]{2,1,0:T(8,128)(2,1)}, u32[]{:S(2)}, u32[]{:S(2)}) collective-permute-start(bf16[6,40,2048]{2,1,0:T(8,128)(2,1)S(1)} %copy-done.32), channel_id=1, source_target_pairs={{0,8},{1,9},{2,4},{3,5},{4,2},{5,3},{6,14},{7,15},{8,0},{9,1},{10,... | collective-permute-start | bytes 2949128 | tf_op jit(solution)/shard_map/ppermute | solution.py:1458
  134.5 74.7 %collective-permute-start.7 = (bf16[24,8,8192]{2,0,1:T(8,128)(2,1)}, bf16[24,8,8192]{2,0,1:T(8,128)(2,1)}, u32[]{:S(2)}, u32[]{:S(2)}) collective-permute-start(bf16[24,8,8192]{2,0,1:T(8,128)(2,1)} %copy.221), channel_id=1, source_target_pairs={{0,1},{1,0},{2,3},{3,2},{4,5},{5,4},{6,7},{7,6},{8,9},{9,8},{10,11... | collective-permute-start | bytes 9437192 | tf_op jit(solution)/shard_map/ppermute | solution.py:1419
  135.1 58.8 %collective-permute-start.5 = (bf16[6,160,1024]{2,1,0:T(8,128)(2,1)}, bf16[6,160,1024]{2,1,0:T(8,128)(2,1)}, u32[]{:S(2)}, u32[]{:S(2)}) collective-permute-start(bf16[6,160,1024]{2,1,0:T(8,128)(2,1)} %get-tuple-element.157.refs_6_), channel_id=1, source_target_pairs={{0,2},{1,3},{2,0},{3,1},{4,6},{5,7},{6,4},{7,5},{8,10},{9,11},{10,... | collective-permute-start | bytes 5898248 | tf_op jit(solution)/shard_map/ppermute | solution.py:1458
  138.2 55.7 %collective-permute-start.6 = (bf16[6,160,1024]{2,1,0:T(8,128)(2,1)}, bf16[6,160,1024]{2,1,0:T(8,128)(2,1)}, u32[]{:S(2)}, u32[]{:S(2)}) collective-permute-start(bf16[6,160,1024]{2,1,0:T(8,128)(2,1)} %get-tuple-element.158.refs_7_), channel_id=1, source_target_pairs={{0,8},{1,9},{2,4},{3,5},{4,2},{5,3},{6,14},{7,15},{8,0},{9,1},{10,... | collective-permute-start | bytes 5898248 | tf_op jit(solution)/shard_map/ppermute | solution.py:1458
  176.9 33.6 %collective-permute-start.8 = (bf16[3,16,8192]{2,1,0:T(8,128)(2,1)}, bf16[3,16,8192]{2,1,0:T(8,128)(2,1)}, u32[]{:S(2)}, u32[]{:S(2)}) collective-permute-start(bf16[3,16,8192]{2,1,0:T(8,128)(2,1)} %get-tuple-element.425), channel_id=1, source_target_pairs={{0,2},{1,3},{2,0},{3,1},{4,6},{5,7},{6,4},{7,5},{8,10},{9,11},{10,... | collective-permute-start | bytes 2359304 | tf_op jit(solution)/shard_map/ppermute | solution.py:1458
  177.9 32.7 %collective-permute-start.9 = (bf16[3,16,8192]{2,1,0:T(8,128)(2,1)}, bf16[3,16,8192]{2,1,0:T(8,128)(2,1)}, u32[]{:S(2)}, u32[]{:S(2)}) collective-permute-start(bf16[3,16,8192]{2,1,0:T(8,128)(2,1)} %get-tuple-element.424), channel_id=1, source_target_pairs={{0,8},{1,9},{2,4},{3,5},{4,2},{5,3},{6,14},{7,15},{8,0},{9,1},{10,... | collective-permute-start | bytes 2359304 | tf_op jit(solution)/shard_map/ppermute | solution.py:1458
  230.0 66.4 %collective-permute-start.14 = (bf16[3,24,8192]{2,1,0:T(8,128)(2,1)}, bf16[3,24,8192]{2,1,0:T(8,128)(2,1)}, u32[]{:S(2)}, u32[]{:S(2)}) collective-permute-start(bf16[3,24,8192]{2,1,0:T(8,128)(2,1)} %get-tuple-element.423), channel_id=1, source_target_pairs={{0,2},{1,3},{2,0},{3,1},{4,6},{5,7},{6,4},{7,5},{8,10},{9,11},{10,... | collective-permute-start | bytes 3538952 | tf_op jit(solution)/shard_map/ppermute | solution.py:1458
  230.6 65.7 %collective-permute-start.15 = (bf16[3,24,8192]{2,1,0:T(8,128)(2,1)}, bf16[3,24,8192]{2,1,0:T(8,128)(2,1)}, u32[]{:S(2)}, u32[]{:S(2)}) collective-permute-start(bf16[3,24,8192]{2,1,0:T(8,128)(2,1)} %get-tuple-element.422), channel_id=1, source_target_pairs={{0,8},{1,9},{2,4},{3,5},{4,2},{5,3},{6,14},{7,15},{8,0},{9,1},{10,... | collective-permute-start | bytes 3538952 | tf_op jit(solution)/shard_map/ppermute | solution.py:1458
  230.6 59.9 %collective-permute-start.10 = (bf16[4,80,4096]{2,1,0:T(8,128)(2,1)}, bf16[4,80,4096]{2,1,0:T(8,128)(2,1)S(1)}, u32[]{:S(2)}, u32[]{:S(2)}) collective-permute-start(bf16[4,80,4096]{2,1,0:T(8,128)(2,1)} %bitcast.51), channel_id=1, source_target_pairs={{0,1},{1,0},{2,3},{3,2},{4,5},{5,4},{6,7},{7,6},{8,9},{9,8},{10,11... | collective-permute-start | bytes 7864328 | tf_op jit(solution)/shard_map/ppermute | solution.py:1419
  231.4 93.0 %collective-permute-start.13 = (bf16[4,40,4096]{2,1,0:T(8,128)(2,1)}, bf16[4,40,4096]{2,1,0:T(8,128)(2,1)}, u32[]{:S(2)}, u32[]{:S(2)}) collective-permute-start(bf16[4,40,4096]{2,1,0:T(8,128)(2,1)} %get-tuple-element.177), channel_id=1, source_target_pairs={{0,1},{1,0},{2,3},{3,2},{4,5},{5,4},{6,7},{7,6},{8,9},{9,8},{10,11... | collective-permute-start | bytes 3932168 | tf_op jit(solution)/shard_map/ppermute | solution.py:1419
  232.7 133.9 %collective-permute-start.18 = (bf16[4,40,4096]{2,1,0:T(8,128)(2,1)}, bf16[4,40,4096]{2,1,0:T(8,128)(2,1)S(1)}, u32[]{:S(2)}, u32[]{:S(2)}) collective-permute-start(bf16[4,40,4096]{2,1,0:T(8,128)(2,1)} %get-tuple-element.187), channel_id=1, source_target_pairs={{0,1},{1,0},{2,3},{3,2},{4,5},{5,4},{6,7},{7,6},{8,9},{9,8},{10,11... | collective-permute-start | bytes 3932168 | tf_op jit(solution)/shard_map/ppermute | solution.py:1419
  293.2 47.1 %collective-permute-start.11 = (bf16[3,80,4096]{2,1,0:T(8,128)(2,1)}, bf16[3,80,4096]{2,1,0:T(8,128)(2,1)S(1)}, u32[]{:S(2)}, u32[]{:S(2)}) collective-permute-start(bf16[3,80,4096]{2,1,0:T(8,128)(2,1)} %get-tuple-element.421), channel_id=1, source_target_pairs={{0,2},{1,3},{2,0},{3,1},{4,6},{5,7},{6,4},{7,5},{8,10},{9,11},{10,... | collective-permute-start | bytes 5898248 | tf_op jit(solution)/shard_map/ppermute | solution.py:1458
  296.4 43.9 %collective-permute-start.12 = (bf16[3,80,4096]{2,1,0:T(8,128)(2,1)}, bf16[3,80,4096]{2,1,0:T(8,128)(2,1)S(1)}, u32[]{:S(2)}, u32[]{:S(2)}) collective-permute-start(bf16[3,80,4096]{2,1,0:T(8,128)(2,1)} %get-tuple-element.420), channel_id=1, source_target_pairs={{0,8},{1,9},{2,4},{3,5},{4,2},{5,3},{6,14},{7,15},{8,0},{9,1},{10,... | collective-permute-start | bytes 5898248 | tf_op jit(solution)/shard_map/ppermute | solution.py:1458
  326.7 44.8 %collective-permute-start.16 = (bf16[3,40,4096]{2,1,0:T(8,128)(2,1)S(1)}, bf16[3,40,4096]{2,1,0:T(8,128)(2,1)}, u32[]{:S(2)}, u32[]{:S(2)}) collective-permute-start(bf16[3,40,4096]{2,1,0:T(8,128)(2,1)S(1)} %get-tuple-element.413), channel_id=1, source_target_pairs={{0,2},{1,3},{2,0},{3,1},{4,6},{5,7},{6,4},{7,5},{8,10},{9,11},{10,... | collective-permute-start | bytes 2949128 | tf_op jit(solution)/shard_map/ppermute | solution.py:1458
  327.2 44.3 %collective-permute-start.17 = (bf16[3,40,4096]{2,1,0:T(8,128)(2,1)S(1)}, bf16[3,40,4096]{2,1,0:T(8,128)(2,1)}, u32[]{:S(2)}, u32[]{:S(2)}) collective-permute-start(bf16[3,40,4096]{2,1,0:T(8,128)(2,1)S(1)} %get-tuple-element.412), channel_id=1, source_target_pairs={{0,8},{1,9},{2,4},{3,5},{4,2},{5,3},{6,14},{7,15},{8,0},{9,1},{10,... | collective-permute-start | bytes 2949128 | tf_op jit(solution)/shard_map/ppermute | solution.py:1458
  415.1 31.9 %all-to-all-start.1 = ((bf16[4,4,40,1024]{3,2,1,0:T(8,128)(2,1)}), bf16[4,4,40,1024]{3,2,1,0:T(8,128)(2,1)S(1)}, u32[]{:S(2)}, u32[]{:S(2)}) async-start(bf16[4,4,40,1024]{3,2,1,0:T(8,128)(2,1)} %bitcast.264), calls=%async_computation.1 | async-start | bytes 2621440 | tf_op jit(solution)/shard_map/all_to_all | solution.py:1482
  473.2 31.1 %collective-permute-start.21 = (bf16[4,160,1024]{2,1,0:T(8,128)(2,1)}, bf16[4,160,1024]{2,1,0:T(8,128)(2,1)S(1)}, u32[]{:S(2)}, u32[]{:S(2)}) collective-permute-start(bf16[4,160,1024]{2,1,0:T(8,128)(2,1)} %get-tuple-element.230), channel_id=1, source_target_pairs={{0,1},{1,0},{2,3},{3,2},{4,5},{5,4},{6,7},{7,6},{8,9},{9,8},{10,11... | collective-permute-start | bytes 3932168 | tf_op jit(solution)/shard_map/ppermute | solution.py:1419
  530.4 41.0 %collective-permute-start.22 = (bf16[8,40,2048]{2,1,0:T(8,128)(2,1)}, bf16[8,40,2048]{2,1,0:T(8,128)(2,1)}, u32[]{:S(2)}, u32[]{:S(2)}) collective-permute-start(bf16[8,40,2048]{2,1,0:T(8,128)(2,1)} %slice.350.refs_11_), channel_id=1, source_target_pairs={{0,1},{1,0},{2,3},{3,2},{4,5},{5,4},{6,7},{7,6},{8,9},{9,8},{10,11... | collective-permute-start | bytes 3932168 | tf_op jit(solution)/shard_map/ppermute | solution.py:1419
  534.2 36.1 %all-to-all-start.2 = ((bf16[4,8,10,2048]{3,1,2,0:T(8,128)(2,1)}), bf16[4,8,10,2048]{3,1,2,0:T(8,128)(2,1)S(1)}, u32[]{:S(2)}, u32[]{:S(2)}) async-start(bf16[4,8,10,2048]{3,1,2,0:T(8,128)(2,1)} %bitcast.70), calls=%async_computation.2 | async-start | bytes 2621440 | tf_op jit(solution)/shard_map/all_to_all | solution.py:1482
  (59 other events, 454.9 us)

commit v5 on v4

--- a/solution.py
+++ b/solution.py
@@ -1673,12 +1673,12 @@
     )
     loss_sums = factors[2]
 
-    def to_owners(res, *others):
-        low = after(lows[res][:, : images[res]], *others)
+    def to_owners(res, first, last, *others):
+        low = after(lows[res][first:last, : images[res]], *others)
         rows, _, lanes = low.shape
         return among_slabs(low.reshape(rows, slabs, per_device[res], lanes), 1)
 
-    out_parts = [to_owners(0, factors[2])]
+    out_parts = [to_owners(0, 0, p_counts[0], factors[2])]
 
     flows, grads, flow_sums, second_parts, shortcut_parts = [], [], [], [], []
     for res in both:
@@ -1730,6 +1730,7 @@
         )
         if res == 0:
             held = rows[0]
+            half_out = to_owners(1, 0, p_counts[1] // 2, held)
         first_parts.append(first_part)
         entry_flow_sums.append(sums)
         rows = [r[:, : images[res]] for r in rows]
@@ -1753,7 +1754,7 @@
         [first_parts, second_parts, shortcut_parts, entry_flow_sums, [loss_sums]],
         axes,
         4,
-        (entry_parts[0][1:], entry_parts[1]),
+        (entry_parts[0][1:], entry_parts[1], half_out),
     )
     first_state, second_state, bypass_state, entry_state, image_tables, total_loss = update(
         packed,
@@ -1765,7 +1766,7 @@
     )
     rows = entry_parts[1]
     rows[1:] = [send(after(r, packed), to_sub(d + 1)) for d, r in enumerate(rows[1:])]
-    out_parts.append(to_owners(1, packed))
+    out_parts.append(jnp.concatenate([half_out, to_owners(1, p_counts[1] // 2, p_counts[1], packed)], axis=1))
     first_state = [k.reshape(first_conv.shape) for k in first_state]
     second_state = [k.reshape(second_conv.shape) for k in second_state]
     inner_folded = flow_total.reshape(8, 128 // CS_OUT, CS_OUT).sum(axis=1)

time: 590 us -> 585 us (level)
  waiting for transfers between devices: 58.1 us -> 44.7 us
    all_to_all x3 -> x4, waiting for transfers between devices: 14 us -> 0.59 us  [among_slabs(): lax.all_to_all(array, 'space', 0, 0, axis_index_groups=by_slab, tiled=True)]
    all_to_all x3 -> x4, starting transfers between devices: 14.6 us -> 19.2 us  [among_slabs(): lax.all_to_all(array, 'space', 0, 0, axis_index_groups=by_slab, tiled=True)]
    unnamed x120 -> x118, local copies, waits for them, and re-layouts: 20 us -> 19.1 us
    optimization_barrier x3 -> x4, local copies, waits for them, and re-layouts: 12.4 us -> 13.3 us  [after(): return lax.optimization_barrier((value, others))[0]]
  transfers between devices with their start and end apart: 26 -> 27, of which waited for: 9 -> 8; matrix products, arithmetic and copies ran while one was open for 27% -> 27% of each run, Pallas kernels for 34% -> 34%
where the time goes in v5:
time: 585 us; the launch traced here: 577 us
  Pallas kernels  293 us (50%)
  local copies, waits for them, and re-layouts  121 us (21%)
  other arithmetic  74.6 us (13%)
  waiting for transfers between devices  44.7 us (8%)
  starting transfers between devices  42.4 us (7%)
    pallas_call x5, Pallas kernels, teacher_energies(): pl.pallas_call(functools.partial(teacher_kernel, p_rows, width, group, 4)...  97.3 us
    pallas_call x3, Pallas kernels, total_over_devices(): pl.pallas_call(functools.partial(total_kernel, axes, len(parts)), out_sha...  34.3 us
    pallas_call x2, Pallas kernels, student_block(): pl.pallas_call(functools.partial(block_kernel, p_rows, 4), grid_spec=pltp...  33 us
    ppermute x14, waiting for transfers between devices, to_neighbours(): lax.ppermute(r, ('batch', 'space'), pairs)  28.4 us
    pallas_call x2, Pallas kernels, student_entry(): pl.pallas_call(functools.partial(entry_kernel, p_rows, 4), grid_spec=pltp...  28 us
    pallas_call x2, Pallas kernels, student_forward(): pl.pallas_call(functools.partial(forward_kernel, p_rows, group, 4), grid_...  27.9 us
    pallas_call x2, Pallas kernels, student_back(): pl.pallas_call(functools.partial(back_kernel, p_rows, 4), grid_spec=pltpu...  27.5 us
    pallas_call x1, Pallas kernels, gradient_sum(): pl.pallas_call(functools.partial(gradient_sum_kernel, axes, tuple(layout)...  21.2 us
  transfers between devices with their start and end apart: 27, of which 8 were waited for; matrix products, arithmetic and copies ran while one was open for 27% of the time, Pallas kernels for 34%

profile of v5, /device:TPU:0, one launch (start us, length us, event | category | flops | bytes accessed | tf_op | source)
XLA Modules:
  0.0 577.4 jit_solution(11085667208245781548)
XLA Ops:
  26.9 9.4 %constant_dynamic-slice_fusion.5 = (bf16[4,1,10,8,8192]{4,3,2,1,0:T(8,128)(2,1)}, bf16[4,1,10,8,8192]{4,3,2,1,0:T(8,128)(2,1)}) fusion(bf16[4,2,10,8,8192]{4,3,2,1,0:T(8,128)(2,1)} %bitcast.258, s32[]{:T(128)S(6)} %select_n.393, s32[]{:T(128)S(6)} %select_n.381), kind=kLoop, calls=%fused_computation.118 | loop fusion | bytes 20971528 | tf_op jit(solution)/shard_map/jit(dynamic_index_in_dim)/dynamic_slice | solution.py:1424
  68.9 13.0 %multiply_convert_fusion = bf16[320,4,4096]{2,0,1:T(8,128)(2,1)} fusion(bf16[320,4,4096]{2,1,0:T(4,128)(2,1)} %param.30, f32[4096]{0:T(1024)S(1)} %bitcast.286, f32[4096]{0:T(1024)S(1)} %bitcast.285), kind=kLoop, calls=%fused_computation | loop fusion | flops 41943040 | bytes 21004288 | tf_op jit(solution)/shard_map/convert_element_type | solution.py:1555
  115.0 11.2 %shard_map.484.refs_5_.tot.refs_1_ = f32[8,128]{1,0:T(8,128)} custom-call(f32[8,128]{1,0:T(8,128)} %shard_map.483.refs_0_, bf16[4,160,1024]{2,1,0:T(8,128)(2,1)} %collective-permute-done.refs_1_, bf16[8,40,2048]{2,1,0:T(8,128)(2,1)} %copy-done.11, bf16[4,500,1024]{2,1,0:T(8,128)(2,1)} %all-to-all-done.refs_3_, bf16[1,8,128]{2,1,0:T(8,128)(2,1)} %copy.277.refs_4_, ...), custom_call_target="tpu_custom_call" | custom-call | flops 12000000000 | bytes 1048576 | tf_op jit(solution)/shard_map/pallas_call | solution.py:219
  143.1 8.8 %collective-permute-done.3 = bf16[6,40,2048]{2,1,0:T(8,128)(2,1)} collective-permute-done((bf16[6,40,2048]{2,1,0:T(8,128)(2,1)}, bf16[6,40,2048]{2,1,0:T(8,128)(2,1)}, u32[]{:S(2)}, u32[]{:S(2)}) %collective-permute-start.3) | collective-permute-done | bytes 983072 | tf_op jit(solution)/shard_map/ppermute | solution.py:1458
  157.3 13.3 %shard_map.486 = (bf16[16,48,2048]{2,1,0:T(8,128)(2,1)}, bf16[9,48,2176]{2,1,0:T(8,128)(2,1)}, bf16[11,48,2176]{2,1,0:T(8,128)(2,1)}, f32[13,48,2048]{2,1,0:T(8,128)}, f32[8,128]{1,0:T(8,128)}) custom-call(s32[2]{0:T(128)} %pad_add_fusion.place, bf16[8,48,2048]{2,1,0:T(8,128)(2,1)} %pad.32.refs_0_, bf16[8,48,2048]{2,1,0:T(8,128)(2,1)} %pad.33.refs_1_, ...), custom_call_target="tpu_custom_call" | custom-call | flops 15000000512 | bytes 1048576 | tf_op jit(solution)/shard_map/pallas_call | solution.py:712
  194.8 14.5 %shard_map.487 = (bf16[8,160,1024]{2,1,0:T(8,128)(2,1)}, bf16[5,160,1152]{2,1,0:T(8,128)(2,1)}, bf16[7,160,1152]{2,1,0:T(8,128)(2,1)}, f32[9,160,1024]{2,1,0:T(8,128)}, f32[8,128]{1,0:T(8,128)}) custom-call(s32[2]{0:T(128)} %pad_add_fusion.place, bf16[4,160,1024]{2,1,0:T(8,128)(2,1)} %bitcast.254, bf16[4,160,1024]{2,1,0:T(8,128)(2,1)} %collective-permute-done.refs_1_, ...), custom_call_target="tpu_custom_call" | custom-call | flops 15000000512 | bytes 1048576 | tf_op jit(solution)/shard_map/pallas_call | solution.py:712
  210.7 11.4 %shard_map.488.inner = f32[8,128]{1,0:T(8,128)} custom-call(f32[8,128]{1,0:T(8,128)} %get-tuple-element.162.refs_0_, f32[8,128]{1,0:T(8,128)} %get-tuple-element.154.refs_1_, bf16[1,8,128]{2,1,0:T(8,128)(2,1)} %copy.286.refs_2_, bf16[3,16,8192]{2,1,0:T(8,128)(2,1)} %collective-permute-done.8.refs_3_.refs_2_, ...), custom_call_target="tpu_custom_call" | custom-call | flops 12000000000 | bytes 1048576 | tf_op jit(solution)/shard_map/pallas_call | solution.py:219
  234.0 17.8 %shard_map.490 = (bf16[10,48,2304]{2,1,0:T(8,128)(2,1)}, f32[9,48,2048]{2,1,0:T(8,128)}, f32[11,48,2048]{2,1,0:T(8,128)}, bf16[8,48,2048]{2,1,0:T(8,128)(2,1)}, f32[48,384]{1,0:T(8,128)}) custom-call(s32[2]{0:T(128)} %pad_add_fusion.place, f32[13,48,2048]{2,1,0:T(8,128)} %get-tuple-element.171.first_ref, bf16[11,48,2176]{2,1,0:T(8,128)(2,1)} %get-tuple-element.172.odd, ...), custom_call_target="tpu_custom_call" | custom-call | flops 17999998976 | bytes 1048576 | tf_op jit(solution)/shard_map/pallas_call | solution.py:800
  251.8 15.2 %shard_map.489 = (bf16[6,160,1280]{2,1,0:T(8,128)(2,1)}, f32[5,160,1024]{2,1,0:T(8,128)}, f32[7,160,1024]{2,1,0:T(8,128)}, bf16[4,160,1024]{2,1,0:T(8,128)(2,1)}, f32[160,128]{1,0:T(8,128)}) custom-call(s32[2]{0:T(128)} %pad_add_fusion.place, f32[9,160,1024]{2,1,0:T(8,128)} %get-tuple-element.160.first_ref, bf16[7,160,1152]{2,1,0:T(8,128)(2,1)} %get-tuple-element.161.odd, ...), custom_call_target="tpu_custom_call" | custom-call | flops 17999998976 | bytes 1048576 | tf_op jit(solution)/shard_map/pallas_call | solution.py:800
  267.0 18.1 %shard_map.491.refs_7_ = f32[16,384]{1,0:T(8,128)} custom-call(s32[2]{0:T(128)} %pad_add_fusion.place, bf16[8,16,8192]{2,1,0:T(8,128)(2,1)} %fusion.26.refs_5_.refs_0_, bf16[8,16,8192]{2,1,0:T(8,128)(2,1)} %copy-done.15, bf16[3,16,8192]{2,1,0:T(8,128)(2,1)} %collective-permute-done.8.refs_3_.refs_2_, ...), custom_call_target="tpu_custom_call" | custom-call | flops 16000000000 | bytes 1048576 | tf_op jit(solution)/shard_map/pallas_call | solution.py:544
  296.9 28.1 %shard_map.492.refs_8_ = f32[24,384]{1,0:T(8,128)} custom-call(s32[2]{0:T(128)} %pad_add_fusion.place, bf16[8,24,8192]{2,1,0:T(8,128)(2,1)} %copy-done.9, bf16[8,24,8192]{2,1,0:T(8,128)(2,1)} %copy-done.8, bf16[3,24,8192]{2,1,0:T(8,128)(2,1)} %collective-permute-done.14.refs_2_, bf16[3,24,8192]{2,1,0:T(8,128)(2,1)} %collective-permute-done.15.refs_3_, ...), custom_call_target="tpu_custom_call" | custom-call | flops 24000000000 | bytes 1048576 | tf_op jit(solution)/shard_map/pallas_call | solution.py:544
  327.9 12.9 %collective-permute-done.11.refs_2_ = bf16[3,80,4096]{2,1,0:T(8,128)(2,1)S(1)} collective-permute-done((bf16[3,80,4096]{2,1,0:T(8,128)(2,1)}, bf16[3,80,4096]{2,1,0:T(8,128)(2,1)S(1)}, u32[]{:S(2)}, u32[]{:S(2)}) %collective-permute-start.11) | collective-permute-done | bytes 1966112 | tf_op jit(solution)/shard_map/ppermute | solution.py:1458
  343.5 23.6 %shard_map.493.refs_4_ = f32[80,128]{1,0:T(8,128)} custom-call(s32[2]{0:T(128)} %pad_add_fusion.place, bf16[4,4,2,40,4096]{4,3,2,1,0:T(8,128)(2,1)} %bitcast.238, bf16[4,80,4096]{2,1,0:T(8,128)(2,1)} %copy-done.16, bf16[3,80,4096]{2,1,0:T(8,128)(2,1)} %copy-done.50, bf16[3,80,4096]{2,1,0:T(8,128)(2,1)} %copy-done.51, bf16[1152,256]{1,0:T(8,128)(2,1)} %bitcast.296, ...), custom_call_target="tpu_custom_call" | custom-call | flops 20000000000 | bytes 1048576 | tf_op jit(solution)/shard_map/pallas_call | solution.py:544
  371.4 13.8 %shard_map.494.refs_5_ = f32[40,128]{1,0:T(8,128)} custom-call(s32[2]{0:T(128)} %pad_add_fusion.place, bf16[4,4,2,40,4096]{4,3,2,1,0:T(8,128)(2,1)} %bitcast.240, bf16[4,40,4096]{2,1,0:T(8,128)(2,1)} %collective-permute-done.13.refs_1_, bf16[3,40,4096]{2,1,0:T(8,128)(2,1)} %collective-permute-done.16.refs_2_, ...), custom_call_target="tpu_custom_call" | custom-call | flops 10000000000 | bytes 1048576 | tf_op jit(solution)/shard_map/pallas_call | solution.py:544
  388.5 13.8 %shard_map.495.refs_6_ = f32[40,128]{1,0:T(8,128)} custom-call(s32[2]{0:T(128)} %pad_add_fusion.place, bf16[4,4,2,40,4096]{4,3,2,1,0:T(8,128)(2,1)} %bitcast.241, bf16[4,40,4096]{2,1,0:T(8,128)(2,1)} %copy-done.23, bf16[3,40,4096]{2,1,0:T(8,128)(2,1)} %copy-done.52, bf16[3,40,4096]{2,1,0:T(8,128)(2,1)} %collective-permute-done.20.refs_3_, ...), custom_call_target="tpu_custom_call" | custom-call | flops 10000000000 | bytes 1048576 | tf_op jit(solution)/shard_map/pallas_call | solution.py:544
  402.3 11.1 %shard_map.496 = (f32[160,128]{1,0:T(8,128)}, f32[48,384]{1,0:T(8,128)}, f32[8,128]{1,0:T(8,128)}) custom-call(f32[160,128]{1,0:T(8,128)} %get-tuple-element.170.refs_0_, f32[48,384]{1,0:T(8,128)} %get-tuple-element.173.refs_1_, f32[160,128]{1,0:T(8,128)} %broadcast_in_dim.161.refs_4_.label_ref.refs_2_, ...), custom_call_target="tpu_custom_call" | custom-call | flops 11000000512 | bytes 1048576 | tf_op jit(solution)/shard_map/pallas_call | solution.py:976
  418.6 13.5 %shard_map.498 = (f32[9,48,2048]{2,1,0:T(8,128)}, bf16[8,48,2048]{2,1,0:T(8,128)(2,1)}, f32[8,128]{1,0:T(8,128)}, f32[576,64]{1,0:T(8,128)}, f32[64,32]{1,0:T(8,128)}) custom-call(s32[2]{0:T(128)} %pad_add_fusion.place, f32[11,48,2048]{2,1,0:T(8,128)} %get-tuple-element.210.sum_ref, bf16[11,48,2048]{2,1,0:T(8,128)(2,1)} %pad.37.cot, ...), custom_call_target="tpu_custom_call" | custom-call | flops 17999998976 | bytes 1048576 | tf_op jit(solution)/shard_map/pallas_call | solution.py:1115
  432.0 14.0 %shard_map.497 = (f32[5,160,1024]{2,1,0:T(8,128)}, bf16[4,160,1024]{2,1,0:T(8,128)(2,1)}, f32[8,128]{1,0:T(8,128)}, f32[576,64]{1,0:T(8,128)}, f32[64,32]{1,0:T(8,128)}) custom-call(s32[2]{0:T(128)} %pad_add_fusion.place, f32[7,160,1024]{2,1,0:T(8,128)} %get-tuple-element.199.sum_ref, bf16[7,160,1024]{2,1,0:T(8,128)(2,1)} %bitcast.276, ...), custom_call_target="tpu_custom_call" | custom-call | flops 17999998976 | bytes 1048576 | tf_op jit(solution)/shard_map/pallas_call | solution.py:1115
  447.1 11.7 %shard_map.499.pulled = f32[8,128]{1,0:T(8,128)} custom-call(f32[8,128]{1,0:T(8,128)} %get-tuple-element.209.refs_0_, f32[8,128]{1,0:T(8,128)} %get-tuple-element.214.refs_1_, bf16[4,4,40,1024]{3,2,1,0:T(8,128)(2,1)} %copy-done.19), custom_call_target="tpu_custom_call" | custom-call | flops 12000000000 | bytes 1048576 | tf_op jit(solution)/shard_map/pallas_call | solution.py:219
  458.8 13.3 %shard_map.500 = (bf16[4,160,1024]{2,1,0:T(8,128)(2,1)}, bf16[4,160,1024]{2,1,0:T(8,128)(2,1)}, f32[576,32]{1,0:T(8,128)}, f32[8,128]{1,0:T(8,128)}) custom-call(s32[2]{0:T(128)} %pad_add_fusion.place, f32[5,160,1024]{2,1,0:T(8,128)} %get-tuple-element.205.flow_ref, f32[5,160,1024]{2,1,0:T(8,128)} %get-tuple-element.202.first_ref, ...), custom_call_target="tpu_custom_call" | custom-call | flops 16000000000 | bytes 1048576 | tf_op jit(solution)/shard_map/pallas_call | solution.py:1253
  478.8 14.6 %shard_map.501 = (bf16[8,48,2048]{2,1,0:T(8,128)(2,1)}, bf16[8,48,2048]{2,1,0:T(8,128)(2,1)}, f32[576,32]{1,0:T(8,128)}, f32[8,128]{1,0:T(8,128)}) custom-call(s32[2]{0:T(128)} %pad_add_fusion.place, f32[9,48,2048]{2,1,0:T(8,128)} %get-tuple-element.221.flow_ref, f32[9,48,2048]{2,1,0:T(8,128)} %get-tuple-element.212.first_ref, ...), custom_call_target="tpu_custom_call" | custom-call | flops 16000000000 | bytes 1048576 | tf_op jit(solution)/shard_map/pallas_call | solution.py:1253
  501.3 7.5 %collective-permute-done.21.refs_9_ = bf16[4,160,1024]{2,1,0:T(8,128)(2,1)S(1)} collective-permute-done((bf16[4,160,1024]{2,1,0:T(8,128)(2,1)}, bf16[4,160,1024]{2,1,0:T(8,128)(2,1)S(1)}, u32[]{:S(2)}, u32[]{:S(2)}) %collective-permute-start.21) | collective-permute-done | bytes 1310752 | tf_op jit(solution)/shard_map/ppermute | solution.py:1419
  509.9 21.2 %shard_map.502.refs_0_ = f32[512,128]{1,0:T(8,128)} custom-call(f32[576,32]{1,0:T(8,128)} %get-tuple-element.219.refs_0_, f32[576,32]{1,0:T(8,128)} %get-tuple-element.225.refs_1_, f32[576,64]{1,0:T(8,128)} %get-tuple-element.226.refs_2_, f32[576,64]{1,0:T(8,128)} %get-tuple-element.227.refs_3_, f32[64,32]{1,0:T(8,128)} %get-tuple-element.228.refs_4_, ...), custom_call_target="tpu_custom_call" | custom-call | flops 20000000000 | bytes 1048576 | tf_op jit(solution)/shard_map/pallas_call | solution.py:379
  551.0 10.1 %fusion.10 = f32[320,4,1024]{2,1,0:T(4,128)} fusion(bf16[320,4,1024]{2,1,0:T(4,128)(2,1)S(1)} %copy-done.5, f32[4,2,40,4,1024]{4,3,2,1,0:T(4,128)S(1)} %copy.297, f32[320,1024]{1,0:T(8,128)S(1)} %get-tuple-element.539, f32[320,1024]{1,0:T(8,128)S(1)} %get-tuple-element.538, f32[320,1024]{1,0:T(8,128)S(1)} %get-tuple-element.537, ...), kind=kLoop, calls=%fused_computation.17 | loop fusion | flops 19660800 | bytes 18350080 | tf_op jit(solution)/shard_map/add | solution.py:1796
  (302 shorter events, 233.5 us)
Async XLA Ops:
  5.8 99.6 %collective-permute-start = (bf16[4,160,1024]{2,1,0:T(8,128)(2,1)}, bf16[4,160,1024]{2,1,0:T(8,128)(2,1)}, u32[]{:S(2)}, u32[]{:S(2)}) collective-permute-start(bf16[4,160,1024]{2,1,0:T(8,128)(2,1)} %bitcast.6.refs_1_), channel_id=1, source_target_pairs={{0,1},{1,0},{2,3},{3,2},{4,5},{5,4},{6,7},{7,6},{8,9},{9,8},{10,11... | collective-permute-start | bytes 3932168 | tf_op jit(solution)/shard_map/ppermute | solution.py:1419
  17.6 97.4 %all-to-all-start = ((bf16[4,500,1024]{2,1,0:T(8,128)(2,1)}), bf16[4,500,1024]{2,1,0:T(8,128)(2,1)}, u32[]{:S(2)}, u32[]{:S(2)}) async-start(bf16[4,500,1024]{2,1,0:T(8,128)(2,1)} %pad_maximum_fusion), calls=%async_computation | async-start | bytes 8257536 | tf_op jit(solution)/shard_map/all_to_all | solution.py:1482
  26.3 77.8 %collective-permute-start.1 = (bf16[8,40,2048]{2,1,0:T(8,128)(2,1)}, bf16[8,40,2048]{2,1,0:T(8,128)(2,1)S(1)}, u32[]{:S(2)}, u32[]{:S(2)}) collective-permute-start(bf16[8,40,2048]{2,1,0:T(8,128)(2,1)} %bitcast.233.refs_3_), channel_id=1, source_target_pairs={{0,1},{1,0},{2,3},{3,2},{4,5},{5,4},{6,7},{7,6},{8,9},{9,8},{10,11... | collective-permute-start | bytes 3932168 | tf_op jit(solution)/shard_map/ppermute | solution.py:1419
  40.5 72.6 %collective-permute-start.2 = (bf16[16,8,8192]{2,0,1:T(8,128)(2,1)}, bf16[16,8,8192]{2,0,1:T(8,128)(2,1)}, u32[]{:S(2)}, u32[]{:S(2)}) collective-permute-start(bf16[16,8,8192]{2,0,1:T(8,128)(2,1)} %copy.305), channel_id=1, source_target_pairs={{0,1},{1,0},{2,3},{3,2},{4,5},{5,4},{6,7},{7,6},{8,9},{9,8},{10,11... | collective-permute-start | bytes 6291464 | tf_op jit(solution)/shard_map/ppermute | solution.py:1419
  127.0 24.9 %collective-permute-start.3 = (bf16[6,40,2048]{2,1,0:T(8,128)(2,1)}, bf16[6,40,2048]{2,1,0:T(8,128)(2,1)}, u32[]{:S(2)}, u32[]{:S(2)}) collective-permute-start(bf16[6,40,2048]{2,1,0:T(8,128)(2,1)} %get-tuple-element.148.refs_8_), channel_id=1, source_target_pairs={{0,2},{1,3},{2,0},{3,1},{4,6},{5,7},{6,4},{7,5},{8,10},{9,11},{10,... | collective-permute-start | bytes 2949128 | tf_op jit(solution)/shard_map/ppermute | solution.py:1458
  128.3 26.0 %collective-permute-start.4 = (bf16[6,40,2048]{2,1,0:T(8,128)(2,1)S(1)}, bf16[6,40,2048]{2,1,0:T(8,128)(2,1)}, u32[]{:S(2)}, u32[]{:S(2)}) collective-permute-start(bf16[6,40,2048]{2,1,0:T(8,128)(2,1)S(1)} %copy-done.32), channel_id=1, source_target_pairs={{0,8},{1,9},{2,4},{3,5},{4,2},{5,3},{6,14},{7,15},{8,0},{9,1},{10,... | collective-permute-start | bytes 2949128 | tf_op jit(solution)/shard_map/ppermute | solution.py:1458
  135.1 74.2 %collective-permute-start.7 = (bf16[24,8,8192]{2,0,1:T(8,128)(2,1)}, bf16[24,8,8192]{2,0,1:T(8,128)(2,1)}, u32[]{:S(2)}, u32[]{:S(2)}) collective-permute-start(bf16[24,8,8192]{2,0,1:T(8,128)(2,1)} %copy.307), channel_id=1, source_target_pairs={{0,1},{1,0},{2,3},{3,2},{4,5},{5,4},{6,7},{7,6},{8,9},{9,8},{10,11... | collective-permute-start | bytes 9437192 | tf_op jit(solution)/shard_map/ppermute | solution.py:1419
  135.7 58.4 %collective-permute-start.5 = (bf16[6,160,1024]{2,1,0:T(8,128)(2,1)}, bf16[6,160,1024]{2,1,0:T(8,128)(2,1)}, u32[]{:S(2)}, u32[]{:S(2)}) collective-permute-start(bf16[6,160,1024]{2,1,0:T(8,128)(2,1)} %get-tuple-element.158.refs_6_), channel_id=1, source_target_pairs={{0,2},{1,3},{2,0},{3,1},{4,6},{5,7},{6,4},{7,5},{8,10},{9,11},{10,... | collective-permute-start | bytes 5898248 | tf_op jit(solution)/shard_map/ppermute | solution.py:1458
  138.8 55.3 %collective-permute-start.6 = (bf16[6,160,1024]{2,1,0:T(8,128)(2,1)}, bf16[6,160,1024]{2,1,0:T(8,128)(2,1)}, u32[]{:S(2)}, u32[]{:S(2)}) collective-permute-start(bf16[6,160,1024]{2,1,0:T(8,128)(2,1)} %get-tuple-element.159.refs_7_), channel_id=1, source_target_pairs={{0,8},{1,9},{2,4},{3,5},{4,2},{5,3},{6,14},{7,15},{8,0},{9,1},{10,... | collective-permute-start | bytes 5898248 | tf_op jit(solution)/shard_map/ppermute | solution.py:1458
  177.1 33.6 %collective-permute-start.8 = (bf16[3,16,8192]{2,1,0:T(8,128)(2,1)}, bf16[3,16,8192]{2,1,0:T(8,128)(2,1)}, u32[]{:S(2)}, u32[]{:S(2)}) collective-permute-start(bf16[3,16,8192]{2,1,0:T(8,128)(2,1)} %get-tuple-element.483), channel_id=1, source_target_pairs={{0,2},{1,3},{2,0},{3,1},{4,6},{5,7},{6,4},{7,5},{8,10},{9,11},{10,... | collective-permute-start | bytes 2359304 | tf_op jit(solution)/shard_map/ppermute | solution.py:1458
  178.4 32.2 %collective-permute-start.9 = (bf16[3,16,8192]{2,1,0:T(8,128)(2,1)}, bf16[3,16,8192]{2,1,0:T(8,128)(2,1)}, u32[]{:S(2)}, u32[]{:S(2)}) collective-permute-start(bf16[3,16,8192]{2,1,0:T(8,128)(2,1)} %get-tuple-element.482), channel_id=1, source_target_pairs={{0,8},{1,9},{2,4},{3,5},{4,2},{5,3},{6,14},{7,15},{8,0},{9,1},{10,... | collective-permute-start | bytes 2359304 | tf_op jit(solution)/shard_map/ppermute | solution.py:1458
  230.5 66.4 %collective-permute-start.14 = (bf16[3,24,8192]{2,1,0:T(8,128)(2,1)}, bf16[3,24,8192]{2,1,0:T(8,128)(2,1)}, u32[]{:S(2)}, u32[]{:S(2)}) collective-permute-start(bf16[3,24,8192]{2,1,0:T(8,128)(2,1)} %get-tuple-element.481), channel_id=1, source_target_pairs={{0,2},{1,3},{2,0},{3,1},{4,6},{5,7},{6,4},{7,5},{8,10},{9,11},{10,... | collective-permute-start | bytes 3538952 | tf_op jit(solution)/shard_map/ppermute | solution.py:1458
  231.2 65.7 %collective-permute-start.15 = (bf16[3,24,8192]{2,1,0:T(8,128)(2,1)}, bf16[3,24,8192]{2,1,0:T(8,128)(2,1)}, u32[]{:S(2)}, u32[]{:S(2)}) collective-permute-start(bf16[3,24,8192]{2,1,0:T(8,128)(2,1)} %get-tuple-element.480), channel_id=1, source_target_pairs={{0,8},{1,9},{2,4},{3,5},{4,2},{5,3},{6,14},{7,15},{8,0},{9,1},{10,... | collective-permute-start | bytes 3538952 | tf_op jit(solution)/shard_map/ppermute | solution.py:1458
  231.2 59.9 %collective-permute-start.10 = (bf16[4,80,4096]{2,1,0:T(8,128)(2,1)}, bf16[4,80,4096]{2,1,0:T(8,128)(2,1)S(1)}, u32[]{:S(2)}, u32[]{:S(2)}) collective-permute-start(bf16[4,80,4096]{2,1,0:T(8,128)(2,1)} %bitcast.51), channel_id=1, source_target_pairs={{0,1},{1,0},{2,3},{3,2},{4,5},{5,4},{6,7},{7,6},{8,9},{9,8},{10,11... | collective-permute-start | bytes 7864328 | tf_op jit(solution)/shard_map/ppermute | solution.py:1419
  232.0 93.0 %collective-permute-start.13 = (bf16[4,40,4096]{2,1,0:T(8,128)(2,1)}, bf16[4,40,4096]{2,1,0:T(8,128)(2,1)}, u32[]{:S(2)}, u32[]{:S(2)}) collective-permute-start(bf16[4,40,4096]{2,1,0:T(8,128)(2,1)} %get-tuple-element.178), channel_id=1, source_target_pairs={{0,1},{1,0},{2,3},{3,2},{4,5},{5,4},{6,7},{7,6},{8,9},{9,8},{10,11... | collective-permute-start | bytes 3932168 | tf_op jit(solution)/shard_map/ppermute | solution.py:1419
  233.2 133.8 %collective-permute-start.18 = (bf16[4,40,4096]{2,1,0:T(8,128)(2,1)}, bf16[4,40,4096]{2,1,0:T(8,128)(2,1)S(1)}, u32[]{:S(2)}, u32[]{:S(2)}) collective-permute-start(bf16[4,40,4096]{2,1,0:T(8,128)(2,1)} %get-tuple-element.188), channel_id=1, source_target_pairs={{0,1},{1,0},{2,3},{3,2},{4,5},{5,4},{6,7},{7,6},{8,9},{9,8},{10,11... | collective-permute-start | bytes 3932168 | tf_op jit(solution)/shard_map/ppermute | solution.py:1419
  293.7 47.1 %collective-permute-start.11 = (bf16[3,80,4096]{2,1,0:T(8,128)(2,1)}, bf16[3,80,4096]{2,1,0:T(8,128)(2,1)S(1)}, u32[]{:S(2)}, u32[]{:S(2)}) collective-permute-start(bf16[3,80,4096]{2,1,0:T(8,128)(2,1)} %get-tuple-element.479), channel_id=1, source_target_pairs={{0,2},{1,3},{2,0},{3,1},{4,6},{5,7},{6,4},{7,5},{8,10},{9,11},{10,... | collective-permute-start | bytes 5898248 | tf_op jit(solution)/shard_map/ppermute | solution.py:1458
  296.9 43.9 %collective-permute-start.12 = (bf16[3,80,4096]{2,1,0:T(8,128)(2,1)}, bf16[3,80,4096]{2,1,0:T(8,128)(2,1)S(1)}, u32[]{:S(2)}, u32[]{:S(2)}) collective-permute-start(bf16[3,80,4096]{2,1,0:T(8,128)(2,1)} %get-tuple-element.478), channel_id=1, source_target_pairs={{0,8},{1,9},{2,4},{3,5},{4,2},{5,3},{6,14},{7,15},{8,0},{9,1},{10,... | collective-permute-start | bytes 5898248 | tf_op jit(solution)/shard_map/ppermute | solution.py:1458
  327.3 44.1 %collective-permute-start.16 = (bf16[3,40,4096]{2,1,0:T(8,128)(2,1)S(1)}, bf16[3,40,4096]{2,1,0:T(8,128)(2,1)}, u32[]{:S(2)}, u32[]{:S(2)}) collective-permute-start(bf16[3,40,4096]{2,1,0:T(8,128)(2,1)S(1)} %get-tuple-element.471), channel_id=1, source_target_pairs={{0,2},{1,3},{2,0},{3,1},{4,6},{5,7},{6,4},{7,5},{8,10},{9,11},{10,... | collective-permute-start | bytes 2949128 | tf_op jit(solution)/shard_map/ppermute | solution.py:1458
  327.7 43.6 %collective-permute-start.17 = (bf16[3,40,4096]{2,1,0:T(8,128)(2,1)S(1)}, bf16[3,40,4096]{2,1,0:T(8,128)(2,1)}, u32[]{:S(2)}, u32[]{:S(2)}) collective-permute-start(bf16[3,40,4096]{2,1,0:T(8,128)(2,1)S(1)} %get-tuple-element.470), channel_id=1, source_target_pairs={{0,8},{1,9},{2,4},{3,5},{4,2},{5,3},{6,14},{7,15},{8,0},{9,1},{10,... | collective-permute-start | bytes 2949128 | tf_op jit(solution)/shard_map/ppermute | solution.py:1458
  414.6 31.4 %all-to-all-start.1 = ((bf16[4,4,40,1024]{3,2,1,0:T(8,128)(2,1)}), bf16[4,4,40,1024]{3,2,1,0:T(8,128)(2,1)S(1)}, u32[]{:S(2)}, u32[]{:S(2)}) async-start(bf16[4,4,40,1024]{3,2,1,0:T(8,128)(2,1)} %bitcast.232), calls=%async_computation.1 | async-start | bytes 2621440 | tf_op jit(solution)/shard_map/all_to_all | solution.py:1482
  473.6 26.3 %all-to-all-start.2 = ((bf16[4,4,10,2048]{3,1,2,0:T(4,128)(2,1)}), bf16[4,4,10,2048]{3,1,2,0:T(4,128)(2,1)S(1)}, u32[]{:S(2)}, u32[]{:S(2)}) async-start(bf16[4,4,10,2048]{3,1,2,0:T(4,128)(2,1)} %bitcast.70), calls=%async_computation.2 | async-start | bytes 1310720 | tf_op jit(solution)/shard_map/all_to_all | solution.py:1482
  478.1 30.7 %collective-permute-start.21 = (bf16[4,160,1024]{2,1,0:T(8,128)(2,1)}, bf16[4,160,1024]{2,1,0:T(8,128)(2,1)S(1)}, u32[]{:S(2)}, u32[]{:S(2)}) collective-permute-start(bf16[4,160,1024]{2,1,0:T(8,128)(2,1)} %get-tuple-element.232), channel_id=1, source_target_pairs={{0,1},{1,0},{2,3},{3,2},{4,5},{5,4},{6,7},{7,6},{8,9},{9,8},{10,11... | collective-permute-start | bytes 3932168 | tf_op jit(solution)/shard_map/ppermute | solution.py:1419
  535.5 31.1 %collective-permute-start.22 = (bf16[8,40,2048]{2,1,0:T(8,128)(2,1)}, bf16[8,40,2048]{2,1,0:T(8,128)(2,1)}, u32[]{:S(2)}, u32[]{:S(2)}) collective-permute-start(bf16[8,40,2048]{2,1,0:T(8,128)(2,1)} %slice.354.refs_11_), channel_id=1, source_target_pairs={{0,1},{1,0},{2,3},{3,2},{4,5},{5,4},{6,7},{7,6},{8,9},{9,8},{10,11... | collective-permute-start | bytes 3932168 | tf_op jit(solution)/shard_map/ppermute | solution.py:1419
  (59 other events, 478.2 us)

commit v6 on v5

--- a/solution.py
+++ b/solution.py
@@ -1674,9 +1674,10 @@
     loss_sums = factors[2]
 
     def to_owners(res, first, last, *others):
-        low = after(lows[res][first:last, : images[res]], *others)
+        low = lows[res][first:last, : images[res]]
         rows, _, lanes = low.shape
-        return among_slabs(low.reshape(rows, slabs, per_device[res], lanes), 1)
+        low = jnp.moveaxis(low.reshape(rows, slabs, per_device[res], lanes), 1, 0)
+        return among_slabs(after(low, *others), 0)
 
     out_parts = [to_owners(0, 0, p_counts[0], factors[2])]
 

time: 585 us -> 586 us (level)
    optimization_barrier x4 -> x2, local copies, waits for them, and re-layouts: 13.3 us -> 10.6 us  [after(): return lax.optimization_barrier((value, others))[0]]
    unnamed x118 -> x120, local copies, waits for them, and re-layouts: 19.1 us -> 20 us
  transfers between devices with their start and end apart: 27 -> 27, of which waited for: 8 -> 8; matrix products, arithmetic and copies ran while one was open for 27% -> 28% of each run, Pallas kernels for 34% -> 34%
where the time goes in v6:
time: 586 us; the launch traced here: 579 us
  Pallas kernels  292 us (50%)
  local copies, waits for them, and re-layouts  122 us (21%)
  other arithmetic  74.5 us (13%)
  waiting for transfers between devices  47.3 us (8%)
  starting transfers between devices  41.1 us (7%)
    pallas_call x5, Pallas kernels, teacher_energies(): pl.pallas_call(functools.partial(teacher_kernel, p_rows, width, group, 4)...  97.7 us
    pallas_call x3, Pallas kernels, total_over_devices(): pl.pallas_call(functools.partial(total_kernel, axes, len(parts)), out_sha...  33.5 us
    pallas_call x2, Pallas kernels, student_block(): pl.pallas_call(functools.partial(block_kernel, p_rows, 4), grid_spec=pltp...  33 us
    pallas_call x2, Pallas kernels, student_entry(): pl.pallas_call(functools.partial(entry_kernel, p_rows, 4), grid_spec=pltp...  28 us
    pallas_call x2, Pallas kernels, student_forward(): pl.pallas_call(functools.partial(forward_kernel, p_rows, group, 4), grid_...  27.8 us
    pallas_call x2, Pallas kernels, student_back(): pl.pallas_call(functools.partial(back_kernel, p_rows, 4), grid_spec=pltpu...  27.4 us
    ppermute x14, waiting for transfers between devices, to_neighbours(): lax.ppermute(r, ('batch', 'space'), pairs)  26.1 us
    pallas_call x1, Pallas kernels, gradient_sum(): pl.pallas_call(functools.partial(gradient_sum_kernel, axes, tuple(layout)...  21.1 us
  transfers between devices with their start and end apart: 27, of which 8 were waited for; matrix products, arithmetic and copies ran while one was open for 28% of the time, Pallas kernels for 34%

profile of v6, /device:TPU:0, one launch (start us, length us, event | category | flops | bytes accessed | tf_op | source)
XLA Modules:
  0.0 578.6 jit_solution(17208425925409574231)
XLA Ops:
  26.9 9.4 %constant_dynamic-slice_fusion.5 = (bf16[4,1,10,8,8192]{4,3,2,1,0:T(8,128)(2,1)}, bf16[4,1,10,8,8192]{4,3,2,1,0:T(8,128)(2,1)}) fusion(bf16[4,2,10,8,8192]{4,3,2,1,0:T(8,128)(2,1)} %bitcast.258, s32[]{:T(128)S(6)} %select_n.393, s32[]{:T(128)S(6)} %select_n.381), kind=kLoop, calls=%fused_computation.118 | loop fusion | bytes 20971528 | tf_op jit(solution)/shard_map/jit(dynamic_index_in_dim)/dynamic_slice | solution.py:1424
  68.9 13.0 %multiply_convert_fusion = bf16[320,4,4096]{2,0,1:T(8,128)(2,1)} fusion(bf16[320,4,4096]{2,1,0:T(4,128)(2,1)} %param.30, f32[4096]{0:T(1024)S(1)} %bitcast.286, f32[4096]{0:T(1024)S(1)} %bitcast.285), kind=kLoop, calls=%fused_computation | loop fusion | flops 41943040 | bytes 21004288 | tf_op jit(solution)/shard_map/convert_element_type | solution.py:1555
  115.0 11.1 %shard_map.484.refs_5_.tot.refs_1_ = f32[8,128]{1,0:T(8,128)} custom-call(f32[8,128]{1,0:T(8,128)} %shard_map.483.refs_0_, bf16[4,160,1024]{2,1,0:T(8,128)(2,1)} %collective-permute-done.refs_1_, bf16[8,40,2048]{2,1,0:T(8,128)(2,1)} %copy-done.11, bf16[4,500,1024]{2,1,0:T(8,128)(2,1)} %all-to-all-done.refs_3_, bf16[1,8,128]{2,1,0:T(8,128)(2,1)} %copy.277.refs_4_, ...), custom_call_target="tpu_custom_call" | custom-call | flops 12000000000 | bytes 1048576 | tf_op jit(solution)/shard_map/pallas_call | solution.py:219
  143.0 8.8 %collective-permute-done.3 = bf16[6,40,2048]{2,1,0:T(8,128)(2,1)} collective-permute-done((bf16[6,40,2048]{2,1,0:T(8,128)(2,1)}, bf16[6,40,2048]{2,1,0:T(8,128)(2,1)}, u32[]{:S(2)}, u32[]{:S(2)}) %collective-permute-start.3) | collective-permute-done | bytes 983072 | tf_op jit(solution)/shard_map/ppermute | solution.py:1458
  157.2 13.3 %shard_map.486 = (bf16[16,48,2048]{2,1,0:T(8,128)(2,1)}, bf16[9,48,2176]{2,1,0:T(8,128)(2,1)}, bf16[11,48,2176]{2,1,0:T(8,128)(2,1)}, f32[13,48,2048]{2,1,0:T(8,128)}, f32[8,128]{1,0:T(8,128)}) custom-call(s32[2]{0:T(128)} %pad_add_fusion.place, bf16[8,48,2048]{2,1,0:T(8,128)(2,1)} %pad.32.refs_0_, bf16[8,48,2048]{2,1,0:T(8,128)(2,1)} %pad.33.refs_1_, ...), custom_call_target="tpu_custom_call" | custom-call | flops 15000000512 | bytes 1048576 | tf_op jit(solution)/shard_map/pallas_call | solution.py:712
  194.7 14.5 %shard_map.487 = (bf16[8,160,1024]{2,1,0:T(8,128)(2,1)}, bf16[5,160,1152]{2,1,0:T(8,128)(2,1)}, bf16[7,160,1152]{2,1,0:T(8,128)(2,1)}, f32[9,160,1024]{2,1,0:T(8,128)}, f32[8,128]{1,0:T(8,128)}) custom-call(s32[2]{0:T(128)} %pad_add_fusion.place, bf16[4,160,1024]{2,1,0:T(8,128)(2,1)} %bitcast.254, bf16[4,160,1024]{2,1,0:T(8,128)(2,1)} %collective-permute-done.refs_1_, ...), custom_call_target="tpu_custom_call" | custom-call | flops 15000000512 | bytes 1048576 | tf_op jit(solution)/shard_map/pallas_call | solution.py:712
  210.6 11.4 %shard_map.488.inner = f32[8,128]{1,0:T(8,128)} custom-call(f32[8,128]{1,0:T(8,128)} %get-tuple-element.162.refs_0_, f32[8,128]{1,0:T(8,128)} %get-tuple-element.154.refs_1_, bf16[1,8,128]{2,1,0:T(8,128)(2,1)} %copy.286.refs_2_, bf16[3,16,8192]{2,1,0:T(8,128)(2,1)} %collective-permute-done.8.refs_3_.refs_2_, ...), custom_call_target="tpu_custom_call" | custom-call | flops 12000000000 | bytes 1048576 | tf_op jit(solution)/shard_map/pallas_call | solution.py:219
  233.9 17.8 %shard_map.490 = (bf16[10,48,2304]{2,1,0:T(8,128)(2,1)}, f32[9,48,2048]{2,1,0:T(8,128)}, f32[11,48,2048]{2,1,0:T(8,128)}, bf16[8,48,2048]{2,1,0:T(8,128)(2,1)}, f32[48,384]{1,0:T(8,128)}) custom-call(s32[2]{0:T(128)} %pad_add_fusion.place, f32[13,48,2048]{2,1,0:T(8,128)} %get-tuple-element.171.first_ref, bf16[11,48,2176]{2,1,0:T(8,128)(2,1)} %get-tuple-element.172.odd, ...), custom_call_target="tpu_custom_call" | custom-call | flops 17999998976 | bytes 1048576 | tf_op jit(solution)/shard_map/pallas_call | solution.py:800
  251.7 15.2 %shard_map.489 = (bf16[6,160,1280]{2,1,0:T(8,128)(2,1)}, f32[5,160,1024]{2,1,0:T(8,128)}, f32[7,160,1024]{2,1,0:T(8,128)}, bf16[4,160,1024]{2,1,0:T(8,128)(2,1)}, f32[160,128]{1,0:T(8,128)}) custom-call(s32[2]{0:T(128)} %pad_add_fusion.place, f32[9,160,1024]{2,1,0:T(8,128)} %get-tuple-element.160.first_ref, bf16[7,160,1152]{2,1,0:T(8,128)(2,1)} %get-tuple-element.161.odd, ...), custom_call_target="tpu_custom_call" | custom-call | flops 17999998976 | bytes 1048576 | tf_op jit(solution)/shard_map/pallas_call | solution.py:800
  266.9 18.1 %shard_map.491.refs_7_ = f32[16,384]{1,0:T(8,128)} custom-call(s32[2]{0:T(128)} %pad_add_fusion.place, bf16[8,16,8192]{2,1,0:T(8,128)(2,1)} %fusion.26.refs_5_.refs_0_, bf16[8,16,8192]{2,1,0:T(8,128)(2,1)} %copy-done.15, bf16[3,16,8192]{2,1,0:T(8,128)(2,1)} %collective-permute-done.8.refs_3_.refs_2_, ...), custom_call_target="tpu_custom_call" | custom-call | flops 16000000000 | bytes 1048576 | tf_op jit(solution)/shard_map/pallas_call | solution.py:544
  296.8 28.1 %shard_map.492.refs_8_ = f32[24,384]{1,0:T(8,128)} custom-call(s32[2]{0:T(128)} %pad_add_fusion.place, bf16[8,24,8192]{2,1,0:T(8,128)(2,1)} %copy-done.9, bf16[8,24,8192]{2,1,0:T(8,128)(2,1)} %copy-done.8, bf16[3,24,8192]{2,1,0:T(8,128)(2,1)} %collective-permute-done.14.refs_2_, bf16[3,24,8192]{2,1,0:T(8,128)(2,1)} %collective-permute-done.15.refs_3_, ...), custom_call_target="tpu_custom_call" | custom-call | flops 24000000000 | bytes 1048576 | tf_op jit(solution)/shard_map/pallas_call | solution.py:544
  327.8 12.9 %collective-permute-done.11.refs_2_ = bf16[3,80,4096]{2,1,0:T(8,128)(2,1)S(1)} collective-permute-done((bf16[3,80,4096]{2,1,0:T(8,128)(2,1)}, bf16[3,80,4096]{2,1,0:T(8,128)(2,1)S(1)}, u32[]{:S(2)}, u32[]{:S(2)}) %collective-permute-start.11) | collective-permute-done | bytes 1966112 | tf_op jit(solution)/shard_map/ppermute | solution.py:1458
  343.4 23.6 %shard_map.493.refs_4_ = f32[80,128]{1,0:T(8,128)} custom-call(s32[2]{0:T(128)} %pad_add_fusion.place, bf16[4,4,2,40,4096]{4,3,2,1,0:T(8,128)(2,1)} %bitcast.238, bf16[4,80,4096]{2,1,0:T(8,128)(2,1)} %copy-done.16, bf16[3,80,4096]{2,1,0:T(8,128)(2,1)} %copy-done.50, bf16[3,80,4096]{2,1,0:T(8,128)(2,1)} %copy-done.51, bf16[1152,256]{1,0:T(8,128)(2,1)} %bitcast.296, ...), custom_call_target="tpu_custom_call" | custom-call | flops 20000000000 | bytes 1048576 | tf_op jit(solution)/shard_map/pallas_call | solution.py:544
  375.1 13.8 %shard_map.494.refs_5_ = f32[40,128]{1,0:T(8,128)} custom-call(s32[2]{0:T(128)} %pad_add_fusion.place, bf16[4,4,2,40,4096]{4,3,2,1,0:T(8,128)(2,1)} %bitcast.240, bf16[4,40,4096]{2,1,0:T(8,128)(2,1)} %collective-permute-done.13.refs_1_, bf16[3,40,4096]{2,1,0:T(8,128)(2,1)} %collective-permute-done.16.refs_2_, ...), custom_call_target="tpu_custom_call" | custom-call | flops 10000000000 | bytes 1048576 | tf_op jit(solution)/shard_map/pallas_call | solution.py:544
  390.9 14.2 %shard_map.495.refs_6_ = f32[40,128]{1,0:T(8,128)} custom-call(s32[2]{0:T(128)} %pad_add_fusion.place, bf16[4,4,2,40,4096]{4,3,2,1,0:T(8,128)(2,1)} %bitcast.241, bf16[4,40,4096]{2,1,0:T(8,128)(2,1)} %copy-done.23, bf16[3,40,4096]{2,1,0:T(8,128)(2,1)} %copy-done.52, bf16[3,40,4096]{2,1,0:T(8,128)(2,1)} %copy-done.53, bf16[1152,256]{1,0:T(8,128)(2,1)} %bitcast.298, ...), custom_call_target="tpu_custom_call" | custom-call | flops 10000000000 | bytes 1048576 | tf_op jit(solution)/shard_map/pallas_call | solution.py:544
  405.0 11.0 %shard_map.496 = (f32[160,128]{1,0:T(8,128)}, f32[48,384]{1,0:T(8,128)}, f32[8,128]{1,0:T(8,128)}) custom-call(f32[160,128]{1,0:T(8,128)} %get-tuple-element.170.refs_0_, f32[48,384]{1,0:T(8,128)} %get-tuple-element.173.refs_1_, f32[160,128]{1,0:T(8,128)} %broadcast_in_dim.161.refs_4_.label_ref.refs_2_, ...), custom_call_target="tpu_custom_call" | custom-call | flops 11000000512 | bytes 1048576 | tf_op jit(solution)/shard_map/pallas_call | solution.py:976
  419.6 13.4 %shard_map.498 = (f32[9,48,2048]{2,1,0:T(8,128)}, bf16[8,48,2048]{2,1,0:T(8,128)(2,1)}, f32[8,128]{1,0:T(8,128)}, f32[576,64]{1,0:T(8,128)}, f32[64,32]{1,0:T(8,128)}) custom-call(s32[2]{0:T(128)} %pad_add_fusion.place, f32[11,48,2048]{2,1,0:T(8,128)} %get-tuple-element.210.sum_ref, bf16[11,48,2048]{2,1,0:T(8,128)(2,1)} %pad.37.cot, ...), custom_call_target="tpu_custom_call" | custom-call | flops 17999998976 | bytes 1048576 | tf_op jit(solution)/shard_map/pallas_call | solution.py:1115
  433.0 14.0 %shard_map.497 = (f32[5,160,1024]{2,1,0:T(8,128)}, bf16[4,160,1024]{2,1,0:T(8,128)(2,1)}, f32[8,128]{1,0:T(8,128)}, f32[576,64]{1,0:T(8,128)}, f32[64,32]{1,0:T(8,128)}) custom-call(s32[2]{0:T(128)} %pad_add_fusion.place, f32[7,160,1024]{2,1,0:T(8,128)} %get-tuple-element.199.sum_ref, bf16[7,160,1024]{2,1,0:T(8,128)(2,1)} %bitcast.276, ...), custom_call_target="tpu_custom_call" | custom-call | flops 17999998976 | bytes 1048576 | tf_op jit(solution)/shard_map/pallas_call | solution.py:1115
  451.2 11.0 %shard_map.499.pulled = f32[8,128]{1,0:T(8,128)} custom-call(f32[8,128]{1,0:T(8,128)} %get-tuple-element.209.refs_0_, f32[8,128]{1,0:T(8,128)} %get-tuple-element.214.refs_1_, bf16[4,4,40,1024]{3,2,1,0:T(8,128)(2,1)} %copy-done.19), custom_call_target="tpu_custom_call" | custom-call | flops 12000000000 | bytes 1048576 | tf_op jit(solution)/shard_map/pallas_call | solution.py:219
  462.1 13.3 %shard_map.500 = (bf16[4,160,1024]{2,1,0:T(8,128)(2,1)}, bf16[4,160,1024]{2,1,0:T(8,128)(2,1)}, f32[576,32]{1,0:T(8,128)}, f32[8,128]{1,0:T(8,128)}) custom-call(s32[2]{0:T(128)} %pad_add_fusion.place, f32[5,160,1024]{2,1,0:T(8,128)} %get-tuple-element.205.flow_ref, f32[5,160,1024]{2,1,0:T(8,128)} %get-tuple-element.202.first_ref, ...), custom_call_target="tpu_custom_call" | custom-call | flops 16000000000 | bytes 1048576 | tf_op jit(solution)/shard_map/pallas_call | solution.py:1253
  479.8 14.6 %shard_map.501 = (bf16[8,48,2048]{2,1,0:T(8,128)(2,1)}, bf16[8,48,2048]{2,1,0:T(8,128)(2,1)}, f32[576,32]{1,0:T(8,128)}, f32[8,128]{1,0:T(8,128)}) custom-call(s32[2]{0:T(128)} %pad_add_fusion.place, f32[9,48,2048]{2,1,0:T(8,128)} %get-tuple-element.221.flow_ref, f32[9,48,2048]{2,1,0:T(8,128)} %get-tuple-element.212.first_ref, ...), custom_call_target="tpu_custom_call" | custom-call | flops 16000000000 | bytes 1048576 | tf_op jit(solution)/shard_map/pallas_call | solution.py:1253
  502.2 7.9 %collective-permute-done.21.refs_9_ = bf16[4,160,1024]{2,1,0:T(8,128)(2,1)S(1)} collective-permute-done((bf16[4,160,1024]{2,1,0:T(8,128)(2,1)}, bf16[4,160,1024]{2,1,0:T(8,128)(2,1)S(1)}, u32[]{:S(2)}, u32[]{:S(2)}) %collective-permute-start.21) | collective-permute-done | bytes 1310752 | tf_op jit(solution)/shard_map/ppermute | solution.py:1419
  511.1 21.1 %shard_map.502.refs_0_ = f32[512,128]{1,0:T(8,128)} custom-call(f32[576,32]{1,0:T(8,128)} %get-tuple-element.219.refs_0_, f32[576,32]{1,0:T(8,128)} %get-tuple-element.225.refs_1_, f32[576,64]{1,0:T(8,128)} %get-tuple-element.226.refs_2_, f32[576,64]{1,0:T(8,128)} %get-tuple-element.227.refs_3_, f32[64,32]{1,0:T(8,128)} %get-tuple-element.228.refs_4_, ...), custom_call_target="tpu_custom_call" | custom-call | flops 20000000000 | bytes 1048576 | tf_op jit(solution)/shard_map/pallas_call | solution.py:379
  550.9 10.1 %fusion.10 = f32[320,4,1024]{2,1,0:T(4,128)} fusion(bf16[320,4,1024]{2,1,0:T(4,128)(2,1)S(1)} %copy-done.5, f32[4,2,40,4,1024]{4,3,2,1,0:T(4,128)S(1)} %copy.297, f32[320,1024]{1,0:T(8,128)S(1)} %get-tuple-element.539, f32[320,1024]{1,0:T(8,128)S(1)} %get-tuple-element.538, f32[320,1024]{1,0:T(8,128)S(1)} %get-tuple-element.537, ...), kind=kLoop, calls=%fused_computation.17 | loop fusion | flops 19660800 | bytes 18350080 | tf_op jit(solution)/shard_map/add | solution.py:1797
  (304 shorter events, 235.2 us)
Async XLA Ops:
  5.8 99.5 %collective-permute-start = (bf16[4,160,1024]{2,1,0:T(8,128)(2,1)}, bf16[4,160,1024]{2,1,0:T(8,128)(2,1)}, u32[]{:S(2)}, u32[]{:S(2)}) collective-permute-start(bf16[4,160,1024]{2,1,0:T(8,128)(2,1)} %bitcast.6.refs_1_), channel_id=1, source_target_pairs={{0,1},{1,0},{2,3},{3,2},{4,5},{5,4},{6,7},{7,6},{8,9},{9,8},{10,11... | collective-permute-start | bytes 3932168 | tf_op jit(solution)/shard_map/ppermute | solution.py:1419
  17.6 97.4 %all-to-all-start = ((bf16[4,500,1024]{2,1,0:T(8,128)(2,1)}), bf16[4,500,1024]{2,1,0:T(8,128)(2,1)}, u32[]{:S(2)}, u32[]{:S(2)}) async-start(bf16[4,500,1024]{2,1,0:T(8,128)(2,1)} %pad_maximum_fusion), calls=%async_computation | async-start | bytes 8257536 | tf_op jit(solution)/shard_map/all_to_all | solution.py:1482
  26.3 77.7 %collective-permute-start.1 = (bf16[8,40,2048]{2,1,0:T(8,128)(2,1)}, bf16[8,40,2048]{2,1,0:T(8,128)(2,1)S(1)}, u32[]{:S(2)}, u32[]{:S(2)}) collective-permute-start(bf16[8,40,2048]{2,1,0:T(8,128)(2,1)} %bitcast.233.refs_3_), channel_id=1, source_target_pairs={{0,1},{1,0},{2,3},{3,2},{4,5},{5,4},{6,7},{7,6},{8,9},{9,8},{10,11... | collective-permute-start | bytes 3932168 | tf_op jit(solution)/shard_map/ppermute | solution.py:1419
  40.5 72.5 %collective-permute-start.2 = (bf16[16,8,8192]{2,0,1:T(8,128)(2,1)}, bf16[16,8,8192]{2,0,1:T(8,128)(2,1)}, u32[]{:S(2)}, u32[]{:S(2)}) collective-permute-start(bf16[16,8,8192]{2,0,1:T(8,128)(2,1)} %copy.305), channel_id=1, source_target_pairs={{0,1},{1,0},{2,3},{3,2},{4,5},{5,4},{6,7},{7,6},{8,9},{9,8},{10,11... | collective-permute-start | bytes 6291464 | tf_op jit(solution)/shard_map/ppermute | solution.py:1419
  126.9 24.9 %collective-permute-start.3 = (bf16[6,40,2048]{2,1,0:T(8,128)(2,1)}, bf16[6,40,2048]{2,1,0:T(8,128)(2,1)}, u32[]{:S(2)}, u32[]{:S(2)}) collective-permute-start(bf16[6,40,2048]{2,1,0:T(8,128)(2,1)} %get-tuple-element.148.refs_8_), channel_id=1, source_target_pairs={{0,2},{1,3},{2,0},{3,1},{4,6},{5,7},{6,4},{7,5},{8,10},{9,11},{10,... | collective-permute-start | bytes 2949128 | tf_op jit(solution)/shard_map/ppermute | solution.py:1458
  128.2 26.0 %collective-permute-start.4 = (bf16[6,40,2048]{2,1,0:T(8,128)(2,1)S(1)}, bf16[6,40,2048]{2,1,0:T(8,128)(2,1)}, u32[]{:S(2)}, u32[]{:S(2)}) collective-permute-start(bf16[6,40,2048]{2,1,0:T(8,128)(2,1)S(1)} %copy-done.32), channel_id=1, source_target_pairs={{0,8},{1,9},{2,4},{3,5},{4,2},{5,3},{6,14},{7,15},{8,0},{9,1},{10,... | collective-permute-start | bytes 2949128 | tf_op jit(solution)/shard_map/ppermute | solution.py:1458
  135.0 74.2 %collective-permute-start.7 = (bf16[24,8,8192]{2,0,1:T(8,128)(2,1)}, bf16[24,8,8192]{2,0,1:T(8,128)(2,1)}, u32[]{:S(2)}, u32[]{:S(2)}) collective-permute-start(bf16[24,8,8192]{2,0,1:T(8,128)(2,1)} %copy.307), channel_id=1, source_target_pairs={{0,1},{1,0},{2,3},{3,2},{4,5},{5,4},{6,7},{7,6},{8,9},{9,8},{10,11... | collective-permute-start | bytes 9437192 | tf_op jit(solution)/shard_map/ppermute | solution.py:1419
  135.6 58.4 %collective-permute-start.5 = (bf16[6,160,1024]{2,1,0:T(8,128)(2,1)}, bf16[6,160,1024]{2,1,0:T(8,128)(2,1)}, u32[]{:S(2)}, u32[]{:S(2)}) collective-permute-start(bf16[6,160,1024]{2,1,0:T(8,128)(2,1)} %get-tuple-element.158.refs_6_), channel_id=1, source_target_pairs={{0,2},{1,3},{2,0},{3,1},{4,6},{5,7},{6,4},{7,5},{8,10},{9,11},{10,... | collective-permute-start | bytes 5898248 | tf_op jit(solution)/shard_map/ppermute | solution.py:1458
  138.7 55.3 %collective-permute-start.6 = (bf16[6,160,1024]{2,1,0:T(8,128)(2,1)}, bf16[6,160,1024]{2,1,0:T(8,128)(2,1)}, u32[]{:S(2)}, u32[]{:S(2)}) collective-permute-start(bf16[6,160,1024]{2,1,0:T(8,128)(2,1)} %get-tuple-element.159.refs_7_), channel_id=1, source_target_pairs={{0,8},{1,9},{2,4},{3,5},{4,2},{5,3},{6,14},{7,15},{8,0},{9,1},{10,... | collective-permute-start | bytes 5898248 | tf_op jit(solution)/shard_map/ppermute | solution.py:1458
  177.0 33.5 %collective-permute-start.8 = (bf16[3,16,8192]{2,1,0:T(8,128)(2,1)}, bf16[3,16,8192]{2,1,0:T(8,128)(2,1)}, u32[]{:S(2)}, u32[]{:S(2)}) collective-permute-start(bf16[3,16,8192]{2,1,0:T(8,128)(2,1)} %get-tuple-element.483), channel_id=1, source_target_pairs={{0,2},{1,3},{2,0},{3,1},{4,6},{5,7},{6,4},{7,5},{8,10},{9,11},{10,... | collective-permute-start | bytes 2359304 | tf_op jit(solution)/shard_map/ppermute | solution.py:1458
  178.4 32.2 %collective-permute-start.9 = (bf16[3,16,8192]{2,1,0:T(8,128)(2,1)}, bf16[3,16,8192]{2,1,0:T(8,128)(2,1)}, u32[]{:S(2)}, u32[]{:S(2)}) collective-permute-start(bf16[3,16,8192]{2,1,0:T(8,128)(2,1)} %get-tuple-element.482), channel_id=1, source_target_pairs={{0,8},{1,9},{2,4},{3,5},{4,2},{5,3},{6,14},{7,15},{8,0},{9,1},{10,... | collective-permute-start | bytes 2359304 | tf_op jit(solution)/shard_map/ppermute | solution.py:1458
  230.4 66.3 %collective-permute-start.14 = (bf16[3,24,8192]{2,1,0:T(8,128)(2,1)}, bf16[3,24,8192]{2,1,0:T(8,128)(2,1)}, u32[]{:S(2)}, u32[]{:S(2)}) collective-permute-start(bf16[3,24,8192]{2,1,0:T(8,128)(2,1)} %get-tuple-element.481), channel_id=1, source_target_pairs={{0,2},{1,3},{2,0},{3,1},{4,6},{5,7},{6,4},{7,5},{8,10},{9,11},{10,... | collective-permute-start | bytes 3538952 | tf_op jit(solution)/shard_map/ppermute | solution.py:1458
  231.1 65.7 %collective-permute-start.15 = (bf16[3,24,8192]{2,1,0:T(8,128)(2,1)}, bf16[3,24,8192]{2,1,0:T(8,128)(2,1)}, u32[]{:S(2)}, u32[]{:S(2)}) collective-permute-start(bf16[3,24,8192]{2,1,0:T(8,128)(2,1)} %get-tuple-element.480), channel_id=1, source_target_pairs={{0,8},{1,9},{2,4},{3,5},{4,2},{5,3},{6,14},{7,15},{8,0},{9,1},{10,... | collective-permute-start | bytes 3538952 | tf_op jit(solution)/shard_map/ppermute | solution.py:1458
  231.1 59.9 %collective-permute-start.10 = (bf16[4,80,4096]{2,1,0:T(8,128)(2,1)}, bf16[4,80,4096]{2,1,0:T(8,128)(2,1)S(1)}, u32[]{:S(2)}, u32[]{:S(2)}) collective-permute-start(bf16[4,80,4096]{2,1,0:T(8,128)(2,1)} %bitcast.53), channel_id=1, source_target_pairs={{0,1},{1,0},{2,3},{3,2},{4,5},{5,4},{6,7},{7,6},{8,9},{9,8},{10,11... | collective-permute-start | bytes 7864328 | tf_op jit(solution)/shard_map/ppermute | solution.py:1419
  231.9 93.0 %collective-permute-start.13 = (bf16[4,40,4096]{2,1,0:T(8,128)(2,1)}, bf16[4,40,4096]{2,1,0:T(8,128)(2,1)}, u32[]{:S(2)}, u32[]{:S(2)}) collective-permute-start(bf16[4,40,4096]{2,1,0:T(8,128)(2,1)} %get-tuple-element.178), channel_id=1, source_target_pairs={{0,1},{1,0},{2,3},{3,2},{4,5},{5,4},{6,7},{7,6},{8,9},{9,8},{10,11... | collective-permute-start | bytes 3932168 | tf_op jit(solution)/shard_map/ppermute | solution.py:1419
  233.1 133.8 %collective-permute-start.18 = (bf16[4,40,4096]{2,1,0:T(8,128)(2,1)}, bf16[4,40,4096]{2,1,0:T(8,128)(2,1)S(1)}, u32[]{:S(2)}, u32[]{:S(2)}) collective-permute-start(bf16[4,40,4096]{2,1,0:T(8,128)(2,1)} %get-tuple-element.188), channel_id=1, source_target_pairs={{0,1},{1,0},{2,3},{3,2},{4,5},{5,4},{6,7},{7,6},{8,9},{9,8},{10,11... | collective-permute-start | bytes 3932168 | tf_op jit(solution)/shard_map/ppermute | solution.py:1419
  293.6 47.1 %collective-permute-start.11 = (bf16[3,80,4096]{2,1,0:T(8,128)(2,1)}, bf16[3,80,4096]{2,1,0:T(8,128)(2,1)S(1)}, u32[]{:S(2)}, u32[]{:S(2)}) collective-permute-start(bf16[3,80,4096]{2,1,0:T(8,128)(2,1)} %get-tuple-element.479), channel_id=1, source_target_pairs={{0,2},{1,3},{2,0},{3,1},{4,6},{5,7},{6,4},{7,5},{8,10},{9,11},{10,... | collective-permute-start | bytes 5898248 | tf_op jit(solution)/shard_map/ppermute | solution.py:1458
  296.8 43.9 %collective-permute-start.12 = (bf16[3,80,4096]{2,1,0:T(8,128)(2,1)}, bf16[3,80,4096]{2,1,0:T(8,128)(2,1)S(1)}, u32[]{:S(2)}, u32[]{:S(2)}) collective-permute-start(bf16[3,80,4096]{2,1,0:T(8,128)(2,1)} %get-tuple-element.478), channel_id=1, source_target_pairs={{0,8},{1,9},{2,4},{3,5},{4,2},{5,3},{6,14},{7,15},{8,0},{9,1},{10,... | collective-permute-start | bytes 5898248 | tf_op jit(solution)/shard_map/ppermute | solution.py:1458
  327.2 48.0 %collective-permute-start.16 = (bf16[3,40,4096]{2,1,0:T(8,128)(2,1)S(1)}, bf16[3,40,4096]{2,1,0:T(8,128)(2,1)}, u32[]{:S(2)}, u32[]{:S(2)}) collective-permute-start(bf16[3,40,4096]{2,1,0:T(8,128)(2,1)S(1)} %get-tuple-element.471), channel_id=1, source_target_pairs={{0,2},{1,3},{2,0},{3,1},{4,6},{5,7},{6,4},{7,5},{8,10},{9,11},{10,... | collective-permute-start | bytes 2949128 | tf_op jit(solution)/shard_map/ppermute | solution.py:1458
  327.6 47.5 %collective-permute-start.17 = (bf16[3,40,4096]{2,1,0:T(8,128)(2,1)S(1)}, bf16[3,40,4096]{2,1,0:T(8,128)(2,1)}, u32[]{:S(2)}, u32[]{:S(2)}) collective-permute-start(bf16[3,40,4096]{2,1,0:T(8,128)(2,1)S(1)} %get-tuple-element.470), channel_id=1, source_target_pairs={{0,8},{1,9},{2,4},{3,5},{4,2},{5,3},{6,14},{7,15},{8,0},{9,1},{10,... | collective-permute-start | bytes 2949128 | tf_op jit(solution)/shard_map/ppermute | solution.py:1458
  416.0 34.1 %all-to-all-start.1 = ((bf16[4,4,40,1024]{3,2,1,0:T(8,128)(2,1)}), bf16[4,4,40,1024]{3,2,1,0:T(8,128)(2,1)S(1)}, u32[]{:S(2)}, u32[]{:S(2)}) async-start(bf16[4,4,40,1024]{3,2,1,0:T(8,128)(2,1)} %bitcast.232), calls=%async_computation.1 | async-start | bytes 2621440 | tf_op jit(solution)/shard_map/all_to_all | solution.py:1482
  475.5 25.3 %all-to-all-start.2 = ((bf16[4,4,10,2048]{3,1,2,0:T(4,128)(2,1)}), bf16[4,4,10,2048]{3,1,2,0:T(4,128)(2,1)S(1)}, u32[]{:S(2)}, u32[]{:S(2)}) async-start(bf16[4,4,10,2048]{3,1,2,0:T(4,128)(2,1)} %bitcast.69), calls=%async_computation.2 | async-start | bytes 1310720 | tf_op jit(solution)/shard_map/all_to_all | solution.py:1482
  479.0 31.1 %collective-permute-start.21 = (bf16[4,160,1024]{2,1,0:T(8,128)(2,1)}, bf16[4,160,1024]{2,1,0:T(8,128)(2,1)S(1)}, u32[]{:S(2)}, u32[]{:S(2)}) collective-permute-start(bf16[4,160,1024]{2,1,0:T(8,128)(2,1)} %get-tuple-element.232), channel_id=1, source_target_pairs={{0,1},{1,0},{2,3},{3,2},{4,5},{5,4},{6,7},{7,6},{8,9},{9,8},{10,11... | collective-permute-start | bytes 3932168 | tf_op jit(solution)/shard_map/ppermute | solution.py:1419
  536.7 31.1 %collective-permute-start.22 = (bf16[8,40,2048]{2,1,0:T(8,128)(2,1)}, bf16[8,40,2048]{2,1,0:T(8,128)(2,1)}, u32[]{:S(2)}, u32[]{:S(2)}) collective-permute-start(bf16[8,40,2048]{2,1,0:T(8,128)(2,1)} %slice.354.refs_11_), channel_id=1, source_target_pairs={{0,1},{1,0},{2,3},{3,2},{4,5},{5,4},{6,7},{7,6},{8,9},{9,8},{10,11... | collective-permute-start | bytes 3932168 | tf_op jit(solution)/shard_map/ppermute | solution.py:1419
  (60 other events, 474.8 us)
